TPU v7x, 256 devices: a whole 4x4x8 slice. The times are simulated.
256 devices in a mesh: cuts: 4 (over y_hi, core), fsdp: 64 (over y_lo, z, x).
Axes of the slice: x: 4, y: 4 (y_hi: 2, y_lo: 2; y = y_hi * 2 + y_lo), z: 8, core: 2. Of those that a mesh axis runs over, the one named last changes fastest.
Arguments:
- hid_shared: bfloat16 [196608, 1536], P(('cuts', 'fsdp')), may hold values from -24 to 24
- hid_routed: bfloat16 [24576, 768], P(('cuts', 'fsdp')), may hold values from -96 to 96
- out_grad: bfloat16 [196608, 2560], P(('cuts', 'fsdp')), may hold values from -0.040527344 to 0.040527344
- slot_token: int32 [24576], P(('cuts', 'fsdp')), may hold values from 0 to 767, as said below
- slot_count: int32 [256], P(('cuts', 'fsdp')), may hold values from 24 to 96, as said below
- master_shared: float32 [1536, 2560], P(('cuts', 'fsdp')), may hold values from -6 to 6
- moment_shared: float32 [1536, 2560], P(('cuts', 'fsdp')), may hold values from -1.8 to 1.8
- second_shared: float32 [1536, 2560], P(('cuts', 'fsdp')), may hold values from 0.01 to 1
- master_routed: float32 [768, 2560], P(('cuts', 'fsdp')), may hold values from -6 to 6
- moment_routed: float32 [768, 2560], P(('cuts', 'fsdp')), may hold values from -1.8 to 1.8
- second_routed: float32 [768, 2560], P(('cuts', 'fsdp')), may hold values from 0.01 to 1
Outputs:
- new_moment_shared: float32 [1536, 2560], P(('cuts', 'fsdp'))
- new_second_shared: float32 [1536, 2560], P(('cuts', 'fsdp'))
- new_moment_routed: float32 [768, 2560], P(('cuts', 'fsdp'))
- new_second_routed: float32 [768, 2560], P(('cuts', 'fsdp'))
- weight_shared: bfloat16 [1536, 2560], P('cuts')
- weight_routed: bfloat16 [768, 2560], P('cuts')
Inputs may be any that keep to these rules, and one draw needn't show every extreme that they name: `slot_token`: within one device the 96 slots name distinct tokens of that device. `slot_count`: at least one device has all 96 slots live.
All inputs are finite; a program needn't handle non-finite values.
Results may differ from a plain program's by a relative error of at most 0.001.
Values may be sent and summed in bfloat16 or wider, within the bound.
No kernel may reach another device: no remote copies, remote signals or barrier semaphores. Data moves between devices by JAX's collectives and lax.ppermute only.
A program may use at most 192 MiB of HBM per device.

v0:
```python
import jax
import jax.numpy as jnp
import numpy as np
from jax import lax
from jax.experimental import pallas as pl
from jax.experimental.pallas import tpu as pltpu
from jax.sharding import Mesh, PartitionSpec as P

AXES = ("yh", "core", "yl", "z", "x")
NX, NY, NZ = 4, 4, 8
SCALE = 0.25
BF = jnp.bfloat16
F32 = jnp.float32
F16 = jnp.float16


def adamw(grad, master, moment, second):
    corr_one = 1.0 - 0.9**20
    corr_two = 1.0 - 0.95**20
    new_moment = 0.9 * moment + 0.1 * grad
    new_second = 0.95 * second + 0.05 * grad * grad
    step_dir = new_moment / corr_one / (jnp.sqrt(new_second / corr_two) + 1e-08)
    new_master = master - 0.02 * (step_dir + 0.1 * master)
    return (new_moment, new_second, new_master.astype(BF))


def x_ring(v, d):
    return lax.ppermute(v, "x", [(i, (i + d) % NX) for i in range(NX)])


def y_ring(v, d):
    return lax.ppermute(v, ("yh", "yl"), [(i, (i + d) % NY) for i in range(NY)])


def y_swap(v):
    return lax.ppermute(v, "yl", [(0, 1), (1, 0)])


def core_swap(v):
    return lax.ppermute(v, "core", [(0, 1), (1, 0)])


def row_order(sr, rr):
    rows = sr + rr
    n = NX * 2 * NZ * rows
    xs, ys, zs, i = np.meshgrid(np.arange(NX), np.arange(2), np.arange(NZ), np.arange(rows), indexing="ij")
    dev = (ys * NZ + zs) * NX + xs
    flat = np.arange(n)
    keep = (i < sr).reshape(-1)
    shared = np.zeros((n, 2 * NZ * NX * sr), np.float32)
    shared[flat[keep], (dev * sr + i).reshape(-1)[keep]] = 1
    routed = np.zeros((2, n, 2, 2 * NZ * NX * rr), np.float32)
    for core in range(2):
        routed[core, flat[~keep], core, (dev * rr + i - sr).reshape(-1)[~keep]] = 1
    return shared.astype(BF), routed.reshape(2, n, -1).astype(BF)


def dot_t(a, b):
    return lax.dot_general(a, b, (((1,), (1,)), ((), ())), preferred_element_type=F32)


def dot(a, b):
    return jnp.dot(a, b, preferred_element_type=F32)


def order_kernel(core_ref, count_ref, token_ref, shared_ref, routed_ref, shared_order_ref, routed_order_ref, out_ref):
    tok, slots = shared_ref.shape[0], routed_ref.shape[0]
    names = lax.broadcasted_iota(jnp.int32, (tok, slots), 0) == token_ref[...]
    live = lax.broadcasted_iota(jnp.int32, (tok, slots), 1) < count_ref[0]
    place = jnp.where(names & live, 1.0, 0.0).astype(BF)
    slot_rows = dot_t(routed_order_ref[0], routed_ref[...]).astype(BF)
    total = dot_t(shared_order_ref[...], shared_ref[...]) + dot_t(slot_rows, place)
    out_ref[...] = total.astype(BF).reshape(out_ref.shape)


def ordered(core, count, token, hid_shared, hid_routed, shared_order, routed_order):
    tok = hid_shared.shape[0]
    slots = hid_routed.shape[0]
    n, cut = shared_order.shape
    pair = routed_order.shape[2]
    return pl.pallas_call(
        order_kernel,
        grid_spec=pltpu.PrefetchScalarGridSpec(
            num_scalar_prefetch=2,
            grid=(2,),
            in_specs=[
                pl.BlockSpec((1, slots), lambda h, c, m: (0, 0)),
                pl.BlockSpec((tok, cut), lambda h, c, m: (0, h * 2 + c[0])),
                pl.BlockSpec((slots, pair), lambda h, c, m: (0, h)),
                pl.BlockSpec((n, cut), lambda h, c, m: (0, 0)),
                pl.BlockSpec((1, n, pair), lambda h, c, m: (c[0], 0, 0)),
            ],
            out_specs=pl.BlockSpec((NX, 1, n // NX, tok), lambda h, c, m: (0, h, 0, 0)),
        ),
        out_shape=jax.ShapeDtypeStruct((NX, 2, n // NX, tok), BF),
        compiler_params=pltpu.CompilerParams(vmem_limit_bytes=56 * 2**20),
        cost_estimate=pl.CostEstimate(flops=8 * n * cut * tok, bytes_accessed=6 * n * tok, transcendentals=0),
    )(core.reshape(1), count, token.reshape(1, slots), hid_shared, hid_routed, shared_order, routed_order)


def local(
    hid_shared,
    hid_routed,
    out_grad,
    slot_token,
    slot_count,
    master_shared,
    moment_shared,
    second_shared,
    master_routed,
    moment_routed,
    second_routed,
):
    tok, width = out_grad.shape
    slots = hid_routed.shape[0]
    sr, rr = master_shared.shape[0], master_routed.shape[0]
    rows = sr + rr
    half = width // 2
    group = NZ * rows
    core = lax.axis_index("core")
    x = lax.axis_index("x")
    yh, yl = lax.axis_index("yh"), lax.axis_index("yl")
    y = yh * 2 + yl

    shared_order, routed_order = (jnp.asarray(v) for v in row_order(sr, rr))
    def activ(k):
        rows_of = ordered(k, slot_count, slot_token, hid_shared, hid_routed, shared_order, routed_order)
        return rows_of.reshape(NX, NY, group, tok)

    out_far = core_swap(out_grad)
    act_far = core_swap(activ(1 - core))
    act_near = activ(core)

    def first(part):
        def lined(v):
            return (v.swapaxes(0, 1) if part else v).reshape(-1, tok)

        cols = slice(part * half, (part + 1) * half)
        total = dot(lined(act_near), out_grad[:, cols]) + dot(lined(act_far), out_far[:, cols])
        return (SCALE * total).astype(F16).reshape(4, 4 * group, half)

    def reduce_x(v):
        return lax.all_to_all(v, "x", 0, 0).astype(F32).sum(axis=0).astype(F16)

    def reduce_y(v):
        def pick(step):
            return lax.dynamic_index_in_dim(v, (y + step) % NY, 0, keepdims=False)

        back = [y_ring(pick(d), d) for d in (2, 1, 3)]
        return sum((b.astype(F32) for b in back), pick(0).astype(F32)).astype(F16)

    one_a, one_b = reduce_x(first(0)), reduce_y(first(1))
    two = [reduce_y(one_a.reshape(NY, group, half)), reduce_x(one_b.reshape(NX, group, half))]
    last = jnp.concatenate(two, axis=1).reshape(NZ, rows * width // 128, 128)
    last = lax.all_to_all(last, "z", 0, 0)
    grad = (last.astype(F32).sum(axis=0) * (1.0 / SCALE)).reshape(rows, width)

    moment_s, second_s, weight_s = adamw(grad[:sr], master_shared, moment_shared, second_shared)
    moment_r, second_r, weight_r = adamw(grad[sr:], master_routed, moment_routed, second_routed)

    weight = jnp.concatenate([weight_s, weight_r], axis=0).reshape(1, rows * width // 128, 128)
    weight = lax.all_to_all(jnp.broadcast_to(weight, (NZ,) + weight.shape[1:]), "z", 0, 0)
    weight = weight.reshape(group, width)
    one_a, one_b = weight[:, :half], weight[:, half:]
    one_a = jnp.concatenate([one_a, y_swap(one_a)], axis=0)
    one_b = jnp.concatenate([one_b] + [x_ring(one_b, d) for d in (1, 2, 3)], axis=0)
    all_a = [one_a] + [x_ring(one_a, d) for d in (1, 2, 3)]
    all_b = [one_b, y_swap(one_b)]

    def want(count, low, index):
        r = lax.iota(jnp.int32, 2 * NZ * NX * count)
        back = (x - (r // count) % NX) % NX
        zz = (r // (count * NX)) % NZ
        flip = (r // (count * NX * NZ)) ^ yl
        return (index(back, flip) * NZ + zz) * rows + low + r % count

    def wanted(index, blocks):
        r = jnp.concatenate([want(sr, 0, index), want(rr, sr, index)])
        r = lax.optimization_barrier(r)
        n = r.shape[0]
        q = lax.broadcasted_iota(jnp.int32, (blocks, n, n // blocks), 0) * (n // blocks)
        q = q + lax.broadcasted_iota(jnp.int32, q.shape, 2)
        return (r[None, :, None] == q).astype(BF)

    take_a = wanted(lambda back, flip: back * 2 + flip, len(all_a))
    take_b = wanted(lambda back, flip: flip * NX + back, len(all_b))
    shared, routed = settled(take_a, take_b, all_a, all_b, 2 * NZ * NX * sr)
    return (moment_s, second_s, moment_r, second_r, shared, routed)


def settle_kernel(take_a, take_b, *refs):
    a, b, (shared, routed) = refs[:4], refs[4:6], refs[6:]
    split = shared.shape[0]

    def put(take, blocks):
        total = sum(dot(take[k], v[...]) for k, v in enumerate(blocks)).astype(BF)
        shared[...] = total[:split]
        routed[...] = total[split:]

    first = pl.program_id(0) < pl.num_programs(0) // 2

    @pl.when(first)
    def _():
        put(take_a, a)

    @pl.when(jnp.logical_not(first))
    def _():
        put(take_b, b)


def settled(take_a, take_b, all_a, all_b, split):
    n = take_a.shape[1]
    half = all_a[0].shape[1]
    tile = 256
    steps = half // tile

    def tiles(v, low):
        return pl.BlockSpec((v.shape[0], tile), lambda j: (0, jnp.clip(j - low, 0, steps - 1)))

    def whole(v):
        return pl.BlockSpec(v.shape, lambda j: (0, 0, 0))

    return pl.pallas_call(
        settle_kernel,
        grid=(2 * steps,),
        in_specs=[whole(take_a), whole(take_b)] + [tiles(v, 0) for v in all_a] + [tiles(v, steps) for v in all_b],
        out_specs=[pl.BlockSpec((split, tile), lambda j: (0, j)), pl.BlockSpec((n - split, tile), lambda j: (0, j))],
        out_shape=[jax.ShapeDtypeStruct((split, 2 * half), BF), jax.ShapeDtypeStruct((n - split, 2 * half), BF)],
        compiler_params=pltpu.CompilerParams(vmem_limit_bytes=32 * 2**20),
    )(take_a, take_b, *all_a, *all_b)


def solution(mesh):
    fine = Mesh(mesh.devices.reshape(2, 2, 2, NZ, NX), AXES)
    split = P(AXES, None)
    flat = P(AXES)
    cuts = P(("yh", "core"), None)
    return jax.shard_map(
        local,
        mesh=fine,
        in_specs=(split, split, split, flat, flat) + (split,) * 6,
        out_specs=(split,) * 4 + (cuts,) * 2,
        check_vma=False,
    )
```

profile of v0, /device:TPU:16, one launch (start us, length us, event | category | flops | bytes accessed | tf_op | source)
XLA Modules:
  0.0 174.2 jit_solution(8050779777628604578)
XLA Ops:
  1.4 4.8 %shard_map.173 = bf16[4,2,144,768]{3,2,1,0:T(8,128)(2,1)} custom-call(s32[1]{0:T(128)} %bitcast.3.core_ref, s32[1]{0:T(128)S(6)} %copy.23.count_ref, s32[1,96]{1,0:T(1,128)} %bitcast.51, bf16[768,1536]{1,0:T(8,128)(2,1)} %shared_ref.3, bf16[96,768]{1,0:T(8,128)(2,1)} %routed_ref.3, bf16[576,384]{1,0:T(8,128)(2,1)} %constant.257.clone.shared_order_ref, ...), custom_call_target="tpu_custom_call" | custom-call | flops 1358954496 | bytes 2654208 | tf_op jit(solution)/shard_map/pallas_call | solution.py:81
  6.2 0.5 collective-permute-start
  6.7 4.8 %shard_map.172 = bf16[4,2,144,768]{3,2,1,0:T(8,128)(2,1)} custom-call(s32[1]{0:T(128)} %bitcast.core_ref, s32[1]{0:T(128)S(6)} %copy.23.count_ref, s32[1,96]{1,0:T(1,128)} %bitcast.52, bf16[768,1536]{1,0:T(8,128)(2,1)} %shared_ref.3, bf16[96,768]{1,0:T(8,128)(2,1)} %routed_ref.3, bf16[576,384]{1,0:T(8,128)(2,1)} %constant.257.clone.shared_order_ref, ...), custom_call_target="tpu_custom_call" | custom-call | flops 1358954496 | bytes 2654208 | tf_op jit(solution)/shard_map/pallas_call | solution.py:81
  11.4 3.0 %copy.21 = bf16[4,4,72,768]{3,2,0,1:T(8,128)(2,1)} copy(bf16[4,4,72,768]{3,2,1,0:T(8,128)(2,1)} %bitcast.38) | data formatting | bytes 3538944 | tf_op jit(solution)/shard_map/reshape | solution.py:128
  14.4 4.2 %fusion.9 = f32[1152,1280]{1,0:T(8,128)S(1)} fusion(bf16[1152,768]{1,0:T(8,128)(2,1)S(1)} %bitcast.39, bf16[768,2560]{1,0:T(8,128)(2,1)} %param.15), kind=kOutput, calls=%fused_computation.13 | convolution fusion | flops 2264924160 | bytes 9633792 | tf_op jit(solution)/shard_map/dot_general | solution.py:63
  18.6 5.0 %fusion.7 = f32[1152,1280]{1,0:T(8,128)} fusion(bf16[1152,768]{1,0:T(8,128)(2,1)S(1)} %bitcast.49, bf16[768,2560]{1,0:T(8,128)(2,1)S(1)} %copy-done.9), kind=kOutput, calls=%fused_computation.11 | convolution fusion | flops 2264924160 | bytes 9633792 | tf_op jit(solution)/shard_map/dot_general | solution.py:63
  23.6 1.3 copy.22
  25.0 5.8 %fusion.2 = f16[1152,1280]{1,0:T(8,128)(2,1)} fusion(f32[1152,1280]{1,0:T(8,128)S(1)} %fusion.9, bf16[1152,768]{1,0:T(8,128)(2,1)S(1)} %bitcast.47, bf16[768,2560]{1,0:T(8,128)(2,1)} %collective-permute-done.1), kind=kOutput, calls=%fused_computation.4 | convolution fusion | flops 2269347840 | bytes 12582912 | tf_op jit(solution)/shard_map/dot_general | solution.py:63
  30.7 4.3 %all-to-all-start = ((f16[4,288,1280]{2,1,0:T(8,128)(2,1)}), f16[4,288,1280]{2,1,0:T(8,128)(2,1)S(1)}, u32[]{:S(2)}, u32[]{:S(2)}) async-start(f16[4,288,1280]{2,1,0:T(8,128)(2,1)} %bitcast.40), calls=%async_computation | async-start | bytes 5898240 | tf_op jit(solution)/shard_map/all_to_all | solution.py:143
  35.0 6.3 %fusion.3 = f16[1152,1280]{1,0:T(8,128)(2,1)S(1)} fusion(f32[1152,1280]{1,0:T(8,128)} %fusion.7, bf16[1152,768]{1,0:T(8,128)(2,1)} %bitcast.50, bf16[768,2560]{1,0:T(8,128)(2,1)} %collective-permute-done.1), kind=kOutput, calls=%fused_computation.5 | convolution fusion | flops 2269347840 | bytes 12582912 | tf_op jit(solution)/shard_map/dot_general | solution.py:63
  41.3 1.8 %dynamic-slice_bitcast_fusion.2 = (f16[288,1280]{1,0:T(8,128)(2,1)}, f16[288,1280]{1,0:T(8,128)(2,1)}, f16[288,1280]{1,0:T(8,128)(2,1)}) fusion(f16[4,288,1280]{2,1,0:T(8,128)(2,1)S(1)} %bitcast.41, s32[]{:T(128)S(6)} %select_n.140, s32[]{:T(128)S(6)} %select_n.144, s32[]{:T(128)S(6)} %select_n.142), kind=kLoop, calls=%fused_computation.26 | loop fusion | bytes 4423692 | tf_op jit(solution)/shard_map/jit(dynamic_index_in_dim)/squeeze | solution.py:147
  43.1 0.5 copy-done.1
  43.6 1.5 collective-permute-start.5
  45.0 1.0 collective-permute-start.6
  46.1 1.0 collective-permute-start.7
  47.1 17.7 %collective-permute-done.5 = f16[288,1280]{1,0:T(8,128)(2,1)} collective-permute-done((f16[288,1280]{1,0:T(8,128)(2,1)}, f16[288,1280]{1,0:T(8,128)(2,1)}, u32[]{:S(2)}, u32[]{:S(2)}) %collective-permute-start.5) | collective-permute-done | bytes 737312 | tf_op jit(solution)/shard_map/ppermute | solution.py:32
  64.8 14.5 %collective-permute-done.6 = f16[288,1280]{1,0:T(8,128)(2,1)} collective-permute-done((f16[288,1280]{1,0:T(8,128)(2,1)}, f16[288,1280]{1,0:T(8,128)(2,1)}, u32[]{:S(2)}, u32[]{:S(2)}) %collective-permute-start.6) | collective-permute-done | bytes 737312 | tf_op jit(solution)/shard_map/ppermute | solution.py:32
  79.3 3.1 %fusion.14 = f16[288,1280]{1,0:T(8,128)(2,1)} fusion(f16[288,1280]{1,0:T(8,128)(2,1)} %collective-permute-done.7, f16[288,1280]{1,0:T(8,128)(2,1)} %collective-permute-done.6, f16[288,1280]{1,0:T(8,128)(2,1)} %collective-permute-done.5, f16[4,288,1280]{2,1,0:T(8,128)(2,1)} %bitcast.42, s32[]{:T(128)S(6)} %select_n.138), kind=kLoop, calls=%fused_computation.20 | loop fusion | flops 2949120 | bytes 3686404 | tf_op jit(solution)/shard_map/convert_element_type | solution.py:150
  82.3 4.5 %all-to-all-start.1 = ((f16[4,72,1280]{2,1,0:T(8,128)(2,1)}), f16[4,72,1280]{2,1,0:T(8,128)(2,1)}, u32[]{:S(2)}, u32[]{:S(2)}) async-start(f16[4,72,1280]{2,1,0:T(8,128)(2,1)} %bitcast.45), calls=%async_computation.1 | async-start | bytes 1474560 | tf_op jit(solution)/shard_map/all_to_all | solution.py:143
  86.8 0.4 convert_reduce_fusion
  87.4 1.9 %collective-permute-start.2 = (f16[72,1280]{1,0:T(8,128)(2,1)S(1)}, f16[72,1280]{1,0:T(8,128)(2,1)S(1)}, u32[]{:S(2)}, u32[]{:S(2)}) collective-permute-start(f16[72,1280]{1,0:T(8,128)(2,1)S(1)} %get-tuple-element.19), channel_id=1, source_target_pairs={{0,128},{32,160},{128,0},{160,32},{1,129},{33,161},{129,1},{161,33... | collective-permute-start | bytes 552968 | tf_op jit(solution)/shard_map/ppermute | solution.py:32
  89.3 1.0 collective-permute-start.3
  90.2 1.1 collective-permute-start.4
  91.3 7.5 %all-to-all-done.1 = f16[4,72,1280]{2,1,0:T(8,128)(2,1)} async-done(((f16[4,72,1280]{2,1,0:T(8,128)(2,1)}), f16[4,72,1280]{2,1,0:T(8,128)(2,1)}, u32[]{:S(2)}, u32[]{:S(2)}) %all-to-all-start.1) | async-done | bytes 737312 | tf_op jit(solution)/shard_map/all_to_all | solution.py:143
  98.8 1.3 convert_reduce_fusion.1
  100.4 0.5 reshape.77
  100.9 20.3 %all_to_all.20 = f16[8,180,128]{2,1,0:T(8,128)(2,1)S(1)} all-to-all(f16[8,180,128]{2,1,0:T(8,128)(2,1)S(1)} %reshape.77), channel_id=1, replica_groups=mesh['yh'=2,'core'=2,'yl'=2,'z'=8,'x'=4] {'z'}, dimensions={0} | all-to-all | bytes 737280 | tf_op jit(solution)/shard_map/all_to_all | solution.py:155
  121.4 0.7 subtract_convert_fusion
  122.1 0.7 subtract_convert_fusion.1
  122.9 0.8 broadcast_in_dim.10
  123.7 3.4 %all-to-all-start.3 = ((bf16[8,180,128]{2,1,0:T(8,128)(2,1)}), bf16[8,180,128]{2,1,0:T(8,128)(2,1)S(1)}, u32[]{:S(2)}, u32[]{:S(2)}) async-start(bf16[8,180,128]{2,1,0:T(8,128)(2,1)} %broadcast_in_dim.10), calls=%async_computation.3 | async-start | bytes 753664 | tf_op jit(solution)/shard_map/all_to_all | solution.py:162
  127.2 12.0 %all-to-all-done.3 = bf16[8,180,128]{2,1,0:T(8,128)(2,1)S(1)} async-done(((bf16[8,180,128]{2,1,0:T(8,128)(2,1)}), bf16[8,180,128]{2,1,0:T(8,128)(2,1)S(1)}, u32[]{:S(2)}, u32[]{:S(2)}) %all-to-all-start.3) | async-done | bytes 368672 | tf_op jit(solution)/shard_map/all_to_all | solution.py:162
  139.2 0.4 reshape.78
  139.7 1.5 collective-permute-start.12
  141.2 2.7 %collective-permute-start.13 = (bf16[72,1280]{1,0:T(8,128)(2,1)S(1)}, bf16[72,1280]{1,0:T(8,128)(2,1)S(1)}, u32[]{:S(2)}, u32[]{:S(2)}) collective-permute-start(bf16[72,1280]{1,0:T(8,128)(2,1)S(1)} %get-tuple-element.22), channel_id=1, source_target_pairs={{0,2},{1,3},{2,0},{3,1},{4,6},{5,7},{6,4},{7,5},{8,10},{9,11},{10,... | collective-permute-start | bytes 552968 | tf_op jit(solution)/shard_map/ppermute | solution.py:28
  143.8 1.5 collective-permute-start.14
  145.3 3.0 %collective-permute-start.8 = (bf16[72,1280]{1,0:T(8,128)(2,1)S(1)}, bf16[72,1280]{1,0:T(8,128)(2,1)S(1)}, u32[]{:S(2)}, u32[]{:S(2)}) collective-permute-start(bf16[72,1280]{1,0:T(8,128)(2,1)S(1)} %get-tuple-element.23), channel_id=1, source_target_pairs={{0,32},{32,0},{1,33},{33,1},{2,34},{34,2},{3,35},{35,3},{4,36},{36... | collective-permute-start | bytes 552968 | tf_op jit(solution)/shard_map/ppermute | solution.py:36
  148.3 1.1 collective-permute-done.13
  149.4 3.3 %collective-permute-start.15 = (bf16[288,1280]{1,0:T(8,128)(2,1)S(1)}, bf16[288,1280]{1,0:T(8,128)(2,1)S(1)}, u32[]{:S(2)}, u32[]{:S(2)}) collective-permute-start(bf16[288,1280]{1,0:T(8,128)(2,1)S(1)} %pad_maximum_fusion.refs_4_), channel_id=1, source_target_pairs={{0,32},{32,0},{1,33},{33,1},{2,34},{34,2},{3,35},{35,3},{4,36},{36... | collective-permute-start | bytes 2211848 | tf_op jit(solution)/shard_map/ppermute | solution.py:36
  152.8 0.2 fusion.11.take_b
  153.0 0.8 collective-permute-done.8
  153.8 2.7 %collective-permute-start.10 = (bf16[144,1280]{1,0:T(8,128)(2,1)S(1)}, bf16[144,1280]{1,0:T(8,128)(2,1)S(1)}, u32[]{:S(2)}, u32[]{:S(2)}) collective-permute-start(bf16[144,1280]{1,0:T(8,128)(2,1)S(1)} %pad_maximum_fusion.2.refs_0_), channel_id=1, source_target_pairs={{0,2},{1,3},{2,0},{3,1},{4,6},{5,7},{6,4},{7,5},{8,10},{9,11},{10,... | collective-permute-start | bytes 1105928 | tf_op jit(solution)/shard_map/ppermute | solution.py:28
  156.5 1.9 %collective-permute-start.11 = (bf16[144,1280]{1,0:T(8,128)(2,1)S(1)}, bf16[144,1280]{1,0:T(8,128)(2,1)S(1)}, u32[]{:S(2)}, u32[]{:S(2)}) collective-permute-start(bf16[144,1280]{1,0:T(8,128)(2,1)S(1)} %pad_maximum_fusion.2.refs_0_), channel_id=1, source_target_pairs={{0,3},{1,0},{2,1},{3,2},{4,7},{5,4},{6,5},{7,6},{8,11},{9,8},{10,9... | collective-permute-start | bytes 1105928 | tf_op jit(solution)/shard_map/ppermute | solution.py:28
  158.5 0.3 fusion.4.take_a
  158.8 4.9 %collective-permute-done.10.refs_2_ = bf16[144,1280]{1,0:T(8,128)(2,1)S(1)} collective-permute-done((bf16[144,1280]{1,0:T(8,128)(2,1)S(1)}, bf16[144,1280]{1,0:T(8,128)(2,1)S(1)}, u32[]{:S(2)}, u32[]{:S(2)}) %collective-permute-start.10) | collective-permute-done | bytes 368672 | tf_op jit(solution)/shard_map/ppermute | solution.py:28
  163.7 3.7 %collective-permute-done.11.refs_3_ = bf16[144,1280]{1,0:T(8,128)(2,1)S(1)} collective-permute-done((bf16[144,1280]{1,0:T(8,128)(2,1)S(1)}, bf16[144,1280]{1,0:T(8,128)(2,1)S(1)}, u32[]{:S(2)}, u32[]{:S(2)}) %collective-permute-start.11) | collective-permute-done | bytes 368672 | tf_op jit(solution)/shard_map/ppermute | solution.py:28
  167.4 0.2 collective-permute-done.9.refs_1_
  167.6 6.6 %shard_map.174 = (bf16[384,2560]{1,0:T(8,128)(2,1)}, bf16[192,2560]{1,0:T(8,128)(2,1)}) custom-call(bf16[4,576,144]{2,1,0:T(8,128)(2,1)S(1)} %fusion.4.take_a, bf16[2,576,288]{2,1,0:T(8,128)(2,1)S(1)} %fusion.11.take_b, bf16[144,1280]{1,0:T(8,128)(2,1)S(1)} %pad_maximum_fusion.2.refs_0_, bf16[144,1280]{1,0:T(8,128)(2,1)S(1)} %collective-permute-done.9.refs_1_, ...), custom_call_target="tpu_custom_call" | custom-call | tf_op jit(solution)/shard_map/pallas_call | solution.py:223
  (53 shorter events, 1.2 us)
Async XLA Ops:
  0.6 24.3 %collective-permute-start.1 = (bf16[768,2560]{1,0:T(8,128)(2,1)}, bf16[768,2560]{1,0:T(8,128)(2,1)}, u32[]{:S(2)}, u32[]{:S(2)}) collective-permute-start(bf16[768,2560]{1,0:T(8,128)(2,1)} %param.15), channel_id=1, source_target_pairs={{0,64},{64,0},{1,65},{65,1},{2,66},{66,2},{3,67},{67,3},{4,68},{68... | collective-permute-start | bytes 11796488 | tf_op jit(solution)/shard_map/ppermute | solution.py:40
  6.2 17.4 %collective-permute-start = (bf16[4,4,72,768]{3,2,1,0:T(8,128)(2,1)}, bf16[4,4,72,768]{3,2,1,0:T(8,128)(2,1)S(1)}, u32[]{:S(2)}, u32[]{:S(2)}) collective-permute-start(bf16[4,4,72,768]{3,2,1,0:T(8,128)(2,1)} %bitcast.48), channel_id=1, source_target_pairs={{0,64},{64,0},{1,65},{65,1},{2,66},{66,2},{3,67},{67,3},{4,68},{68... | collective-permute-start | bytes 5308424 | tf_op jit(solution)/shard_map/ppermute | solution.py:40
  11.4 3.0 %copy-start = (bf16[4,2,144,768]{3,2,1,0:T(8,128)(2,1)S(1)}, bf16[4,2,144,768]{3,2,1,0:T(8,128)(2,1)}, u32[]{:S(2)}) copy-start(bf16[4,2,144,768]{3,2,1,0:T(8,128)(2,1)} %shard_map.172) | copy-start | bytes 5308420
  14.4 4.2 %copy-start.2 = (bf16[4,4,72,768]{3,2,0,1:T(8,128)(2,1)S(1)}, bf16[4,4,72,768]{3,2,0,1:T(8,128)(2,1)}, u32[]{:S(2)}) copy-start(bf16[4,4,72,768]{3,2,0,1:T(8,128)(2,1)} %copy.21) | copy-start | bytes 5308420
  14.4 4.2 %copy-start.9 = (bf16[768,2560]{1,0:T(8,128)(2,1)S(1)}, bf16[768,2560]{1,0:T(8,128)(2,1)}, u32[]{:S(2)}) copy-start(bf16[768,2560]{1,0:T(8,128)(2,1)} %param.15) | copy-start | bytes 11796484
  30.7 51.6 %all-to-all-start = ((f16[4,288,1280]{2,1,0:T(8,128)(2,1)}), f16[4,288,1280]{2,1,0:T(8,128)(2,1)S(1)}, u32[]{:S(2)}, u32[]{:S(2)}) async-start(f16[4,288,1280]{2,1,0:T(8,128)(2,1)} %bitcast.40), calls=%async_computation | async-start | bytes 5898240 | tf_op jit(solution)/shard_map/all_to_all | solution.py:143
  41.3 2.2 %copy-start.1 = (f16[1152,1280]{1,0:T(8,128)(2,1)}, f16[1152,1280]{1,0:T(8,128)(2,1)S(1)}, u32[]{:S(2)}) copy-start(f16[1152,1280]{1,0:T(8,128)(2,1)S(1)} %fusion.3) | copy-start | bytes 8847364
  43.6 21.2 %collective-permute-start.5 = (f16[288,1280]{1,0:T(8,128)(2,1)}, f16[288,1280]{1,0:T(8,128)(2,1)}, u32[]{:S(2)}, u32[]{:S(2)}) collective-permute-start(f16[288,1280]{1,0:T(8,128)(2,1)} %get-tuple-element.16), channel_id=1, source_target_pairs={{0,128},{32,160},{128,0},{160,32},{1,129},{33,161},{129,1},{161,33... | collective-permute-start | bytes 2211848 | tf_op jit(solution)/shard_map/ppermute | solution.py:32
  45.0 34.3 %collective-permute-start.6 = (f16[288,1280]{1,0:T(8,128)(2,1)}, f16[288,1280]{1,0:T(8,128)(2,1)}, u32[]{:S(2)}, u32[]{:S(2)}) collective-permute-start(f16[288,1280]{1,0:T(8,128)(2,1)} %get-tuple-element.18), channel_id=1, source_target_pairs={{0,32},{32,128},{128,160},{160,0},{1,33},{33,129},{129,161},{161,1... | collective-permute-start | bytes 2211848 | tf_op jit(solution)/shard_map/ppermute | solution.py:32
  46.1 33.2 %collective-permute-start.7 = (f16[288,1280]{1,0:T(8,128)(2,1)}, f16[288,1280]{1,0:T(8,128)(2,1)}, u32[]{:S(2)}, u32[]{:S(2)}) collective-permute-start(f16[288,1280]{1,0:T(8,128)(2,1)} %get-tuple-element.17), channel_id=1, source_target_pairs={{0,160},{32,0},{128,32},{160,128},{1,161},{33,1},{129,33},{161,129... | collective-permute-start | bytes 2211848 | tf_op jit(solution)/shard_map/ppermute | solution.py:32
  82.3 16.5 %all-to-all-start.1 = ((f16[4,72,1280]{2,1,0:T(8,128)(2,1)}), f16[4,72,1280]{2,1,0:T(8,128)(2,1)}, u32[]{:S(2)}, u32[]{:S(2)}) async-start(f16[4,72,1280]{2,1,0:T(8,128)(2,1)} %bitcast.45), calls=%async_computation.1 | async-start | bytes 1474560 | tf_op jit(solution)/shard_map/all_to_all | solution.py:143
  87.4 12.7 %collective-permute-start.2 = (f16[72,1280]{1,0:T(8,128)(2,1)S(1)}, f16[72,1280]{1,0:T(8,128)(2,1)S(1)}, u32[]{:S(2)}, u32[]{:S(2)}) collective-permute-start(f16[72,1280]{1,0:T(8,128)(2,1)S(1)} %get-tuple-element.19), channel_id=1, source_target_pairs={{0,128},{32,160},{128,0},{160,32},{1,129},{33,161},{129,1},{161,33... | collective-permute-start | bytes 552968 | tf_op jit(solution)/shard_map/ppermute | solution.py:32
  89.3 10.8 %collective-permute-start.3 = (f16[72,1280]{1,0:T(8,128)(2,1)S(1)}, f16[72,1280]{1,0:T(8,128)(2,1)S(1)}, u32[]{:S(2)}, u32[]{:S(2)}) collective-permute-start(f16[72,1280]{1,0:T(8,128)(2,1)S(1)} %get-tuple-element.21), channel_id=1, source_target_pairs={{0,32},{32,128},{128,160},{160,0},{1,33},{33,129},{129,161},{161,1... | collective-permute-start | bytes 552968 | tf_op jit(solution)/shard_map/ppermute | solution.py:32
  90.2 9.9 %collective-permute-start.4 = (f16[72,1280]{1,0:T(8,128)(2,1)S(1)}, f16[72,1280]{1,0:T(8,128)(2,1)S(1)}, u32[]{:S(2)}, u32[]{:S(2)}) collective-permute-start(f16[72,1280]{1,0:T(8,128)(2,1)S(1)} %get-tuple-element.20), channel_id=1, source_target_pairs={{0,160},{32,0},{128,32},{160,128},{1,161},{33,1},{129,33},{161,129... | collective-permute-start | bytes 552968 | tf_op jit(solution)/shard_map/ppermute | solution.py:32
  100.1 21.3 %copy-start.3 = (f32[6,2560]{1,0:T(8,128)S(1)}, f32[6,2560]{1,0:T(8,128)}, u32[]{:S(2)}) copy-start(f32[6,2560]{1,0:T(8,128)} %param.18) | copy-start | bytes 184324
  100.1 21.3 %copy-start.4 = (f32[6,2560]{1,0:T(8,128)S(1)}, f32[6,2560]{1,0:T(8,128)}, u32[]{:S(2)}) copy-start(f32[6,2560]{1,0:T(8,128)} %param.20) | copy-start | bytes 184324
  100.1 21.2 %copy-start.5 = (f32[6,2560]{1,0:T(8,128)S(1)}, f32[6,2560]{1,0:T(8,128)}, u32[]{:S(2)}) copy-start(f32[6,2560]{1,0:T(8,128)} %param.19) | copy-start | bytes 184324
  100.3 21.8 %copy-start.6 = (f32[3,2560]{1,0:T(4,128)S(1)}, f32[3,2560]{1,0:T(4,128)}, u32[]{:S(2)}) copy-start(f32[3,2560]{1,0:T(4,128)} %param.21) | copy-start | bytes 92164
  100.3 21.8 %copy-start.7 = (f32[3,2560]{1,0:T(4,128)S(1)}, f32[3,2560]{1,0:T(4,128)}, u32[]{:S(2)}) copy-start(f32[3,2560]{1,0:T(4,128)} %param.23) | copy-start | bytes 92164
  100.3 21.8 %copy-start.8 = (f32[3,2560]{1,0:T(4,128)S(1)}, f32[3,2560]{1,0:T(4,128)}, u32[]{:S(2)}) copy-start(f32[3,2560]{1,0:T(4,128)} %param.22) | copy-start | bytes 92164
  123.7 15.5 %all-to-all-start.3 = ((bf16[8,180,128]{2,1,0:T(8,128)(2,1)}), bf16[8,180,128]{2,1,0:T(8,128)(2,1)S(1)}, u32[]{:S(2)}, u32[]{:S(2)}) async-start(bf16[8,180,128]{2,1,0:T(8,128)(2,1)} %broadcast_in_dim.10), calls=%async_computation.3 | async-start | bytes 753664 | tf_op jit(solution)/shard_map/all_to_all | solution.py:162
  139.7 8.6 %collective-permute-start.12 = (bf16[72,1280]{1,0:T(8,128)(2,1)S(1)}, bf16[72,1280]{1,0:T(8,128)(2,1)S(1)}, u32[]{:S(2)}, u32[]{:S(2)}) collective-permute-start(bf16[72,1280]{1,0:T(8,128)(2,1)S(1)} %get-tuple-element.22), channel_id=1, source_target_pairs={{0,1},{1,2},{2,3},{3,0},{4,5},{5,6},{6,7},{7,4},{8,9},{9,10},{10,1... | collective-permute-start | bytes 552968 | tf_op jit(solution)/shard_map/ppermute | solution.py:28
  141.2 8.2 %collective-permute-start.13 = (bf16[72,1280]{1,0:T(8,128)(2,1)S(1)}, bf16[72,1280]{1,0:T(8,128)(2,1)S(1)}, u32[]{:S(2)}, u32[]{:S(2)}) collective-permute-start(bf16[72,1280]{1,0:T(8,128)(2,1)S(1)} %get-tuple-element.22), channel_id=1, source_target_pairs={{0,2},{1,3},{2,0},{3,1},{4,6},{5,7},{6,4},{7,5},{8,10},{9,11},{10,... | collective-permute-start | bytes 552968 | tf_op jit(solution)/shard_map/ppermute | solution.py:28
  143.8 5.5 %collective-permute-start.14 = (bf16[72,1280]{1,0:T(8,128)(2,1)S(1)}, bf16[72,1280]{1,0:T(8,128)(2,1)S(1)}, u32[]{:S(2)}, u32[]{:S(2)}) collective-permute-start(bf16[72,1280]{1,0:T(8,128)(2,1)S(1)} %get-tuple-element.22), channel_id=1, source_target_pairs={{0,3},{1,0},{2,1},{3,2},{4,7},{5,4},{6,5},{7,6},{8,11},{9,8},{10,9... | collective-permute-start | bytes 552968 | tf_op jit(solution)/shard_map/ppermute | solution.py:28
  145.3 8.5 %collective-permute-start.8 = (bf16[72,1280]{1,0:T(8,128)(2,1)S(1)}, bf16[72,1280]{1,0:T(8,128)(2,1)S(1)}, u32[]{:S(2)}, u32[]{:S(2)}) collective-permute-start(bf16[72,1280]{1,0:T(8,128)(2,1)S(1)} %get-tuple-element.23), channel_id=1, source_target_pairs={{0,32},{32,0},{1,33},{33,1},{2,34},{34,2},{3,35},{35,3},{4,36},{36... | collective-permute-start | bytes 552968 | tf_op jit(solution)/shard_map/ppermute | solution.py:36
  149.4 18.2 %collective-permute-start.15 = (bf16[288,1280]{1,0:T(8,128)(2,1)S(1)}, bf16[288,1280]{1,0:T(8,128)(2,1)S(1)}, u32[]{:S(2)}, u32[]{:S(2)}) collective-permute-start(bf16[288,1280]{1,0:T(8,128)(2,1)S(1)} %pad_maximum_fusion.refs_4_), channel_id=1, source_target_pairs={{0,32},{32,0},{1,33},{33,1},{2,34},{34,2},{3,35},{35,3},{4,36},{36... | collective-permute-start | bytes 2211848 | tf_op jit(solution)/shard_map/ppermute | solution.py:36
  153.8 9.9 %collective-permute-start.10 = (bf16[144,1280]{1,0:T(8,128)(2,1)S(1)}, bf16[144,1280]{1,0:T(8,128)(2,1)S(1)}, u32[]{:S(2)}, u32[]{:S(2)}) collective-permute-start(bf16[144,1280]{1,0:T(8,128)(2,1)S(1)} %pad_maximum_fusion.2.refs_0_), channel_id=1, source_target_pairs={{0,2},{1,3},{2,0},{3,1},{4,6},{5,7},{6,4},{7,5},{8,10},{9,11},{10,... | collective-permute-start | bytes 1105928 | tf_op jit(solution)/shard_map/ppermute | solution.py:28
  156.5 10.9 %collective-permute-start.11 = (bf16[144,1280]{1,0:T(8,128)(2,1)S(1)}, bf16[144,1280]{1,0:T(8,128)(2,1)S(1)}, u32[]{:S(2)}, u32[]{:S(2)}) collective-permute-start(bf16[144,1280]{1,0:T(8,128)(2,1)S(1)} %pad_maximum_fusion.2.refs_0_), channel_id=1, source_target_pairs={{0,3},{1,0},{2,1},{3,2},{4,7},{5,4},{6,5},{7,6},{8,11},{9,8},{10,9... | collective-permute-start | bytes 1105928 | tf_op jit(solution)/shard_map/ppermute | solution.py:28
  158.4 9.2 %collective-permute-start.9 = (bf16[144,1280]{1,0:T(8,128)(2,1)S(1)}, bf16[144,1280]{1,0:T(8,128)(2,1)S(1)}, u32[]{:S(2)}, u32[]{:S(2)}) collective-permute-start(bf16[144,1280]{1,0:T(8,128)(2,1)S(1)} %pad_maximum_fusion.2.refs_0_), channel_id=1, source_target_pairs={{0,1},{1,2},{2,3},{3,0},{4,5},{5,6},{6,7},{7,4},{8,9},{9,10},{10,1... | collective-permute-start | bytes 1105928 | tf_op jit(solution)/shard_map/ppermute | solution.py:28
where the time goes:
time: 177 us; the launch traced here: 174 us
  waiting for transfers between devices  62.5 us (35%)
  starting transfers between devices  36.8 us (21%)
  matrix products  21.2 us (12%)
  blocking collectives  20.3 us (11%)
  Pallas kernels  16.1 us (9%)
  local copies, waits for them, and re-layouts  8.52 us (5%)
  other arithmetic  7.17 us (4%)
    ppermute x6, waiting for transfers between devices, y_ring(): return lax.ppermute(v, ('yh', 'yl'), [(i, (i + d) % NY) for i in range(NY)])  32.2 us
    dot_general x4, matrix products, dot(): return jnp.dot(a, b, preferred_element_type=F32)  21.2 us
    all_to_all x1, blocking collectives, local(): last = lax.all_to_all(last, 'z', 0, 0)  20.3 us
    all_to_all x1, waiting for transfers between devices, local(): lax.all_to_all(jnp.broadcast_to(weight, (NZ,) + weight.shape[1:]), 'z', 0...  12 us
    ppermute x6, starting transfers between devices, x_ring(): return lax.ppermute(v, 'x', [(i, (i + d) % NX) for i in range(NX)])  10.3 us
    ppermute x6, waiting for transfers between devices, x_ring(): return lax.ppermute(v, 'x', [(i, (i + d) % NX) for i in range(NX)])  9.91 us
    pallas_call x2, Pallas kernels, ordered(): pl.pallas_call(order_kernel, grid_spec=pltpu.PrefetchScalarGridSpec(num_s...  9.56 us
    all_to_all x2, starting transfers between devices, reduce_x(): return lax.all_to_all(v, 'x', 0, 0).astype(F32).sum(axis=0).astype(F16)  8.78 us
  transfers between devices with their start and end apart: 19, of which 10 were waited for; matrix products, arithmetic and copies ran while one was open for 16% of the time, Pallas kernels for 5%

commit v1 on v0

--- a/solution.py
+++ b/solution.py
@@ -63,14 +63,29 @@
     return jnp.dot(a, b, preferred_element_type=F32)
 
 
-def order_kernel(core_ref, count_ref, token_ref, shared_ref, routed_ref, shared_order_ref, routed_order_ref, out_ref):
+def order_kernel(core_ref, count_ref, token_ref, shared_ref, routed_ref, shared_order_ref, routed_order_ref, far_a, far_b, near_a, near_b):
     tok, slots = shared_ref.shape[0], routed_ref.shape[0]
     names = lax.broadcasted_iota(jnp.int32, (tok, slots), 0) == token_ref[...]
     live = lax.broadcasted_iota(jnp.int32, (tok, slots), 1) < count_ref[0]
     place = jnp.where(names & live, 1.0, 0.0).astype(BF)
     slot_rows = dot_t(routed_order_ref[0], routed_ref[...]).astype(BF)
     total = dot_t(shared_order_ref[...], shared_ref[...]) + dot_t(slot_rows, place)
-    out_ref[...] = total.astype(BF).reshape(out_ref.shape)
+    group = total.shape[0] // (2 * NX)
+
+    def put(a, b):
+        a[...] = total.astype(BF).reshape(a.shape)
+        for xx in range(NX):
+            for yy in range(2):
+                start = (xx * 2 + yy) * group
+                b[yy, xx] = total[start : start + group].astype(BF)
+
+    @pl.when(pl.program_id(0) < 2)
+    def _():
+        put(far_a, far_b)
+
+    @pl.when(pl.program_id(0) >= 2)
+    def _():
+        put(near_a, near_b)
 
 
 def ordered(core, count, token, hid_shared, hid_routed, shared_order, routed_order):
@@ -78,24 +93,66 @@
     slots = hid_routed.shape[0]
     n, cut = shared_order.shape
     pair = routed_order.shape[2]
+    group = n // (2 * NX)
+
+    def who(j, c):
+        return jnp.where(j < 2, 1 - c[0], c[0])
+
+    def out(low):
+        def at(j):
+            return jnp.clip(j - low, 0, 1)
+
+        return [
+            pl.BlockSpec((NX, 1, n // NX, tok), lambda j, c, m: (0, at(j), 0, 0)),
+            pl.BlockSpec((2, NX, group, tok), lambda j, c, m: (at(j), 0, 0, 0)),
+        ]
+
+    shapes = [
+        jax.ShapeDtypeStruct((NX, 2, n // NX, tok), BF),
+        jax.ShapeDtypeStruct((NY, NX, group, tok), BF),
+    ]
     return pl.pallas_call(
         order_kernel,
         grid_spec=pltpu.PrefetchScalarGridSpec(
             num_scalar_prefetch=2,
-            grid=(2,),
+            grid=(4,),
             in_specs=[
-                pl.BlockSpec((1, slots), lambda h, c, m: (0, 0)),
-                pl.BlockSpec((tok, cut), lambda h, c, m: (0, h * 2 + c[0])),
-                pl.BlockSpec((slots, pair), lambda h, c, m: (0, h)),
-                pl.BlockSpec((n, cut), lambda h, c, m: (0, 0)),
-                pl.BlockSpec((1, n, pair), lambda h, c, m: (c[0], 0, 0)),
+                pl.BlockSpec((1, slots), lambda j, c, m: (0, 0)),
+                pl.BlockSpec((tok, cut), lambda j, c, m: (0, (j % 2) * 2 + who(j, c))),
+                pl.BlockSpec((slots, pair), lambda j, c, m: (0, j % 2)),
+                pl.BlockSpec((n, cut), lambda j, c, m: (0, 0)),
+                pl.BlockSpec((1, n, pair), lambda j, c, m: (who(j, c), 0, 0)),
             ],
-            out_specs=pl.BlockSpec((NX, 1, n // NX, tok), lambda h, c, m: (0, h, 0, 0)),
+            out_specs=out(0) + out(2),
         ),
-        out_shape=jax.ShapeDtypeStruct((NX, 2, n // NX, tok), BF),
+        out_shape=shapes + shapes,
         compiler_params=pltpu.CompilerParams(vmem_limit_bytes=56 * 2**20),
-        cost_estimate=pl.CostEstimate(flops=8 * n * cut * tok, bytes_accessed=6 * n * tok, transcendentals=0),
+        cost_estimate=pl.CostEstimate(flops=16 * n * cut * tok, bytes_accessed=20 * n * tok, transcendentals=0),
     )(core.reshape(1), count, token.reshape(1, slots), hid_shared, hid_routed, shared_order, routed_order)
+
+
+def product_kernel(near_ref, far_ref, out_near_ref, out_far_ref, total_ref):
+    total_ref[...] = SCALE * (dot(near_ref[...], out_near_ref[...]) + dot(far_ref[...], out_far_ref[...]))
+
+
+def product(near, far, out_near, out_far, low):
+    n, tok = near.shape
+    width = out_near.shape[1] - low
+    tile = 256
+
+    def whole(v):
+        return pl.BlockSpec(v.shape, lambda j: (0, 0))
+
+    cols = pl.BlockSpec((tok, tile), lambda j: (0, j + low // tile))
+    return pl.pallas_call(
+        product_kernel,
+        grid=(width // tile,),
+        in_specs=[whole(near), whole(far), cols, cols],
+        out_specs=pl.BlockSpec((n, tile), lambda j: (0, j)),
+        out_shape=jax.ShapeDtypeStruct((n, width), F32),
+        compiler_params=pltpu.CompilerParams(vmem_limit_bytes=40 * 2**20),
+        cost_estimate=pl.CostEstimate(flops=4 * n * tok * width, bytes_accessed=4 * n * (tok + width), transcendentals=0),
+    )(near, far, out_near, out_far)
 
 
 def local(
@@ -123,34 +180,36 @@
     y = yh * 2 + yl
 
     shared_order, routed_order = (jnp.asarray(v) for v in row_order(sr, rr))
-    def activ(k):
-        rows_of = ordered(k, slot_count, slot_token, hid_shared, hid_routed, shared_order, routed_order)
-        return rows_of.reshape(NX, NY, group, tok)
-
+    part_a = width * 3 // 5
     out_far = core_swap(out_grad)
-    act_far = core_swap(activ(1 - core))
-    act_near = activ(core)
-
-    def first(part):
-        def lined(v):
-            return (v.swapaxes(0, 1) if part else v).reshape(-1, tok)
-
-        cols = slice(part * half, (part + 1) * half)
-        total = dot(lined(act_near), out_grad[:, cols]) + dot(lined(act_far), out_far[:, cols])
-        return (SCALE * total).astype(F16).reshape(4, 4 * group, half)
+    far_a, far_b, near_a, near_b = ordered(
+        core, slot_count, slot_token, hid_shared, hid_routed, shared_order, routed_order
+    )
+    far_a, far_b = core_swap(far_a), core_swap(far_b)
+
+    def flat(v):
+        return v.reshape(-1, tok)
+
+    total_a = dot(flat(near_a), out_grad[:, :part_a]) + dot(flat(far_a), out_far[:, :part_a])
+    total_a = (SCALE * total_a).astype(F16)
+    near_b, total_a = lax.optimization_barrier((near_b, total_a))
+    total_b = product(flat(near_b), flat(far_b), out_grad, out_far, part_a)
 
     def reduce_x(v):
-        return lax.all_to_all(v, "x", 0, 0).astype(F32).sum(axis=0).astype(F16)
+        return lax.all_to_all(v, "x", 0, 0).astype(F32).sum(axis=0)
 
     def reduce_y(v):
         def pick(step):
             return lax.dynamic_index_in_dim(v, (y + step) % NY, 0, keepdims=False)
 
-        back = [y_ring(pick(d), d) for d in (2, 1, 3)]
-        return sum((b.astype(F32) for b in back), pick(0).astype(F32)).astype(F16)
-
-    one_a, one_b = reduce_x(first(0)), reduce_y(first(1))
-    two = [reduce_y(one_a.reshape(NY, group, half)), reduce_x(one_b.reshape(NX, group, half))]
+        back = [y_ring(pick(d).astype(F16), d) for d in (2, 1, 3)]
+        return sum((b.astype(F32) for b in back), pick(0).astype(F32))
+
+    one_a = reduce_x(total_a.reshape(NX, NY * group, -1))
+    one_b = reduce_y(total_b.reshape(NY, NX * group, -1)).astype(F16)
+    two_a = reduce_y(one_a.reshape(NY, group, -1)).astype(F16)
+    two_b = reduce_x(one_b.reshape(NX, group, -1)).astype(F16)
+    two = [two_a, two_b]
     last = jnp.concatenate(two, axis=1).reshape(NZ, rows * width // 128, 128)
     last = lax.all_to_all(last, "z", 0, 0)
     grad = (last.astype(F32).sum(axis=0) * (1.0 / SCALE)).reshape(rows, width)
@@ -211,7 +270,7 @@
 def settled(take_a, take_b, all_a, all_b, split):
     n = take_a.shape[1]
     half = all_a[0].shape[1]
-    tile = 256
+    tile = half // 2
     steps = half // tile
 
     def tiles(v, low):

time: 177 us -> 167 us (0.944)
  matrix products: 21.2 us -> 10.4 us
  Pallas kernels: 16.1 us -> 21.7 us
  local copies, waits for them, and re-layouts: 8.52 us -> 3.99 us
  other arithmetic: 7.17 us -> 10.9 us
  starting transfers between devices: 36.8 us -> 33.7 us
    dot_general x4 -> x2, matrix products: 21.2 us -> 10.4 us  [dot(): return jnp.dot(a, b, preferred_element_type=F32)]
    pallas_call x0 -> x1, Pallas kernels: none -> 6.8 us  [product(): pl.pallas_call(product_kernel, grid=(width // tile,), in_specs=[whole(nea...]
    ppermute x6, waiting for transfers between devices: 9.91 us -> 16.5 us  [x_ring(): return lax.ppermute(v, 'x', [(i, (i + d) % NX) for i in range(NX)])]
    all_to_all x2, waiting for transfers between devices: 7.49 us -> 1.33 us  [reduce_x(): return lax.all_to_all(v, 'x', 0, 0).astype(F32).sum(axis=0)]
    ppermute x2, starting transfers between devices: 6.28 us -> 2.6 us  [y_swap(): return lax.ppermute(v, 'yl', [(0, 1), (1, 0)])]
    reshape x1 -> x0, local copies, waits for them, and re-layouts: 2.96 us -> none  [activ(): return rows_of.reshape(NX, NY, group, tok)]
    convert_element_type x4 -> x5, other arithmetic: 3.29 us -> 5.79 us  [the longest x2 3.09 us: reduce_y(): back = [y_ring(pick(d).astype(F16), d) for d in (2, 1, 3)]]
    squeeze x2 -> x0, local copies, waits for them, and re-layouts: 1.87 us -> none  [pick(): return lax.dynamic_index_in_dim(v, (y + step) % NY, 0, keepdims=False)]
  transfers between devices with their start and end apart: 19 -> 20, of which waited for: 10 -> 14; matrix products, arithmetic and copies ran while one was open for 16% -> 12% of each run, Pallas kernels for 5% -> 10%
where the time goes in v1:
time: 167 us; the launch traced here: 164 us
  waiting for transfers between devices  62.2 us (37%)
  starting transfers between devices  33.7 us (20%)
  Pallas kernels  21.7 us (13%)
  blocking collectives  19.9 us (12%)
  other arithmetic  10.9 us (7%)
  matrix products  10.4 us (6%)
  local copies, waits for them, and re-layouts  3.99 us (2%)
    ppermute x6, waiting for transfers between devices, y_ring(): return lax.ppermute(v, ('yh', 'yl'), [(i, (i + d) % NY) for i in range(NY)])  32.8 us
    all_to_all x1, blocking collectives, local(): last = lax.all_to_all(last, 'z', 0, 0)  19.9 us
    ppermute x6, waiting for transfers between devices, x_ring(): return lax.ppermute(v, 'x', [(i, (i + d) % NX) for i in range(NX)])  16.5 us
    all_to_all x1, waiting for transfers between devices, local(): lax.all_to_all(jnp.broadcast_to(weight, (NZ,) + weight.shape[1:]), 'z', 0...  11.5 us
    dot_general x2, matrix products, dot(): return jnp.dot(a, b, preferred_element_type=F32)  10.4 us
    pallas_call x1, Pallas kernels, ordered(): pl.pallas_call(order_kernel, grid_spec=pltpu.PrefetchScalarGridSpec(num_s...  9.38 us
    all_to_all x2, starting transfers between devices, reduce_x(): return lax.all_to_all(v, 'x', 0, 0).astype(F32).sum(axis=0)  9.26 us
    ppermute x6, starting transfers between devices, x_ring(): return lax.ppermute(v, 'x', [(i, (i + d) % NX) for i in range(NX)])  9.02 us
  transfers between devices with their start and end apart: 20, of which 14 were waited for; matrix products, arithmetic and copies ran while one was open for 12% of the time, Pallas kernels for 10%

profile of v1, /device:TPU:16, one launch (start us, length us, event | category | flops | bytes accessed | tf_op | source)
XLA Modules:
  0.0 164.3 jit_solution(2762585302320826165)
XLA Ops:
  1.4 9.4 %shard_map.172 = (bf16[4,2,144,768]{3,2,1,0:T(8,128)(2,1)}, bf16[4,4,72,768]{3,2,1,0:T(8,128)(2,1)}, bf16[4,2,144,768]{3,2,1,0:T(8,128)(2,1)}, bf16[4,4,72,768]{3,2,1,0:T(8,128)(2,1)}) custom-call(s32[1]{0:T(128)} %bitcast.core_ref, s32[1]{0:T(128)S(6)} %copy.19.count_ref, s32[1,96]{1,0:T(1,128)} %bitcast.48, bf16[768,1536]{1,0:T(8,128)(2,1)} %shared_ref.1, ...), custom_call_target="tpu_custom_call" | custom-call | flops 2717908992 | bytes 8847360 | tf_op jit(solution)/shard_map/pallas_call | solution.py:114
  10.8 0.5 collective-permute-start
  11.4 4.4 %fusion.3 = f32[1152,1536]{1,0:T(8,128)S(1)} fusion(bf16[1152,768]{1,0:T(8,128)(2,1)} %bitcast.49, bf16[768,2560]{1,0:T(8,128)(2,1)S(1)} %copy-done), kind=kOutput, calls=%fused_computation.6 | convolution fusion | flops 2717908992 | bytes 11206656 | tf_op jit(solution)/shard_map/dot_general | solution.py:63
  15.8 6.0 %fusion.1 = f16[1152,1536]{1,0:T(8,128)(2,1)} fusion(f32[1152,1536]{1,0:T(8,128)S(1)} %fusion.3, bf16[1152,768]{1,0:T(8,128)(2,1)S(1)} %bitcast.47, bf16[768,2560]{1,0:T(8,128)(2,1)} %collective-permute-done.1.out_far_ref), kind=kOutput, calls=%fused_computation.2 | convolution fusion | flops 2723217408 | bytes 14745600 | tf_op jit(solution)/shard_map/dot_general | solution.py:63
  21.8 4.9 %all-to-all-start = ((f16[4,288,1536]{2,1,0:T(8,128)(2,1)}), f16[4,288,1536]{2,1,0:T(8,128)(2,1)}, u32[]{:S(2)}, u32[]{:S(2)}) async-start(f16[4,288,1536]{2,1,0:T(8,128)(2,1)} %bitcast.46), calls=%async_computation | async-start | bytes 7077888 | tf_op jit(solution)/shard_map/all_to_all | solution.py:199
  26.8 2.1 %copy-done.1 = bf16[768,2560]{1,0:T(8,128)(2,1)S(1)} copy-done((bf16[768,2560]{1,0:T(8,128)(2,1)S(1)}, bf16[768,2560]{1,0:T(8,128)(2,1)}, u32[]{:S(2)}) %copy-start.1) | copy-done | bytes 3932184
  28.9 6.8 %shard_map.173 = f32[1152,1024]{1,0:T(8,128)} custom-call(bf16[1152,768]{1,0:T(8,128)(2,1)S(1)} %bitcast.40, bf16[1152,768]{1,0:T(8,128)(2,1)S(1)} %bitcast.41, bf16[768,2560]{1,0:T(8,128)(2,1)S(1)} %copy-done.1, bf16[768,2560]{1,0:T(8,128)(2,1)} %collective-permute-done.1.out_far_ref), custom_call_target="tpu_custom_call" | custom-call | flops 3623878656 | bytes 8257536 | tf_op jit(solution)/shard_map/pallas_call | solution.py:147
  35.7 2.3 %fusion.10 = (f16[288,1024]{1,0:T(8,128)(2,1)S(1)}, f16[288,1024]{1,0:T(8,128)(2,1)S(1)}, f16[288,1024]{1,0:T(8,128)(2,1)S(1)}) fusion(f32[4,288,1024]{2,1,0:T(8,128)} %bitcast.42, s32[]{:T(128)S(6)} %select_n.140, s32[]{:T(128)S(6)} %select_n.144, s32[]{:T(128)S(6)} %select_n.142), kind=kLoop, calls=%fused_computation.21 | loop fusion | flops 884736 | bytes 5308428 | tf_op jit(solution)/shard_map/convert_element_type | solution.py:205
  38.0 0.5 collective-permute-start.8
  38.5 1.6 collective-permute-start.7
  40.1 2.1 %collective-permute-start.6 = (f16[288,1024]{1,0:T(8,128)(2,1)S(1)}, f16[288,1024]{1,0:T(8,128)(2,1)S(1)}, u32[]{:S(2)}, u32[]{:S(2)}) collective-permute-start(f16[288,1024]{1,0:T(8,128)(2,1)S(1)} %get-tuple-element.28), channel_id=1, source_target_pairs={{0,128},{32,160},{128,0},{160,32},{1,129},{33,161},{129,1},{161,33... | collective-permute-start | bytes 1769480 | tf_op jit(solution)/shard_map/ppermute | solution.py:32
  42.2 12.0 %collective-permute-done.8 = f16[288,1024]{1,0:T(8,128)(2,1)S(1)} collective-permute-done((f16[288,1024]{1,0:T(8,128)(2,1)S(1)}, f16[288,1024]{1,0:T(8,128)(2,1)S(1)}, u32[]{:S(2)}, u32[]{:S(2)}) %collective-permute-start.8) | collective-permute-done | bytes 589856 | tf_op jit(solution)/shard_map/ppermute | solution.py:32
  54.2 0.1 collective-permute-done.7
  54.4 13.8 %collective-permute-done.6 = f16[288,1024]{1,0:T(8,128)(2,1)S(1)} collective-permute-done((f16[288,1024]{1,0:T(8,128)(2,1)S(1)}, f16[288,1024]{1,0:T(8,128)(2,1)S(1)}, u32[]{:S(2)}, u32[]{:S(2)}) %collective-permute-start.6) | collective-permute-done | bytes 589856 | tf_op jit(solution)/shard_map/ppermute | solution.py:32
  68.2 2.5 %fusion.9 = f16[288,1024]{1,0:T(8,128)(2,1)} fusion(f16[288,1024]{1,0:T(8,128)(2,1)S(1)} %collective-permute-done.8, f16[288,1024]{1,0:T(8,128)(2,1)S(1)} %collective-permute-done.7, f16[288,1024]{1,0:T(8,128)(2,1)S(1)} %collective-permute-done.6, f32[4,288,1024]{2,1,0:T(8,128)} %bitcast.43, s32[]{:T(128)S(6)} %select_n.138), kind=kLoop, calls=%fused_computation.14 | loop fusion | flops 2064384 | bytes 3538948 | tf_op jit(solution)/shard_map/convert_element_type | solution.py:209
  70.7 4.4 %all-to-all-start.1 = ((f16[4,72,1024]{2,1,0:T(8,128)(2,1)}), f16[4,72,1024]{2,1,0:T(8,128)(2,1)S(1)}, u32[]{:S(2)}, u32[]{:S(2)}) async-start(f16[4,72,1024]{2,1,0:T(8,128)(2,1)} %bitcast.17), calls=%async_computation.1 | async-start | bytes 1179648 | tf_op jit(solution)/shard_map/all_to_all | solution.py:199
  75.1 2.7 %convert_reduce_fusion = f32[288,1536]{1,0:T(8,128)S(1)} fusion(f16[4,288,1536]{2,1,0:T(8,128)(2,1)} %all-to-all-done), kind=kLoop, calls=%fused_computation.3 | loop fusion | flops 3096576 | bytes 5308416 | tf_op jit(solution)/shard_map/reduce_sum | solution.py:199
  77.8 0.8 fusion.16
  78.6 2.0 %collective-permute-start.3 = (f16[72,1536]{1,0:T(8,128)(2,1)S(1)}, f16[72,1536]{1,0:T(8,128)(2,1)S(1)}, u32[]{:S(2)}, u32[]{:S(2)}) collective-permute-start(f16[72,1536]{1,0:T(8,128)(2,1)S(1)} %get-tuple-element.33), channel_id=1, source_target_pairs={{0,32},{32,128},{128,160},{160,0},{1,33},{33,129},{129,161},{161,1... | collective-permute-start | bytes 663560 | tf_op jit(solution)/shard_map/ppermute | solution.py:32
  80.6 2.5 %collective-permute-start.2 = (f16[72,1536]{1,0:T(8,128)(2,1)S(1)}, f16[72,1536]{1,0:T(8,128)(2,1)S(1)}, u32[]{:S(2)}, u32[]{:S(2)}) collective-permute-start(f16[72,1536]{1,0:T(8,128)(2,1)S(1)} %get-tuple-element.31), channel_id=1, source_target_pairs={{0,128},{32,160},{128,0},{160,32},{1,129},{33,161},{129,1},{161,33... | collective-permute-start | bytes 663560 | tf_op jit(solution)/shard_map/ppermute | solution.py:32
  83.1 1.3 all-to-all-done.1
  84.6 2.6 %collective-permute-done.4 = f16[72,1536]{1,0:T(8,128)(2,1)S(1)} collective-permute-done((f16[72,1536]{1,0:T(8,128)(2,1)}, f16[72,1536]{1,0:T(8,128)(2,1)S(1)}, u32[]{:S(2)}, u32[]{:S(2)}) %collective-permute-start.4) | collective-permute-done | bytes 221216 | tf_op jit(solution)/shard_map/ppermute | solution.py:32
  87.3 4.1 %collective-permute-done.2 = f16[72,1536]{1,0:T(8,128)(2,1)S(1)} collective-permute-done((f16[72,1536]{1,0:T(8,128)(2,1)S(1)}, f16[72,1536]{1,0:T(8,128)(2,1)S(1)}, u32[]{:S(2)}, u32[]{:S(2)}) %collective-permute-start.2) | collective-permute-done | bytes 221216 | tf_op jit(solution)/shard_map/ppermute | solution.py:32
  91.4 0.1 fusion.15
  91.7 0.5 reshape.71
  92.2 19.9 %all_to_all.20 = f16[8,180,128]{2,1,0:T(8,128)(2,1)S(1)} all-to-all(f16[8,180,128]{2,1,0:T(8,128)(2,1)S(1)} %reshape.71), channel_id=1, replica_groups=mesh['yh'=2,'core'=2,'yl'=2,'z'=8,'x'=4] {'z'}, dimensions={0} | all-to-all | bytes 737280 | tf_op jit(solution)/shard_map/all_to_all | solution.py:214
  112.2 0.7 subtract_convert_fusion
  113.0 0.7 subtract_convert_fusion.1
  113.8 0.8 broadcast_in_dim.10
  114.6 3.4 %all-to-all-start.3 = ((bf16[8,180,128]{2,1,0:T(8,128)(2,1)}), bf16[8,180,128]{2,1,0:T(8,128)(2,1)S(1)}, u32[]{:S(2)}, u32[]{:S(2)}) async-start(bf16[8,180,128]{2,1,0:T(8,128)(2,1)} %broadcast_in_dim.10), calls=%async_computation.3 | async-start | bytes 753664 | tf_op jit(solution)/shard_map/all_to_all | solution.py:221
  118.1 11.5 %all-to-all-done.3 = bf16[8,180,128]{2,1,0:T(8,128)(2,1)S(1)} async-done(((bf16[8,180,128]{2,1,0:T(8,128)(2,1)}), bf16[8,180,128]{2,1,0:T(8,128)(2,1)S(1)}, u32[]{:S(2)}, u32[]{:S(2)}) %all-to-all-start.3) | async-done | bytes 368672 | tf_op jit(solution)/shard_map/all_to_all | solution.py:221
  129.7 0.4 reshape.72
  130.1 3.0 %collective-permute-start.15 = (bf16[72,1280]{1,0:T(8,128)(2,1)S(1)}, bf16[72,1280]{1,0:T(8,128)(2,1)S(1)}, u32[]{:S(2)}, u32[]{:S(2)}) collective-permute-start(bf16[72,1280]{1,0:T(8,128)(2,1)S(1)} %get-tuple-element.34), channel_id=1, source_target_pairs={{0,3},{1,0},{2,1},{3,2},{4,7},{5,4},{6,5},{7,6},{8,11},{9,8},{10,9... | collective-permute-start | bytes 552968 | tf_op jit(solution)/shard_map/ppermute | solution.py:28
  133.1 0.9 collective-permute-start.14
  134.0 0.9 collective-permute-start.13
  134.8 1.2 collective-permute-start.9
  136.0 2.2 %collective-permute-done.15 = bf16[72,1280]{1,0:T(8,128)(2,1)S(1)} collective-permute-done((bf16[72,1280]{1,0:T(8,128)(2,1)S(1)}, bf16[72,1280]{1,0:T(8,128)(2,1)S(1)}, u32[]{:S(2)}, u32[]{:S(2)}) %collective-permute-start.15) | collective-permute-done | bytes 184352 | tf_op jit(solution)/shard_map/ppermute | solution.py:28
  138.2 3.1 %collective-permute-done.14 = bf16[72,1280]{1,0:T(8,128)(2,1)S(1)} collective-permute-done((bf16[72,1280]{1,0:T(8,128)(2,1)S(1)}, bf16[72,1280]{1,0:T(8,128)(2,1)S(1)}, u32[]{:S(2)}, u32[]{:S(2)}) %collective-permute-start.14) | collective-permute-done | bytes 184352 | tf_op jit(solution)/shard_map/ppermute | solution.py:28
  141.3 2.1 %collective-permute-done.13 = bf16[72,1280]{1,0:T(8,128)(2,1)S(1)} collective-permute-done((bf16[72,1280]{1,0:T(8,128)(2,1)S(1)}, bf16[72,1280]{1,0:T(8,128)(2,1)S(1)}, u32[]{:S(2)}, u32[]{:S(2)}) %collective-permute-start.13) | collective-permute-done | bytes 184352 | tf_op jit(solution)/shard_map/ppermute | solution.py:28
  143.5 1.4 collective-permute-start.16
  144.9 0.2 fusion.6.take_b
  145.2 0.4 collective-permute-start.10
  145.6 3.7 %collective-permute-start.11 = (bf16[144,1280]{1,0:T(8,128)(2,1)S(1)}, bf16[144,1280]{1,0:T(8,128)(2,1)S(1)}, u32[]{:S(2)}, u32[]{:S(2)}) collective-permute-start(bf16[144,1280]{1,0:T(8,128)(2,1)S(1)} %pad_maximum_fusion.2.refs_0_), channel_id=1, source_target_pairs={{0,2},{1,3},{2,0},{3,1},{4,6},{5,7},{6,4},{7,5},{8,10},{9,11},{10,... | collective-permute-start | bytes 1105928 | tf_op jit(solution)/shard_map/ppermute | solution.py:28
  149.3 0.1 collective-permute-start.12
  149.5 0.3 fusion.5.take_a
  149.8 4.2 %collective-permute-done.10.refs_1_ = bf16[144,1280]{1,0:T(8,128)(2,1)S(1)} collective-permute-done((bf16[144,1280]{1,0:T(8,128)(2,1)S(1)}, bf16[144,1280]{1,0:T(8,128)(2,1)S(1)}, u32[]{:S(2)}, u32[]{:S(2)}) %collective-permute-start.10) | collective-permute-done | bytes 368672 | tf_op jit(solution)/shard_map/ppermute | solution.py:28
  154.0 4.8 %collective-permute-done.11.refs_2_ = bf16[144,1280]{1,0:T(8,128)(2,1)S(1)} collective-permute-done((bf16[144,1280]{1,0:T(8,128)(2,1)S(1)}, bf16[144,1280]{1,0:T(8,128)(2,1)S(1)}, u32[]{:S(2)}, u32[]{:S(2)}) %collective-permute-start.11) | collective-permute-done | bytes 368672 | tf_op jit(solution)/shard_map/ppermute | solution.py:28
  158.8 5.5 %shard_map.174 = (bf16[384,2560]{1,0:T(8,128)(2,1)}, bf16[192,2560]{1,0:T(8,128)(2,1)}) custom-call(bf16[4,576,144]{2,1,0:T(8,128)(2,1)S(1)} %fusion.5.take_a, bf16[2,576,288]{2,1,0:T(8,128)(2,1)S(1)} %fusion.6.take_b, bf16[144,1280]{1,0:T(8,128)(2,1)S(1)} %pad_maximum_fusion.2.refs_0_, bf16[144,1280]{1,0:T(8,128)(2,1)S(1)} %collective-permute-done.10.refs_1_, ...), custom_call_target="tpu_custom_call" | custom-call | tf_op jit(solution)/shard_map/pallas_call | solution.py:282
  (48 shorter events, 1.1 us)
Async XLA Ops:
  0.6 15.2 %collective-permute-start.1 = (bf16[768,2560]{1,0:T(8,128)(2,1)}, bf16[768,2560]{1,0:T(8,128)(2,1)}, u32[]{:S(2)}, u32[]{:S(2)}) collective-permute-start(bf16[768,2560]{1,0:T(8,128)(2,1)} %out_near_ref.1), channel_id=1, source_target_pairs={{0,64},{64,0},{1,65},{65,1},{2,66},{66,2},{3,67},{67,3},{4,68},{68... | collective-permute-start | bytes 11796488 | tf_op jit(solution)/shard_map/ppermute | solution.py:40
  1.4 10.0 %copy-start = (bf16[768,2560]{1,0:T(8,128)(2,1)S(1)}, bf16[768,2560]{1,0:T(8,128)(2,1)}, u32[]{:S(2)}) copy-start(bf16[768,2560]{1,0:T(8,128)(2,1)} %out_near_ref.1) | copy-start | bytes 11796484
  10.8 5.0 %collective-permute-start = (bf16[4,2,144,768]{3,2,1,0:T(8,128)(2,1)}, bf16[4,2,144,768]{3,2,1,0:T(8,128)(2,1)S(1)}, u32[]{:S(2)}, u32[]{:S(2)}) collective-permute-start(bf16[4,2,144,768]{3,2,1,0:T(8,128)(2,1)} %get-tuple-element.16), channel_id=1, source_target_pairs={{0,64},{64,0},{1,65},{65,1},{2,66},{66,2},{3,67},{67,3},{4,68},{68... | collective-permute-start | bytes 5308424 | tf_op jit(solution)/shard_map/ppermute | solution.py:40
  11.3 15.5 %collective-permute-start.5 = (bf16[4,4,72,768]{3,2,1,0:T(8,128)(2,1)}, bf16[4,4,72,768]{3,2,1,0:T(8,128)(2,1)S(1)}, u32[]{:S(2)}, u32[]{:S(2)}) collective-permute-start(bf16[4,4,72,768]{3,2,1,0:T(8,128)(2,1)} %get-tuple-element.19), channel_id=1, source_target_pairs={{0,64},{64,0},{1,65},{65,1},{2,66},{66,2},{3,67},{67,3},{4,68},{68... | collective-permute-start | bytes 5308424 | tf_op jit(solution)/shard_map/ppermute | solution.py:40
  21.8 4.9 %copy-start.2 = (bf16[4,4,72,768]{3,2,1,0:T(8,128)(2,1)S(1)}, bf16[4,4,72,768]{3,2,1,0:T(8,128)(2,1)}, u32[]{:S(2)}) copy-start(bf16[4,4,72,768]{3,2,1,0:T(8,128)(2,1)} %get-tuple-element.18) | copy-start | bytes 5308420
  21.8 48.9 %all-to-all-start = ((f16[4,288,1536]{2,1,0:T(8,128)(2,1)}), f16[4,288,1536]{2,1,0:T(8,128)(2,1)}, u32[]{:S(2)}, u32[]{:S(2)}) async-start(f16[4,288,1536]{2,1,0:T(8,128)(2,1)} %bitcast.46), calls=%async_computation | async-start | bytes 7077888 | tf_op jit(solution)/shard_map/all_to_all | solution.py:199
  26.7 2.1 %copy-start.1 = (bf16[768,2560]{1,0:T(8,128)(2,1)S(1)}, bf16[768,2560]{1,0:T(8,128)(2,1)}, u32[]{:S(2)}) copy-start(bf16[768,2560]{1,0:T(8,128)(2,1)} %out_near_ref.1) | copy-start | bytes 11796484
  38.0 16.2 %collective-permute-start.8 = (f16[288,1024]{1,0:T(8,128)(2,1)S(1)}, f16[288,1024]{1,0:T(8,128)(2,1)S(1)}, u32[]{:S(2)}, u32[]{:S(2)}) collective-permute-start(f16[288,1024]{1,0:T(8,128)(2,1)S(1)} %get-tuple-element.29), channel_id=1, source_target_pairs={{0,160},{32,0},{128,32},{160,128},{1,161},{33,1},{129,33},{161,129... | collective-permute-start | bytes 1769480 | tf_op jit(solution)/shard_map/ppermute | solution.py:32
  38.5 15.8 %collective-permute-start.7 = (f16[288,1024]{1,0:T(8,128)(2,1)S(1)}, f16[288,1024]{1,0:T(8,128)(2,1)S(1)}, u32[]{:S(2)}, u32[]{:S(2)}) collective-permute-start(f16[288,1024]{1,0:T(8,128)(2,1)S(1)} %get-tuple-element.30), channel_id=1, source_target_pairs={{0,32},{32,128},{128,160},{160,0},{1,33},{33,129},{129,161},{161,1... | collective-permute-start | bytes 1769480 | tf_op jit(solution)/shard_map/ppermute | solution.py:32
  40.1 28.1 %collective-permute-start.6 = (f16[288,1024]{1,0:T(8,128)(2,1)S(1)}, f16[288,1024]{1,0:T(8,128)(2,1)S(1)}, u32[]{:S(2)}, u32[]{:S(2)}) collective-permute-start(f16[288,1024]{1,0:T(8,128)(2,1)S(1)} %get-tuple-element.28), channel_id=1, source_target_pairs={{0,128},{32,160},{128,0},{160,32},{1,129},{33,161},{129,1},{161,33... | collective-permute-start | bytes 1769480 | tf_op jit(solution)/shard_map/ppermute | solution.py:32
  70.7 13.8 %all-to-all-start.1 = ((f16[4,72,1024]{2,1,0:T(8,128)(2,1)}), f16[4,72,1024]{2,1,0:T(8,128)(2,1)S(1)}, u32[]{:S(2)}, u32[]{:S(2)}) async-start(f16[4,72,1024]{2,1,0:T(8,128)(2,1)} %bitcast.17), calls=%async_computation.1 | async-start | bytes 1179648 | tf_op jit(solution)/shard_map/all_to_all | solution.py:199
  78.6 8.6 %collective-permute-start.4 = (f16[72,1536]{1,0:T(8,128)(2,1)}, f16[72,1536]{1,0:T(8,128)(2,1)S(1)}, u32[]{:S(2)}, u32[]{:S(2)}) collective-permute-start(f16[72,1536]{1,0:T(8,128)(2,1)} %get-tuple-element.32), channel_id=1, source_target_pairs={{0,160},{32,0},{128,32},{160,128},{1,161},{33,1},{129,33},{161,129... | collective-permute-start | bytes 663560 | tf_op jit(solution)/shard_map/ppermute | solution.py:32
  78.6 8.7 %collective-permute-start.3 = (f16[72,1536]{1,0:T(8,128)(2,1)S(1)}, f16[72,1536]{1,0:T(8,128)(2,1)S(1)}, u32[]{:S(2)}, u32[]{:S(2)}) collective-permute-start(f16[72,1536]{1,0:T(8,128)(2,1)S(1)} %get-tuple-element.33), channel_id=1, source_target_pairs={{0,32},{32,128},{128,160},{160,0},{1,33},{33,129},{129,161},{161,1... | collective-permute-start | bytes 663560 | tf_op jit(solution)/shard_map/ppermute | solution.py:32
  80.6 10.8 %collective-permute-start.2 = (f16[72,1536]{1,0:T(8,128)(2,1)S(1)}, f16[72,1536]{1,0:T(8,128)(2,1)S(1)}, u32[]{:S(2)}, u32[]{:S(2)}) collective-permute-start(f16[72,1536]{1,0:T(8,128)(2,1)S(1)} %get-tuple-element.31), channel_id=1, source_target_pairs={{0,128},{32,160},{128,0},{160,32},{1,129},{33,161},{129,1},{161,33... | collective-permute-start | bytes 663560 | tf_op jit(solution)/shard_map/ppermute | solution.py:32
  91.6 20.7 %copy-start.3 = (f32[6,2560]{1,0:T(8,128)S(1)}, f32[6,2560]{1,0:T(8,128)}, u32[]{:S(2)}) copy-start(f32[6,2560]{1,0:T(8,128)} %param.18) | copy-start | bytes 184324
  91.6 20.7 %copy-start.4 = (f32[6,2560]{1,0:T(8,128)S(1)}, f32[6,2560]{1,0:T(8,128)}, u32[]{:S(2)}) copy-start(f32[6,2560]{1,0:T(8,128)} %param.20) | copy-start | bytes 184324
  91.6 20.7 %copy-start.5 = (f32[6,2560]{1,0:T(8,128)S(1)}, f32[6,2560]{1,0:T(8,128)}, u32[]{:S(2)}) copy-start(f32[6,2560]{1,0:T(8,128)} %param.19) | copy-start | bytes 184324
  91.6 21.4 %copy-start.6 = (f32[3,2560]{1,0:T(4,128)S(1)}, f32[3,2560]{1,0:T(4,128)}, u32[]{:S(2)}) copy-start(f32[3,2560]{1,0:T(4,128)} %param.21) | copy-start | bytes 92164
  91.6 21.4 %copy-start.7 = (f32[3,2560]{1,0:T(4,128)S(1)}, f32[3,2560]{1,0:T(4,128)}, u32[]{:S(2)}) copy-start(f32[3,2560]{1,0:T(4,128)} %param.23) | copy-start | bytes 92164
  91.6 21.4 %copy-start.8 = (f32[3,2560]{1,0:T(4,128)S(1)}, f32[3,2560]{1,0:T(4,128)}, u32[]{:S(2)}) copy-start(f32[3,2560]{1,0:T(4,128)} %param.22) | copy-start | bytes 92164
  114.6 15.1 %all-to-all-start.3 = ((bf16[8,180,128]{2,1,0:T(8,128)(2,1)}), bf16[8,180,128]{2,1,0:T(8,128)(2,1)S(1)}, u32[]{:S(2)}, u32[]{:S(2)}) async-start(bf16[8,180,128]{2,1,0:T(8,128)(2,1)} %broadcast_in_dim.10), calls=%async_computation.3 | async-start | bytes 753664 | tf_op jit(solution)/shard_map/all_to_all | solution.py:221
  130.1 8.1 %collective-permute-start.15 = (bf16[72,1280]{1,0:T(8,128)(2,1)S(1)}, bf16[72,1280]{1,0:T(8,128)(2,1)S(1)}, u32[]{:S(2)}, u32[]{:S(2)}) collective-permute-start(bf16[72,1280]{1,0:T(8,128)(2,1)S(1)} %get-tuple-element.34), channel_id=1, source_target_pairs={{0,3},{1,0},{2,1},{3,2},{4,7},{5,4},{6,5},{7,6},{8,11},{9,8},{10,9... | collective-permute-start | bytes 552968 | tf_op jit(solution)/shard_map/ppermute | solution.py:28
  133.1 8.2 %collective-permute-start.14 = (bf16[72,1280]{1,0:T(8,128)(2,1)S(1)}, bf16[72,1280]{1,0:T(8,128)(2,1)S(1)}, u32[]{:S(2)}, u32[]{:S(2)}) collective-permute-start(bf16[72,1280]{1,0:T(8,128)(2,1)S(1)} %get-tuple-element.34), channel_id=1, source_target_pairs={{0,2},{1,3},{2,0},{3,1},{4,6},{5,7},{6,4},{7,5},{8,10},{9,11},{10,... | collective-permute-start | bytes 552968 | tf_op jit(solution)/shard_map/ppermute | solution.py:28
  134.0 9.5 %collective-permute-start.13 = (bf16[72,1280]{1,0:T(8,128)(2,1)S(1)}, bf16[72,1280]{1,0:T(8,128)(2,1)S(1)}, u32[]{:S(2)}, u32[]{:S(2)}) collective-permute-start(bf16[72,1280]{1,0:T(8,128)(2,1)S(1)} %get-tuple-element.34), channel_id=1, source_target_pairs={{0,1},{1,2},{2,3},{3,0},{4,5},{5,6},{6,7},{7,4},{8,9},{9,10},{10,1... | collective-permute-start | bytes 552968 | tf_op jit(solution)/shard_map/ppermute | solution.py:28
  134.8 10.3 %collective-permute-start.9 = (bf16[72,1280]{1,0:T(8,128)(2,1)S(1)}, bf16[72,1280]{1,0:T(8,128)(2,1)S(1)}, u32[]{:S(2)}, u32[]{:S(2)}) collective-permute-start(bf16[72,1280]{1,0:T(8,128)(2,1)S(1)} %get-tuple-element.35), channel_id=1, source_target_pairs={{0,32},{32,0},{1,33},{33,1},{2,34},{34,2},{3,35},{35,3},{4,36},{36... | collective-permute-start | bytes 552968 | tf_op jit(solution)/shard_map/ppermute | solution.py:36
  143.5 15.3 %collective-permute-start.16 = (bf16[288,1280]{1,0:T(8,128)(2,1)S(1)}, bf16[288,1280]{1,0:T(8,128)(2,1)S(1)}, u32[]{:S(2)}, u32[]{:S(2)}) collective-permute-start(bf16[288,1280]{1,0:T(8,128)(2,1)S(1)} %pad_maximum_fusion.refs_4_), channel_id=1, source_target_pairs={{0,32},{32,0},{1,33},{33,1},{2,34},{34,2},{3,35},{35,3},{4,36},{36... | collective-permute-start | bytes 2211848 | tf_op jit(solution)/shard_map/ppermute | solution.py:36
  145.2 8.8 %collective-permute-start.10 = (bf16[144,1280]{1,0:T(8,128)(2,1)S(1)}, bf16[144,1280]{1,0:T(8,128)(2,1)S(1)}, u32[]{:S(2)}, u32[]{:S(2)}) collective-permute-start(bf16[144,1280]{1,0:T(8,128)(2,1)S(1)} %pad_maximum_fusion.2.refs_0_), channel_id=1, source_target_pairs={{0,1},{1,2},{2,3},{3,0},{4,5},{5,6},{6,7},{7,4},{8,9},{9,10},{10,1... | collective-permute-start | bytes 1105928 | tf_op jit(solution)/shard_map/ppermute | solution.py:28
  145.6 13.2 %collective-permute-start.11 = (bf16[144,1280]{1,0:T(8,128)(2,1)S(1)}, bf16[144,1280]{1,0:T(8,128)(2,1)S(1)}, u32[]{:S(2)}, u32[]{:S(2)}) collective-permute-start(bf16[144,1280]{1,0:T(8,128)(2,1)S(1)} %pad_maximum_fusion.2.refs_0_), channel_id=1, source_target_pairs={{0,2},{1,3},{2,0},{3,1},{4,6},{5,7},{6,4},{7,5},{8,10},{9,11},{10,... | collective-permute-start | bytes 1105928 | tf_op jit(solution)/shard_map/ppermute | solution.py:28
  149.3 9.5 %collective-permute-start.12 = (bf16[144,1280]{1,0:T(8,128)(2,1)S(1)}, bf16[144,1280]{1,0:T(8,128)(2,1)S(1)}, u32[]{:S(2)}, u32[]{:S(2)}) collective-permute-start(bf16[144,1280]{1,0:T(8,128)(2,1)S(1)} %pad_maximum_fusion.2.refs_0_), channel_id=1, source_target_pairs={{0,3},{1,0},{2,1},{3,2},{4,7},{5,4},{6,5},{7,6},{8,11},{9,8},{10,9... | collective-permute-start | bytes 1105928 | tf_op jit(solution)/shard_map/ppermute | solution.py:28

commit v2 on v0

v2 whole, which is shorter than its diff:
```python
import jax
import jax.numpy as jnp
import numpy as np
from jax import lax
from jax.experimental import pallas as pl
from jax.experimental.pallas import tpu as pltpu
from jax.sharding import Mesh, PartitionSpec as P

AXES = ("yh", "core", "yl", "z", "x")
NX, NY, NZ = 4, 4, 8
SCALE = 0.25
BF = jnp.bfloat16
F32 = jnp.float32
F16 = jnp.float16


def adamw(grad, master, moment, second):
    corr_one = 1.0 - 0.9**20
    corr_two = 1.0 - 0.95**20
    new_moment = 0.9 * moment + 0.1 * grad
    new_second = 0.95 * second + 0.05 * grad * grad
    step_dir = new_moment / corr_one / (jnp.sqrt(new_second / corr_two) + 1e-08)
    new_master = master - 0.02 * (step_dir + 0.1 * master)
    return (new_moment, new_second, new_master.astype(BF))


def x_ring(v, d):
    return lax.ppermute(v, "x", [(i, (i + d) % NX) for i in range(NX)])


def y_ring(v, d):
    return lax.ppermute(v, ("yh", "yl"), [(i, (i + d) % NY) for i in range(NY)])


def y_swap(v):
    return lax.ppermute(v, "yl", [(0, 1), (1, 0)])


def core_swap(v):
    return lax.ppermute(v, "core", [(0, 1), (1, 0)])


def row_order(sr, rr):
    rows = sr + rr
    n = NX * 2 * NZ * rows
    xs, ys, zs, i = np.meshgrid(np.arange(NX), np.arange(2), np.arange(NZ), np.arange(rows), indexing="ij")
    dev = (ys * NZ + zs) * NX + xs
    flat = np.arange(n)
    keep = (i < sr).reshape(-1)
    shared = np.zeros((n, 2 * NZ * NX * sr), np.float32)
    shared[flat[keep], (dev * sr + i).reshape(-1)[keep]] = 1
    routed = np.zeros((2, n, 2, 2 * NZ * NX * rr), np.float32)
    for core in range(2):
        routed[core, flat[~keep], core, (dev * rr + i - sr).reshape(-1)[~keep]] = 1
    return shared.astype(BF), routed.reshape(2, n, -1).astype(BF)


def dot_t(a, b):
    return lax.dot_general(a, b, (((1,), (1,)), ((), ())), preferred_element_type=F32)


def dot(a, b):
    return jnp.dot(a, b, preferred_element_type=F32)


def order_kernel(core_ref, count_ref, token_ref, shared_ref, routed_ref, shared_order_ref, routed_order_ref, far, near):
    tok, slots = shared_ref.shape[0], routed_ref.shape[0]
    names = lax.broadcasted_iota(jnp.int32, (tok, slots), 0) == token_ref[...]
    live = lax.broadcasted_iota(jnp.int32, (tok, slots), 1) < count_ref[0]
    place = jnp.where(names & live, 1.0, 0.0).astype(BF)
    slot_rows = dot_t(routed_order_ref[0], routed_ref[...]).astype(BF)
    total = dot_t(shared_order_ref[...], shared_ref[...]) + dot_t(slot_rows, place)

    @pl.when(pl.program_id(0) < 2)
    def _():
        far[...] = total.astype(BF).reshape(far.shape)

    @pl.when(pl.program_id(0) >= 2)
    def _():
        near[...] = total.astype(BF).reshape(near.shape)


def ordered(core, count, token, hid_shared, hid_routed, shared_order, routed_order):
    tok = hid_shared.shape[0]
    slots = hid_routed.shape[0]
    n, cut = shared_order.shape
    pair = routed_order.shape[2]

    def who(j, c):
        return jnp.where(j < 2, 1 - c[0], c[0])

    def out(low):
        return pl.BlockSpec((NX, 1, n // NX, tok), lambda j, c, m: (0, jnp.clip(j - low, 0, 1), 0, 0))

    shape = jax.ShapeDtypeStruct((NX, 2, n // NX, tok), BF)
    return pl.pallas_call(
        order_kernel,
        grid_spec=pltpu.PrefetchScalarGridSpec(
            num_scalar_prefetch=2,
            grid=(4,),
            in_specs=[
                pl.BlockSpec((1, slots), lambda j, c, m: (0, 0)),
                pl.BlockSpec((tok, cut), lambda j, c, m: (0, (j % 2) * 2 + who(j, c))),
                pl.BlockSpec((slots, pair), lambda j, c, m: (0, j % 2)),
                pl.BlockSpec((n, cut), lambda j, c, m: (0, 0)),
                pl.BlockSpec((1, n, pair), lambda j, c, m: (who(j, c), 0, 0)),
            ],
            out_specs=[out(0), out(2)],
        ),
        out_shape=[shape, shape],
        compiler_params=pltpu.CompilerParams(vmem_limit_bytes=56 * 2**20),
        cost_estimate=pl.CostEstimate(flops=16 * n * cut * tok, bytes_accessed=20 * n * tok, transcendentals=0),
    )(core.reshape(1), count, token.reshape(1, slots), hid_shared, hid_routed, shared_order, routed_order)


def local(
    hid_shared,
    hid_routed,
    out_grad,
    slot_token,
    slot_count,
    master_shared,
    moment_shared,
    second_shared,
    master_routed,
    moment_routed,
    second_routed,
):
    tok, width = out_grad.shape
    slots = hid_routed.shape[0]
    sr, rr = master_shared.shape[0], master_routed.shape[0]
    rows = sr + rr
    group = NZ * rows
    core = lax.axis_index("core")
    x = lax.axis_index("x")
    yh, yl = lax.axis_index("yh"), lax.axis_index("yl")
    y = yh * 2 + yl

    shared_order, routed_order = (jnp.asarray(v) for v in row_order(sr, rr))
    part_a = width * 3 // 5
    out_far = core_swap(out_grad)
    far, near = ordered(core, slot_count, slot_token, hid_shared, hid_routed, shared_order, routed_order)
    far = core_swap(far).reshape(-1, tok)
    near = near.reshape(-1, tok)

    def term(near, cols):
        total = dot(near, out_grad[:, cols]) + dot(far, out_far[:, cols])
        return (SCALE * total).astype(F16).reshape(NX, NY, group, -1)

    def pick(v, dim, step):
        index = ((x, y)[dim] + step) % 4
        return lax.dynamic_index_in_dim(v, index, dim, keepdims=False)

    def cut(v, dim):
        return [pick(v, dim, d).astype(F16) for d in (2, 1, 3)]

    def send(chunks, dim):
        return [(x_ring, y_ring)[dim](v, d) for v, d in zip(chunks, (2, 1, 3))]

    def gathered(v, dim, back):
        return sum((b.astype(F32) for b in back), pick(v, dim, 0).astype(F32))

    total_a = term(near, slice(0, part_a))
    near, total_a = lax.optimization_barrier((near, total_a))
    total_b = term(near, slice(part_a, width))
    back_a = send(cut(total_a, 0), 0)
    back_b = send(cut(total_b, 1), 1)
    one_a = gathered(total_a, 0, back_a)[None]
    chunks_a = cut(one_a, 1)
    back_b[0], *chunks_a = lax.optimization_barrier((back_b[0], *chunks_a))
    two_a = send(chunks_a, 1)
    one_b = gathered(total_b, 1, back_b)[:, None]
    two_b = send(cut(one_b, 0), 0)
    two_a = gathered(one_a, 1, two_a)[0].astype(F16)
    two_a, *two_b = lax.optimization_barrier((two_a, *two_b))
    two_b = gathered(one_b, 0, two_b)[0].astype(F16)
    two = [two_a, two_b]
    last = jnp.concatenate(two, axis=1).reshape(NZ, rows * width // 128, 128)
    last = lax.all_to_all(last, "z", 0, 0)
    grad = (last.astype(F32).sum(axis=0) * (1.0 / SCALE)).reshape(rows, width)

    moment_s, second_s, weight_s = adamw(grad[:sr], master_shared, moment_shared, second_shared)
    moment_r, second_r, weight_r = adamw(grad[sr:], master_routed, moment_routed, second_routed)

    weight = jnp.concatenate([weight_s, weight_r], axis=0).reshape(1, rows * width // 128, 128)
    weight = lax.all_to_all(jnp.broadcast_to(weight, (NZ,) + weight.shape[1:]), "z", 0, 0)
    weight_s = weight[:, : sr * width // 128].reshape(NZ * sr, width)
    weight_r = weight[:, sr * width // 128 :].reshape(NZ * rr, width)
    all_s = jnp.concatenate([weight_s, y_swap(weight_s)], axis=0)
    all_r = jnp.concatenate([weight_r] + [x_ring(weight_r, d) for d in (1, 2, 3)], axis=0)
    all_s = jnp.concatenate([all_s] + [x_ring(all_s, d) for d in (1, 2, 3)], axis=0)
    all_r = jnp.concatenate([all_r, y_swap(all_r)], axis=0)

    def settled(full, count, index):
        n = full.shape[0]
        r = lax.iota(jnp.int32, n)
        back = (x - (r // count) % NX) % NX
        zz = (r // (count * NX)) % NZ
        flip = (r // (count * NX * NZ)) ^ yl
        want = lax.optimization_barrier((index(back, flip) * NZ + zz) * count + r % count)
        take = (want[:, None] == lax.broadcasted_iota(jnp.int32, (n, n), 1)).astype(BF)
        return dot(lax.optimization_barrier(take), full).astype(BF)

    shared = settled(all_s, sr, lambda back, flip: back * 2 + flip)
    routed = settled(all_r, rr, lambda back, flip: flip * NX + back)
    return (moment_s, second_s, moment_r, second_r, shared, routed)


def solution(mesh):
    fine = Mesh(mesh.devices.reshape(2, 2, 2, NZ, NX), AXES)
    split = P(AXES, None)
    flat = P(AXES)
    cuts = P(("yh", "core"), None)
    return jax.shard_map(
        local,
        mesh=fine,
        in_specs=(split, split, split, flat, flat) + (split,) * 6,
        out_specs=(split,) * 4 + (cuts,) * 2,
        check_vma=False,
    )
```

time: 177 us -> 164 us (0.927); the launches traced: 174 us -> 164 us
  waiting for transfers between devices: 62.5 us -> 70.5 us
  Pallas kernels: 16.1 us -> 8.24 us
  local copies, waits for them, and re-layouts: 8.52 us -> 3.91 us
  other arithmetic: 7.17 us -> 3.5 us
    ppermute x6 -> x12, waiting for transfers between devices: 9.91 us -> 50.5 us  [x_ring(): return lax.ppermute(v, 'x', [(i, (i + d) % NX) for i in range(NX)])]
    ppermute x6, waiting for transfers between devices: 32.2 us -> 6.04 us  [y_ring(): return lax.ppermute(v, ('yh', 'yl'), [(i, (i + d) % NY) for i in range(NY)])]
    ppermute x6 -> x12, starting transfers between devices: 10.3 us -> 21.5 us  [x_ring(): return lax.ppermute(v, 'x', [(i, (i + d) % NX) for i in range(NX)])]
    all_to_all x2 -> x0, starting transfers between devices: 8.78 us -> none  [reduce_x(): return lax.all_to_all(v, 'x', 0, 0).astype(F32).sum(axis=0).astype(F16)]
    all_to_all x2 -> x0, waiting for transfers between devices: 7.49 us -> none  [reduce_x(): return lax.all_to_all(v, 'x', 0, 0).astype(F32).sum(axis=0).astype(F16)]
    pallas_call x1 -> x0, Pallas kernels: 6.59 us -> none  [settled(): pl.pallas_call(settle_kernel, grid=(2 * steps,), in_specs=[whole(take_a),...]
    ppermute x2, starting transfers between devices: 6.28 us -> 2.34 us  [y_swap(): return lax.ppermute(v, 'yl', [(0, 1), (1, 0)])]
    convert_element_type x6, other arithmetic: 3.77 us -> 0.62 us  [the longest x2 0.21 us: settled(): (want[:, None] == lax.broadcasted_iota(jnp.int32, (n, n), 1)).astype(BF)]
  transfers between devices with their start and end apart: 19 -> 23, of which waited for: 10 -> 13; matrix products, arithmetic and copies ran while one was open for 16% -> 10% of each run, Pallas kernels for 5% -> 5%
where the time goes in v2:
time: 164 us
  waiting for transfers between devices  70.5 us (43%)
  starting transfers between devices  35.5 us (22%)
  matrix products  20.7 us (13%)
  blocking collectives  20 us (12%)
  Pallas kernels  8.24 us (5%)
  local copies, waits for them, and re-layouts  3.91 us (2%)
  other arithmetic  3.5 us (2%)
  between operations  1.7 us (1%)
    ppermute x12, waiting for transfers between devices, x_ring(): return lax.ppermute(v, 'x', [(i, (i + d) % NX) for i in range(NX)])  50.5 us
    ppermute x12, starting transfers between devices, x_ring(): return lax.ppermute(v, 'x', [(i, (i + d) % NX) for i in range(NX)])  21.5 us
    dot_general x6, matrix products, dot(): return jnp.dot(a, b, preferred_element_type=F32)  20.7 us
    all_to_all x1, blocking collectives, local(): last = lax.all_to_all(last, 'z', 0, 0)  20 us
    all_to_all x1, waiting for transfers between devices, local(): lax.all_to_all(jnp.broadcast_to(weight, (NZ,) + weight.shape[1:]), 'z', 0...  11.3 us
    pallas_call x1, Pallas kernels, ordered(): pl.pallas_call(order_kernel, grid_spec=pltpu.PrefetchScalarGridSpec(num_s...  8.24 us
    ppermute x6, starting transfers between devices, y_ring(): return lax.ppermute(v, ('yh', 'yl'), [(i, (i + d) % NY) for i in range(NY)])  7.53 us
    ppermute x6, waiting for transfers between devices, y_ring(): return lax.ppermute(v, ('yh', 'yl'), [(i, (i + d) % NY) for i in range(NY)])  6.04 us
  transfers between devices with their start and end apart: 23, of which 13 were waited for; matrix products, arithmetic and copies ran while one was open for 10% of the time, Pallas kernels for 5%

profile of v2, /device:TPU:16, one launch (start us, length us, event | category | flops | bytes accessed | tf_op | source)
XLA Modules:
  0.0 164.0 jit_solution(7144561141069386097)
XLA Ops:
  1.4 8.2 %shard_map.172 = (bf16[4,2,144,768]{3,2,1,0:T(8,128)(2,1)}, bf16[4,2,144,768]{3,2,1,0:T(8,128)(2,1)}) custom-call(s32[1]{0:T(128)} %bitcast.core_ref, s32[1]{0:T(128)S(6)} %copy.31.count_ref, s32[1,96]{1,0:T(1,128)} %bitcast.44, bf16[768,1536]{1,0:T(8,128)(2,1)} %shared_ref.1, bf16[96,768]{1,0:T(8,128)(2,1)} %routed_ref.1, ...), custom_call_target="tpu_custom_call" | custom-call | flops 2717908992 | bytes 8847360 | tf_op jit(solution)/shard_map/pallas_call | solution.py:96
  9.6 0.5 collective-permute-start
  10.1 5.1 %fusion.3 = f32[1152,1536]{1,0:T(8,128)S(1)} fusion(bf16[1152,768]{1,0:T(8,128)(2,1)} %bitcast.45, bf16[768,2560]{1,0:T(8,128)(2,1)} %param.15), kind=kOutput, calls=%fused_computation.7 | convolution fusion | flops 2717908992 | bytes 11206656 | tf_op jit(solution)/shard_map/dot_general | solution.py:63
  15.3 4.9 %fusion.1 = f16[1152,1536]{1,0:T(8,128)(2,1)S(1)} fusion(f32[1152,1536]{1,0:T(8,128)S(1)} %fusion.3, bf16[1152,768]{1,0:T(8,128)(2,1)S(1)} %bitcast.42, bf16[768,2560]{1,0:T(8,128)(2,1)} %collective-permute-done.1), kind=kOutput, calls=%fused_computation.2 | convolution fusion | flops 2723217408 | bytes 14745600 | tf_op jit(solution)/shard_map/dot_general | solution.py:63
  20.2 0.6 dynamic-slice_bitcast_fusion.2
  20.7 2.8 %collective-permute-start.4 = (f16[4,72,1536]{2,1,0:T(8,128)(2,1)S(1)}, f16[4,72,1536]{2,1,0:T(8,128)(2,1)S(1)}, u32[]{:S(2)}, u32[]{:S(2)}) collective-permute-start(f16[4,72,1536]{2,1,0:T(8,128)(2,1)S(1)} %get-tuple-element.37), channel_id=1, source_target_pairs={{0,3},{1,0},{2,1},{3,2},{4,7},{5,4},{6,5},{7,6},{8,11},{9,8},{10,9... | collective-permute-start | bytes 2654216 | tf_op jit(solution)/shard_map/ppermute | solution.py:28
  23.6 2.3 %collective-permute-start.2 = (f16[4,72,1536]{2,1,0:T(8,128)(2,1)S(1)}, f16[4,72,1536]{2,1,0:T(8,128)(2,1)S(1)}, u32[]{:S(2)}, u32[]{:S(2)}) collective-permute-start(f16[4,72,1536]{2,1,0:T(8,128)(2,1)S(1)} %get-tuple-element.36), channel_id=1, source_target_pairs={{0,2},{1,3},{2,0},{3,1},{4,6},{5,7},{6,4},{7,5},{8,10},{9,11},{10,... | collective-permute-start | bytes 2654216 | tf_op jit(solution)/shard_map/ppermute | solution.py:28
  25.9 3.4 %fusion.8 = f32[1152,1024]{1,0:T(8,128)S(1)} fusion(bf16[1152,768]{1,0:T(8,128)(2,1)S(1)} %bitcast.46, bf16[768,2560]{1,0:T(8,128)(2,1)} %param.15), kind=kOutput, calls=%fused_computation.13 | convolution fusion | flops 1811939328 | bytes 8060928 | tf_op jit(solution)/shard_map/dot_general | solution.py:63
  29.3 3.5 %multiply_convert_fusion = f16[1152,1024]{1,0:T(8,128)(2,1)S(1)} fusion(f32[1152,1024]{1,0:T(8,128)S(1)} %fusion.8, bf16[1152,768]{1,0:T(8,128)(2,1)S(1)} %bitcast.43, bf16[768,2560]{1,0:T(8,128)(2,1)} %collective-permute-done.1), kind=kOutput, calls=%fused_computation.3 | convolution fusion | flops 1815478272 | bytes 10420224 | tf_op jit(solution)/shard_map/dot_general | solution.py:63
  32.8 0.5 dynamic-slice_bitcast_fusion.4
  33.3 0.4 collective-permute-start.5
  33.7 2.4 %collective-permute-start.10 = (f16[4,72,1024]{2,1,0:T(8,128)(2,1)S(1)}, f16[4,72,1024]{2,1,0:T(8,128)(2,1)S(1)}, u32[]{:S(2)}, u32[]{:S(2)}) collective-permute-start(f16[4,72,1024]{2,1,0:T(8,128)(2,1)S(1)} %get-tuple-element.40), channel_id=1, source_target_pairs={{0,160},{32,0},{128,32},{160,128},{1,161},{33,1},{129,33},{161,129... | collective-permute-start | bytes 1769480 | tf_op jit(solution)/shard_map/ppermute | solution.py:32
  36.1 25.5 %collective-permute-done.4 = f16[4,72,1536]{2,1,0:T(8,128)(2,1)S(1)} collective-permute-done((f16[4,72,1536]{2,1,0:T(8,128)(2,1)S(1)}, f16[4,72,1536]{2,1,0:T(8,128)(2,1)S(1)}, u32[]{:S(2)}, u32[]{:S(2)}) %collective-permute-start.4) | collective-permute-done | bytes 884768 | tf_op jit(solution)/shard_map/ppermute | solution.py:28
  61.7 1.3 collective-permute-start.9
  62.9 2.1 %collective-permute-done.3 = f16[4,72,1536]{2,1,0:T(8,128)(2,1)S(1)} collective-permute-done((f16[4,72,1536]{2,1,0:T(8,128)(2,1)S(1)}, f16[4,72,1536]{2,1,0:T(8,128)(2,1)S(1)}, u32[]{:S(2)}, u32[]{:S(2)}) %collective-permute-start.3) | collective-permute-done | bytes 884768 | tf_op jit(solution)/shard_map/ppermute | solution.py:28
  65.0 0.6 fusion.6
  65.8 0.5 collective-permute-start.8
  66.3 1.6 collective-permute-start.7
  67.9 1.3 collective-permute-start.6
  69.2 6.0 %collective-permute-done.9 = f16[4,72,1024]{2,1,0:T(8,128)(2,1)S(1)} collective-permute-done((f16[4,72,1024]{2,1,0:T(8,128)(2,1)S(1)}, f16[4,72,1024]{2,1,0:T(8,128)(2,1)S(1)}, u32[]{:S(2)}, u32[]{:S(2)}) %collective-permute-start.9) | collective-permute-done | bytes 589856 | tf_op jit(solution)/shard_map/ppermute | solution.py:32
  75.3 0.5 fusion.11
  76.0 7.2 %collective-permute-start.12 = (f16[1,72,1024]{2,1,0:T(8,128)(2,1)S(1)}, f16[1,72,1024]{2,1,0:T(8,128)(2,1)S(1)}, u32[]{:S(2)}, u32[]{:S(2)}) collective-permute-start(f16[1,72,1024]{2,1,0:T(8,128)(2,1)S(1)} %get-tuple-element.46), channel_id=1, source_target_pairs={{0,1},{1,2},{2,3},{3,0},{4,5},{5,6},{6,7},{7,4},{8,9},{9,10},{10,1... | collective-permute-start | bytes 442376 | tf_op jit(solution)/shard_map/ppermute | solution.py:28
  83.3 0.6 collective-permute-done.11
  83.9 1.9 %collective-permute-done.12 = f16[1,72,1024]{2,1,0:T(8,128)(2,1)S(1)} collective-permute-done((f16[1,72,1024]{2,1,0:T(8,128)(2,1)S(1)}, f16[1,72,1024]{2,1,0:T(8,128)(2,1)S(1)}, u32[]{:S(2)}, u32[]{:S(2)}) %collective-permute-start.12) | collective-permute-done | bytes 147488 | tf_op jit(solution)/shard_map/ppermute | solution.py:28
  85.8 2.5 %collective-permute-done.13 = f16[1,72,1024]{2,1,0:T(8,128)(2,1)S(1)} collective-permute-done((f16[1,72,1024]{2,1,0:T(8,128)(2,1)S(1)}, f16[1,72,1024]{2,1,0:T(8,128)(2,1)S(1)}, u32[]{:S(2)}, u32[]{:S(2)}) %collective-permute-start.13) | collective-permute-done | bytes 147488 | tf_op jit(solution)/shard_map/ppermute | solution.py:28
  88.5 0.5 reshape.86
  89.0 20.0 %all_to_all.10 = f16[8,180,128]{2,1,0:T(8,128)(2,1)S(1)} all-to-all(f16[8,180,128]{2,1,0:T(8,128)(2,1)S(1)} %reshape.86), channel_id=1, replica_groups=mesh['yh'=2,'core'=2,'yl'=2,'z'=8,'x'=4] {'z'}, dimensions={0} | all-to-all | bytes 737280 | tf_op jit(solution)/shard_map/all_to_all | solution.py:179
  109.1 0.7 subtract_convert_fusion
  109.9 0.7 subtract_convert_fusion.1
  110.7 0.8 broadcast_in_dim.5
  111.5 3.4 %all-to-all-start.1 = ((bf16[8,180,128]{2,1,0:T(8,128)(2,1)}), bf16[8,180,128]{2,1,0:T(8,128)(2,1)S(1)}, u32[]{:S(2)}, u32[]{:S(2)}) async-start(bf16[8,180,128]{2,1,0:T(8,128)(2,1)} %broadcast_in_dim.5), calls=%async_computation.1 | async-start | bytes 753664 | tf_op jit(solution)/shard_map/all_to_all | solution.py:186
  115.2 11.3 %all-to-all-done.1 = bf16[8,180,128]{2,1,0:T(8,128)(2,1)S(1)} async-done(((bf16[8,180,128]{2,1,0:T(8,128)(2,1)}), bf16[8,180,128]{2,1,0:T(8,128)(2,1)S(1)}, u32[]{:S(2)}, u32[]{:S(2)}) %all-to-all-start.1) | async-done | bytes 368672 | tf_op jit(solution)/shard_map/all_to_all | solution.py:186
  126.6 0.3 reshape.87
  126.9 0.7 constant_dynamic-update-slice_fusion.1
  127.6 1.3 collective-permute-start.14
  128.9 0.2 reshape.88
  129.2 3.7 %collective-permute-start.19 = (bf16[24,2560]{1,0:T(8,128)(2,1)S(1)}, bf16[24,2560]{1,0:T(8,128)(2,1)S(1)}, u32[]{:S(2)}, u32[]{:S(2)}) collective-permute-start(bf16[24,2560]{1,0:T(8,128)(2,1)S(1)} %reshape.88), channel_id=1, source_target_pairs={{0,2},{1,3},{2,0},{3,1},{4,6},{5,7},{6,4},{7,5},{8,10},{9,11},{10,... | collective-permute-start | bytes 368648 | tf_op jit(solution)/shard_map/ppermute | solution.py:28
  132.9 2.5 %collective-permute-done.18 = bf16[24,2560]{1,0:T(8,128)(2,1)S(1)} collective-permute-done((bf16[24,2560]{1,0:T(8,128)(2,1)S(1)}, bf16[24,2560]{1,0:T(8,128)(2,1)S(1)}, u32[]{:S(2)}, u32[]{:S(2)}) %collective-permute-start.18) | collective-permute-done | bytes 122912 | tf_op jit(solution)/shard_map/ppermute | solution.py:28
  135.4 3.3 %collective-permute-done.19 = bf16[24,2560]{1,0:T(8,128)(2,1)S(1)} collective-permute-done((bf16[24,2560]{1,0:T(8,128)(2,1)S(1)}, bf16[24,2560]{1,0:T(8,128)(2,1)S(1)}, u32[]{:S(2)}, u32[]{:S(2)}) %collective-permute-start.19) | collective-permute-done | bytes 122912 | tf_op jit(solution)/shard_map/ppermute | solution.py:28
  138.7 4.1 %collective-permute-done.20 = bf16[24,2560]{1,0:T(8,128)(2,1)S(1)} collective-permute-done((bf16[24,2560]{1,0:T(8,128)(2,1)S(1)}, bf16[24,2560]{1,0:T(8,128)(2,1)S(1)}, u32[]{:S(2)}, u32[]{:S(2)}) %collective-permute-start.20) | collective-permute-done | bytes 122912 | tf_op jit(solution)/shard_map/ppermute | solution.py:28
  142.8 1.1 collective-permute-start.21
  144.0 1.8 %collective-permute-start.15 = (bf16[96,2560]{1,0:T(8,128)(2,1)S(1)}, bf16[96,2560]{1,0:T(8,128)(2,1)S(1)}, u32[]{:S(2)}, u32[]{:S(2)}) collective-permute-start(bf16[96,2560]{1,0:T(8,128)(2,1)S(1)} %get-tuple-element.48), channel_id=1, source_target_pairs={{0,1},{1,2},{2,3},{3,0},{4,5},{5,6},{6,7},{7,4},{8,9},{9,10},{10,1... | collective-permute-start | bytes 1474568 | tf_op jit(solution)/shard_map/ppermute | solution.py:28
  145.8 3.6 %collective-permute-start.16 = (bf16[96,2560]{1,0:T(8,128)(2,1)S(1)}, bf16[96,2560]{1,0:T(8,128)(2,1)S(1)}, u32[]{:S(2)}, u32[]{:S(2)}) collective-permute-start(bf16[96,2560]{1,0:T(8,128)(2,1)S(1)} %get-tuple-element.48), channel_id=1, source_target_pairs={{0,2},{1,3},{2,0},{3,1},{4,6},{5,7},{6,4},{7,5},{8,10},{9,11},{10,... | collective-permute-start | bytes 1474568 | tf_op jit(solution)/shard_map/ppermute | solution.py:28
  149.3 2.6 %collective-permute-done.21 = bf16[96,2560]{1,0:T(8,128)(2,1)S(1)} collective-permute-done((bf16[96,2560]{1,0:T(8,128)(2,1)S(1)}, bf16[96,2560]{1,0:T(8,128)(2,1)S(1)}, u32[]{:S(2)}, u32[]{:S(2)}) %collective-permute-start.21) | collective-permute-done | bytes 491552 | tf_op jit(solution)/shard_map/ppermute | solution.py:36
  152.0 1.4 convolution_convert_fusion.1
  153.3 1.4 collective-permute-done.15
  154.7 6.7 %collective-permute-done.16 = bf16[96,2560]{1,0:T(8,128)(2,1)S(1)} collective-permute-done((bf16[96,2560]{1,0:T(8,128)(2,1)S(1)}, bf16[96,2560]{1,0:T(8,128)(2,1)S(1)}, u32[]{:S(2)}, u32[]{:S(2)}) %collective-permute-start.16) | collective-permute-done | bytes 491552 | tf_op jit(solution)/shard_map/ppermute | solution.py:28
  161.5 2.5 %convolution_convert_fusion = bf16[384,2560]{1,0:T(8,128)(2,1)} fusion(bf16[384,384]{1,0:T(8,128)(2,1)S(1)} %fusion.12, bf16[384,2560]{1,0:T(8,128)(2,1)S(1)} %constant_dynamic-update-slice_fusion.2), kind=kOutput, calls=%fused_computation.4 | convolution fusion | flops 755957760 | bytes 4227072 | tf_op jit(solution)/shard_map/dot_general | solution.py:63
  (62 shorter events, 1.6 us)
Async XLA Ops:
  0.6 14.6 %collective-permute-start.1 = (bf16[768,2560]{1,0:T(8,128)(2,1)}, bf16[768,2560]{1,0:T(8,128)(2,1)}, u32[]{:S(2)}, u32[]{:S(2)}) collective-permute-start(bf16[768,2560]{1,0:T(8,128)(2,1)} %param.15), channel_id=1, source_target_pairs={{0,64},{64,0},{1,65},{65,1},{2,66},{66,2},{3,67},{67,3},{4,68},{68... | collective-permute-start | bytes 11796488 | tf_op jit(solution)/shard_map/ppermute | solution.py:40
  9.6 5.6 %collective-permute-start = (bf16[4,2,144,768]{3,2,1,0:T(8,128)(2,1)}, bf16[4,2,144,768]{3,2,1,0:T(8,128)(2,1)S(1)}, u32[]{:S(2)}, u32[]{:S(2)}) collective-permute-start(bf16[4,2,144,768]{3,2,1,0:T(8,128)(2,1)} %get-tuple-element.19), channel_id=1, source_target_pairs={{0,64},{64,0},{1,65},{65,1},{2,66},{66,2},{3,67},{67,3},{4,68},{68... | collective-permute-start | bytes 5308424 | tf_op jit(solution)/shard_map/ppermute | solution.py:40
  20.1 5.7 %copy-start.7 = (bf16[4,2,144,768]{3,2,1,0:T(8,128)(2,1)S(1)}, bf16[4,2,144,768]{3,2,1,0:T(8,128)(2,1)}, u32[]{:S(2)}) copy-start(bf16[4,2,144,768]{3,2,1,0:T(8,128)(2,1)} %get-tuple-element.18) | copy-start | bytes 5308420
  20.7 40.9 %collective-permute-start.4 = (f16[4,72,1536]{2,1,0:T(8,128)(2,1)S(1)}, f16[4,72,1536]{2,1,0:T(8,128)(2,1)S(1)}, u32[]{:S(2)}, u32[]{:S(2)}) collective-permute-start(f16[4,72,1536]{2,1,0:T(8,128)(2,1)S(1)} %get-tuple-element.37), channel_id=1, source_target_pairs={{0,3},{1,0},{2,1},{3,2},{4,7},{5,4},{6,5},{7,6},{8,11},{9,8},{10,9... | collective-permute-start | bytes 2654216 | tf_op jit(solution)/shard_map/ppermute | solution.py:28
  23.6 41.5 %collective-permute-start.3 = (f16[4,72,1536]{2,1,0:T(8,128)(2,1)S(1)}, f16[4,72,1536]{2,1,0:T(8,128)(2,1)S(1)}, u32[]{:S(2)}, u32[]{:S(2)}) collective-permute-start(f16[4,72,1536]{2,1,0:T(8,128)(2,1)S(1)} %get-tuple-element.38), channel_id=1, source_target_pairs={{0,1},{1,2},{2,3},{3,0},{4,5},{5,6},{6,7},{7,4},{8,9},{9,10},{10,1... | collective-permute-start | bytes 2654216 | tf_op jit(solution)/shard_map/ppermute | solution.py:28
  23.6 41.5 %collective-permute-start.2 = (f16[4,72,1536]{2,1,0:T(8,128)(2,1)S(1)}, f16[4,72,1536]{2,1,0:T(8,128)(2,1)S(1)}, u32[]{:S(2)}, u32[]{:S(2)}) collective-permute-start(f16[4,72,1536]{2,1,0:T(8,128)(2,1)S(1)} %get-tuple-element.36), channel_id=1, source_target_pairs={{0,2},{1,3},{2,0},{3,1},{4,6},{5,7},{6,4},{7,5},{8,10},{9,11},{10,... | collective-permute-start | bytes 2654216 | tf_op jit(solution)/shard_map/ppermute | solution.py:28
  33.3 32.5 %collective-permute-start.5 = (f16[4,72,1024]{2,1,0:T(8,128)(2,1)S(1)}, f16[4,72,1024]{2,1,0:T(8,128)(2,1)S(1)}, u32[]{:S(2)}, u32[]{:S(2)}) collective-permute-start(f16[4,72,1024]{2,1,0:T(8,128)(2,1)S(1)} %get-tuple-element.41), channel_id=1, source_target_pairs={{0,128},{32,160},{128,0},{160,32},{1,129},{33,161},{129,1},{161,33... | collective-permute-start | bytes 1769480 | tf_op jit(solution)/shard_map/ppermute | solution.py:32
  33.7 35.5 %collective-permute-start.10 = (f16[4,72,1024]{2,1,0:T(8,128)(2,1)S(1)}, f16[4,72,1024]{2,1,0:T(8,128)(2,1)S(1)}, u32[]{:S(2)}, u32[]{:S(2)}) collective-permute-start(f16[4,72,1024]{2,1,0:T(8,128)(2,1)S(1)} %get-tuple-element.40), channel_id=1, source_target_pairs={{0,160},{32,0},{128,32},{160,128},{1,161},{33,1},{129,33},{161,129... | collective-permute-start | bytes 1769480 | tf_op jit(solution)/shard_map/ppermute | solution.py:32
  61.7 13.6 %collective-permute-start.9 = (f16[4,72,1024]{2,1,0:T(8,128)(2,1)S(1)}, f16[4,72,1024]{2,1,0:T(8,128)(2,1)S(1)}, u32[]{:S(2)}, u32[]{:S(2)}) collective-permute-start(f16[4,72,1024]{2,1,0:T(8,128)(2,1)S(1)} %get-tuple-element.39), channel_id=1, source_target_pairs={{0,32},{32,128},{128,160},{160,0},{1,33},{33,129},{129,161},{161,1... | collective-permute-start | bytes 1769480 | tf_op jit(solution)/shard_map/ppermute | solution.py:32
  65.8 17.3 %collective-permute-start.8 = (f16[1,72,1536]{2,1,0:T(8,128)(2,1)S(1)}, f16[1,72,1536]{2,1,0:T(8,128)(2,1)S(1)}, u32[]{:S(2)}, u32[]{:S(2)}) collective-permute-start(f16[1,72,1536]{2,1,0:T(8,128)(2,1)S(1)} %get-tuple-element.24), channel_id=1, source_target_pairs={{0,160},{32,0},{128,32},{160,128},{1,161},{33,1},{129,33},{161,129... | collective-permute-start | bytes 663560 | tf_op jit(solution)/shard_map/ppermute | solution.py:32
  66.3 16.8 %collective-permute-start.7 = (f16[1,72,1536]{2,1,0:T(8,128)(2,1)S(1)}, f16[1,72,1536]{2,1,0:T(8,128)(2,1)S(1)}, u32[]{:S(2)}, u32[]{:S(2)}) collective-permute-start(f16[1,72,1536]{2,1,0:T(8,128)(2,1)S(1)} %get-tuple-element.23), channel_id=1, source_target_pairs={{0,32},{32,128},{128,160},{160,0},{1,33},{33,129},{129,161},{161,1... | collective-permute-start | bytes 663560 | tf_op jit(solution)/shard_map/ppermute | solution.py:32
  67.9 15.2 %collective-permute-start.6 = (f16[1,72,1536]{2,1,0:T(8,128)(2,1)S(1)}, f16[1,72,1536]{2,1,0:T(8,128)(2,1)S(1)}, u32[]{:S(2)}, u32[]{:S(2)}) collective-permute-start(f16[1,72,1536]{2,1,0:T(8,128)(2,1)S(1)} %get-tuple-element.22), channel_id=1, source_target_pairs={{0,128},{32,160},{128,0},{160,32},{1,129},{33,161},{129,1},{161,33... | collective-permute-start | bytes 663560 | tf_op jit(solution)/shard_map/ppermute | solution.py:32
  75.9 8.1 %collective-permute-start.11 = (f16[1,72,1024]{2,1,0:T(8,128)(2,1)S(1)}, f16[1,72,1024]{2,1,0:T(8,128)(2,1)S(1)}, u32[]{:S(2)}, u32[]{:S(2)}) collective-permute-start(f16[1,72,1024]{2,1,0:T(8,128)(2,1)S(1)} %get-tuple-element.47), channel_id=1, source_target_pairs={{0,2},{1,3},{2,0},{3,1},{4,6},{5,7},{6,4},{7,5},{8,10},{9,11},{10,... | collective-permute-start | bytes 442376 | tf_op jit(solution)/shard_map/ppermute | solution.py:28
  76.0 9.8 %collective-permute-start.12 = (f16[1,72,1024]{2,1,0:T(8,128)(2,1)S(1)}, f16[1,72,1024]{2,1,0:T(8,128)(2,1)S(1)}, u32[]{:S(2)}, u32[]{:S(2)}) collective-permute-start(f16[1,72,1024]{2,1,0:T(8,128)(2,1)S(1)} %get-tuple-element.46), channel_id=1, source_target_pairs={{0,1},{1,2},{2,3},{3,0},{4,5},{5,6},{6,7},{7,4},{8,9},{9,10},{10,1... | collective-permute-start | bytes 442376 | tf_op jit(solution)/shard_map/ppermute | solution.py:28
  83.1 5.1 %collective-permute-start.13 = (f16[1,72,1024]{2,1,0:T(8,128)(2,1)S(1)}, f16[1,72,1024]{2,1,0:T(8,128)(2,1)S(1)}, u32[]{:S(2)}, u32[]{:S(2)}) collective-permute-start(f16[1,72,1024]{2,1,0:T(8,128)(2,1)S(1)} %get-tuple-element.45), channel_id=1, source_target_pairs={{0,3},{1,0},{2,1},{3,2},{4,7},{5,4},{6,5},{7,6},{8,11},{9,8},{10,9... | collective-permute-start | bytes 442376 | tf_op jit(solution)/shard_map/ppermute | solution.py:28
  83.3 25.8 %copy-start.1 = (f32[6,2560]{1,0:T(8,128)S(1)}, f32[6,2560]{1,0:T(8,128)}, u32[]{:S(2)}) copy-start(f32[6,2560]{1,0:T(8,128)} %param.18) | copy-start | bytes 184324
  83.3 25.8 %copy-start.2 = (f32[6,2560]{1,0:T(8,128)S(1)}, f32[6,2560]{1,0:T(8,128)}, u32[]{:S(2)}) copy-start(f32[6,2560]{1,0:T(8,128)} %param.20) | copy-start | bytes 184324
  83.3 25.8 %copy-start.3 = (f32[6,2560]{1,0:T(8,128)S(1)}, f32[6,2560]{1,0:T(8,128)}, u32[]{:S(2)}) copy-start(f32[6,2560]{1,0:T(8,128)} %param.19) | copy-start | bytes 184324
  88.4 21.5 %copy-start.4 = (f32[3,2560]{1,0:T(4,128)S(1)}, f32[3,2560]{1,0:T(4,128)}, u32[]{:S(2)}) copy-start(f32[3,2560]{1,0:T(4,128)} %param.21) | copy-start | bytes 92164
  88.4 21.5 %copy-start.5 = (f32[3,2560]{1,0:T(4,128)S(1)}, f32[3,2560]{1,0:T(4,128)}, u32[]{:S(2)}) copy-start(f32[3,2560]{1,0:T(4,128)} %param.23) | copy-start | bytes 92164
  88.4 21.5 %copy-start.6 = (f32[3,2560]{1,0:T(4,128)S(1)}, f32[3,2560]{1,0:T(4,128)}, u32[]{:S(2)}) copy-start(f32[3,2560]{1,0:T(4,128)} %param.22) | copy-start | bytes 92164
  111.5 15.1 %all-to-all-start.1 = ((bf16[8,180,128]{2,1,0:T(8,128)(2,1)}), bf16[8,180,128]{2,1,0:T(8,128)(2,1)S(1)}, u32[]{:S(2)}, u32[]{:S(2)}) async-start(bf16[8,180,128]{2,1,0:T(8,128)(2,1)} %broadcast_in_dim.5), calls=%async_computation.1 | async-start | bytes 753664 | tf_op jit(solution)/shard_map/all_to_all | solution.py:186
  127.6 16.3 %collective-permute-start.14 = (bf16[48,2560]{1,0:T(8,128)(2,1)S(1)}, bf16[48,2560]{1,0:T(8,128)(2,1)S(1)}, u32[]{:S(2)}, u32[]{:S(2)}) collective-permute-start(bf16[48,2560]{1,0:T(8,128)(2,1)S(1)} %reshape.87), channel_id=1, source_target_pairs={{0,32},{32,0},{1,33},{33,1},{2,34},{34,2},{3,35},{35,3},{4,36},{36... | collective-permute-start | bytes 737288 | tf_op jit(solution)/shard_map/ppermute | solution.py:36
  129.1 14.8 %copy-start = (bf16[96,2560]{1,0:T(8,128)(2,1)S(1)}, bf16[96,2560]{1,0:T(8,128)(2,1)}, u32[]{:S(2)}) copy-start(bf16[96,2560]{1,0:T(8,128)(2,1)} %get-tuple-element.50) | copy-start | bytes 1474564
  129.1 6.3 %collective-permute-start.18 = (bf16[24,2560]{1,0:T(8,128)(2,1)S(1)}, bf16[24,2560]{1,0:T(8,128)(2,1)S(1)}, u32[]{:S(2)}, u32[]{:S(2)}) collective-permute-start(bf16[24,2560]{1,0:T(8,128)(2,1)S(1)} %reshape.88), channel_id=1, source_target_pairs={{0,1},{1,2},{2,3},{3,0},{4,5},{5,6},{6,7},{7,4},{8,9},{9,10},{10,1... | collective-permute-start | bytes 368648 | tf_op jit(solution)/shard_map/ppermute | solution.py:28
  129.2 9.5 %collective-permute-start.19 = (bf16[24,2560]{1,0:T(8,128)(2,1)S(1)}, bf16[24,2560]{1,0:T(8,128)(2,1)S(1)}, u32[]{:S(2)}, u32[]{:S(2)}) collective-permute-start(bf16[24,2560]{1,0:T(8,128)(2,1)S(1)} %reshape.88), channel_id=1, source_target_pairs={{0,2},{1,3},{2,0},{3,1},{4,6},{5,7},{6,4},{7,5},{8,10},{9,11},{10,... | collective-permute-start | bytes 368648 | tf_op jit(solution)/shard_map/ppermute | solution.py:28
  132.9 9.9 %collective-permute-start.20 = (bf16[24,2560]{1,0:T(8,128)(2,1)S(1)}, bf16[24,2560]{1,0:T(8,128)(2,1)S(1)}, u32[]{:S(2)}, u32[]{:S(2)}) collective-permute-start(bf16[24,2560]{1,0:T(8,128)(2,1)S(1)} %reshape.88), channel_id=1, source_target_pairs={{0,3},{1,0},{2,1},{3,2},{4,7},{5,4},{6,5},{7,6},{8,11},{9,8},{10,9... | collective-permute-start | bytes 368648 | tf_op jit(solution)/shard_map/ppermute | solution.py:28
  142.8 9.1 %collective-permute-start.21 = (bf16[96,2560]{1,0:T(8,128)(2,1)S(1)}, bf16[96,2560]{1,0:T(8,128)(2,1)S(1)}, u32[]{:S(2)}, u32[]{:S(2)}) collective-permute-start(bf16[96,2560]{1,0:T(8,128)(2,1)S(1)} %pad_maximum_fusion), channel_id=1, source_target_pairs={{0,32},{32,0},{1,33},{33,1},{2,34},{34,2},{3,35},{35,3},{4,36},{36... | collective-permute-start | bytes 1474568 | tf_op jit(solution)/shard_map/ppermute | solution.py:36
  144.0 10.7 %collective-permute-start.15 = (bf16[96,2560]{1,0:T(8,128)(2,1)S(1)}, bf16[96,2560]{1,0:T(8,128)(2,1)S(1)}, u32[]{:S(2)}, u32[]{:S(2)}) collective-permute-start(bf16[96,2560]{1,0:T(8,128)(2,1)S(1)} %get-tuple-element.48), channel_id=1, source_target_pairs={{0,1},{1,2},{2,3},{3,0},{4,5},{5,6},{6,7},{7,4},{8,9},{9,10},{10,1... | collective-permute-start | bytes 1474568 | tf_op jit(solution)/shard_map/ppermute | solution.py:28
  145.8 15.7 %collective-permute-start.16 = (bf16[96,2560]{1,0:T(8,128)(2,1)S(1)}, bf16[96,2560]{1,0:T(8,128)(2,1)S(1)}, u32[]{:S(2)}, u32[]{:S(2)}) collective-permute-start(bf16[96,2560]{1,0:T(8,128)(2,1)S(1)} %get-tuple-element.48), channel_id=1, source_target_pairs={{0,2},{1,3},{2,0},{3,1},{4,6},{5,7},{6,4},{7,5},{8,10},{9,11},{10,... | collective-permute-start | bytes 1474568 | tf_op jit(solution)/shard_map/ppermute | solution.py:28
  149.3 12.1 %collective-permute-start.17 = (bf16[96,2560]{1,0:T(8,128)(2,1)S(1)}, bf16[96,2560]{1,0:T(8,128)(2,1)S(1)}, u32[]{:S(2)}, u32[]{:S(2)}) collective-permute-start(bf16[96,2560]{1,0:T(8,128)(2,1)S(1)} %get-tuple-element.48), channel_id=1, source_target_pairs={{0,3},{1,0},{2,1},{3,2},{4,7},{5,4},{6,5},{7,6},{8,11},{9,8},{10,9... | collective-permute-start | bytes 1474568 | tf_op jit(solution)/shard_map/ppermute | solution.py:28

commit v3 on v2

--- a/solution.py
+++ b/solution.py
@@ -38,6 +38,10 @@
 
 def core_swap(v):
     return lax.ppermute(v, "core", [(0, 1), (1, 0)])
+
+
+def after(done, v):
+    return lax.optimization_barrier((v, *done))[0]
 
 
 def row_order(sr, rr):
@@ -160,19 +164,41 @@
     def gathered(v, dim, back):
         return sum((b.astype(F32) for b in back), pick(v, dim, 0).astype(F32))
 
+    def halves(total, dim):
+        two, ahead, behind = (pick(total, dim, d) for d in (2, 1, 3))
+        plus = jnp.concatenate([two[:2], ahead[2:]])
+        minus = jnp.concatenate([two[2:], behind[:2]])
+        return plus, minus
+
+    def both(chunks, dim):
+        ring = (x_ring, y_ring)[dim]
+        return ring(chunks[0], 1), ring(chunks[1], 3)
+
+    def relayed(total, dim, plus, minus):
+        ahead = pick(total, dim, 1)[:2].astype(F32) + plus[:2].astype(F32)
+        behind = pick(total, dim, 3)[2:].astype(F32) + minus[:2].astype(F32)
+        return both((ahead.astype(F16), behind.astype(F16)), dim)
+
+    def summed(total, dim, plus, minus, ahead, behind):
+        got = jnp.concatenate([minus[2:], plus[2:]]).astype(F32)
+        got = got + jnp.concatenate([ahead, behind]).astype(F32)
+        return pick(total, dim, 0).astype(F32) + got
+
     total_a = term(near, slice(0, part_a))
-    near, total_a = lax.optimization_barrier((near, total_a))
+    first_a = halves(total_a, 0)
+    near = after(first_a, near)
     total_b = term(near, slice(part_a, width))
-    back_a = send(cut(total_a, 0), 0)
-    back_b = send(cut(total_b, 1), 1)
-    one_a = gathered(total_a, 0, back_a)[None]
+    first_a = both(first_a, 0)
+    first_b = both(halves(total_b, 1), 1)
+    one_a = summed(total_a, 0, *first_a, *relayed(total_a, 0, *first_a))[None]
+    last_b = relayed(total_b, 1, *first_b)
     chunks_a = cut(one_a, 1)
-    back_b[0], *chunks_a = lax.optimization_barrier((back_b[0], *chunks_a))
+    last_b = [after(chunks_a, v) for v in last_b]
     two_a = send(chunks_a, 1)
-    one_b = gathered(total_b, 1, back_b)[:, None]
+    one_b = summed(total_b, 1, *first_b, *last_b)[:, None]
     two_b = send(cut(one_b, 0), 0)
     two_a = gathered(one_a, 1, two_a)[0].astype(F16)
-    two_a, *two_b = lax.optimization_barrier((two_a, *two_b))
+    two_b = [after([two_a], v) for v in two_b]
     two_b = gathered(one_b, 0, two_b)[0].astype(F16)
     two = [two_a, two_b]
     last = jnp.concatenate(two, axis=1).reshape(NZ, rows * width // 128, 128)
@@ -188,7 +214,10 @@
     weight_r = weight[:, sr * width // 128 :].reshape(NZ * rr, width)
     all_s = jnp.concatenate([weight_s, y_swap(weight_s)], axis=0)
     all_r = jnp.concatenate([weight_r] + [x_ring(weight_r, d) for d in (1, 2, 3)], axis=0)
-    all_s = jnp.concatenate([all_s] + [x_ring(all_s, d) for d in (1, 2, 3)], axis=0)
+    one_way, other_way = x_ring(all_s, 1), x_ring(all_s, 3)
+    split = all_s.shape[0] // 2
+    two_away = [x_ring(one_way[:split], 1), x_ring(other_way[split:], 3)]
+    all_s = jnp.concatenate([all_s, one_way] + two_away + [other_way], axis=0)
     all_r = jnp.concatenate([all_r, y_swap(all_r)], axis=0)
 
     def settled(full, count, index):

time: 164 us -> 154 us (0.939); the launches traced: 164 us -> 151 us
  waiting for transfers between devices: 70.5 us -> 44.2 us
  other arithmetic: 3.5 us -> 10.8 us
  starting transfers between devices: 35.5 us -> 39 us
  local copies, waits for them, and re-layouts: 3.91 us -> 6.12 us
    ppermute x12 -> x14, waiting for transfers between devices: 50.5 us -> 28 us  [x_ring(): return lax.ppermute(v, 'x', [(i, (i + d) % NX) for i in range(NX)])]
    ppermute x6 -> x7, waiting for transfers between devices: 6.04 us -> 1 us  [y_ring(): return lax.ppermute(v, ('yh', 'yl'), [(i, (i + d) % NY) for i in range(NY)])]
    ppermute x12 -> x14, starting transfers between devices: 21.5 us -> 24.8 us  [x_ring(): return lax.ppermute(v, 'x', [(i, (i + d) % NX) for i in range(NX)])]
    convert_element_type x0 -> x2, other arithmetic: none -> 2.76 us  [relayed(): return both((ahead.astype(F16), behind.astype(F16)), dim)]
    slice x0 -> x10, local copies, waits for them, and re-layouts: none -> 2.75 us  [the longest x6 2.03 us: summed(): got = jnp.concatenate([minus[2:], plus[2:]]).astype(F32)]
    concatenate x0 -> x4, other arithmetic: none -> 2.67 us  [the longest x2 1.5 us: halves(): minus = jnp.concatenate([two[2:], behind[:2]])]
    add x2, other arithmetic: 1.17 us -> 3.1 us  [summed(): return pick(total, dim, 0).astype(F32) + got]
    ppermute x6 -> x7, starting transfers between devices: 7.53 us -> 7.07 us  [y_ring(): return lax.ppermute(v, ('yh', 'yl'), [(i, (i + d) % NY) for i in range(NY)])]
  transfers between devices with their start and end apart: 23 -> 26, of which waited for: 13 -> 12; matrix products, arithmetic and copies ran while one was open for 10% -> 17% of each run, Pallas kernels for 5% -> 5%
where the time goes in v3:
time: 154 us; the launch traced here: 151 us
  waiting for transfers between devices  44.2 us (29%)
  starting transfers between devices  39 us (25%)
  matrix products  21.1 us (14%)
  blocking collectives  20 us (13%)
  other arithmetic  10.8 us (7%)
  Pallas kernels  8.31 us (5%)
  local copies, waits for them, and re-layouts  6.12 us (4%)
  between operations  1.8 us (1%)
    ppermute x14, waiting for transfers between devices, x_ring(): return lax.ppermute(v, 'x', [(i, (i + d) % NX) for i in range(NX)])  28 us
    ppermute x14, starting transfers between devices, x_ring(): return lax.ppermute(v, 'x', [(i, (i + d) % NX) for i in range(NX)])  24.8 us
    dot_general x6, matrix products, dot(): return jnp.dot(a, b, preferred_element_type=F32)  21.1 us
    all_to_all x1, blocking collectives, local(): last = lax.all_to_all(last, 'z', 0, 0)  20 us
    all_to_all x1, waiting for transfers between devices, local(): lax.all_to_all(jnp.broadcast_to(weight, (NZ,) + weight.shape[1:]), 'z', 0...  11.1 us
    pallas_call x1, Pallas kernels, ordered(): pl.pallas_call(order_kernel, grid_spec=pltpu.PrefetchScalarGridSpec(num_s...  8.31 us
    ppermute x7, starting transfers between devices, y_ring(): return lax.ppermute(v, ('yh', 'yl'), [(i, (i + d) % NY) for i in range(NY)])  7.07 us
    ppermute x2, waiting for transfers between devices, y_swap(): return lax.ppermute(v, 'yl', [(0, 1), (1, 0)])  4.06 us
  transfers between devices with their start and end apart: 26, of which 12 were waited for; matrix products, arithmetic and copies ran while one was open for 17% of the time, Pallas kernels for 5%

profile of v3, /device:TPU:16, one launch (start us, length us, event | category | flops | bytes accessed | tf_op | source)
XLA Modules:
  0.0 151.4 jit_solution(4193611435241501934)
XLA Ops:
  1.4 8.3 %shard_map.172 = (bf16[4,2,144,768]{3,2,1,0:T(8,128)(2,1)}, bf16[4,2,144,768]{3,2,1,0:T(8,128)(2,1)}) custom-call(s32[1]{0:T(128)} %bitcast.core_ref, s32[1]{0:T(128)S(6)} %copy.47.count_ref, s32[1,96]{1,0:T(1,128)} %bitcast.85, bf16[768,1536]{1,0:T(8,128)(2,1)} %shared_ref.1, bf16[96,768]{1,0:T(8,128)(2,1)} %routed_ref.1, ...), custom_call_target="tpu_custom_call" | custom-call | flops 2717908992 | bytes 8847360 | tf_op jit(solution)/shard_map/pallas_call | solution.py:100
  9.7 0.5 collective-permute-start
  10.2 5.1 %fusion.3 = f32[1152,1536]{1,0:T(8,128)S(1)} fusion(bf16[1152,768]{1,0:T(8,128)(2,1)} %bitcast.86, bf16[768,2560]{1,0:T(8,128)(2,1)} %param.15), kind=kOutput, calls=%fused_computation.7 | convolution fusion | flops 2717908992 | bytes 11206656 | tf_op jit(solution)/shard_map/dot_general | solution.py:67
  15.4 1.2 copy-done.9
  16.6 5.2 %fusion.1 = f16[1152,1536]{1,0:T(8,128)(2,1)S(1)} fusion(f32[1152,1536]{1,0:T(8,128)S(1)} %fusion.3, bf16[1152,768]{1,0:T(8,128)(2,1)} %bitcast.83, bf16[768,2560]{1,0:T(8,128)(2,1)} %collective-permute-done.1), kind=kOutput, calls=%fused_computation.2 | convolution fusion | flops 2723217408 | bytes 14745600 | tf_op jit(solution)/shard_map/dot_general | solution.py:67
  22.4 2.8 %collective-permute-start.2 = (f16[4,72,1536]{2,1,0:T(8,128)(2,1)S(1)}, f16[4,72,1536]{2,1,0:T(8,128)(2,1)S(1)}, u32[]{:S(2)}, u32[]{:S(2)}) collective-permute-start(f16[4,72,1536]{2,1,0:T(8,128)(2,1)S(1)} %pad_maximum_fusion), channel_id=1, source_target_pairs={{0,3},{1,0},{2,1},{3,2},{4,7},{5,4},{6,5},{7,6},{8,11},{9,8},{10,9... | collective-permute-start | bytes 2654216 | tf_op jit(solution)/shard_map/ppermute | solution.py:28
  25.5 3.5 %fusion.6 = f32[1152,1024]{1,0:T(8,128)S(1)} fusion(bf16[1152,768]{1,0:T(8,128)(2,1)S(1)} %bitcast.87, bf16[768,2560]{1,0:T(8,128)(2,1)} %param.15), kind=kOutput, calls=%fused_computation.11 | convolution fusion | flops 1811939328 | bytes 8060928 | tf_op jit(solution)/shard_map/dot_general | solution.py:67
  29.1 3.4 %multiply_convert_fusion = f16[1152,1024]{1,0:T(8,128)(2,1)S(1)} fusion(f32[1152,1024]{1,0:T(8,128)S(1)} %fusion.6, bf16[1152,768]{1,0:T(8,128)(2,1)S(1)} %bitcast.84, bf16[768,2560]{1,0:T(8,128)(2,1)} %collective-permute-done.1), kind=kOutput, calls=%fused_computation.3 | convolution fusion | flops 1815478272 | bytes 10420224 | tf_op jit(solution)/shard_map/dot_general | solution.py:67
  32.9 1.3 pad_maximum_fusion.2
  34.6 1.0 pad_maximum_fusion.3
  35.6 1.6 %collective-permute-start.10 = (f16[4,72,1024]{2,1,0:T(8,128)(2,1)}, f16[4,72,1024]{2,1,0:T(8,128)(2,1)}, u32[]{:S(2)}, u32[]{:S(2)}) collective-permute-start(f16[4,72,1024]{2,1,0:T(8,128)(2,1)} %pad_maximum_fusion.3), channel_id=1, source_target_pairs={{0,32},{32,128},{128,160},{160,0},{1,33},{33,129},{129,161},{161,1... | collective-permute-start | bytes 1769480 | tf_op jit(solution)/shard_map/ppermute | solution.py:32
  37.1 7.1 %collective-permute-done.2 = f16[4,72,1536]{2,1,0:T(8,128)(2,1)S(1)} collective-permute-done((f16[4,72,1536]{2,1,0:T(8,128)(2,1)S(1)}, f16[4,72,1536]{2,1,0:T(8,128)(2,1)S(1)}, u32[]{:S(2)}, u32[]{:S(2)}) %collective-permute-start.2) | collective-permute-done | bytes 884768 | tf_op jit(solution)/shard_map/ppermute | solution.py:28
  44.3 3.7 %collective-permute-done.3 = f16[4,72,1536]{2,1,0:T(8,128)(2,1)S(1)} collective-permute-done((f16[4,72,1536]{2,1,0:T(8,128)(2,1)S(1)}, f16[4,72,1536]{2,1,0:T(8,128)(2,1)S(1)}, u32[]{:S(2)}, u32[]{:S(2)}) %collective-permute-start.3) | collective-permute-done | bytes 884768 | tf_op jit(solution)/shard_map/ppermute | solution.py:28
  48.0 1.2 fusion.9
  49.2 3.2 %collective-permute-start.5 = (f16[2,72,1536]{2,1,0:T(8,128)(2,1)}, f16[2,72,1536]{2,1,0:T(8,128)(2,1)}, u32[]{:S(2)}, u32[]{:S(2)}) collective-permute-start(f16[2,72,1536]{2,1,0:T(8,128)(2,1)} %get-tuple-element.29), channel_id=1, source_target_pairs={{0,3},{1,0},{2,1},{3,2},{4,7},{5,4},{6,5},{7,6},{8,11},{9,8},{10,9... | collective-permute-start | bytes 1327112 | tf_op jit(solution)/shard_map/ppermute | solution.py:28
  52.4 1.6 %fusion.11 = (f16[2,72,1024]{2,1,0:T(8,128)(2,1)S(1)}, f16[2,72,1024]{2,1,0:T(8,128)(2,1)S(1)}) fusion(f16[4,72,1024]{2,1,0:T(8,128)(2,1)} %collective-permute-done.10, f16[4,4,72,1024]{3,2,1,0:T(8,128)(2,1)} %bitcast.81, s32[]{:T(128)S(6)} %select_n.170, f16[4,72,1024]{2,1,0:T(8,128)(2,1)} %collective-permute-done.9, s32[]{:T(128)S(6)} %add.309, ...), kind=kLoop, calls=%fused_computation.26 | loop fusion | flops 1179648 | bytes 1769484 | tf_op jit(solution)/shard_map/convert_element_type | solution.py:180
  54.0 1.4 collective-permute-start.11
  55.4 0.7 collective-permute-start.12
  56.1 1.0 slice.170
  57.1 1.0 slice.171
  58.1 3.5 %collective-permute-done.4 = f16[2,72,1536]{2,1,0:T(8,128)(2,1)} collective-permute-done((f16[2,72,1536]{2,1,0:T(8,128)(2,1)}, f16[2,72,1536]{2,1,0:T(8,128)(2,1)}, u32[]{:S(2)}, u32[]{:S(2)}) %collective-permute-start.4) | collective-permute-done | bytes 442400 | tf_op jit(solution)/shard_map/ppermute | solution.py:28
  61.6 1.6 %convert_add_fusion = f32[4,72,1536]{2,1,0:T(8,128)S(1)} fusion(f16[2,72,1536]{2,1,0:T(8,128)(2,1)S(1)} %slice-done.1, f16[2,72,1536]{2,1,0:T(8,128)(2,1)S(1)} %slice-done, f16[2,72,1536]{2,1,0:T(8,128)(2,1)} %collective-permute-done.5, f16[2,72,1536]{2,1,0:T(8,128)(2,1)} %collective-permute-done.4, f16[4,4,72,1536]{3,2,1,0:T(8,128)(2,1)S(1)} %bitcast.79, ...), kind=kLoop, calls=%fused_computation.9 | loop fusion | flops 3096576 | bytes 4423684 | tf_op jit(solution)/shard_map/add | solution.py:185
  63.4 0.5 collective-permute-start.6
  63.9 2.1 %collective-permute-start.7 = (f16[1,72,1536]{2,1,0:T(8,128)(2,1)S(1)}, f16[1,72,1536]{2,1,0:T(8,128)(2,1)S(1)}, u32[]{:S(2)}, u32[]{:S(2)}) collective-permute-start(f16[1,72,1536]{2,1,0:T(8,128)(2,1)S(1)} %get-tuple-element.41), channel_id=1, source_target_pairs={{0,32},{32,128},{128,160},{160,0},{1,33},{33,129},{129,161},{161,1... | collective-permute-start | bytes 663560 | tf_op jit(solution)/shard_map/ppermute | solution.py:32
  66.3 1.5 convert_add_fusion.1
  67.9 1.5 %collective-permute-start.13 = (f16[1,72,1024]{2,1,0:T(8,128)(2,1)S(1)}, f16[1,72,1024]{2,1,0:T(8,128)(2,1)S(1)}, u32[]{:S(2)}, u32[]{:S(2)}) collective-permute-start(f16[1,72,1024]{2,1,0:T(8,128)(2,1)S(1)} %get-tuple-element.43), channel_id=1, source_target_pairs={{0,2},{1,3},{2,0},{3,1},{4,6},{5,7},{6,4},{7,5},{8,10},{9,11},{10,... | collective-permute-start | bytes 442376 | tf_op jit(solution)/shard_map/ppermute | solution.py:28
  69.4 2.3 %collective-permute-start.14 = (f16[1,72,1024]{2,1,0:T(8,128)(2,1)S(1)}, f16[1,72,1024]{2,1,0:T(8,128)(2,1)S(1)}, u32[]{:S(2)}, u32[]{:S(2)}) collective-permute-start(f16[1,72,1024]{2,1,0:T(8,128)(2,1)S(1)} %get-tuple-element.45), channel_id=1, source_target_pairs={{0,1},{1,2},{2,3},{3,0},{4,5},{5,6},{6,7},{7,4},{8,9},{9,10},{10,1... | collective-permute-start | bytes 442376 | tf_op jit(solution)/shard_map/ppermute | solution.py:28
  71.8 1.0 collective-permute-done.6
  72.7 2.7 %collective-permute-start.15 = (f16[1,72,1024]{2,1,0:T(8,128)(2,1)S(1)}, f16[1,72,1024]{2,1,0:T(8,128)(2,1)S(1)}, u32[]{:S(2)}, u32[]{:S(2)}) collective-permute-start(f16[1,72,1024]{2,1,0:T(8,128)(2,1)S(1)} %get-tuple-element.44), channel_id=1, source_target_pairs={{0,3},{1,0},{2,1},{3,2},{4,7},{5,4},{6,5},{7,6},{8,11},{9,8},{10,9... | collective-permute-start | bytes 442376 | tf_op jit(solution)/shard_map/ppermute | solution.py:28
  75.6 0.6 collective-permute-done.14
  76.2 1.9 %collective-permute-done.15 = f16[1,72,1024]{2,1,0:T(8,128)(2,1)S(1)} collective-permute-done((f16[1,72,1024]{2,1,0:T(8,128)(2,1)S(1)}, f16[1,72,1024]{2,1,0:T(8,128)(2,1)S(1)}, u32[]{:S(2)}, u32[]{:S(2)}) %collective-permute-start.15) | collective-permute-done | bytes 147488 | tf_op jit(solution)/shard_map/ppermute | solution.py:28
  78.8 20.0 %all_to_all.10 = f16[8,180,128]{2,1,0:T(8,128)(2,1)S(1)} all-to-all(f16[8,180,128]{2,1,0:T(8,128)(2,1)S(1)} %reshape.106), channel_id=1, replica_groups=mesh['yh'=2,'core'=2,'yl'=2,'z'=8,'x'=4] {'z'}, dimensions={0} | all-to-all | bytes 737280 | tf_op jit(solution)/shard_map/all_to_all | solution.py:205
  98.9 0.7 subtract_convert_fusion
  99.7 0.7 subtract_convert_fusion.1
  100.5 0.8 broadcast_in_dim.5
  101.3 3.7 %all-to-all-start.1 = ((bf16[8,180,128]{2,1,0:T(8,128)(2,1)}), bf16[8,180,128]{2,1,0:T(8,128)(2,1)S(1)}, u32[]{:S(2)}, u32[]{:S(2)}) async-start(bf16[8,180,128]{2,1,0:T(8,128)(2,1)} %broadcast_in_dim.5), calls=%async_computation.1 | async-start | bytes 753664 | tf_op jit(solution)/shard_map/all_to_all | solution.py:212
  105.3 11.1 %all-to-all-done.1 = bf16[8,180,128]{2,1,0:T(8,128)(2,1)S(1)} async-done(((bf16[8,180,128]{2,1,0:T(8,128)(2,1)}), bf16[8,180,128]{2,1,0:T(8,128)(2,1)S(1)}, u32[]{:S(2)}, u32[]{:S(2)}) %all-to-all-start.1) | async-done | bytes 368672 | tf_op jit(solution)/shard_map/all_to_all | solution.py:212
  116.6 5.1 %collective-permute-start.22 = (bf16[24,2560]{1,0:T(8,128)(2,1)S(1)}, bf16[24,2560]{1,0:T(8,128)(2,1)S(1)}, u32[]{:S(2)}, u32[]{:S(2)}) collective-permute-start(bf16[24,2560]{1,0:T(8,128)(2,1)S(1)} %reshape.108), channel_id=1, source_target_pairs={{0,2},{1,3},{2,0},{3,1},{4,6},{5,7},{6,4},{7,5},{8,10},{9,11},{10,... | collective-permute-start | bytes 368648 | tf_op jit(solution)/shard_map/ppermute | solution.py:28
  122.2 1.5 collective-permute-start.16
  124.0 4.6 %collective-permute-done.22 = bf16[24,2560]{1,0:T(8,128)(2,1)S(1)} collective-permute-done((bf16[24,2560]{1,0:T(8,128)(2,1)S(1)}, bf16[24,2560]{1,0:T(8,128)(2,1)S(1)}, u32[]{:S(2)}, u32[]{:S(2)}) %collective-permute-start.22) | collective-permute-done | bytes 122912 | tf_op jit(solution)/shard_map/ppermute | solution.py:28
  128.7 1.4 collective-permute-start.24
  130.6 3.0 %collective-permute-start.19 = (bf16[96,2560]{1,0:T(8,128)(2,1)S(1)}, bf16[96,2560]{1,0:T(8,128)(2,1)S(1)}, u32[]{:S(2)}, u32[]{:S(2)}) collective-permute-start(bf16[96,2560]{1,0:T(8,128)(2,1)S(1)} %get-tuple-element.46), channel_id=1, source_target_pairs={{0,3},{1,0},{2,1},{3,2},{4,7},{5,4},{6,5},{7,6},{8,11},{9,8},{10,9... | collective-permute-start | bytes 1474568 | tf_op jit(solution)/shard_map/ppermute | solution.py:28
  133.6 4.1 %collective-permute-done.24 = bf16[96,2560]{1,0:T(8,128)(2,1)S(1)} collective-permute-done((bf16[96,2560]{1,0:T(8,128)(2,1)S(1)}, bf16[96,2560]{1,0:T(8,128)(2,1)S(1)}, u32[]{:S(2)}, u32[]{:S(2)}) %collective-permute-start.24) | collective-permute-done | bytes 491552 | tf_op jit(solution)/shard_map/ppermute | solution.py:36
  137.6 1.4 convolution_convert_fusion.1
  139.0 2.4 %collective-permute-done.17 = bf16[96,2560]{1,0:T(8,128)(2,1)S(1)} collective-permute-done((bf16[96,2560]{1,0:T(8,128)(2,1)S(1)}, bf16[96,2560]{1,0:T(8,128)(2,1)S(1)}, u32[]{:S(2)}, u32[]{:S(2)}) %collective-permute-start.17) | collective-permute-done | bytes 491552 | tf_op jit(solution)/shard_map/ppermute | solution.py:28
  141.5 3.5 %collective-permute-start.20 = (bf16[48,2560]{1,0:T(8,128)(2,1)S(1)}, bf16[48,2560]{1,0:T(8,128)(2,1)S(1)}, u32[]{:S(2)}, u32[]{:S(2)}) collective-permute-start(bf16[48,2560]{1,0:T(8,128)(2,1)S(1)} %slice.178), channel_id=1, source_target_pairs={{0,3},{1,0},{2,1},{3,2},{4,7},{5,4},{6,5},{7,6},{8,11},{9,8},{10,9... | collective-permute-start | bytes 737288 | tf_op jit(solution)/shard_map/ppermute | solution.py:28
  145.0 3.9 %collective-permute-done.18 = bf16[48,2560]{1,0:T(8,128)(2,1)S(1)} collective-permute-done((bf16[48,2560]{1,0:T(8,128)(2,1)S(1)}, bf16[48,2560]{1,0:T(8,128)(2,1)S(1)}, u32[]{:S(2)}, u32[]{:S(2)}) %collective-permute-start.18) | collective-permute-done | bytes 245792 | tf_op jit(solution)/shard_map/ppermute | solution.py:28
  149.0 2.5 %convolution_convert_fusion = bf16[384,2560]{1,0:T(8,128)(2,1)} fusion(bf16[384,384]{1,0:T(8,128)(2,1)S(1)} %fusion.12, bf16[384,2560]{1,0:T(8,128)(2,1)S(1)} %constant_dynamic-update-slice_fusion.2), kind=kOutput, calls=%fused_computation.4 | convolution fusion | flops 755957760 | bytes 4227072 | tf_op jit(solution)/shard_map/dot_general | solution.py:67
  (91 shorter events, 5.3 us)
Async XLA Ops:
  0.6 14.7 %collective-permute-start.1 = (bf16[768,2560]{1,0:T(8,128)(2,1)}, bf16[768,2560]{1,0:T(8,128)(2,1)}, u32[]{:S(2)}, u32[]{:S(2)}) collective-permute-start(bf16[768,2560]{1,0:T(8,128)(2,1)} %param.15), channel_id=1, source_target_pairs={{0,64},{64,0},{1,65},{65,1},{2,66},{66,2},{3,67},{67,3},{4,68},{68... | collective-permute-start | bytes 11796488 | tf_op jit(solution)/shard_map/ppermute | solution.py:40
  9.7 5.6 %collective-permute-start = (bf16[4,2,144,768]{3,2,1,0:T(8,128)(2,1)}, bf16[4,2,144,768]{3,2,1,0:T(8,128)(2,1)S(1)}, u32[]{:S(2)}, u32[]{:S(2)}) collective-permute-start(bf16[4,2,144,768]{3,2,1,0:T(8,128)(2,1)} %get-tuple-element.15), channel_id=1, source_target_pairs={{0,64},{64,0},{1,65},{65,1},{2,66},{66,2},{3,67},{67,3},{4,68},{68... | collective-permute-start | bytes 5308424 | tf_op jit(solution)/shard_map/ppermute | solution.py:40
  15.3 1.2 copy-start.9
  22.1 3.4 %copy-start.11 = (bf16[4,2,144,768]{3,2,1,0:T(8,128)(2,1)S(1)}, bf16[4,2,144,768]{3,2,1,0:T(8,128)(2,1)}, u32[]{:S(2)}) copy-start(bf16[4,2,144,768]{3,2,1,0:T(8,128)(2,1)} %get-tuple-element.14) | copy-start | bytes 5308420
  22.4 21.9 %collective-permute-start.2 = (f16[4,72,1536]{2,1,0:T(8,128)(2,1)S(1)}, f16[4,72,1536]{2,1,0:T(8,128)(2,1)S(1)}, u32[]{:S(2)}, u32[]{:S(2)}) collective-permute-start(f16[4,72,1536]{2,1,0:T(8,128)(2,1)S(1)} %pad_maximum_fusion), channel_id=1, source_target_pairs={{0,3},{1,0},{2,1},{3,2},{4,7},{5,4},{6,5},{7,6},{8,11},{9,8},{10,9... | collective-permute-start | bytes 2654216 | tf_op jit(solution)/shard_map/ppermute | solution.py:28
  25.4 3.7 %copy-start.10 = (bf16[4,2,144,768]{3,2,1,0:T(8,128)(2,1)S(1)}, bf16[4,2,144,768]{3,2,1,0:T(8,128)(2,1)}, u32[]{:S(2)}) copy-start(bf16[4,2,144,768]{3,2,1,0:T(8,128)(2,1)} %copy-done.9) | copy-start | bytes 5308420
  25.4 22.6 %collective-permute-start.3 = (f16[4,72,1536]{2,1,0:T(8,128)(2,1)S(1)}, f16[4,72,1536]{2,1,0:T(8,128)(2,1)S(1)}, u32[]{:S(2)}, u32[]{:S(2)}) collective-permute-start(f16[4,72,1536]{2,1,0:T(8,128)(2,1)S(1)} %pad_maximum_fusion.1), channel_id=1, source_target_pairs={{0,1},{1,2},{2,3},{3,0},{4,5},{5,6},{6,7},{7,4},{8,9},{9,10},{10,1... | collective-permute-start | bytes 2654216 | tf_op jit(solution)/shard_map/ppermute | solution.py:28
  32.5 3.1 %copy-start = (f16[1152,1024]{1,0:T(8,128)(2,1)}, f16[1152,1024]{1,0:T(8,128)(2,1)S(1)}, u32[]{:S(2)}) copy-start(f16[1152,1024]{1,0:T(8,128)(2,1)S(1)} %multiply_convert_fusion) | copy-start | bytes 7077892
  34.1 18.3 %collective-permute-start.9 = (f16[4,72,1024]{2,1,0:T(8,128)(2,1)}, f16[4,72,1024]{2,1,0:T(8,128)(2,1)}, u32[]{:S(2)}, u32[]{:S(2)}) collective-permute-start(f16[4,72,1024]{2,1,0:T(8,128)(2,1)} %pad_maximum_fusion.2), channel_id=1, source_target_pairs={{0,160},{32,0},{128,32},{160,128},{1,161},{33,1},{129,33},{161,129... | collective-permute-start | bytes 1769480 | tf_op jit(solution)/shard_map/ppermute | solution.py:32
  35.6 16.9 %collective-permute-start.10 = (f16[4,72,1024]{2,1,0:T(8,128)(2,1)}, f16[4,72,1024]{2,1,0:T(8,128)(2,1)}, u32[]{:S(2)}, u32[]{:S(2)}) collective-permute-start(f16[4,72,1024]{2,1,0:T(8,128)(2,1)} %pad_maximum_fusion.3), channel_id=1, source_target_pairs={{0,32},{32,128},{128,160},{160,0},{1,33},{33,129},{129,161},{161,1... | collective-permute-start | bytes 1769480 | tf_op jit(solution)/shard_map/ppermute | solution.py:32
  44.3 3.7 %copy-start.1 = (f16[4,72,1536]{2,1,0:T(8,128)(2,1)}, f16[4,72,1536]{2,1,0:T(8,128)(2,1)S(1)}, u32[]{:S(2)}) copy-start(f16[4,72,1536]{2,1,0:T(8,128)(2,1)S(1)} %collective-permute-done.2) | copy-start | bytes 2654212
  48.0 1.2 copy-start.2
  49.2 12.4 %collective-permute-start.4 = (f16[2,72,1536]{2,1,0:T(8,128)(2,1)}, f16[2,72,1536]{2,1,0:T(8,128)(2,1)}, u32[]{:S(2)}, u32[]{:S(2)}) collective-permute-start(f16[2,72,1536]{2,1,0:T(8,128)(2,1)} %get-tuple-element.28), channel_id=1, source_target_pairs={{0,1},{1,2},{2,3},{3,0},{4,5},{5,6},{6,7},{7,4},{8,9},{9,10},{10,1... | collective-permute-start | bytes 1327112 | tf_op jit(solution)/shard_map/ppermute | solution.py:28
  49.2 12.4 %collective-permute-start.5 = (f16[2,72,1536]{2,1,0:T(8,128)(2,1)}, f16[2,72,1536]{2,1,0:T(8,128)(2,1)}, u32[]{:S(2)}, u32[]{:S(2)}) collective-permute-start(f16[2,72,1536]{2,1,0:T(8,128)(2,1)} %get-tuple-element.29), channel_id=1, source_target_pairs={{0,3},{1,0},{2,1},{3,2},{4,7},{5,4},{6,5},{7,6},{8,11},{9,8},{10,9... | collective-permute-start | bytes 1327112 | tf_op jit(solution)/shard_map/ppermute | solution.py:28
  52.4 9.2 %slice-start = ((f16[4,72,1536]{2,1,0:T(8,128)(2,1)}), f16[2,72,1536]{2,1,0:T(8,128)(2,1)S(1)}, s32[]{:S(2)}) async-start(f16[4,72,1536]{2,1,0:T(8,128)(2,1)} %copy-done.1), calls=%async_computation.2 | async-start | bytes 884736 | tf_op jit(solution)/shard_map/slice | solution.py:183
  52.4 9.2 %slice-start.1 = ((f16[4,72,1536]{2,1,0:T(8,128)(2,1)}), f16[2,72,1536]{2,1,0:T(8,128)(2,1)S(1)}, s32[]{:S(2)}) async-start(f16[4,72,1536]{2,1,0:T(8,128)(2,1)} %copy-done.2), calls=%async_computation.3 | async-start | bytes 884736 | tf_op jit(solution)/shard_map/slice | solution.py:183
  54.0 12.3 %collective-permute-start.11 = (f16[2,72,1024]{2,1,0:T(8,128)(2,1)S(1)}, f16[2,72,1024]{2,1,0:T(8,128)(2,1)S(1)}, u32[]{:S(2)}, u32[]{:S(2)}) collective-permute-start(f16[2,72,1024]{2,1,0:T(8,128)(2,1)S(1)} %get-tuple-element.34), channel_id=1, source_target_pairs={{0,32},{32,128},{128,160},{160,0},{1,33},{33,129},{129,161},{161,1... | collective-permute-start | bytes 884744 | tf_op jit(solution)/shard_map/ppermute | solution.py:32
  55.4 11.0 %collective-permute-start.12 = (f16[2,72,1024]{2,1,0:T(8,128)(2,1)S(1)}, f16[2,72,1024]{2,1,0:T(8,128)(2,1)S(1)}, u32[]{:S(2)}, u32[]{:S(2)}) collective-permute-start(f16[2,72,1024]{2,1,0:T(8,128)(2,1)S(1)} %get-tuple-element.35), channel_id=1, source_target_pairs={{0,160},{32,0},{128,32},{160,128},{1,161},{33,1},{129,33},{161,129... | collective-permute-start | bytes 884744 | tf_op jit(solution)/shard_map/ppermute | solution.py:32
  63.4 9.4 %collective-permute-start.6 = (f16[1,72,1536]{2,1,0:T(8,128)(2,1)S(1)}, f16[1,72,1536]{2,1,0:T(8,128)(2,1)S(1)}, u32[]{:S(2)}, u32[]{:S(2)}) collective-permute-start(f16[1,72,1536]{2,1,0:T(8,128)(2,1)S(1)} %get-tuple-element.42), channel_id=1, source_target_pairs={{0,128},{32,160},{128,0},{160,32},{1,129},{33,161},{129,1},{161,33... | collective-permute-start | bytes 663560 | tf_op jit(solution)/shard_map/ppermute | solution.py:32
  63.9 11.5 %collective-permute-start.7 = (f16[1,72,1536]{2,1,0:T(8,128)(2,1)S(1)}, f16[1,72,1536]{2,1,0:T(8,128)(2,1)S(1)}, u32[]{:S(2)}, u32[]{:S(2)}) collective-permute-start(f16[1,72,1536]{2,1,0:T(8,128)(2,1)S(1)} %get-tuple-element.41), channel_id=1, source_target_pairs={{0,32},{32,128},{128,160},{160,0},{1,33},{33,129},{129,161},{161,1... | collective-permute-start | bytes 663560 | tf_op jit(solution)/shard_map/ppermute | solution.py:32
  66.0 9.4 %collective-permute-start.8 = (f16[1,72,1536]{2,1,0:T(8,128)(2,1)S(1)}, f16[1,72,1536]{2,1,0:T(8,128)(2,1)S(1)}, u32[]{:S(2)}, u32[]{:S(2)}) collective-permute-start(f16[1,72,1536]{2,1,0:T(8,128)(2,1)S(1)} %get-tuple-element.40), channel_id=1, source_target_pairs={{0,160},{32,0},{128,32},{160,128},{1,161},{33,1},{129,33},{161,129... | collective-permute-start | bytes 663560 | tf_op jit(solution)/shard_map/ppermute | solution.py:32
  67.9 7.7 %collective-permute-start.13 = (f16[1,72,1024]{2,1,0:T(8,128)(2,1)S(1)}, f16[1,72,1024]{2,1,0:T(8,128)(2,1)S(1)}, u32[]{:S(2)}, u32[]{:S(2)}) collective-permute-start(f16[1,72,1024]{2,1,0:T(8,128)(2,1)S(1)} %get-tuple-element.43), channel_id=1, source_target_pairs={{0,2},{1,3},{2,0},{3,1},{4,6},{5,7},{6,4},{7,5},{8,10},{9,11},{10,... | collective-permute-start | bytes 442376 | tf_op jit(solution)/shard_map/ppermute | solution.py:28
  69.4 6.8 %collective-permute-start.14 = (f16[1,72,1024]{2,1,0:T(8,128)(2,1)S(1)}, f16[1,72,1024]{2,1,0:T(8,128)(2,1)S(1)}, u32[]{:S(2)}, u32[]{:S(2)}) collective-permute-start(f16[1,72,1024]{2,1,0:T(8,128)(2,1)S(1)} %get-tuple-element.45), channel_id=1, source_target_pairs={{0,1},{1,2},{2,3},{3,0},{4,5},{5,6},{6,7},{7,4},{8,9},{9,10},{10,1... | collective-permute-start | bytes 442376 | tf_op jit(solution)/shard_map/ppermute | solution.py:28
  72.7 5.3 %collective-permute-start.15 = (f16[1,72,1024]{2,1,0:T(8,128)(2,1)S(1)}, f16[1,72,1024]{2,1,0:T(8,128)(2,1)S(1)}, u32[]{:S(2)}, u32[]{:S(2)}) collective-permute-start(f16[1,72,1024]{2,1,0:T(8,128)(2,1)S(1)} %get-tuple-element.44), channel_id=1, source_target_pairs={{0,3},{1,0},{2,1},{3,2},{4,7},{5,4},{6,5},{7,6},{8,11},{9,8},{10,9... | collective-permute-start | bytes 442376 | tf_op jit(solution)/shard_map/ppermute | solution.py:28
  75.6 23.4 %copy-start.3 = (f32[6,2560]{1,0:T(8,128)S(1)}, f32[6,2560]{1,0:T(8,128)}, u32[]{:S(2)}) copy-start(f32[6,2560]{1,0:T(8,128)} %param.18) | copy-start | bytes 184324
  75.6 23.4 %copy-start.4 = (f32[6,2560]{1,0:T(8,128)S(1)}, f32[6,2560]{1,0:T(8,128)}, u32[]{:S(2)}) copy-start(f32[6,2560]{1,0:T(8,128)} %param.20) | copy-start | bytes 184324
  75.6 23.3 %copy-start.5 = (f32[6,2560]{1,0:T(8,128)S(1)}, f32[6,2560]{1,0:T(8,128)}, u32[]{:S(2)}) copy-start(f32[6,2560]{1,0:T(8,128)} %param.19) | copy-start | bytes 184324
  78.2 21.5 %copy-start.6 = (f32[3,2560]{1,0:T(4,128)S(1)}, f32[3,2560]{1,0:T(4,128)}, u32[]{:S(2)}) copy-start(f32[3,2560]{1,0:T(4,128)} %param.21) | copy-start | bytes 92164
  78.2 21.5 %copy-start.7 = (f32[3,2560]{1,0:T(4,128)S(1)}, f32[3,2560]{1,0:T(4,128)}, u32[]{:S(2)}) copy-start(f32[3,2560]{1,0:T(4,128)} %param.23) | copy-start | bytes 92164
  78.2 21.5 %copy-start.8 = (f32[3,2560]{1,0:T(4,128)S(1)}, f32[3,2560]{1,0:T(4,128)}, u32[]{:S(2)}) copy-start(f32[3,2560]{1,0:T(4,128)} %param.22) | copy-start | bytes 92164
  101.3 15.1 %all-to-all-start.1 = ((bf16[8,180,128]{2,1,0:T(8,128)(2,1)}), bf16[8,180,128]{2,1,0:T(8,128)(2,1)S(1)}, u32[]{:S(2)}, u32[]{:S(2)}) async-start(bf16[8,180,128]{2,1,0:T(8,128)(2,1)} %broadcast_in_dim.5), calls=%async_computation.1 | async-start | bytes 753664 | tf_op jit(solution)/shard_map/all_to_all | solution.py:212
  116.6 7.5 %collective-permute-start.21 = (bf16[24,2560]{1,0:T(8,128)(2,1)S(1)}, bf16[24,2560]{1,0:T(8,128)(2,1)S(1)}, u32[]{:S(2)}, u32[]{:S(2)}) collective-permute-start(bf16[24,2560]{1,0:T(8,128)(2,1)S(1)} %reshape.108), channel_id=1, source_target_pairs={{0,1},{1,2},{2,3},{3,0},{4,5},{5,6},{6,7},{7,4},{8,9},{9,10},{10,1... | collective-permute-start | bytes 368648 | tf_op jit(solution)/shard_map/ppermute | solution.py:28
  116.6 12.0 %collective-permute-start.22 = (bf16[24,2560]{1,0:T(8,128)(2,1)S(1)}, bf16[24,2560]{1,0:T(8,128)(2,1)S(1)}, u32[]{:S(2)}, u32[]{:S(2)}) collective-permute-start(bf16[24,2560]{1,0:T(8,128)(2,1)S(1)} %reshape.108), channel_id=1, source_target_pairs={{0,2},{1,3},{2,0},{3,1},{4,6},{5,7},{6,4},{7,5},{8,10},{9,11},{10,... | collective-permute-start | bytes 368648 | tf_op jit(solution)/shard_map/ppermute | solution.py:28
  121.8 6.9 %collective-permute-start.23 = (bf16[24,2560]{1,0:T(8,128)(2,1)S(1)}, bf16[24,2560]{1,0:T(8,128)(2,1)S(1)}, u32[]{:S(2)}, u32[]{:S(2)}) collective-permute-start(bf16[24,2560]{1,0:T(8,128)(2,1)S(1)} %reshape.108), channel_id=1, source_target_pairs={{0,3},{1,0},{2,1},{3,2},{4,7},{5,4},{6,5},{7,6},{8,11},{9,8},{10,9... | collective-permute-start | bytes 368648 | tf_op jit(solution)/shard_map/ppermute | solution.py:28
  122.2 8.0 %collective-permute-start.16 = (bf16[48,2560]{1,0:T(8,128)(2,1)S(1)}, bf16[48,2560]{1,0:T(8,128)(2,1)S(1)}, u32[]{:S(2)}, u32[]{:S(2)}) collective-permute-start(bf16[48,2560]{1,0:T(8,128)(2,1)S(1)} %reshape.107), channel_id=1, source_target_pairs={{0,32},{32,0},{1,33},{33,1},{2,34},{34,2},{3,35},{35,3},{4,36},{36... | collective-permute-start | bytes 737288 | tf_op jit(solution)/shard_map/ppermute | solution.py:36
  128.7 8.9 %collective-permute-start.24 = (bf16[96,2560]{1,0:T(8,128)(2,1)S(1)}, bf16[96,2560]{1,0:T(8,128)(2,1)S(1)}, u32[]{:S(2)}, u32[]{:S(2)}) collective-permute-start(bf16[96,2560]{1,0:T(8,128)(2,1)S(1)} %pad_maximum_fusion.4), channel_id=1, source_target_pairs={{0,32},{32,0},{1,33},{33,1},{2,34},{34,2},{3,35},{35,3},{4,36},{36... | collective-permute-start | bytes 1474568 | tf_op jit(solution)/shard_map/ppermute | solution.py:36
  130.2 11.1 %collective-permute-start.17 = (bf16[96,2560]{1,0:T(8,128)(2,1)S(1)}, bf16[96,2560]{1,0:T(8,128)(2,1)S(1)}, u32[]{:S(2)}, u32[]{:S(2)}) collective-permute-start(bf16[96,2560]{1,0:T(8,128)(2,1)S(1)} %get-tuple-element.46), channel_id=1, source_target_pairs={{0,1},{1,2},{2,3},{3,0},{4,5},{5,6},{6,7},{7,4},{8,9},{9,10},{10,1... | collective-permute-start | bytes 1474568 | tf_op jit(solution)/shard_map/ppermute | solution.py:28
  130.6 10.9 %collective-permute-start.19 = (bf16[96,2560]{1,0:T(8,128)(2,1)S(1)}, bf16[96,2560]{1,0:T(8,128)(2,1)S(1)}, u32[]{:S(2)}, u32[]{:S(2)}) collective-permute-start(bf16[96,2560]{1,0:T(8,128)(2,1)S(1)} %get-tuple-element.46), channel_id=1, source_target_pairs={{0,3},{1,0},{2,1},{3,2},{4,7},{5,4},{6,5},{7,6},{8,11},{9,8},{10,9... | collective-permute-start | bytes 1474568 | tf_op jit(solution)/shard_map/ppermute | solution.py:28
  141.4 7.5 %collective-permute-start.18 = (bf16[48,2560]{1,0:T(8,128)(2,1)S(1)}, bf16[48,2560]{1,0:T(8,128)(2,1)S(1)}, u32[]{:S(2)}, u32[]{:S(2)}) collective-permute-start(bf16[48,2560]{1,0:T(8,128)(2,1)S(1)} %slice.177), channel_id=1, source_target_pairs={{0,1},{1,2},{2,3},{3,0},{4,5},{5,6},{6,7},{7,4},{8,9},{9,10},{10,1... | collective-permute-start | bytes 737288 | tf_op jit(solution)/shard_map/ppermute | solution.py:28
  141.5 7.4 %collective-permute-start.20 = (bf16[48,2560]{1,0:T(8,128)(2,1)S(1)}, bf16[48,2560]{1,0:T(8,128)(2,1)S(1)}, u32[]{:S(2)}, u32[]{:S(2)}) collective-permute-start(bf16[48,2560]{1,0:T(8,128)(2,1)S(1)} %slice.178), channel_id=1, source_target_pairs={{0,3},{1,0},{2,1},{3,2},{4,7},{5,4},{6,5},{7,6},{8,11},{9,8},{10,9... | collective-permute-start | bytes 737288 | tf_op jit(solution)/shard_map/ppermute | solution.py:28

commit v4 on v3

--- a/solution.py
+++ b/solution.py
@@ -73,7 +73,8 @@
     live = lax.broadcasted_iota(jnp.int32, (tok, slots), 1) < count_ref[0]
     place = jnp.where(names & live, 1.0, 0.0).astype(BF)
     slot_rows = dot_t(routed_order_ref[0], routed_ref[...]).astype(BF)
-    total = dot_t(shared_order_ref[...], shared_ref[...]) + dot_t(slot_rows, place)
+    order = jnp.concatenate([shared_order_ref[...], slot_rows], axis=1)
+    total = dot_t(order, jnp.concatenate([shared_ref[...], place], axis=1))
 
     @pl.when(pl.program_id(0) < 2)
     def _():
@@ -164,11 +165,12 @@
     def gathered(v, dim, back):
         return sum((b.astype(F32) for b in back), pick(v, dim, 0).astype(F32))
 
+    def front(v):
+        return lax.broadcasted_iota(jnp.int32, v.shape, 0) < 2
+
     def halves(total, dim):
         two, ahead, behind = (pick(total, dim, d) for d in (2, 1, 3))
-        plus = jnp.concatenate([two[:2], ahead[2:]])
-        minus = jnp.concatenate([two[2:], behind[:2]])
-        return plus, minus
+        return jnp.where(front(two), two, ahead), jnp.where(front(two), behind, two)
 
     def both(chunks, dim):
         ring = (x_ring, y_ring)[dim]
@@ -176,11 +178,11 @@
 
     def relayed(total, dim, plus, minus):
         ahead = pick(total, dim, 1)[:2].astype(F32) + plus[:2].astype(F32)
-        behind = pick(total, dim, 3)[2:].astype(F32) + minus[:2].astype(F32)
+        behind = pick(total, dim, 3)[2:].astype(F32) + minus[2:].astype(F32)
         return both((ahead.astype(F16), behind.astype(F16)), dim)
 
     def summed(total, dim, plus, minus, ahead, behind):
-        got = jnp.concatenate([minus[2:], plus[2:]]).astype(F32)
+        got = jnp.where(front(plus), minus, plus).astype(F32)
         got = got + jnp.concatenate([ahead, behind]).astype(F32)
         return pick(total, dim, 0).astype(F32) + got
 
@@ -212,13 +214,16 @@
     weight = lax.all_to_all(jnp.broadcast_to(weight, (NZ,) + weight.shape[1:]), "z", 0, 0)
     weight_s = weight[:, : sr * width // 128].reshape(NZ * sr, width)
     weight_r = weight[:, sr * width // 128 :].reshape(NZ * rr, width)
-    all_s = jnp.concatenate([weight_s, y_swap(weight_s)], axis=0)
-    all_r = jnp.concatenate([weight_r] + [x_ring(weight_r, d) for d in (1, 2, 3)], axis=0)
-    one_way, other_way = x_ring(all_s, 1), x_ring(all_s, 3)
-    split = all_s.shape[0] // 2
-    two_away = [x_ring(one_way[:split], 1), x_ring(other_way[split:], 3)]
-    all_s = jnp.concatenate([all_s, one_way] + two_away + [other_way], axis=0)
+    mine, other = weight_s, y_swap(weight_s)
+    mine_plus, mine_minus = x_ring(mine, 1), x_ring(mine, 3)
+    other_plus, other_minus = x_ring(other, 1), x_ring(other, 3)
+    mine_two, other_two = x_ring(mine_plus, 1), x_ring(other_minus, 3)
+    around = [after([other, mine_plus], x_ring(weight_r, d)) for d in (1, 2, 3)]
+    all_r = jnp.concatenate([weight_r] + around, axis=0)
     all_r = jnp.concatenate([all_r, y_swap(all_r)], axis=0)
+    all_s = jnp.concatenate(
+        [mine, other, mine_plus, other_plus, mine_two, other_two, mine_minus, other_minus], axis=0
+    )
 
     def settled(full, count, index):
         n = full.shape[0]

time: 154 us -> 147 us (0.955)
  other arithmetic: 10.8 us -> 5.26 us
  local copies, waits for them, and re-layouts: 6.12 us -> 2.43 us
  waiting for transfers between devices: 44.2 us -> 47.4 us
  starting transfers between devices: 39 us -> 41.5 us
  Pallas kernels: 8.31 us -> 6.76 us
    ppermute x14 -> x16, waiting for transfers between devices: 28 us -> 34.1 us  [x_ring(): return lax.ppermute(v, 'x', [(i, (i + d) % NX) for i in range(NX)])]
    ppermute x2, waiting for transfers between devices: 4.06 us -> 0.01 us  [y_swap(): return lax.ppermute(v, 'yl', [(0, 1), (1, 0)])]
    ppermute x14 -> x16, starting transfers between devices: 24.8 us -> 27.9 us  [x_ring(): return lax.ppermute(v, 'x', [(i, (i + d) % NX) for i in range(NX)])]
    slice x10 -> x0, local copies, waits for them, and re-layouts: 2.75 us -> none  [the longest x6 2.03 us: summed(): got = jnp.concatenate([minus[2:], plus[2:]]).astype(F32)]
    concatenate x5 -> x1, other arithmetic: 2.71 us -> 0.04 us  [local(): all_r = jnp.concatenate([weight_r] + around, axis=0)]
    convert_element_type x2 -> x3, other arithmetic: 2.76 us -> 0.46 us  [relayed(): return both((ahead.astype(F16), behind.astype(F16)), dim)]
    add x2, other arithmetic: 3.1 us -> 1.2 us  [summed(): return pick(total, dim, 0).astype(F32) + got]
    pallas_call x1, Pallas kernels: 8.31 us -> 6.76 us  [ordered(): pl.pallas_call(order_kernel, grid_spec=pltpu.PrefetchScalarGridSpec(num_s...]
  transfers between devices with their start and end apart: 26 -> 28, of which waited for: 12 -> 9; matrix products, arithmetic and copies ran while one was open for 17% -> 12% of each run, Pallas kernels for 5% -> 5%
where the time goes in v4:
time: 147 us; the launch traced here: 146 us
  waiting for transfers between devices  47.4 us (32%)
  starting transfers between devices  41.5 us (28%)
  matrix products  20.7 us (14%)
  blocking collectives  20 us (14%)
  Pallas kernels  6.76 us (5%)
  other arithmetic  5.26 us (4%)
  local copies, waits for them, and re-layouts  2.43 us (2%)
  between operations  1.76 us (1%)
    ppermute x16, waiting for transfers between devices, x_ring(): return lax.ppermute(v, 'x', [(i, (i + d) % NX) for i in range(NX)])  34.1 us
    ppermute x16, starting transfers between devices, x_ring(): return lax.ppermute(v, 'x', [(i, (i + d) % NX) for i in range(NX)])  27.9 us
    dot_general x6, matrix products, dot(): return jnp.dot(a, b, preferred_element_type=F32)  20.7 us
    all_to_all x1, blocking collectives, local(): last = lax.all_to_all(last, 'z', 0, 0)  20 us
    all_to_all x1, waiting for transfers between devices, local(): lax.all_to_all(jnp.broadcast_to(weight, (NZ,) + weight.shape[1:]), 'z', 0...  11.3 us
    ppermute x7, starting transfers between devices, y_ring(): return lax.ppermute(v, ('yh', 'yl'), [(i, (i + d) % NY) for i in range(NY)])  7.12 us
    pallas_call x1, Pallas kernels, ordered(): pl.pallas_call(order_kernel, grid_spec=pltpu.PrefetchScalarGridSpec(num_s...  6.76 us
    all_to_all x1, starting transfers between devices, local(): lax.all_to_all(jnp.broadcast_to(weight, (NZ,) + weight.shape[1:]), 'z', 0...  3.45 us
  transfers between devices with their start and end apart: 28, of which 9 were waited for; matrix products, arithmetic and copies ran while one was open for 12% of the time, Pallas kernels for 5%

profile of v4, /device:TPU:16, one launch (start us, length us, event | category | flops | bytes accessed | tf_op | source)
XLA Modules:
  0.0 145.7 jit_solution(792329861328617545)
XLA Ops:
  1.4 6.8 %shard_map.172 = (bf16[4,2,144,768]{3,2,1,0:T(8,128)(2,1)}, bf16[4,2,144,768]{3,2,1,0:T(8,128)(2,1)}) custom-call(s32[1]{0:T(128)} %bitcast.core_ref, s32[1]{0:T(128)S(6)} %copy.39.count_ref, s32[1,96]{1,0:T(1,128)} %bitcast.74, bf16[768,1536]{1,0:T(8,128)(2,1)} %shared_ref.1, bf16[96,768]{1,0:T(8,128)(2,1)} %routed_ref.1, ...), custom_call_target="tpu_custom_call" | custom-call | flops 2717908992 | bytes 8847360 | tf_op jit(solution)/shard_map/pallas_call | solution.py:101
  8.2 0.5 collective-permute-start
  8.6 5.1 %fusion.3 = f32[1152,1536]{1,0:T(8,128)S(1)} fusion(bf16[1152,768]{1,0:T(8,128)(2,1)} %bitcast.75, bf16[768,2560]{1,0:T(8,128)(2,1)} %param.15), kind=kOutput, calls=%fused_computation.7 | convolution fusion | flops 2717908992 | bytes 11206656 | tf_op jit(solution)/shard_map/dot_general | solution.py:67
  13.8 4.9 %fusion.1 = f16[1152,1536]{1,0:T(8,128)(2,1)S(1)} fusion(f32[1152,1536]{1,0:T(8,128)S(1)} %fusion.3, bf16[1152,768]{1,0:T(8,128)(2,1)S(1)} %bitcast.72, bf16[768,2560]{1,0:T(8,128)(2,1)} %collective-permute-done.1), kind=kOutput, calls=%fused_computation.2 | convolution fusion | flops 2723217408 | bytes 14745600 | tf_op jit(solution)/shard_map/dot_general | solution.py:67
  18.7 0.7 bitcast_select_fusion.1
  19.3 2.8 %collective-permute-start.2 = (f16[4,72,1536]{2,1,0:T(8,128)(2,1)S(1)}, f16[4,72,1536]{2,1,0:T(8,128)(2,1)S(1)}, u32[]{:S(2)}, u32[]{:S(2)}) collective-permute-start(f16[4,72,1536]{2,1,0:T(8,128)(2,1)S(1)} %get-tuple-element.34), channel_id=1, source_target_pairs={{0,3},{1,0},{2,1},{3,2},{4,7},{5,4},{6,5},{7,6},{8,11},{9,8},{10,9... | collective-permute-start | bytes 2654216 | tf_op jit(solution)/shard_map/ppermute | solution.py:28
  22.2 3.4 %fusion.6 = f32[1152,1024]{1,0:T(8,128)S(1)} fusion(bf16[1152,768]{1,0:T(8,128)(2,1)S(1)} %bitcast.76, bf16[768,2560]{1,0:T(8,128)(2,1)} %param.15), kind=kOutput, calls=%fused_computation.11 | convolution fusion | flops 1811939328 | bytes 8060928 | tf_op jit(solution)/shard_map/dot_general | solution.py:67
  25.6 3.5 %multiply_convert_fusion = f16[1152,1024]{1,0:T(8,128)(2,1)S(1)} fusion(f32[1152,1024]{1,0:T(8,128)S(1)} %fusion.6, bf16[1152,768]{1,0:T(8,128)(2,1)S(1)} %bitcast.73, bf16[768,2560]{1,0:T(8,128)(2,1)} %collective-permute-done.1), kind=kOutput, calls=%fused_computation.3 | convolution fusion | flops 1815478272 | bytes 10420224 | tf_op jit(solution)/shard_map/dot_general | solution.py:67
  29.1 0.6 bitcast_select_fusion.2
  29.7 1.4 collective-permute-start.10
  31.1 0.7 collective-permute-start.9
  31.8 0.3 dynamic-slice_bitcast_fusion
  32.1 9.2 %collective-permute-done.2 = f16[4,72,1536]{2,1,0:T(8,128)(2,1)S(1)} collective-permute-done((f16[4,72,1536]{2,1,0:T(8,128)(2,1)S(1)}, f16[4,72,1536]{2,1,0:T(8,128)(2,1)S(1)}, u32[]{:S(2)}, u32[]{:S(2)}) %collective-permute-start.2) | collective-permute-done | bytes 884768 | tf_op jit(solution)/shard_map/ppermute | solution.py:28
  41.3 3.4 %collective-permute-done.3 = f16[4,72,1536]{2,1,0:T(8,128)(2,1)S(1)} collective-permute-done((f16[4,72,1536]{2,1,0:T(8,128)(2,1)S(1)}, f16[4,72,1536]{2,1,0:T(8,128)(2,1)S(1)}, u32[]{:S(2)}, u32[]{:S(2)}) %collective-permute-start.3) | collective-permute-done | bytes 884768 | tf_op jit(solution)/shard_map/ppermute | solution.py:28
  45.0 3.2 %collective-permute-start.5 = (f16[2,72,1536]{2,1,0:T(8,128)(2,1)S(1)}, f16[2,72,1536]{2,1,0:T(8,128)(2,1)S(1)}, u32[]{:S(2)}, u32[]{:S(2)}) collective-permute-start(f16[2,72,1536]{2,1,0:T(8,128)(2,1)S(1)} %get-tuple-element.37), channel_id=1, source_target_pairs={{0,3},{1,0},{2,1},{3,2},{4,7},{5,4},{6,5},{7,6},{8,11},{9,8},{10,9... | collective-permute-start | bytes 1327112 | tf_op jit(solution)/shard_map/ppermute | solution.py:28
  48.4 1.4 collective-permute-start.11
  49.8 0.8 collective-permute-start.12
  50.7 6.5 %collective-permute-done.4 = f16[2,72,1536]{2,1,0:T(8,128)(2,1)S(1)} collective-permute-done((f16[2,72,1536]{2,1,0:T(8,128)(2,1)S(1)}, f16[2,72,1536]{2,1,0:T(8,128)(2,1)S(1)}, u32[]{:S(2)}, u32[]{:S(2)}) %collective-permute-start.4) | collective-permute-done | bytes 442400 | tf_op jit(solution)/shard_map/ppermute | solution.py:28
  57.2 0.6 convert_add_fusion
  57.9 0.4 collective-permute-start.6
  58.3 2.2 %collective-permute-start.7 = (f16[1,72,1536]{2,1,0:T(8,128)(2,1)S(1)}, f16[1,72,1536]{2,1,0:T(8,128)(2,1)S(1)}, u32[]{:S(2)}, u32[]{:S(2)}) collective-permute-start(f16[1,72,1536]{2,1,0:T(8,128)(2,1)S(1)} %get-tuple-element.43), channel_id=1, source_target_pairs={{0,32},{32,128},{128,160},{160,0},{1,33},{33,129},{129,161},{161,1... | collective-permute-start | bytes 663560 | tf_op jit(solution)/shard_map/ppermute | solution.py:32
  60.7 0.6 convert_add_fusion.1
  61.4 1.5 %collective-permute-start.13 = (f16[1,72,1024]{2,1,0:T(8,128)(2,1)S(1)}, f16[1,72,1024]{2,1,0:T(8,128)(2,1)S(1)}, u32[]{:S(2)}, u32[]{:S(2)}) collective-permute-start(f16[1,72,1024]{2,1,0:T(8,128)(2,1)S(1)} %get-tuple-element.45), channel_id=1, source_target_pairs={{0,2},{1,3},{2,0},{3,1},{4,6},{5,7},{6,4},{7,5},{8,10},{9,11},{10,... | collective-permute-start | bytes 442376 | tf_op jit(solution)/shard_map/ppermute | solution.py:28
  63.0 2.3 %collective-permute-start.14 = (f16[1,72,1024]{2,1,0:T(8,128)(2,1)S(1)}, f16[1,72,1024]{2,1,0:T(8,128)(2,1)S(1)}, u32[]{:S(2)}, u32[]{:S(2)}) collective-permute-start(f16[1,72,1024]{2,1,0:T(8,128)(2,1)S(1)} %get-tuple-element.47), channel_id=1, source_target_pairs={{0,1},{1,2},{2,3},{3,0},{4,5},{5,6},{6,7},{7,4},{8,9},{9,10},{10,1... | collective-permute-start | bytes 442376 | tf_op jit(solution)/shard_map/ppermute | solution.py:28
  65.3 2.0 %collective-permute-done.6 = f16[1,72,1536]{2,1,0:T(8,128)(2,1)S(1)} collective-permute-done((f16[1,72,1536]{2,1,0:T(8,128)(2,1)S(1)}, f16[1,72,1536]{2,1,0:T(8,128)(2,1)S(1)}, u32[]{:S(2)}, u32[]{:S(2)}) %collective-permute-start.6) | collective-permute-done | bytes 221216 | tf_op jit(solution)/shard_map/ppermute | solution.py:32
  67.3 2.7 %collective-permute-start.15 = (f16[1,72,1024]{2,1,0:T(8,128)(2,1)S(1)}, f16[1,72,1024]{2,1,0:T(8,128)(2,1)S(1)}, u32[]{:S(2)}, u32[]{:S(2)}) collective-permute-start(f16[1,72,1024]{2,1,0:T(8,128)(2,1)S(1)} %get-tuple-element.46), channel_id=1, source_target_pairs={{0,3},{1,0},{2,1},{3,2},{4,7},{5,4},{6,5},{7,6},{8,11},{9,8},{10,9... | collective-permute-start | bytes 442376 | tf_op jit(solution)/shard_map/ppermute | solution.py:28
  70.2 2.5 %collective-permute-done.15 = f16[1,72,1024]{2,1,0:T(8,128)(2,1)S(1)} collective-permute-done((f16[1,72,1024]{2,1,0:T(8,128)(2,1)S(1)}, f16[1,72,1024]{2,1,0:T(8,128)(2,1)S(1)}, u32[]{:S(2)}, u32[]{:S(2)}) %collective-permute-start.15) | collective-permute-done | bytes 147488 | tf_op jit(solution)/shard_map/ppermute | solution.py:28
  72.9 0.5 reshape.98
  73.4 20.0 %all_to_all.10 = f16[8,180,128]{2,1,0:T(8,128)(2,1)S(1)} all-to-all(f16[8,180,128]{2,1,0:T(8,128)(2,1)S(1)} %reshape.98), channel_id=1, replica_groups=mesh['yh'=2,'core'=2,'yl'=2,'z'=8,'x'=4] {'z'}, dimensions={0} | all-to-all | bytes 737280 | tf_op jit(solution)/shard_map/all_to_all | solution.py:207
  93.5 0.7 subtract_convert_fusion
  94.2 0.7 subtract_convert_fusion.1
  95.1 0.8 broadcast_in_dim.5
  95.9 3.4 %all-to-all-start.1 = ((bf16[8,180,128]{2,1,0:T(8,128)(2,1)}), bf16[8,180,128]{2,1,0:T(8,128)(2,1)S(1)}, u32[]{:S(2)}, u32[]{:S(2)}) async-start(bf16[8,180,128]{2,1,0:T(8,128)(2,1)} %broadcast_in_dim.5), calls=%async_computation.1 | async-start | bytes 753664 | tf_op jit(solution)/shard_map/all_to_all | solution.py:214
  99.6 11.3 %all-to-all-done.1 = bf16[8,180,128]{2,1,0:T(8,128)(2,1)S(1)} async-done(((bf16[8,180,128]{2,1,0:T(8,128)(2,1)}), bf16[8,180,128]{2,1,0:T(8,128)(2,1)S(1)}, u32[]{:S(2)}, u32[]{:S(2)}) %all-to-all-start.1) | async-done | bytes 368672 | tf_op jit(solution)/shard_map/all_to_all | solution.py:214
  111.3 1.3 collective-permute-start.16
  112.8 3.7 %collective-permute-start.25 = (bf16[24,2560]{1,0:T(8,128)(2,1)S(1)}, bf16[24,2560]{1,0:T(8,128)(2,1)S(1)}, u32[]{:S(2)}, u32[]{:S(2)}) collective-permute-start(bf16[24,2560]{1,0:T(8,128)(2,1)S(1)} %reshape.100), channel_id=1, source_target_pairs={{0,3},{1,0},{2,1},{3,2},{4,7},{5,4},{6,5},{7,6},{8,11},{9,8},{10,9... | collective-permute-start | bytes 368648 | tf_op jit(solution)/shard_map/ppermute | solution.py:28
  116.5 1.6 %collective-permute-start.24 = (bf16[24,2560]{1,0:T(8,128)(2,1)S(1)}, bf16[24,2560]{1,0:T(8,128)(2,1)S(1)}, u32[]{:S(2)}, u32[]{:S(2)}) collective-permute-start(bf16[24,2560]{1,0:T(8,128)(2,1)S(1)} %reshape.100), channel_id=1, source_target_pairs={{0,2},{1,3},{2,0},{3,1},{4,6},{5,7},{6,4},{7,5},{8,10},{9,11},{10,... | collective-permute-start | bytes 368648 | tf_op jit(solution)/shard_map/ppermute | solution.py:28
  118.1 1.3 collective-permute-start.23
  119.4 3.2 %collective-permute-start.22 = (bf16[48,2560]{1,0:T(8,128)(2,1)S(1)}, bf16[48,2560]{1,0:T(8,128)(2,1)S(1)}, u32[]{:S(2)}, u32[]{:S(2)}) collective-permute-start(bf16[48,2560]{1,0:T(8,128)(2,1)S(1)} %reshape.99), channel_id=1, source_target_pairs={{0,3},{1,0},{2,1},{3,2},{4,7},{5,4},{6,5},{7,6},{8,11},{9,8},{10,9... | collective-permute-start | bytes 737288 | tf_op jit(solution)/shard_map/ppermute | solution.py:28
  122.6 4.4 %collective-permute-done.24 = bf16[24,2560]{1,0:T(8,128)(2,1)S(1)} collective-permute-done((bf16[24,2560]{1,0:T(8,128)(2,1)S(1)}, bf16[24,2560]{1,0:T(8,128)(2,1)S(1)}, u32[]{:S(2)}, u32[]{:S(2)}) %collective-permute-start.24) | collective-permute-done | bytes 122912 | tf_op jit(solution)/shard_map/ppermute | solution.py:28
  127.0 1.1 collective-permute-start.26
  128.2 2.1 %collective-permute-start.19 = (bf16[48,2560]{1,0:T(8,128)(2,1)S(1)}, bf16[48,2560]{1,0:T(8,128)(2,1)S(1)}, u32[]{:S(2)}, u32[]{:S(2)}) collective-permute-start(bf16[48,2560]{1,0:T(8,128)(2,1)S(1)} %collective-permute-done.17), channel_id=1, source_target_pairs={{0,1},{1,2},{2,3},{3,0},{4,5},{5,6},{6,7},{7,4},{8,9},{9,10},{10,1... | collective-permute-start | bytes 737288 | tf_op jit(solution)/shard_map/ppermute | solution.py:28
  130.3 1.2 collective-permute-start.20
  131.6 5.3 %collective-permute-done.20 = bf16[48,2560]{1,0:T(8,128)(2,1)S(1)} collective-permute-done((bf16[48,2560]{1,0:T(8,128)(2,1)S(1)}, bf16[48,2560]{1,0:T(8,128)(2,1)S(1)}, u32[]{:S(2)}, u32[]{:S(2)}) %collective-permute-start.20) | collective-permute-done | bytes 245792 | tf_op jit(solution)/shard_map/ppermute | solution.py:28
  137.0 2.0 %collective-permute-start.21 = (bf16[48,2560]{1,0:T(8,128)(2,1)S(1)}, bf16[48,2560]{1,0:T(8,128)(2,1)S(1)}, u32[]{:S(2)}, u32[]{:S(2)}) collective-permute-start(bf16[48,2560]{1,0:T(8,128)(2,1)S(1)} %collective-permute-done.20), channel_id=1, source_target_pairs={{0,3},{1,0},{2,1},{3,2},{4,7},{5,4},{6,5},{7,6},{8,11},{9,8},{10,9... | collective-permute-start | bytes 737288 | tf_op jit(solution)/shard_map/ppermute | solution.py:28
  139.1 1.4 convolution_convert_fusion.1
  140.4 2.7 %collective-permute-done.21 = bf16[48,2560]{1,0:T(8,128)(2,1)S(1)} collective-permute-done((bf16[48,2560]{1,0:T(8,128)(2,1)S(1)}, bf16[48,2560]{1,0:T(8,128)(2,1)S(1)}, u32[]{:S(2)}, u32[]{:S(2)}) %collective-permute-start.21) | collective-permute-done | bytes 245792 | tf_op jit(solution)/shard_map/ppermute | solution.py:28
  143.2 2.5 %convolution_convert_fusion = bf16[384,2560]{1,0:T(8,128)(2,1)} fusion(bf16[384,384]{1,0:T(8,128)(2,1)S(1)} %fusion.12, bf16[384,2560]{1,0:T(8,128)(2,1)S(1)} %constant_dynamic-update-slice_fusion), kind=kOutput, calls=%fused_computation.4 | convolution fusion | flops 755957760 | bytes 4227072 | tf_op jit(solution)/shard_map/dot_general | solution.py:67
  (78 shorter events, 2.8 us)
Async XLA Ops:
  0.6 13.2 %collective-permute-start.1 = (bf16[768,2560]{1,0:T(8,128)(2,1)}, bf16[768,2560]{1,0:T(8,128)(2,1)}, u32[]{:S(2)}, u32[]{:S(2)}) collective-permute-start(bf16[768,2560]{1,0:T(8,128)(2,1)} %param.15), channel_id=1, source_target_pairs={{0,64},{64,0},{1,65},{65,1},{2,66},{66,2},{3,67},{67,3},{4,68},{68... | collective-permute-start | bytes 11796488 | tf_op jit(solution)/shard_map/ppermute | solution.py:40
  8.2 5.6 %collective-permute-start = (bf16[4,2,144,768]{3,2,1,0:T(8,128)(2,1)}, bf16[4,2,144,768]{3,2,1,0:T(8,128)(2,1)S(1)}, u32[]{:S(2)}, u32[]{:S(2)}) collective-permute-start(bf16[4,2,144,768]{3,2,1,0:T(8,128)(2,1)} %get-tuple-element.18), channel_id=1, source_target_pairs={{0,64},{64,0},{1,65},{65,1},{2,66},{66,2},{3,67},{67,3},{4,68},{68... | collective-permute-start | bytes 5308424 | tf_op jit(solution)/shard_map/ppermute | solution.py:40
  18.7 3.5 %copy-start.6 = (bf16[4,2,144,768]{3,2,1,0:T(8,128)(2,1)S(1)}, bf16[4,2,144,768]{3,2,1,0:T(8,128)(2,1)}, u32[]{:S(2)}) copy-start(bf16[4,2,144,768]{3,2,1,0:T(8,128)(2,1)} %get-tuple-element.17) | copy-start | bytes 5308420
  19.3 21.9 %collective-permute-start.2 = (f16[4,72,1536]{2,1,0:T(8,128)(2,1)S(1)}, f16[4,72,1536]{2,1,0:T(8,128)(2,1)S(1)}, u32[]{:S(2)}, u32[]{:S(2)}) collective-permute-start(f16[4,72,1536]{2,1,0:T(8,128)(2,1)S(1)} %get-tuple-element.34), channel_id=1, source_target_pairs={{0,3},{1,0},{2,1},{3,2},{4,7},{5,4},{6,5},{7,6},{8,11},{9,8},{10,9... | collective-permute-start | bytes 2654216 | tf_op jit(solution)/shard_map/ppermute | solution.py:28
  22.2 22.5 %collective-permute-start.3 = (f16[4,72,1536]{2,1,0:T(8,128)(2,1)S(1)}, f16[4,72,1536]{2,1,0:T(8,128)(2,1)S(1)}, u32[]{:S(2)}, u32[]{:S(2)}) collective-permute-start(f16[4,72,1536]{2,1,0:T(8,128)(2,1)S(1)} %get-tuple-element.35), channel_id=1, source_target_pairs={{0,1},{1,2},{2,3},{3,0},{4,5},{5,6},{6,7},{7,4},{8,9},{9,10},{10,1... | collective-permute-start | bytes 2654216 | tf_op jit(solution)/shard_map/ppermute | solution.py:28
  29.7 18.6 %collective-permute-start.10 = (f16[4,72,1024]{2,1,0:T(8,128)(2,1)S(1)}, f16[4,72,1024]{2,1,0:T(8,128)(2,1)S(1)}, u32[]{:S(2)}, u32[]{:S(2)}) collective-permute-start(f16[4,72,1024]{2,1,0:T(8,128)(2,1)S(1)} %get-tuple-element.38), channel_id=1, source_target_pairs={{0,32},{32,128},{128,160},{160,0},{1,33},{33,129},{129,161},{161,1... | collective-permute-start | bytes 1769480 | tf_op jit(solution)/shard_map/ppermute | solution.py:32
  31.1 18.7 %collective-permute-start.9 = (f16[4,72,1024]{2,1,0:T(8,128)(2,1)S(1)}, f16[4,72,1024]{2,1,0:T(8,128)(2,1)S(1)}, u32[]{:S(2)}, u32[]{:S(2)}) collective-permute-start(f16[4,72,1024]{2,1,0:T(8,128)(2,1)S(1)} %get-tuple-element.39), channel_id=1, source_target_pairs={{0,160},{32,0},{128,32},{160,128},{1,161},{33,1},{129,33},{161,129... | collective-permute-start | bytes 1769480 | tf_op jit(solution)/shard_map/ppermute | solution.py:32
  45.0 12.2 %collective-permute-start.4 = (f16[2,72,1536]{2,1,0:T(8,128)(2,1)S(1)}, f16[2,72,1536]{2,1,0:T(8,128)(2,1)S(1)}, u32[]{:S(2)}, u32[]{:S(2)}) collective-permute-start(f16[2,72,1536]{2,1,0:T(8,128)(2,1)S(1)} %get-tuple-element.36), channel_id=1, source_target_pairs={{0,1},{1,2},{2,3},{3,0},{4,5},{5,6},{6,7},{7,4},{8,9},{9,10},{10,1... | collective-permute-start | bytes 1327112 | tf_op jit(solution)/shard_map/ppermute | solution.py:28
  45.0 12.1 %collective-permute-start.5 = (f16[2,72,1536]{2,1,0:T(8,128)(2,1)S(1)}, f16[2,72,1536]{2,1,0:T(8,128)(2,1)S(1)}, u32[]{:S(2)}, u32[]{:S(2)}) collective-permute-start(f16[2,72,1536]{2,1,0:T(8,128)(2,1)S(1)} %get-tuple-element.37), channel_id=1, source_target_pairs={{0,3},{1,0},{2,1},{3,2},{4,7},{5,4},{6,5},{7,6},{8,11},{9,8},{10,9... | collective-permute-start | bytes 1327112 | tf_op jit(solution)/shard_map/ppermute | solution.py:28
  48.4 12.4 %collective-permute-start.11 = (f16[2,72,1024]{2,1,0:T(8,128)(2,1)S(1)}, f16[2,72,1024]{2,1,0:T(8,128)(2,1)S(1)}, u32[]{:S(2)}, u32[]{:S(2)}) collective-permute-start(f16[2,72,1024]{2,1,0:T(8,128)(2,1)S(1)} %fusion.11), channel_id=1, source_target_pairs={{0,32},{32,128},{128,160},{160,0},{1,33},{33,129},{129,161},{161,1... | collective-permute-start | bytes 884744 | tf_op jit(solution)/shard_map/ppermute | solution.py:32
  49.8 10.9 %collective-permute-start.12 = (f16[2,72,1024]{2,1,0:T(8,128)(2,1)S(1)}, f16[2,72,1024]{2,1,0:T(8,128)(2,1)S(1)}, u32[]{:S(2)}, u32[]{:S(2)}) collective-permute-start(f16[2,72,1024]{2,1,0:T(8,128)(2,1)S(1)} %fusion.10), channel_id=1, source_target_pairs={{0,160},{32,0},{128,32},{160,128},{1,161},{33,1},{129,33},{161,129... | collective-permute-start | bytes 884744 | tf_op jit(solution)/shard_map/ppermute | solution.py:32
  57.9 9.4 %collective-permute-start.6 = (f16[1,72,1536]{2,1,0:T(8,128)(2,1)S(1)}, f16[1,72,1536]{2,1,0:T(8,128)(2,1)S(1)}, u32[]{:S(2)}, u32[]{:S(2)}) collective-permute-start(f16[1,72,1536]{2,1,0:T(8,128)(2,1)S(1)} %get-tuple-element.44), channel_id=1, source_target_pairs={{0,128},{32,160},{128,0},{160,32},{1,129},{33,161},{129,1},{161,33... | collective-permute-start | bytes 663560 | tf_op jit(solution)/shard_map/ppermute | solution.py:32
  58.3 11.7 %collective-permute-start.7 = (f16[1,72,1536]{2,1,0:T(8,128)(2,1)S(1)}, f16[1,72,1536]{2,1,0:T(8,128)(2,1)S(1)}, u32[]{:S(2)}, u32[]{:S(2)}) collective-permute-start(f16[1,72,1536]{2,1,0:T(8,128)(2,1)S(1)} %get-tuple-element.43), channel_id=1, source_target_pairs={{0,32},{32,128},{128,160},{160,0},{1,33},{33,129},{129,161},{161,1... | collective-permute-start | bytes 663560 | tf_op jit(solution)/shard_map/ppermute | solution.py:32
  60.5 9.5 %collective-permute-start.8 = (f16[1,72,1536]{2,1,0:T(8,128)(2,1)S(1)}, f16[1,72,1536]{2,1,0:T(8,128)(2,1)S(1)}, u32[]{:S(2)}, u32[]{:S(2)}) collective-permute-start(f16[1,72,1536]{2,1,0:T(8,128)(2,1)S(1)} %get-tuple-element.42), channel_id=1, source_target_pairs={{0,160},{32,0},{128,32},{160,128},{1,161},{33,1},{129,33},{161,129... | collective-permute-start | bytes 663560 | tf_op jit(solution)/shard_map/ppermute | solution.py:32
  61.4 8.7 %collective-permute-start.13 = (f16[1,72,1024]{2,1,0:T(8,128)(2,1)S(1)}, f16[1,72,1024]{2,1,0:T(8,128)(2,1)S(1)}, u32[]{:S(2)}, u32[]{:S(2)}) collective-permute-start(f16[1,72,1024]{2,1,0:T(8,128)(2,1)S(1)} %get-tuple-element.45), channel_id=1, source_target_pairs={{0,2},{1,3},{2,0},{3,1},{4,6},{5,7},{6,4},{7,5},{8,10},{9,11},{10,... | collective-permute-start | bytes 442376 | tf_op jit(solution)/shard_map/ppermute | solution.py:28
  63.0 7.2 %collective-permute-start.14 = (f16[1,72,1024]{2,1,0:T(8,128)(2,1)S(1)}, f16[1,72,1024]{2,1,0:T(8,128)(2,1)S(1)}, u32[]{:S(2)}, u32[]{:S(2)}) collective-permute-start(f16[1,72,1024]{2,1,0:T(8,128)(2,1)S(1)} %get-tuple-element.47), channel_id=1, source_target_pairs={{0,1},{1,2},{2,3},{3,0},{4,5},{5,6},{6,7},{7,4},{8,9},{9,10},{10,1... | collective-permute-start | bytes 442376 | tf_op jit(solution)/shard_map/ppermute | solution.py:28
  67.3 5.3 %collective-permute-start.15 = (f16[1,72,1024]{2,1,0:T(8,128)(2,1)S(1)}, f16[1,72,1024]{2,1,0:T(8,128)(2,1)S(1)}, u32[]{:S(2)}, u32[]{:S(2)}) collective-permute-start(f16[1,72,1024]{2,1,0:T(8,128)(2,1)S(1)} %get-tuple-element.46), channel_id=1, source_target_pairs={{0,3},{1,0},{2,1},{3,2},{4,7},{5,4},{6,5},{7,6},{8,11},{9,8},{10,9... | collective-permute-start | bytes 442376 | tf_op jit(solution)/shard_map/ppermute | solution.py:28
  70.1 23.4 %copy-start = (f32[6,2560]{1,0:T(8,128)S(1)}, f32[6,2560]{1,0:T(8,128)}, u32[]{:S(2)}) copy-start(f32[6,2560]{1,0:T(8,128)} %param.18) | copy-start | bytes 184324
  70.1 23.4 %copy-start.1 = (f32[6,2560]{1,0:T(8,128)S(1)}, f32[6,2560]{1,0:T(8,128)}, u32[]{:S(2)}) copy-start(f32[6,2560]{1,0:T(8,128)} %param.20) | copy-start | bytes 184324
  70.1 23.4 %copy-start.2 = (f32[6,2560]{1,0:T(8,128)S(1)}, f32[6,2560]{1,0:T(8,128)}, u32[]{:S(2)}) copy-start(f32[6,2560]{1,0:T(8,128)} %param.19) | copy-start | bytes 184324
  72.7 21.5 %copy-start.3 = (f32[3,2560]{1,0:T(4,128)S(1)}, f32[3,2560]{1,0:T(4,128)}, u32[]{:S(2)}) copy-start(f32[3,2560]{1,0:T(4,128)} %param.21) | copy-start | bytes 92164
  72.8 21.5 %copy-start.4 = (f32[3,2560]{1,0:T(4,128)S(1)}, f32[3,2560]{1,0:T(4,128)}, u32[]{:S(2)}) copy-start(f32[3,2560]{1,0:T(4,128)} %param.23) | copy-start | bytes 92164
  72.8 21.5 %copy-start.5 = (f32[3,2560]{1,0:T(4,128)S(1)}, f32[3,2560]{1,0:T(4,128)}, u32[]{:S(2)}) copy-start(f32[3,2560]{1,0:T(4,128)} %param.22) | copy-start | bytes 92164
  95.9 15.1 %all-to-all-start.1 = ((bf16[8,180,128]{2,1,0:T(8,128)(2,1)}), bf16[8,180,128]{2,1,0:T(8,128)(2,1)S(1)}, u32[]{:S(2)}, u32[]{:S(2)}) async-start(bf16[8,180,128]{2,1,0:T(8,128)(2,1)} %broadcast_in_dim.5), calls=%async_computation.1 | async-start | bytes 753664 | tf_op jit(solution)/shard_map/all_to_all | solution.py:214
  111.3 11.4 %collective-permute-start.16 = (bf16[48,2560]{1,0:T(8,128)(2,1)S(1)}, bf16[48,2560]{1,0:T(8,128)(2,1)S(1)}, u32[]{:S(2)}, u32[]{:S(2)}) collective-permute-start(bf16[48,2560]{1,0:T(8,128)(2,1)S(1)} %reshape.99), channel_id=1, source_target_pairs={{0,32},{32,0},{1,33},{33,1},{2,34},{34,2},{3,35},{35,3},{4,36},{36... | collective-permute-start | bytes 737288 | tf_op jit(solution)/shard_map/ppermute | solution.py:36
  112.6 10.0 %collective-permute-start.17 = (bf16[48,2560]{1,0:T(8,128)(2,1)S(1)}, bf16[48,2560]{1,0:T(8,128)(2,1)S(1)}, u32[]{:S(2)}, u32[]{:S(2)}) collective-permute-start(bf16[48,2560]{1,0:T(8,128)(2,1)S(1)} %reshape.99), channel_id=1, source_target_pairs={{0,1},{1,2},{2,3},{3,0},{4,5},{5,6},{6,7},{7,4},{8,9},{9,10},{10,1... | collective-permute-start | bytes 737288 | tf_op jit(solution)/shard_map/ppermute | solution.py:28
  112.8 6.7 %collective-permute-start.25 = (bf16[24,2560]{1,0:T(8,128)(2,1)S(1)}, bf16[24,2560]{1,0:T(8,128)(2,1)S(1)}, u32[]{:S(2)}, u32[]{:S(2)}) collective-permute-start(bf16[24,2560]{1,0:T(8,128)(2,1)S(1)} %reshape.100), channel_id=1, source_target_pairs={{0,3},{1,0},{2,1},{3,2},{4,7},{5,4},{6,5},{7,6},{8,11},{9,8},{10,9... | collective-permute-start | bytes 368648 | tf_op jit(solution)/shard_map/ppermute | solution.py:28
  116.5 10.5 %collective-permute-start.24 = (bf16[24,2560]{1,0:T(8,128)(2,1)S(1)}, bf16[24,2560]{1,0:T(8,128)(2,1)S(1)}, u32[]{:S(2)}, u32[]{:S(2)}) collective-permute-start(bf16[24,2560]{1,0:T(8,128)(2,1)S(1)} %reshape.100), channel_id=1, source_target_pairs={{0,2},{1,3},{2,0},{3,1},{4,6},{5,7},{6,4},{7,5},{8,10},{9,11},{10,... | collective-permute-start | bytes 368648 | tf_op jit(solution)/shard_map/ppermute | solution.py:28
  118.1 8.9 %collective-permute-start.23 = (bf16[24,2560]{1,0:T(8,128)(2,1)S(1)}, bf16[24,2560]{1,0:T(8,128)(2,1)S(1)}, u32[]{:S(2)}, u32[]{:S(2)}) collective-permute-start(bf16[24,2560]{1,0:T(8,128)(2,1)S(1)} %reshape.100), channel_id=1, source_target_pairs={{0,1},{1,2},{2,3},{3,0},{4,5},{5,6},{6,7},{7,4},{8,9},{9,10},{10,1... | collective-permute-start | bytes 368648 | tf_op jit(solution)/shard_map/ppermute | solution.py:28
  119.4 23.7 %collective-permute-start.22 = (bf16[48,2560]{1,0:T(8,128)(2,1)S(1)}, bf16[48,2560]{1,0:T(8,128)(2,1)S(1)}, u32[]{:S(2)}, u32[]{:S(2)}) collective-permute-start(bf16[48,2560]{1,0:T(8,128)(2,1)S(1)} %reshape.99), channel_id=1, source_target_pairs={{0,3},{1,0},{2,1},{3,2},{4,7},{5,4},{6,5},{7,6},{8,11},{9,8},{10,9... | collective-permute-start | bytes 737288 | tf_op jit(solution)/shard_map/ppermute | solution.py:28
  127.0 12.0 %collective-permute-start.26 = (bf16[96,2560]{1,0:T(8,128)(2,1)S(1)}, bf16[96,2560]{1,0:T(8,128)(2,1)S(1)}, u32[]{:S(2)}, u32[]{:S(2)}) collective-permute-start(bf16[96,2560]{1,0:T(8,128)(2,1)S(1)} %pad_maximum_fusion), channel_id=1, source_target_pairs={{0,32},{32,0},{1,33},{33,1},{2,34},{34,2},{3,35},{35,3},{4,36},{36... | collective-permute-start | bytes 1474568 | tf_op jit(solution)/shard_map/ppermute | solution.py:36
  128.1 10.8 %collective-permute-start.18 = (bf16[48,2560]{1,0:T(8,128)(2,1)S(1)}, bf16[48,2560]{1,0:T(8,128)(2,1)S(1)}, u32[]{:S(2)}, u32[]{:S(2)}) collective-permute-start(bf16[48,2560]{1,0:T(8,128)(2,1)S(1)} %collective-permute-done.16), channel_id=1, source_target_pairs={{0,1},{1,2},{2,3},{3,0},{4,5},{5,6},{6,7},{7,4},{8,9},{9,10},{10,1... | collective-permute-start | bytes 737288 | tf_op jit(solution)/shard_map/ppermute | solution.py:28
  128.2 10.8 %collective-permute-start.19 = (bf16[48,2560]{1,0:T(8,128)(2,1)S(1)}, bf16[48,2560]{1,0:T(8,128)(2,1)S(1)}, u32[]{:S(2)}, u32[]{:S(2)}) collective-permute-start(bf16[48,2560]{1,0:T(8,128)(2,1)S(1)} %collective-permute-done.17), channel_id=1, source_target_pairs={{0,1},{1,2},{2,3},{3,0},{4,5},{5,6},{6,7},{7,4},{8,9},{9,10},{10,1... | collective-permute-start | bytes 737288 | tf_op jit(solution)/shard_map/ppermute | solution.py:28
  130.3 6.6 %collective-permute-start.20 = (bf16[48,2560]{1,0:T(8,128)(2,1)S(1)}, bf16[48,2560]{1,0:T(8,128)(2,1)S(1)}, u32[]{:S(2)}, u32[]{:S(2)}) collective-permute-start(bf16[48,2560]{1,0:T(8,128)(2,1)S(1)} %collective-permute-done.16), channel_id=1, source_target_pairs={{0,3},{1,0},{2,1},{3,2},{4,7},{5,4},{6,5},{7,6},{8,11},{9,8},{10,9... | collective-permute-start | bytes 737288 | tf_op jit(solution)/shard_map/ppermute | solution.py:28
  137.0 6.2 %collective-permute-start.21 = (bf16[48,2560]{1,0:T(8,128)(2,1)S(1)}, bf16[48,2560]{1,0:T(8,128)(2,1)S(1)}, u32[]{:S(2)}, u32[]{:S(2)}) collective-permute-start(bf16[48,2560]{1,0:T(8,128)(2,1)S(1)} %collective-permute-done.20), channel_id=1, source_target_pairs={{0,3},{1,0},{2,1},{3,2},{4,7},{5,4},{6,5},{7,6},{8,11},{9,8},{10,9... | collective-permute-start | bytes 737288 | tf_op jit(solution)/shard_map/ppermute | solution.py:28

commit v5 on v4

--- a/solution.py
+++ b/solution.py
@@ -198,10 +198,9 @@
     last_b = [after(chunks_a, v) for v in last_b]
     two_a = send(chunks_a, 1)
     one_b = summed(total_b, 1, *first_b, *last_b)[:, None]
-    two_b = send(cut(one_b, 0), 0)
+    two_b = lax.all_to_all(one_b[:, 0].astype(F16), "x", 0, 0)
     two_a = gathered(one_a, 1, two_a)[0].astype(F16)
-    two_b = [after([two_a], v) for v in two_b]
-    two_b = gathered(one_b, 0, two_b)[0].astype(F16)
+    two_b = after([two_a], two_b).astype(F32).sum(axis=0).astype(F16)
     two = [two_a, two_b]
     last = jnp.concatenate(two, axis=1).reshape(NZ, rows * width // 128, 128)
     last = lax.all_to_all(last, "z", 0, 0)
@@ -212,31 +211,30 @@
 
     weight = jnp.concatenate([weight_s, weight_r], axis=0).reshape(1, rows * width // 128, 128)
     weight = lax.all_to_all(jnp.broadcast_to(weight, (NZ,) + weight.shape[1:]), "z", 0, 0)
-    weight_s = weight[:, : sr * width // 128].reshape(NZ * sr, width)
-    weight_r = weight[:, sr * width // 128 :].reshape(NZ * rr, width)
-    mine, other = weight_s, y_swap(weight_s)
+    mine = weight.reshape(group, width)
+    part = group // 32 * 16
     mine_plus, mine_minus = x_ring(mine, 1), x_ring(mine, 3)
+    other = y_swap(mine)
+    two = [x_ring(mine_plus[:part], 1), x_ring(mine_minus[part:], 3)]
     other_plus, other_minus = x_ring(other, 1), x_ring(other, 3)
-    mine_two, other_two = x_ring(mine_plus, 1), x_ring(other_minus, 3)
-    around = [after([other, mine_plus], x_ring(weight_r, d)) for d in (1, 2, 3)]
-    all_r = jnp.concatenate([weight_r] + around, axis=0)
-    all_r = jnp.concatenate([all_r, y_swap(all_r)], axis=0)
-    all_s = jnp.concatenate(
+    mine_two = jnp.concatenate(two, axis=0)
+    other_two = y_swap(mine_two)
+    full = jnp.concatenate(
         [mine, other, mine_plus, other_plus, mine_two, other_two, mine_minus, other_minus], axis=0
     )
 
-    def settled(full, count, index):
-        n = full.shape[0]
+    def settled(count, low):
+        n = 2 * NZ * NX * count
         r = lax.iota(jnp.int32, n)
         back = (x - (r // count) % NX) % NX
         zz = (r // (count * NX)) % NZ
         flip = (r // (count * NX * NZ)) ^ yl
-        want = lax.optimization_barrier((index(back, flip) * NZ + zz) * count + r % count)
-        take = (want[:, None] == lax.broadcasted_iota(jnp.int32, (n, n), 1)).astype(BF)
+        want = ((back * 2 + flip) * NZ + zz) * rows + low + r % count
+        want = lax.optimization_barrier(want)
+        take = (want[:, None] == lax.broadcasted_iota(jnp.int32, (n, full.shape[0]), 1)).astype(BF)
         return dot(lax.optimization_barrier(take), full).astype(BF)
 
-    shared = settled(all_s, sr, lambda back, flip: back * 2 + flip)
-    routed = settled(all_r, rr, lambda back, flip: flip * NX + back)
+    shared, routed = settled(sr, 0), settled(rr, sr)
     return (moment_s, second_s, moment_r, second_r, shared, routed)
 
 

time: 147 us -> 152 us (1.034)
  starting transfers between devices: 41.5 us -> 33.3 us
  waiting for transfers between devices: 47.4 us -> 54.8 us
  other arithmetic: 5.26 us -> 8.69 us
    ppermute x16 -> x10, starting transfers between devices: 27.9 us -> 14.1 us  [x_ring(): return lax.ppermute(v, 'x', [(i, (i + d) % NX) for i in range(NX)])]
    all_to_all x0 -> x1, waiting for transfers between devices: none -> 5.97 us  [local(): two_b = lax.all_to_all(one_b[:, 0].astype(F16), 'x', 0, 0)]
    all_to_all x0 -> x1, starting transfers between devices: none -> 4.22 us  [local(): two_b = lax.all_to_all(one_b[:, 0].astype(F16), 'x', 0, 0)]
    ppermute x2, waiting for transfers between devices: 0.01 us -> 3.61 us  [y_swap(): return lax.ppermute(v, 'yl', [(0, 1), (1, 0)])]
    ppermute x16 -> x10, waiting for transfers between devices: 34.1 us -> 31.5 us  [x_ring(): return lax.ppermute(v, 'x', [(i, (i + d) % NX) for i in range(NX)])]
    convert_element_type x2, other arithmetic: 1.41 us -> 3.15 us  [adamw(): return (new_moment, new_second, new_master.astype(BF))]
    ppermute x2, starting transfers between devices: 2.39 us -> 4.01 us  [y_swap(): return lax.ppermute(v, 'yl', [(0, 1), (1, 0)])]
  transfers between devices with their start and end apart: 28 -> 23, of which waited for: 9 -> 11; matrix products, arithmetic and copies ran while one was open for 12% -> 11% of each run, Pallas kernels for 5% -> 5%
where the time goes in v5:
time: 152 us; the launch traced here: 149 us
  waiting for transfers between devices  54.8 us (36%)
  starting transfers between devices  33.3 us (22%)
  matrix products  21.8 us (14%)
  blocking collectives  20 us (13%)
  other arithmetic  8.69 us (6%)
  Pallas kernels  6.81 us (4%)
  local copies, waits for them, and re-layouts  2.16 us (1%)
  between operations  1.61 us (1%)
    ppermute x10, waiting for transfers between devices, x_ring(): return lax.ppermute(v, 'x', [(i, (i + d) % NX) for i in range(NX)])  31.5 us
    dot_general x6, matrix products, dot(): return jnp.dot(a, b, preferred_element_type=F32)  21.8 us
    all_to_all x1, blocking collectives, local(): last = lax.all_to_all(last, 'z', 0, 0)  20 us
    ppermute x10, starting transfers between devices, x_ring(): return lax.ppermute(v, 'x', [(i, (i + d) % NX) for i in range(NX)])  14.1 us
    all_to_all x1, waiting for transfers between devices, local(): lax.all_to_all(jnp.broadcast_to(weight, (NZ,) + weight.shape[1:]), 'z', 0...  11.4 us
    ppermute x7, starting transfers between devices, y_ring(): return lax.ppermute(v, ('yh', 'yl'), [(i, (i + d) % NY) for i in range(NY)])  7.03 us
    pallas_call x1, Pallas kernels, ordered(): pl.pallas_call(order_kernel, grid_spec=pltpu.PrefetchScalarGridSpec(num_s...  6.81 us
    all_to_all x1, waiting for transfers between devices, local(): two_b = lax.all_to_all(one_b[:, 0].astype(F16), 'x', 0, 0)  5.97 us
  transfers between devices with their start and end apart: 23, of which 11 were waited for; matrix products, arithmetic and copies ran while one was open for 11% of the time, Pallas kernels for 5%

profile of v5, /device:TPU:16, one launch (start us, length us, event | category | flops | bytes accessed | tf_op | source)
XLA Modules:
  0.0 149.2 jit_solution(8131057061040901664)
XLA Ops:
  1.4 6.8 %shard_map.172 = (bf16[4,2,144,768]{3,2,1,0:T(8,128)(2,1)}, bf16[4,2,144,768]{3,2,1,0:T(8,128)(2,1)}) custom-call(s32[1]{0:T(128)} %bitcast.core_ref, s32[1]{0:T(128)S(6)} %copy.33.count_ref, s32[1,96]{1,0:T(1,128)} %bitcast.70, bf16[768,1536]{1,0:T(8,128)(2,1)} %shared_ref.1, bf16[96,768]{1,0:T(8,128)(2,1)} %routed_ref.1, ...), custom_call_target="tpu_custom_call" | custom-call | flops 2717908992 | bytes 8847360 | tf_op jit(solution)/shard_map/pallas_call | solution.py:101
  8.2 0.5 collective-permute-start
  8.7 5.1 %fusion.3 = f32[1152,1536]{1,0:T(8,128)S(1)} fusion(bf16[1152,768]{1,0:T(8,128)(2,1)} %bitcast.71, bf16[768,2560]{1,0:T(8,128)(2,1)} %param.15), kind=kOutput, calls=%fused_computation.7 | convolution fusion | flops 2717908992 | bytes 11206656 | tf_op jit(solution)/shard_map/dot_general | solution.py:67
  13.9 4.9 %fusion.1 = f16[1152,1536]{1,0:T(8,128)(2,1)S(1)} fusion(f32[1152,1536]{1,0:T(8,128)S(1)} %fusion.3, bf16[1152,768]{1,0:T(8,128)(2,1)S(1)} %bitcast.68, bf16[768,2560]{1,0:T(8,128)(2,1)} %collective-permute-done.1), kind=kOutput, calls=%fused_computation.2 | convolution fusion | flops 2723217408 | bytes 14745600 | tf_op jit(solution)/shard_map/dot_general | solution.py:67
  18.7 0.6 bitcast_select_fusion.1
  19.4 2.8 %collective-permute-start.2 = (f16[4,72,1536]{2,1,0:T(8,128)(2,1)S(1)}, f16[4,72,1536]{2,1,0:T(8,128)(2,1)S(1)}, u32[]{:S(2)}, u32[]{:S(2)}) collective-permute-start(f16[4,72,1536]{2,1,0:T(8,128)(2,1)S(1)} %get-tuple-element.24), channel_id=1, source_target_pairs={{0,3},{1,0},{2,1},{3,2},{4,7},{5,4},{6,5},{7,6},{8,11},{9,8},{10,9... | collective-permute-start | bytes 2654216 | tf_op jit(solution)/shard_map/ppermute | solution.py:28
  22.2 3.4 %fusion.6 = f32[1152,1024]{1,0:T(8,128)S(1)} fusion(bf16[1152,768]{1,0:T(8,128)(2,1)S(1)} %bitcast.72, bf16[768,2560]{1,0:T(8,128)(2,1)} %param.15), kind=kOutput, calls=%fused_computation.11 | convolution fusion | flops 1811939328 | bytes 8060928 | tf_op jit(solution)/shard_map/dot_general | solution.py:67
  25.6 3.5 %multiply_convert_fusion = f16[1152,1024]{1,0:T(8,128)(2,1)S(1)} fusion(f32[1152,1024]{1,0:T(8,128)S(1)} %fusion.6, bf16[1152,768]{1,0:T(8,128)(2,1)S(1)} %bitcast.69, bf16[768,2560]{1,0:T(8,128)(2,1)} %collective-permute-done.1), kind=kOutput, calls=%fused_computation.3 | convolution fusion | flops 1815478272 | bytes 10420224 | tf_op jit(solution)/shard_map/dot_general | solution.py:67
  29.2 0.6 bitcast_select_fusion.3
  29.8 1.4 collective-permute-start.10
  31.2 0.7 collective-permute-start.9
  32.0 9.3 %collective-permute-done.2 = f16[4,72,1536]{2,1,0:T(8,128)(2,1)S(1)} collective-permute-done((f16[4,72,1536]{2,1,0:T(8,128)(2,1)S(1)}, f16[4,72,1536]{2,1,0:T(8,128)(2,1)S(1)}, u32[]{:S(2)}, u32[]{:S(2)}) %collective-permute-start.2) | collective-permute-done | bytes 884768 | tf_op jit(solution)/shard_map/ppermute | solution.py:28
  41.3 3.4 %collective-permute-done.3 = f16[4,72,1536]{2,1,0:T(8,128)(2,1)S(1)} collective-permute-done((f16[4,72,1536]{2,1,0:T(8,128)(2,1)S(1)}, f16[4,72,1536]{2,1,0:T(8,128)(2,1)S(1)}, u32[]{:S(2)}, u32[]{:S(2)}) %collective-permute-start.3) | collective-permute-done | bytes 884768 | tf_op jit(solution)/shard_map/ppermute | solution.py:28
  44.7 0.3 fusion.11
  45.1 3.2 %collective-permute-start.5 = (f16[2,72,1536]{2,1,0:T(8,128)(2,1)S(1)}, f16[2,72,1536]{2,1,0:T(8,128)(2,1)S(1)}, u32[]{:S(2)}, u32[]{:S(2)}) collective-permute-start(f16[2,72,1536]{2,1,0:T(8,128)(2,1)S(1)} %get-tuple-element.27), channel_id=1, source_target_pairs={{0,3},{1,0},{2,1},{3,2},{4,7},{5,4},{6,5},{7,6},{8,11},{9,8},{10,9... | collective-permute-start | bytes 1327112 | tf_op jit(solution)/shard_map/ppermute | solution.py:28
  48.4 1.4 collective-permute-start.11
  49.9 0.8 collective-permute-start.12
  50.7 6.5 %collective-permute-done.4 = f16[2,72,1536]{2,1,0:T(8,128)(2,1)S(1)} collective-permute-done((f16[2,72,1536]{2,1,0:T(8,128)(2,1)S(1)}, f16[2,72,1536]{2,1,0:T(8,128)(2,1)S(1)}, u32[]{:S(2)}, u32[]{:S(2)}) %collective-permute-start.4) | collective-permute-done | bytes 442400 | tf_op jit(solution)/shard_map/ppermute | solution.py:28
  57.2 0.7 convert_add_fusion
  57.9 0.8 dynamic-slice_convert_fusion
  58.7 0.3 collective-permute-start.6
  59.1 2.2 %collective-permute-start.7 = (f16[1,72,1536]{2,1,0:T(8,128)(2,1)S(1)}, f16[1,72,1536]{2,1,0:T(8,128)(2,1)S(1)}, u32[]{:S(2)}, u32[]{:S(2)}) collective-permute-start(f16[1,72,1536]{2,1,0:T(8,128)(2,1)S(1)} %get-tuple-element.31), channel_id=1, source_target_pairs={{0,32},{32,128},{128,160},{160,0},{1,33},{33,129},{129,161},{161,1... | collective-permute-start | bytes 663560 | tf_op jit(solution)/shard_map/ppermute | solution.py:32
  61.2 0.2 collective-permute-start.8
  61.5 1.5 fusion.8
  63.0 4.2 %all-to-all-start = ((f16[4,72,1024]{2,1,0:T(8,128)(2,1)}), f16[4,72,1024]{2,1,0:T(8,128)(2,1)S(1)}, u32[]{:S(2)}, u32[]{:S(2)}) async-start(f16[4,72,1024]{2,1,0:T(8,128)(2,1)} %fusion.8), calls=%async_computation | async-start | bytes 1179648 | tf_op jit(solution)/shard_map/all_to_all | solution.py:201
  67.2 1.0 collective-permute-done.6
  68.2 1.2 collective-permute-done.7
  69.6 6.0 %all-to-all-done = f16[4,72,1024]{2,1,0:T(8,128)(2,1)S(1)} async-done(((f16[4,72,1024]{2,1,0:T(8,128)(2,1)}), f16[4,72,1024]{2,1,0:T(8,128)(2,1)S(1)}, u32[]{:S(2)}, u32[]{:S(2)}) %all-to-all-start) | async-done | bytes 589856 | tf_op jit(solution)/shard_map/all_to_all | solution.py:201
  75.8 0.5 reshape.80
  76.3 20.0 %all_to_all.15 = f16[8,180,128]{2,1,0:T(8,128)(2,1)S(1)} all-to-all(f16[8,180,128]{2,1,0:T(8,128)(2,1)S(1)} %reshape.80), channel_id=1, replica_groups=mesh['yh'=2,'core'=2,'yl'=2,'z'=8,'x'=4] {'z'}, dimensions={0} | all-to-all | bytes 737280 | tf_op jit(solution)/shard_map/all_to_all | solution.py:206
  96.5 1.6 %subtract_convert_fusion = (bf16[6,2560]{1,0:T(8,128)(2,1)S(1)}, f32[6,2560]{1,0:T(8,128)}, f32[6,2560]{1,0:T(8,128)}) fusion(f32[6,2560]{1,0:T(8,128)S(1)} %copy-done, f32[6,2560]{1,0:T(8,128)S(1)} %slice.71, f32[6,2560]{1,0:T(8,128)} %param.20, f32[6,2560]{1,0:T(8,128)} %param.19), kind=kLoop, calls=%fused_computation.48 | loop fusion | flops 245760 | bytes 399360 | tf_op jit(solution)/shard_map/convert_element_type | solution.py:24
  98.1 1.5 %subtract_convert_fusion.1 = (bf16[3,2560]{1,0:T(4,128)(2,1)S(1)}, f32[3,2560]{1,0:T(4,128)}, f32[3,2560]{1,0:T(4,128)}) fusion(f32[3,2560]{1,0:T(4,128)} %param.21, f32[3,2560]{1,0:T(4,128)S(1)} %slice.73, f32[3,2560]{1,0:T(4,128)} %param.23, f32[3,2560]{1,0:T(4,128)} %param.22), kind=kLoop, calls=%fused_computation.53 | loop fusion | flops 122880 | bytes 199680 | tf_op jit(solution)/shard_map/convert_element_type | solution.py:24
  99.7 0.8 broadcast_in_dim.5
  100.5 3.4 %all-to-all-start.2 = ((bf16[8,180,128]{2,1,0:T(8,128)(2,1)}), bf16[8,180,128]{2,1,0:T(8,128)(2,1)S(1)}, u32[]{:S(2)}, u32[]{:S(2)}) async-start(bf16[8,180,128]{2,1,0:T(8,128)(2,1)} %broadcast_in_dim.5), calls=%async_computation.2 | async-start | bytes 753664 | tf_op jit(solution)/shard_map/all_to_all | solution.py:213
  104.2 11.4 %all-to-all-done.2 = bf16[8,180,128]{2,1,0:T(8,128)(2,1)S(1)} async-done(((bf16[8,180,128]{2,1,0:T(8,128)(2,1)}), bf16[8,180,128]{2,1,0:T(8,128)(2,1)S(1)}, u32[]{:S(2)}, u32[]{:S(2)}) %all-to-all-start.2) | async-done | bytes 368672 | tf_op jit(solution)/shard_map/all_to_all | solution.py:213
  115.6 0.4 reshape.81
  116.0 1.2 collective-permute-start.17
  117.3 0.9 collective-permute-start.14
  118.1 2.0 %collective-permute-start.13 = (bf16[72,2560]{1,0:T(8,128)(2,1)S(1)}, bf16[72,2560]{1,0:T(8,128)(2,1)S(1)}, u32[]{:S(2)}, u32[]{:S(2)}) collective-permute-start(bf16[72,2560]{1,0:T(8,128)(2,1)S(1)} %reshape.81), channel_id=1, source_target_pairs={{0,32},{32,0},{1,33},{33,1},{2,34},{34,2},{3,35},{35,3},{4,36},{36... | collective-permute-start | bytes 1105928 | tf_op jit(solution)/shard_map/ppermute | solution.py:36
  120.2 7.3 %collective-permute-done.17 = bf16[72,2560]{1,0:T(8,128)(2,1)S(1)} collective-permute-done((bf16[72,2560]{1,0:T(8,128)(2,1)S(1)}, bf16[72,2560]{1,0:T(8,128)(2,1)S(1)}, u32[]{:S(2)}, u32[]{:S(2)}) %collective-permute-start.17) | collective-permute-done | bytes 368672 | tf_op jit(solution)/shard_map/ppermute | solution.py:28
  127.6 2.4 %collective-permute-start.18 = (bf16[40,2560]{1,0:T(8,128)(2,1)S(1)}, bf16[40,2560]{1,0:T(8,128)(2,1)S(1)}, u32[]{:S(2)}, u32[]{:S(2)}) collective-permute-start(bf16[40,2560]{1,0:T(8,128)(2,1)S(1)} %slice.86), channel_id=1, source_target_pairs={{0,3},{1,0},{2,1},{3,2},{4,7},{5,4},{6,5},{7,6},{8,11},{9,8},{10,9... | collective-permute-start | bytes 614408 | tf_op jit(solution)/shard_map/ppermute | solution.py:28
  130.3 3.2 %collective-permute-start.20 = (bf16[72,2560]{1,0:T(8,128)(2,1)S(1)}, bf16[72,2560]{1,0:T(8,128)(2,1)S(1)}, u32[]{:S(2)}, u32[]{:S(2)}) collective-permute-start(bf16[72,2560]{1,0:T(8,128)(2,1)S(1)} %collective-permute-done.13), channel_id=1, source_target_pairs={{0,3},{1,0},{2,1},{3,2},{4,7},{5,4},{6,5},{7,6},{8,11},{9,8},{10,9... | collective-permute-start | bytes 1105928 | tf_op jit(solution)/shard_map/ppermute | solution.py:28
  133.5 3.1 %collective-permute-done.16 = bf16[32,2560]{1,0:T(8,128)(2,1)S(1)} collective-permute-done((bf16[32,2560]{1,0:T(8,128)(2,1)S(1)}, bf16[32,2560]{1,0:T(8,128)(2,1)S(1)}, u32[]{:S(2)}, u32[]{:S(2)}) %collective-permute-start.16) | collective-permute-done | bytes 163872 | tf_op jit(solution)/shard_map/ppermute | solution.py:28
  136.7 2.0 %collective-permute-start.19 = (bf16[72,2560]{1,0:T(8,128)(2,1)S(1)}, bf16[72,2560]{1,0:T(8,128)(2,1)S(1)}, u32[]{:S(2)}, u32[]{:S(2)}) collective-permute-start(bf16[72,2560]{1,0:T(8,128)(2,1)S(1)} %pad_maximum_fusion.1), channel_id=1, source_target_pairs={{0,32},{32,0},{1,33},{33,1},{2,34},{34,2},{3,35},{35,3},{4,36},{36... | collective-permute-start | bytes 1105928 | tf_op jit(solution)/shard_map/ppermute | solution.py:36
  138.7 1.9 %collective-permute-done.15 = bf16[72,2560]{1,0:T(8,128)(2,1)S(1)} collective-permute-done((bf16[72,2560]{1,0:T(8,128)(2,1)S(1)}, bf16[72,2560]{1,0:T(8,128)(2,1)S(1)}, u32[]{:S(2)}, u32[]{:S(2)}) %collective-permute-start.15) | collective-permute-done | bytes 368672 | tf_op jit(solution)/shard_map/ppermute | solution.py:28
  140.7 3.6 %collective-permute-done.19 = bf16[72,2560]{1,0:T(8,128)(2,1)S(1)} collective-permute-done((bf16[72,2560]{1,0:T(8,128)(2,1)S(1)}, bf16[72,2560]{1,0:T(8,128)(2,1)S(1)}, u32[]{:S(2)}, u32[]{:S(2)}) %collective-permute-start.19) | collective-permute-done | bytes 368672 | tf_op jit(solution)/shard_map/ppermute | solution.py:36
  144.4 3.0 %convolution_convert_fusion = bf16[384,2560]{1,0:T(8,128)(2,1)} fusion(bf16[384,576]{1,0:T(8,128)(2,1)S(1)} %fusion.9, bf16[576,2560]{1,0:T(8,128)(2,1)S(1)} %constant_dynamic-update-slice_fusion), kind=kOutput, calls=%fused_computation.4 | convolution fusion | flops 1133445120 | bytes 5357568 | tf_op jit(solution)/shard_map/dot_general | solution.py:67
  147.3 1.9 %convolution_convert_fusion.1 = bf16[192,2560]{1,0:T(8,128)(2,1)} fusion(bf16[192,576]{1,0:T(8,128)(2,1)S(1)} %fusion.14, bf16[576,2560]{1,0:T(8,128)(2,1)S(1)} %constant_dynamic-update-slice_fusion), kind=kOutput, calls=%fused_computation.5 | convolution fusion | flops 566722560 | bytes 4153344 | tf_op jit(solution)/shard_map/dot_general | solution.py:67
  (53 shorter events, 2.0 us)
Async XLA Ops:
  0.6 13.2 %collective-permute-start.1 = (bf16[768,2560]{1,0:T(8,128)(2,1)}, bf16[768,2560]{1,0:T(8,128)(2,1)}, u32[]{:S(2)}, u32[]{:S(2)}) collective-permute-start(bf16[768,2560]{1,0:T(8,128)(2,1)} %param.15), channel_id=1, source_target_pairs={{0,64},{64,0},{1,65},{65,1},{2,66},{66,2},{3,67},{67,3},{4,68},{68... | collective-permute-start | bytes 11796488 | tf_op jit(solution)/shard_map/ppermute | solution.py:40
  8.2 5.6 %collective-permute-start = (bf16[4,2,144,768]{3,2,1,0:T(8,128)(2,1)}, bf16[4,2,144,768]{3,2,1,0:T(8,128)(2,1)S(1)}, u32[]{:S(2)}, u32[]{:S(2)}) collective-permute-start(bf16[4,2,144,768]{3,2,1,0:T(8,128)(2,1)} %get-tuple-element.13), channel_id=1, source_target_pairs={{0,64},{64,0},{1,65},{65,1},{2,66},{66,2},{3,67},{67,3},{4,68},{68... | collective-permute-start | bytes 5308424 | tf_op jit(solution)/shard_map/ppermute | solution.py:40
  18.7 3.5 %copy-start.1 = (bf16[4,2,144,768]{3,2,1,0:T(8,128)(2,1)S(1)}, bf16[4,2,144,768]{3,2,1,0:T(8,128)(2,1)}, u32[]{:S(2)}) copy-start(bf16[4,2,144,768]{3,2,1,0:T(8,128)(2,1)} %get-tuple-element.12) | copy-start | bytes 5308420
  19.4 21.9 %collective-permute-start.2 = (f16[4,72,1536]{2,1,0:T(8,128)(2,1)S(1)}, f16[4,72,1536]{2,1,0:T(8,128)(2,1)S(1)}, u32[]{:S(2)}, u32[]{:S(2)}) collective-permute-start(f16[4,72,1536]{2,1,0:T(8,128)(2,1)S(1)} %get-tuple-element.24), channel_id=1, source_target_pairs={{0,3},{1,0},{2,1},{3,2},{4,7},{5,4},{6,5},{7,6},{8,11},{9,8},{10,9... | collective-permute-start | bytes 2654216 | tf_op jit(solution)/shard_map/ppermute | solution.py:28
  22.2 22.5 %collective-permute-start.3 = (f16[4,72,1536]{2,1,0:T(8,128)(2,1)S(1)}, f16[4,72,1536]{2,1,0:T(8,128)(2,1)S(1)}, u32[]{:S(2)}, u32[]{:S(2)}) collective-permute-start(f16[4,72,1536]{2,1,0:T(8,128)(2,1)S(1)} %get-tuple-element.25), channel_id=1, source_target_pairs={{0,1},{1,2},{2,3},{3,0},{4,5},{5,6},{6,7},{7,4},{8,9},{9,10},{10,1... | collective-permute-start | bytes 2654216 | tf_op jit(solution)/shard_map/ppermute | solution.py:28
  29.8 18.6 %collective-permute-start.10 = (f16[4,72,1024]{2,1,0:T(8,128)(2,1)S(1)}, f16[4,72,1024]{2,1,0:T(8,128)(2,1)S(1)}, u32[]{:S(2)}, u32[]{:S(2)}) collective-permute-start(f16[4,72,1024]{2,1,0:T(8,128)(2,1)S(1)} %get-tuple-element.28), channel_id=1, source_target_pairs={{0,32},{32,128},{128,160},{160,0},{1,33},{33,129},{129,161},{161,1... | collective-permute-start | bytes 1769480 | tf_op jit(solution)/shard_map/ppermute | solution.py:32
  31.2 18.7 %collective-permute-start.9 = (f16[4,72,1024]{2,1,0:T(8,128)(2,1)S(1)}, f16[4,72,1024]{2,1,0:T(8,128)(2,1)S(1)}, u32[]{:S(2)}, u32[]{:S(2)}) collective-permute-start(f16[4,72,1024]{2,1,0:T(8,128)(2,1)S(1)} %get-tuple-element.29), channel_id=1, source_target_pairs={{0,160},{32,0},{128,32},{160,128},{1,161},{33,1},{129,33},{161,129... | collective-permute-start | bytes 1769480 | tf_op jit(solution)/shard_map/ppermute | solution.py:32
  45.0 12.2 %collective-permute-start.4 = (f16[2,72,1536]{2,1,0:T(8,128)(2,1)S(1)}, f16[2,72,1536]{2,1,0:T(8,128)(2,1)S(1)}, u32[]{:S(2)}, u32[]{:S(2)}) collective-permute-start(f16[2,72,1536]{2,1,0:T(8,128)(2,1)S(1)} %get-tuple-element.26), channel_id=1, source_target_pairs={{0,1},{1,2},{2,3},{3,0},{4,5},{5,6},{6,7},{7,4},{8,9},{9,10},{10,1... | collective-permute-start | bytes 1327112 | tf_op jit(solution)/shard_map/ppermute | solution.py:28
  45.1 12.1 %collective-permute-start.5 = (f16[2,72,1536]{2,1,0:T(8,128)(2,1)S(1)}, f16[2,72,1536]{2,1,0:T(8,128)(2,1)S(1)}, u32[]{:S(2)}, u32[]{:S(2)}) collective-permute-start(f16[2,72,1536]{2,1,0:T(8,128)(2,1)S(1)} %get-tuple-element.27), channel_id=1, source_target_pairs={{0,3},{1,0},{2,1},{3,2},{4,7},{5,4},{6,5},{7,6},{8,11},{9,8},{10,9... | collective-permute-start | bytes 1327112 | tf_op jit(solution)/shard_map/ppermute | solution.py:28
  48.4 13.0 %collective-permute-start.11 = (f16[2,72,1024]{2,1,0:T(8,128)(2,1)S(1)}, f16[2,72,1024]{2,1,0:T(8,128)(2,1)S(1)}, u32[]{:S(2)}, u32[]{:S(2)}) collective-permute-start(f16[2,72,1024]{2,1,0:T(8,128)(2,1)S(1)} %fusion.13), channel_id=1, source_target_pairs={{0,32},{32,128},{128,160},{160,0},{1,33},{33,129},{129,161},{161,1... | collective-permute-start | bytes 884744 | tf_op jit(solution)/shard_map/ppermute | solution.py:32
  49.9 11.6 %collective-permute-start.12 = (f16[2,72,1024]{2,1,0:T(8,128)(2,1)S(1)}, f16[2,72,1024]{2,1,0:T(8,128)(2,1)S(1)}, u32[]{:S(2)}, u32[]{:S(2)}) collective-permute-start(f16[2,72,1024]{2,1,0:T(8,128)(2,1)S(1)} %fusion.12), channel_id=1, source_target_pairs={{0,160},{32,0},{128,32},{160,128},{1,161},{33,1},{129,33},{161,129... | collective-permute-start | bytes 884744 | tf_op jit(solution)/shard_map/ppermute | solution.py:32
  58.7 9.5 %collective-permute-start.6 = (f16[1,72,1536]{2,1,0:T(8,128)(2,1)}, f16[1,72,1536]{2,1,0:T(8,128)(2,1)S(1)}, u32[]{:S(2)}, u32[]{:S(2)}) collective-permute-start(f16[1,72,1536]{2,1,0:T(8,128)(2,1)} %get-tuple-element.32), channel_id=1, source_target_pairs={{0,128},{32,160},{128,0},{160,32},{1,129},{33,161},{129,1},{161,33... | collective-permute-start | bytes 663560 | tf_op jit(solution)/shard_map/ppermute | solution.py:32
  59.1 10.4 %collective-permute-start.7 = (f16[1,72,1536]{2,1,0:T(8,128)(2,1)S(1)}, f16[1,72,1536]{2,1,0:T(8,128)(2,1)S(1)}, u32[]{:S(2)}, u32[]{:S(2)}) collective-permute-start(f16[1,72,1536]{2,1,0:T(8,128)(2,1)S(1)} %get-tuple-element.31), channel_id=1, source_target_pairs={{0,32},{32,128},{128,160},{160,0},{1,33},{33,129},{129,161},{161,1... | collective-permute-start | bytes 663560 | tf_op jit(solution)/shard_map/ppermute | solution.py:32
  61.2 8.2 %collective-permute-start.8 = (f16[1,72,1536]{2,1,0:T(8,128)(2,1)S(1)}, f16[1,72,1536]{2,1,0:T(8,128)(2,1)S(1)}, u32[]{:S(2)}, u32[]{:S(2)}) collective-permute-start(f16[1,72,1536]{2,1,0:T(8,128)(2,1)S(1)} %get-tuple-element.30), channel_id=1, source_target_pairs={{0,160},{32,0},{128,32},{160,128},{1,161},{33,1},{129,33},{161,129... | collective-permute-start | bytes 663560 | tf_op jit(solution)/shard_map/ppermute | solution.py:32
  63.0 12.7 %all-to-all-start = ((f16[4,72,1024]{2,1,0:T(8,128)(2,1)}), f16[4,72,1024]{2,1,0:T(8,128)(2,1)S(1)}, u32[]{:S(2)}, u32[]{:S(2)}) async-start(f16[4,72,1024]{2,1,0:T(8,128)(2,1)} %fusion.8), calls=%async_computation | async-start | bytes 1179648 | tf_op jit(solution)/shard_map/all_to_all | solution.py:201
  67.2 29.3 %copy-start = (f32[6,2560]{1,0:T(8,128)S(1)}, f32[6,2560]{1,0:T(8,128)}, u32[]{:S(2)}) copy-start(f32[6,2560]{1,0:T(8,128)} %param.18) | copy-start | bytes 184324
  100.5 15.1 %all-to-all-start.2 = ((bf16[8,180,128]{2,1,0:T(8,128)(2,1)}), bf16[8,180,128]{2,1,0:T(8,128)(2,1)S(1)}, u32[]{:S(2)}, u32[]{:S(2)}) async-start(bf16[8,180,128]{2,1,0:T(8,128)(2,1)} %broadcast_in_dim.5), calls=%async_computation.2 | async-start | bytes 753664 | tf_op jit(solution)/shard_map/all_to_all | solution.py:213
  116.0 11.5 %collective-permute-start.17 = (bf16[72,2560]{1,0:T(8,128)(2,1)S(1)}, bf16[72,2560]{1,0:T(8,128)(2,1)S(1)}, u32[]{:S(2)}, u32[]{:S(2)}) collective-permute-start(bf16[72,2560]{1,0:T(8,128)(2,1)S(1)} %reshape.81), channel_id=1, source_target_pairs={{0,3},{1,0},{2,1},{3,2},{4,7},{5,4},{6,5},{7,6},{8,11},{9,8},{10,9... | collective-permute-start | bytes 1105928 | tf_op jit(solution)/shard_map/ppermute | solution.py:28
  117.3 12.7 %collective-permute-start.14 = (bf16[72,2560]{1,0:T(8,128)(2,1)S(1)}, bf16[72,2560]{1,0:T(8,128)(2,1)S(1)}, u32[]{:S(2)}, u32[]{:S(2)}) collective-permute-start(bf16[72,2560]{1,0:T(8,128)(2,1)S(1)} %reshape.81), channel_id=1, source_target_pairs={{0,1},{1,2},{2,3},{3,0},{4,5},{5,6},{6,7},{7,4},{8,9},{9,10},{10,1... | collective-permute-start | bytes 1105928 | tf_op jit(solution)/shard_map/ppermute | solution.py:28
  118.1 12.0 %collective-permute-start.13 = (bf16[72,2560]{1,0:T(8,128)(2,1)S(1)}, bf16[72,2560]{1,0:T(8,128)(2,1)S(1)}, u32[]{:S(2)}, u32[]{:S(2)}) collective-permute-start(bf16[72,2560]{1,0:T(8,128)(2,1)S(1)} %reshape.81), channel_id=1, source_target_pairs={{0,32},{32,0},{1,33},{33,1},{2,34},{34,2},{3,35},{35,3},{4,36},{36... | collective-permute-start | bytes 1105928 | tf_op jit(solution)/shard_map/ppermute | solution.py:36
  127.6 9.0 %collective-permute-start.18 = (bf16[40,2560]{1,0:T(8,128)(2,1)S(1)}, bf16[40,2560]{1,0:T(8,128)(2,1)S(1)}, u32[]{:S(2)}, u32[]{:S(2)}) collective-permute-start(bf16[40,2560]{1,0:T(8,128)(2,1)S(1)} %slice.86), channel_id=1, source_target_pairs={{0,3},{1,0},{2,1},{3,2},{4,7},{5,4},{6,5},{7,6},{8,11},{9,8},{10,9... | collective-permute-start | bytes 614408 | tf_op jit(solution)/shard_map/ppermute | solution.py:28
  130.0 6.6 %collective-permute-start.16 = (bf16[32,2560]{1,0:T(8,128)(2,1)S(1)}, bf16[32,2560]{1,0:T(8,128)(2,1)S(1)}, u32[]{:S(2)}, u32[]{:S(2)}) collective-permute-start(bf16[32,2560]{1,0:T(8,128)(2,1)S(1)} %slice.85), channel_id=1, source_target_pairs={{0,1},{1,2},{2,3},{3,0},{4,5},{5,6},{6,7},{7,4},{8,9},{9,10},{10,1... | collective-permute-start | bytes 491528 | tf_op jit(solution)/shard_map/ppermute | solution.py:28
  130.1 10.5 %collective-permute-start.15 = (bf16[72,2560]{1,0:T(8,128)(2,1)S(1)}, bf16[72,2560]{1,0:T(8,128)(2,1)S(1)}, u32[]{:S(2)}, u32[]{:S(2)}) collective-permute-start(bf16[72,2560]{1,0:T(8,128)(2,1)S(1)} %collective-permute-done.13), channel_id=1, source_target_pairs={{0,1},{1,2},{2,3},{3,0},{4,5},{5,6},{6,7},{7,4},{8,9},{9,10},{10,1... | collective-permute-start | bytes 1105928 | tf_op jit(solution)/shard_map/ppermute | solution.py:28
  130.3 14.0 %collective-permute-start.20 = (bf16[72,2560]{1,0:T(8,128)(2,1)S(1)}, bf16[72,2560]{1,0:T(8,128)(2,1)S(1)}, u32[]{:S(2)}, u32[]{:S(2)}) collective-permute-start(bf16[72,2560]{1,0:T(8,128)(2,1)S(1)} %collective-permute-done.13), channel_id=1, source_target_pairs={{0,3},{1,0},{2,1},{3,2},{4,7},{5,4},{6,5},{7,6},{8,11},{9,8},{10,9... | collective-permute-start | bytes 1105928 | tf_op jit(solution)/shard_map/ppermute | solution.py:28
  136.7 7.6 %collective-permute-start.19 = (bf16[72,2560]{1,0:T(8,128)(2,1)S(1)}, bf16[72,2560]{1,0:T(8,128)(2,1)S(1)}, u32[]{:S(2)}, u32[]{:S(2)}) collective-permute-start(bf16[72,2560]{1,0:T(8,128)(2,1)S(1)} %pad_maximum_fusion.1), channel_id=1, source_target_pairs={{0,32},{32,0},{1,33},{33,1},{2,34},{34,2},{3,35},{35,3},{4,36},{36... | collective-permute-start | bytes 1105928 | tf_op jit(solution)/shard_map/ppermute | solution.py:36

commit v6 on v5

--- a/solution.py
+++ b/solution.py
@@ -30,6 +30,14 @@
 
 def y_ring(v, d):
     return lax.ppermute(v, ("yh", "yl"), [(i, (i + d) % NY) for i in range(NY)])
+
+
+def z_ring(v, d):
+    return lax.ppermute(v, "z", [(i, (i + d) % NZ) for i in range(NZ)])
+
+
+def z_swap(v):
+    return lax.ppermute(v, "z", [(i, i ^ 1) for i in range(NZ)])
 
 
 def y_swap(v):
@@ -138,6 +146,7 @@
     group = NZ * rows
     core = lax.axis_index("core")
     x = lax.axis_index("x")
+    z = lax.axis_index("z")
     yh, yl = lax.axis_index("yh"), lax.axis_index("yl")
     y = yh * 2 + yl
 
@@ -198,9 +207,10 @@
     last_b = [after(chunks_a, v) for v in last_b]
     two_a = send(chunks_a, 1)
     one_b = summed(total_b, 1, *first_b, *last_b)[:, None]
-    two_b = lax.all_to_all(one_b[:, 0].astype(F16), "x", 0, 0)
+    two_b = send(cut(one_b, 0), 0)
     two_a = gathered(one_a, 1, two_a)[0].astype(F16)
-    two_b = after([two_a], two_b).astype(F32).sum(axis=0).astype(F16)
+    two_b = [after([two_a], v) for v in two_b]
+    two_b = gathered(one_b, 0, two_b)[0].astype(F16)
     two = [two_a, two_b]
     last = jnp.concatenate(two, axis=1).reshape(NZ, rows * width // 128, 128)
     last = lax.all_to_all(last, "z", 0, 0)
@@ -209,9 +219,9 @@
     moment_s, second_s, weight_s = adamw(grad[:sr], master_shared, moment_shared, second_shared)
     moment_r, second_r, weight_r = adamw(grad[sr:], master_routed, moment_routed, second_routed)
 
-    weight = jnp.concatenate([weight_s, weight_r], axis=0).reshape(1, rows * width // 128, 128)
-    weight = lax.all_to_all(jnp.broadcast_to(weight, (NZ,) + weight.shape[1:]), "z", 0, 0)
-    mine = weight.reshape(group, width)
+    weight = jnp.concatenate([weight_s, weight_r], axis=0).reshape(rows * width // 128, 128)
+    mine = jnp.concatenate([weight] + [z_ring(weight, d) for d in (2, 4, 6)], axis=0)
+    mine = jnp.concatenate([mine, z_swap(mine)], axis=0).reshape(group, width)
     part = group // 32 * 16
     mine_plus, mine_minus = x_ring(mine, 1), x_ring(mine, 3)
     other = y_swap(mine)
@@ -219,22 +229,30 @@
     other_plus, other_minus = x_ring(other, 1), x_ring(other, 3)
     mine_two = jnp.concatenate(two, axis=0)
     other_two = y_swap(mine_two)
-    full = jnp.concatenate(
-        [mine, other, mine_plus, other_plus, mine_two, other_two, mine_minus, other_minus], axis=0
-    )
-
-    def settled(count, low):
+    early = jnp.concatenate([mine, mine_plus, mine_minus, other, mine_two], axis=0)
+    late = [other_plus, other_minus, other_two]
+    slot = jnp.array([0, 1, 4, 2, 3, 5, 7, 6], jnp.int32)
+
+    def wanted(count, low):
         n = 2 * NZ * NX * count
         r = lax.iota(jnp.int32, n)
         back = (x - (r // count) % NX) % NX
         zz = (r // (count * NX)) % NZ
         flip = (r // (count * NX * NZ)) ^ yl
-        want = ((back * 2 + flip) * NZ + zz) * rows + low + r % count
-        want = lax.optimization_barrier(want)
-        take = (want[:, None] == lax.broadcasted_iota(jnp.int32, (n, full.shape[0]), 1)).astype(BF)
-        return dot(lax.optimization_barrier(take), full).astype(BF)
-
-    shared, routed = settled(sr, 0), settled(rr, sr)
+        odd = (zz ^ z) & 1
+        steps = ((z ^ odd) - zz) % NZ // 2
+        block = slot[flip * NX + back]
+        want = (block * NZ + odd * (NZ // 2) + steps) * rows + low + r % count
+        return lax.optimization_barrier(want)
+
+    def take(want, start, full):
+        q = lax.broadcasted_iota(jnp.int32, (want.shape[0], full.shape[0]), 1) + start
+        return dot(lax.optimization_barrier((want[:, None] == q).astype(BF)), full)
+
+    wants = [wanted(sr, 0), wanted(rr, sr)]
+    firsts = [take(want, 0, early) for want in wants]
+    late = jnp.concatenate([after(firsts, v) for v in late], axis=0)
+    shared, routed = ((f + take(want, early.shape[0], late)).astype(BF) for f, want in zip(firsts, wants))
     return (moment_s, second_s, moment_r, second_r, shared, routed)
 
 

time: 152 us -> 148 us (0.974); the launches traced: 149 us -> 147 us
  blocking collectives: 20 us -> 0 us
  starting transfers between devices: 33.3 us -> 48.1 us
  waiting for transfers between devices: 54.8 us -> 59.6 us
  other arithmetic: 8.69 us -> 5.67 us
    all_to_all x1 -> x0, blocking collectives: 20 us -> none  [local(): last = lax.all_to_all(last, 'z', 0, 0)]
    ppermute x0 -> x4, waiting for transfers between devices: none -> 10 us  [the longest x3 5.01 us: z_ring(): return lax.ppermute(v, 'z', [(i, (i + d) % NZ) for i in range(NZ)])]
    ppermute x10 -> x13, starting transfers between devices: 14.1 us -> 23.6 us  [x_ring(): return lax.ppermute(v, 'x', [(i, (i + d) % NX) for i in range(NX)])]
    all_to_all x2 -> x1, waiting for transfers between devices: 17.4 us -> 11.8 us  [local(): last = lax.all_to_all(last, 'z', 0, 0)]
    ppermute x0 -> x4, starting transfers between devices: none -> 4.94 us  [the longest x3 4.41 us: z_ring(): return lax.ppermute(v, 'z', [(i, (i + d) % NZ) for i in range(NZ)])]
    ppermute x10 -> x13, waiting for transfers between devices: 31.5 us -> 33.7 us  [x_ring(): return lax.ppermute(v, 'x', [(i, (i + d) % NX) for i in range(NX)])]
    convert_element_type x2, other arithmetic: 3.15 us -> 1.41 us  [adamw(): return (new_moment, new_second, new_master.astype(BF))]
    all_to_all x2 -> x1, starting transfers between devices: 7.67 us -> 8.47 us  [local(): last = lax.all_to_all(last, 'z', 0, 0)]
  transfers between devices with their start and end apart: 23 -> 29, of which waited for: 11 -> 14; matrix products, arithmetic and copies ran while one was open for 11% -> 12% of each run, Pallas kernels for 5% -> 5%
where the time goes in v6:
time: 148 us; the launch traced here: 147 us
  waiting for transfers between devices  59.6 us (40%)
  starting transfers between devices  48.1 us (32%)
  matrix products  22.1 us (15%)
  Pallas kernels  6.78 us (5%)
  other arithmetic  5.67 us (4%)
  local copies, waits for them, and re-layouts  2.97 us (2%)
  between operations  1.8 us (1%)
    ppermute x13, waiting for transfers between devices, x_ring(): return lax.ppermute(v, 'x', [(i, (i + d) % NX) for i in range(NX)])  33.7 us
    ppermute x13, starting transfers between devices, x_ring(): return lax.ppermute(v, 'x', [(i, (i + d) % NX) for i in range(NX)])  23.6 us
    dot_general x8, matrix products, dot(): return jnp.dot(a, b, preferred_element_type=F32)  22.1 us
    all_to_all x1, waiting for transfers between devices, local(): last = lax.all_to_all(last, 'z', 0, 0)  11.8 us
    all_to_all x1, starting transfers between devices, local(): last = lax.all_to_all(last, 'z', 0, 0)  8.47 us
    ppermute x7, starting transfers between devices, y_ring(): return lax.ppermute(v, ('yh', 'yl'), [(i, (i + d) % NY) for i in range(NY)])  7.12 us
    pallas_call x1, Pallas kernels, ordered(): pl.pallas_call(order_kernel, grid_spec=pltpu.PrefetchScalarGridSpec(num_s...  6.78 us
    ppermute x3, waiting for transfers between devices, z_ring(): return lax.ppermute(v, 'z', [(i, (i + d) % NZ) for i in range(NZ)])  5.01 us
  transfers between devices with their start and end apart: 29, of which 14 were waited for; matrix products, arithmetic and copies ran while one was open for 12% of the time, Pallas kernels for 5%

profile of v6, /device:TPU:16, one launch (start us, length us, event | category | flops | bytes accessed | tf_op | source)
XLA Modules:
  0.0 147.0 jit_solution(13587026771723787047)
XLA Ops:
  1.4 6.8 %shard_map.181 = (bf16[4,2,144,768]{3,2,1,0:T(8,128)(2,1)}, bf16[4,2,144,768]{3,2,1,0:T(8,128)(2,1)}) custom-call(s32[1]{0:T(128)} %bitcast.core_ref, s32[1]{0:T(128)S(6)} %copy.36.count_ref, s32[1,96]{1,0:T(1,128)} %bitcast.80, bf16[768,1536]{1,0:T(8,128)(2,1)} %shared_ref.1, bf16[96,768]{1,0:T(8,128)(2,1)} %routed_ref.1, ...), custom_call_target="tpu_custom_call" | custom-call | flops 2717908992 | bytes 8847360 | tf_op jit(solution)/shard_map/pallas_call | solution.py:109
  8.9 5.1 %fusion.5 = f32[1152,1536]{1,0:T(8,128)S(1)} fusion(bf16[1152,768]{1,0:T(8,128)(2,1)} %bitcast.81, bf16[768,2560]{1,0:T(8,128)(2,1)} %param.16), kind=kOutput, calls=%fused_computation.9 | convolution fusion | flops 2717908992 | bytes 11206656 | tf_op jit(solution)/shard_map/dot_general | solution.py:75
  14.0 4.9 %fusion.1 = f16[1152,1536]{1,0:T(8,128)(2,1)S(1)} fusion(f32[1152,1536]{1,0:T(8,128)S(1)} %fusion.5, bf16[1152,768]{1,0:T(8,128)(2,1)S(1)} %bitcast.78, bf16[768,2560]{1,0:T(8,128)(2,1)} %collective-permute-done.1), kind=kOutput, calls=%fused_computation.2 | convolution fusion | flops 2723217408 | bytes 14745600 | tf_op jit(solution)/shard_map/dot_general | solution.py:75
  18.9 0.7 bitcast_select_fusion.1
  19.6 2.8 %collective-permute-start.2 = (f16[4,72,1536]{2,1,0:T(8,128)(2,1)S(1)}, f16[4,72,1536]{2,1,0:T(8,128)(2,1)S(1)}, u32[]{:S(2)}, u32[]{:S(2)}) collective-permute-start(f16[4,72,1536]{2,1,0:T(8,128)(2,1)S(1)} %get-tuple-element.34), channel_id=1, source_target_pairs={{0,3},{1,0},{2,1},{3,2},{4,7},{5,4},{6,5},{7,6},{8,11},{9,8},{10,9... | collective-permute-start | bytes 2654216 | tf_op jit(solution)/shard_map/ppermute | solution.py:28
  22.4 3.4 %fusion.8 = f32[1152,1024]{1,0:T(8,128)S(1)} fusion(bf16[1152,768]{1,0:T(8,128)(2,1)S(1)} %bitcast.82, bf16[768,2560]{1,0:T(8,128)(2,1)} %param.16), kind=kOutput, calls=%fused_computation.13 | convolution fusion | flops 1811939328 | bytes 8060928 | tf_op jit(solution)/shard_map/dot_general | solution.py:75
  25.9 3.5 %multiply_convert_fusion = f16[1152,1024]{1,0:T(8,128)(2,1)S(1)} fusion(f32[1152,1024]{1,0:T(8,128)S(1)} %fusion.8, bf16[1152,768]{1,0:T(8,128)(2,1)S(1)} %bitcast.79, bf16[768,2560]{1,0:T(8,128)(2,1)} %collective-permute-done.1), kind=kOutput, calls=%fused_computation.3 | convolution fusion | flops 1815478272 | bytes 10420224 | tf_op jit(solution)/shard_map/dot_general | solution.py:75
  29.4 0.6 bitcast_select_fusion.2
  30.0 1.4 collective-permute-start.10
  31.4 0.7 collective-permute-start.9
  32.4 9.1 %collective-permute-done.2 = f16[4,72,1536]{2,1,0:T(8,128)(2,1)S(1)} collective-permute-done((f16[4,72,1536]{2,1,0:T(8,128)(2,1)S(1)}, f16[4,72,1536]{2,1,0:T(8,128)(2,1)S(1)}, u32[]{:S(2)}, u32[]{:S(2)}) %collective-permute-start.2) | collective-permute-done | bytes 884768 | tf_op jit(solution)/shard_map/ppermute | solution.py:28
  41.5 3.4 %collective-permute-done.3 = f16[4,72,1536]{2,1,0:T(8,128)(2,1)S(1)} collective-permute-done((f16[4,72,1536]{2,1,0:T(8,128)(2,1)S(1)}, f16[4,72,1536]{2,1,0:T(8,128)(2,1)S(1)}, u32[]{:S(2)}, u32[]{:S(2)}) %collective-permute-start.3) | collective-permute-done | bytes 884768 | tf_op jit(solution)/shard_map/ppermute | solution.py:28
  45.3 3.2 %collective-permute-start.5 = (f16[2,72,1536]{2,1,0:T(8,128)(2,1)S(1)}, f16[2,72,1536]{2,1,0:T(8,128)(2,1)S(1)}, u32[]{:S(2)}, u32[]{:S(2)}) collective-permute-start(f16[2,72,1536]{2,1,0:T(8,128)(2,1)S(1)} %get-tuple-element.37), channel_id=1, source_target_pairs={{0,3},{1,0},{2,1},{3,2},{4,7},{5,4},{6,5},{7,6},{8,11},{9,8},{10,9... | collective-permute-start | bytes 1327112 | tf_op jit(solution)/shard_map/ppermute | solution.py:28
  48.6 1.4 collective-permute-start.11
  50.1 0.8 collective-permute-start.12
  50.9 6.5 %collective-permute-done.4 = f16[2,72,1536]{2,1,0:T(8,128)(2,1)S(1)} collective-permute-done((f16[2,72,1536]{2,1,0:T(8,128)(2,1)S(1)}, f16[2,72,1536]{2,1,0:T(8,128)(2,1)S(1)}, u32[]{:S(2)}, u32[]{:S(2)}) %collective-permute-start.4) | collective-permute-done | bytes 442400 | tf_op jit(solution)/shard_map/ppermute | solution.py:28
  58.5 2.2 %collective-permute-start.7 = (f16[1,72,1536]{2,1,0:T(8,128)(2,1)S(1)}, f16[1,72,1536]{2,1,0:T(8,128)(2,1)S(1)}, u32[]{:S(2)}, u32[]{:S(2)}) collective-permute-start(f16[1,72,1536]{2,1,0:T(8,128)(2,1)S(1)} %get-tuple-element.43), channel_id=1, source_target_pairs={{0,32},{32,128},{128,160},{160,0},{1,33},{33,129},{129,161},{161,1... | collective-permute-start | bytes 663560 | tf_op jit(solution)/shard_map/ppermute | solution.py:32
  61.0 0.6 convert_add_fusion.1
  61.6 1.5 %collective-permute-start.13 = (f16[1,72,1024]{2,1,0:T(8,128)(2,1)S(1)}, f16[1,72,1024]{2,1,0:T(8,128)(2,1)S(1)}, u32[]{:S(2)}, u32[]{:S(2)}) collective-permute-start(f16[1,72,1024]{2,1,0:T(8,128)(2,1)S(1)} %get-tuple-element.45), channel_id=1, source_target_pairs={{0,2},{1,3},{2,0},{3,1},{4,6},{5,7},{6,4},{7,5},{8,10},{9,11},{10,... | collective-permute-start | bytes 442376 | tf_op jit(solution)/shard_map/ppermute | solution.py:28
  63.2 2.3 %collective-permute-start.14 = (f16[1,72,1024]{2,1,0:T(8,128)(2,1)S(1)}, f16[1,72,1024]{2,1,0:T(8,128)(2,1)S(1)}, u32[]{:S(2)}, u32[]{:S(2)}) collective-permute-start(f16[1,72,1024]{2,1,0:T(8,128)(2,1)S(1)} %get-tuple-element.47), channel_id=1, source_target_pairs={{0,1},{1,2},{2,3},{3,0},{4,5},{5,6},{6,7},{7,4},{8,9},{9,10},{10,1... | collective-permute-start | bytes 442376 | tf_op jit(solution)/shard_map/ppermute | solution.py:28
  65.5 1.9 %collective-permute-done.6 = f16[1,72,1536]{2,1,0:T(8,128)(2,1)S(1)} collective-permute-done((f16[1,72,1536]{2,1,0:T(8,128)(2,1)S(1)}, f16[1,72,1536]{2,1,0:T(8,128)(2,1)S(1)}, u32[]{:S(2)}, u32[]{:S(2)}) %collective-permute-start.6) | collective-permute-done | bytes 221216 | tf_op jit(solution)/shard_map/ppermute | solution.py:32
  67.5 2.7 %collective-permute-start.15 = (f16[1,72,1024]{2,1,0:T(8,128)(2,1)S(1)}, f16[1,72,1024]{2,1,0:T(8,128)(2,1)S(1)}, u32[]{:S(2)}, u32[]{:S(2)}) collective-permute-start(f16[1,72,1024]{2,1,0:T(8,128)(2,1)S(1)} %get-tuple-element.46), channel_id=1, source_target_pairs={{0,3},{1,0},{2,1},{3,2},{4,7},{5,4},{6,5},{7,6},{8,11},{9,8},{10,9... | collective-permute-start | bytes 442376 | tf_op jit(solution)/shard_map/ppermute | solution.py:28
  70.3 2.5 %collective-permute-done.15 = f16[1,72,1024]{2,1,0:T(8,128)(2,1)S(1)} collective-permute-done((f16[1,72,1024]{2,1,0:T(8,128)(2,1)S(1)}, f16[1,72,1024]{2,1,0:T(8,128)(2,1)S(1)}, u32[]{:S(2)}, u32[]{:S(2)}) %collective-permute-start.15) | collective-permute-done | bytes 147488 | tf_op jit(solution)/shard_map/ppermute | solution.py:28
  73.1 1.2 reshape.386
  74.3 8.5 %all-to-all-start = ((f16[8,180,128]{2,1,0:T(8,128)(2,1)}), f16[8,180,128]{2,1,0:T(8,128)(2,1)S(1)}, u32[]{:S(2)}, u32[]{:S(2)}) async-start(f16[8,180,128]{2,1,0:T(8,128)(2,1)} %reshape.386), calls=%async_computation | async-start | bytes 753664 | tf_op jit(solution)/shard_map/all_to_all | solution.py:216
  83.1 11.8 %all-to-all-done = f16[8,180,128]{2,1,0:T(8,128)(2,1)S(1)} async-done(((f16[8,180,128]{2,1,0:T(8,128)(2,1)}), f16[8,180,128]{2,1,0:T(8,128)(2,1)S(1)}, u32[]{:S(2)}, u32[]{:S(2)}) %all-to-all-start) | async-done | bytes 368672 | tf_op jit(solution)/shard_map/all_to_all | solution.py:216
  95.0 0.7 subtract_convert_fusion
  95.8 0.7 subtract_convert_fusion.1
  97.0 1.8 %collective-permute-start.17 = (bf16[180,128]{1,0:T(8,128)(2,1)S(1)}, bf16[180,128]{1,0:T(8,128)(2,1)S(1)}, u32[]{:S(2)}, u32[]{:S(2)}) collective-permute-start(bf16[180,128]{1,0:T(8,128)(2,1)S(1)} %reshape.387), channel_id=1, source_target_pairs={{0,16},{4,20},{8,24},{12,28},{16,0},{20,4},{24,8},{28,12},{1,17},{... | collective-permute-start | bytes 138248 | tf_op jit(solution)/shard_map/ppermute | solution.py:36
  98.8 2.2 %collective-permute-start.18 = (bf16[180,128]{1,0:T(8,128)(2,1)S(1)}, bf16[180,128]{1,0:T(8,128)(2,1)S(1)}, u32[]{:S(2)}, u32[]{:S(2)}) collective-permute-start(bf16[180,128]{1,0:T(8,128)(2,1)S(1)} %reshape.387), channel_id=1, source_target_pairs={{0,24},{4,28},{8,0},{12,4},{16,8},{20,12},{24,16},{28,20},{1,25},{... | collective-permute-start | bytes 138248 | tf_op jit(solution)/shard_map/ppermute | solution.py:36
  101.1 1.8 %collective-permute-done.16 = bf16[180,128]{1,0:T(8,128)(2,1)S(1)} collective-permute-done((bf16[180,128]{1,0:T(8,128)(2,1)S(1)}, bf16[180,128]{1,0:T(8,128)(2,1)S(1)}, u32[]{:S(2)}, u32[]{:S(2)}) %collective-permute-start.16) | collective-permute-done | bytes 46112 | tf_op jit(solution)/shard_map/ppermute | solution.py:36
  102.9 2.2 %collective-permute-done.17 = bf16[180,128]{1,0:T(8,128)(2,1)S(1)} collective-permute-done((bf16[180,128]{1,0:T(8,128)(2,1)S(1)}, bf16[180,128]{1,0:T(8,128)(2,1)S(1)}, u32[]{:S(2)}, u32[]{:S(2)}) %collective-permute-start.17) | collective-permute-done | bytes 46112 | tf_op jit(solution)/shard_map/ppermute | solution.py:36
  105.1 1.0 collective-permute-done.18
  106.7 5.0 %collective-permute-done.19 = bf16[720,128]{1,0:T(8,128)(2,1)S(1)} collective-permute-done((bf16[720,128]{1,0:T(8,128)(2,1)S(1)}, bf16[720,128]{1,0:T(8,128)(2,1)S(1)}, u32[]{:S(2)}, u32[]{:S(2)}) %collective-permute-start.19) | collective-permute-done | bytes 184352 | tf_op jit(solution)/shard_map/ppermute | solution.py:40
  111.7 0.6 concatenate.34
  112.8 3.9 %collective-permute-start.21 = (bf16[72,2560]{1,0:T(8,128)(2,1)S(1)}, bf16[72,2560]{1,0:T(8,128)(2,1)S(1)}, u32[]{:S(2)}, u32[]{:S(2)}) collective-permute-start(bf16[72,2560]{1,0:T(8,128)(2,1)S(1)} %reshape.388), channel_id=1, source_target_pairs={{0,3},{1,0},{2,1},{3,2},{4,7},{5,4},{6,5},{7,6},{8,11},{9,8},{10,9... | collective-permute-start | bytes 1105928 | tf_op jit(solution)/shard_map/ppermute | solution.py:28
  116.7 1.6 %collective-permute-start.22 = (bf16[72,2560]{1,0:T(8,128)(2,1)S(1)}, bf16[72,2560]{1,0:T(8,128)(2,1)S(1)}, u32[]{:S(2)}, u32[]{:S(2)}) collective-permute-start(bf16[72,2560]{1,0:T(8,128)(2,1)S(1)} %reshape.388), channel_id=1, source_target_pairs={{0,32},{32,0},{1,33},{33,1},{2,34},{34,2},{3,35},{35,3},{4,36},{36... | collective-permute-start | bytes 1105928 | tf_op jit(solution)/shard_map/ppermute | solution.py:44
  118.4 7.1 %collective-permute-done.21 = bf16[72,2560]{1,0:T(8,128)(2,1)S(1)} collective-permute-done((bf16[72,2560]{1,0:T(8,128)(2,1)S(1)}, bf16[72,2560]{1,0:T(8,128)(2,1)S(1)}, u32[]{:S(2)}, u32[]{:S(2)}) %collective-permute-start.21) | collective-permute-done | bytes 368672 | tf_op jit(solution)/shard_map/ppermute | solution.py:28
  125.6 3.8 %collective-permute-start.24 = (bf16[40,2560]{1,0:T(8,128)(2,1)S(1)}, bf16[40,2560]{1,0:T(8,128)(2,1)S(1)}, u32[]{:S(2)}, u32[]{:S(2)}) collective-permute-start(bf16[40,2560]{1,0:T(8,128)(2,1)S(1)} %slice.105), channel_id=1, source_target_pairs={{0,3},{1,0},{2,1},{3,2},{4,7},{5,4},{6,5},{7,6},{8,11},{9,8},{10,9... | collective-permute-start | bytes 614408 | tf_op jit(solution)/shard_map/ppermute | solution.py:28
  129.5 3.2 %collective-permute-start.26 = (bf16[72,2560]{1,0:T(8,128)(2,1)S(1)}, bf16[72,2560]{1,0:T(8,128)(2,1)S(1)}, u32[]{:S(2)}, u32[]{:S(2)}) collective-permute-start(bf16[72,2560]{1,0:T(8,128)(2,1)S(1)} %collective-permute-done.22), channel_id=1, source_target_pairs={{0,3},{1,0},{2,1},{3,2},{4,7},{5,4},{6,5},{7,6},{8,11},{9,8},{10,9... | collective-permute-start | bytes 1105928 | tf_op jit(solution)/shard_map/ppermute | solution.py:28
  132.8 3.2 %collective-permute-done.23 = bf16[32,2560]{1,0:T(8,128)(2,1)S(1)} collective-permute-done((bf16[32,2560]{1,0:T(8,128)(2,1)S(1)}, bf16[32,2560]{1,0:T(8,128)(2,1)S(1)}, u32[]{:S(2)}, u32[]{:S(2)}) %collective-permute-start.23) | collective-permute-done | bytes 163872 | tf_op jit(solution)/shard_map/ppermute | solution.py:28
  136.0 1.7 %collective-permute-start.27 = (bf16[72,2560]{1,0:T(8,128)(2,1)S(1)}, bf16[72,2560]{1,0:T(8,128)(2,1)S(1)}, u32[]{:S(2)}, u32[]{:S(2)}) collective-permute-start(bf16[72,2560]{1,0:T(8,128)(2,1)S(1)} %pad_maximum_fusion.1), channel_id=1, source_target_pairs={{0,32},{32,0},{1,33},{33,1},{2,34},{34,2},{3,35},{35,3},{4,36},{36... | collective-permute-start | bytes 1105928 | tf_op jit(solution)/shard_map/ppermute | solution.py:44
  137.7 1.2 fusion.55
  138.9 0.7 fusion.56
  139.6 1.8 %collective-permute-done.25 = bf16[72,2560]{1,0:T(8,128)(2,1)S(1)} collective-permute-done((bf16[72,2560]{1,0:T(8,128)(2,1)S(1)}, bf16[72,2560]{1,0:T(8,128)(2,1)S(1)}, u32[]{:S(2)}, u32[]{:S(2)}) %collective-permute-start.25) | collective-permute-done | bytes 368672 | tf_op jit(solution)/shard_map/ppermute | solution.py:28
  141.5 2.2 %collective-permute-done.27 = bf16[72,2560]{1,0:T(8,128)(2,1)S(1)} collective-permute-done((bf16[72,2560]{1,0:T(8,128)(2,1)S(1)}, bf16[72,2560]{1,0:T(8,128)(2,1)S(1)}, u32[]{:S(2)}, u32[]{:S(2)}) %collective-permute-start.27) | collective-permute-done | bytes 368672 | tf_op jit(solution)/shard_map/ppermute | solution.py:44
  143.7 1.4 fusion.3
  145.0 1.9 %fusion.2 = bf16[384,2560]{1,0:T(8,128)(2,1)} fusion(f32[384,2560]{1,0:T(8,128)S(1)} %fusion.55, bf16[384,216]{1,0:T(8,128)(2,1)S(1)} %compare_convert_fusion, bf16[216,2560]{1,0:T(8,128)(2,1)S(1)} %constant_dynamic-update-slice_fusion.6), kind=kOutput, calls=%fused_computation.5 | convolution fusion | flops 426639360 | bytes 7170048 | tf_op jit(solution)/shard_map/dot_general | solution.py:75
  (84 shorter events, 5.9 us)
Async XLA Ops:
  0.6 13.4 %collective-permute-start.1 = (bf16[768,2560]{1,0:T(8,128)(2,1)}, bf16[768,2560]{1,0:T(8,128)(2,1)}, u32[]{:S(2)}, u32[]{:S(2)}) collective-permute-start(bf16[768,2560]{1,0:T(8,128)(2,1)} %param.16), channel_id=1, source_target_pairs={{0,64},{64,0},{1,65},{65,1},{2,66},{66,2},{3,67},{67,3},{4,68},{68... | collective-permute-start | bytes 11796488 | tf_op jit(solution)/shard_map/ppermute | solution.py:48
  8.2 5.9 %collective-permute-start = (bf16[4,2,144,768]{3,2,1,0:T(8,128)(2,1)}, bf16[4,2,144,768]{3,2,1,0:T(8,128)(2,1)S(1)}, u32[]{:S(2)}, u32[]{:S(2)}) collective-permute-start(bf16[4,2,144,768]{3,2,1,0:T(8,128)(2,1)} %get-tuple-element.18), channel_id=1, source_target_pairs={{0,64},{64,0},{1,65},{65,1},{2,66},{66,2},{3,67},{67,3},{4,68},{68... | collective-permute-start | bytes 5308424 | tf_op jit(solution)/shard_map/ppermute | solution.py:48
  18.9 3.5 %copy-start.6 = (bf16[4,2,144,768]{3,2,1,0:T(8,128)(2,1)S(1)}, bf16[4,2,144,768]{3,2,1,0:T(8,128)(2,1)}, u32[]{:S(2)}) copy-start(bf16[4,2,144,768]{3,2,1,0:T(8,128)(2,1)} %get-tuple-element.17) | copy-start | bytes 5308420
  19.6 21.9 %collective-permute-start.2 = (f16[4,72,1536]{2,1,0:T(8,128)(2,1)S(1)}, f16[4,72,1536]{2,1,0:T(8,128)(2,1)S(1)}, u32[]{:S(2)}, u32[]{:S(2)}) collective-permute-start(f16[4,72,1536]{2,1,0:T(8,128)(2,1)S(1)} %get-tuple-element.34), channel_id=1, source_target_pairs={{0,3},{1,0},{2,1},{3,2},{4,7},{5,4},{6,5},{7,6},{8,11},{9,8},{10,9... | collective-permute-start | bytes 2654216 | tf_op jit(solution)/shard_map/ppermute | solution.py:28
  22.4 22.5 %collective-permute-start.3 = (f16[4,72,1536]{2,1,0:T(8,128)(2,1)S(1)}, f16[4,72,1536]{2,1,0:T(8,128)(2,1)S(1)}, u32[]{:S(2)}, u32[]{:S(2)}) collective-permute-start(f16[4,72,1536]{2,1,0:T(8,128)(2,1)S(1)} %get-tuple-element.35), channel_id=1, source_target_pairs={{0,1},{1,2},{2,3},{3,0},{4,5},{5,6},{6,7},{7,4},{8,9},{9,10},{10,1... | collective-permute-start | bytes 2654216 | tf_op jit(solution)/shard_map/ppermute | solution.py:28
  30.0 18.5 %collective-permute-start.10 = (f16[4,72,1024]{2,1,0:T(8,128)(2,1)S(1)}, f16[4,72,1024]{2,1,0:T(8,128)(2,1)S(1)}, u32[]{:S(2)}, u32[]{:S(2)}) collective-permute-start(f16[4,72,1024]{2,1,0:T(8,128)(2,1)S(1)} %get-tuple-element.38), channel_id=1, source_target_pairs={{0,32},{32,128},{128,160},{160,0},{1,33},{33,129},{129,161},{161,1... | collective-permute-start | bytes 1769480 | tf_op jit(solution)/shard_map/ppermute | solution.py:32
  31.4 18.6 %collective-permute-start.9 = (f16[4,72,1024]{2,1,0:T(8,128)(2,1)S(1)}, f16[4,72,1024]{2,1,0:T(8,128)(2,1)S(1)}, u32[]{:S(2)}, u32[]{:S(2)}) collective-permute-start(f16[4,72,1024]{2,1,0:T(8,128)(2,1)S(1)} %get-tuple-element.39), channel_id=1, source_target_pairs={{0,160},{32,0},{128,32},{160,128},{1,161},{33,1},{129,33},{161,129... | collective-permute-start | bytes 1769480 | tf_op jit(solution)/shard_map/ppermute | solution.py:32
  45.2 12.2 %collective-permute-start.4 = (f16[2,72,1536]{2,1,0:T(8,128)(2,1)S(1)}, f16[2,72,1536]{2,1,0:T(8,128)(2,1)S(1)}, u32[]{:S(2)}, u32[]{:S(2)}) collective-permute-start(f16[2,72,1536]{2,1,0:T(8,128)(2,1)S(1)} %get-tuple-element.36), channel_id=1, source_target_pairs={{0,1},{1,2},{2,3},{3,0},{4,5},{5,6},{6,7},{7,4},{8,9},{9,10},{10,1... | collective-permute-start | bytes 1327112 | tf_op jit(solution)/shard_map/ppermute | solution.py:28
  45.3 12.1 %collective-permute-start.5 = (f16[2,72,1536]{2,1,0:T(8,128)(2,1)S(1)}, f16[2,72,1536]{2,1,0:T(8,128)(2,1)S(1)}, u32[]{:S(2)}, u32[]{:S(2)}) collective-permute-start(f16[2,72,1536]{2,1,0:T(8,128)(2,1)S(1)} %get-tuple-element.37), channel_id=1, source_target_pairs={{0,3},{1,0},{2,1},{3,2},{4,7},{5,4},{6,5},{7,6},{8,11},{9,8},{10,9... | collective-permute-start | bytes 1327112 | tf_op jit(solution)/shard_map/ppermute | solution.py:28
  48.6 12.3 %collective-permute-start.11 = (f16[2,72,1024]{2,1,0:T(8,128)(2,1)S(1)}, f16[2,72,1024]{2,1,0:T(8,128)(2,1)S(1)}, u32[]{:S(2)}, u32[]{:S(2)}) collective-permute-start(f16[2,72,1024]{2,1,0:T(8,128)(2,1)S(1)} %fusion.13), channel_id=1, source_target_pairs={{0,32},{32,128},{128,160},{160,0},{1,33},{33,129},{129,161},{161,1... | collective-permute-start | bytes 884744 | tf_op jit(solution)/shard_map/ppermute | solution.py:32
  50.1 10.9 %collective-permute-start.12 = (f16[2,72,1024]{2,1,0:T(8,128)(2,1)S(1)}, f16[2,72,1024]{2,1,0:T(8,128)(2,1)S(1)}, u32[]{:S(2)}, u32[]{:S(2)}) collective-permute-start(f16[2,72,1024]{2,1,0:T(8,128)(2,1)S(1)} %fusion.12), channel_id=1, source_target_pairs={{0,160},{32,0},{128,32},{160,128},{1,161},{33,1},{129,33},{161,129... | collective-permute-start | bytes 884744 | tf_op jit(solution)/shard_map/ppermute | solution.py:32
  58.1 9.4 %collective-permute-start.6 = (f16[1,72,1536]{2,1,0:T(8,128)(2,1)S(1)}, f16[1,72,1536]{2,1,0:T(8,128)(2,1)S(1)}, u32[]{:S(2)}, u32[]{:S(2)}) collective-permute-start(f16[1,72,1536]{2,1,0:T(8,128)(2,1)S(1)} %get-tuple-element.44), channel_id=1, source_target_pairs={{0,128},{32,160},{128,0},{160,32},{1,129},{33,161},{129,1},{161,33... | collective-permute-start | bytes 663560 | tf_op jit(solution)/shard_map/ppermute | solution.py:32
  58.5 11.6 %collective-permute-start.7 = (f16[1,72,1536]{2,1,0:T(8,128)(2,1)S(1)}, f16[1,72,1536]{2,1,0:T(8,128)(2,1)S(1)}, u32[]{:S(2)}, u32[]{:S(2)}) collective-permute-start(f16[1,72,1536]{2,1,0:T(8,128)(2,1)S(1)} %get-tuple-element.43), channel_id=1, source_target_pairs={{0,32},{32,128},{128,160},{160,0},{1,33},{33,129},{129,161},{161,1... | collective-permute-start | bytes 663560 | tf_op jit(solution)/shard_map/ppermute | solution.py:32
  60.7 9.4 %collective-permute-start.8 = (f16[1,72,1536]{2,1,0:T(8,128)(2,1)S(1)}, f16[1,72,1536]{2,1,0:T(8,128)(2,1)S(1)}, u32[]{:S(2)}, u32[]{:S(2)}) collective-permute-start(f16[1,72,1536]{2,1,0:T(8,128)(2,1)S(1)} %get-tuple-element.42), channel_id=1, source_target_pairs={{0,160},{32,0},{128,32},{160,128},{1,161},{33,1},{129,33},{161,129... | collective-permute-start | bytes 663560 | tf_op jit(solution)/shard_map/ppermute | solution.py:32
  61.6 8.7 %collective-permute-start.13 = (f16[1,72,1024]{2,1,0:T(8,128)(2,1)S(1)}, f16[1,72,1024]{2,1,0:T(8,128)(2,1)S(1)}, u32[]{:S(2)}, u32[]{:S(2)}) collective-permute-start(f16[1,72,1024]{2,1,0:T(8,128)(2,1)S(1)} %get-tuple-element.45), channel_id=1, source_target_pairs={{0,2},{1,3},{2,0},{3,1},{4,6},{5,7},{6,4},{7,5},{8,10},{9,11},{10,... | collective-permute-start | bytes 442376 | tf_op jit(solution)/shard_map/ppermute | solution.py:28
  63.2 7.1 %collective-permute-start.14 = (f16[1,72,1024]{2,1,0:T(8,128)(2,1)S(1)}, f16[1,72,1024]{2,1,0:T(8,128)(2,1)S(1)}, u32[]{:S(2)}, u32[]{:S(2)}) collective-permute-start(f16[1,72,1024]{2,1,0:T(8,128)(2,1)S(1)} %get-tuple-element.47), channel_id=1, source_target_pairs={{0,1},{1,2},{2,3},{3,0},{4,5},{5,6},{6,7},{7,4},{8,9},{9,10},{10,1... | collective-permute-start | bytes 442376 | tf_op jit(solution)/shard_map/ppermute | solution.py:28
  67.5 5.3 %collective-permute-start.15 = (f16[1,72,1024]{2,1,0:T(8,128)(2,1)S(1)}, f16[1,72,1024]{2,1,0:T(8,128)(2,1)S(1)}, u32[]{:S(2)}, u32[]{:S(2)}) collective-permute-start(f16[1,72,1024]{2,1,0:T(8,128)(2,1)S(1)} %get-tuple-element.46), channel_id=1, source_target_pairs={{0,3},{1,0},{2,1},{3,2},{4,7},{5,4},{6,5},{7,6},{8,11},{9,8},{10,9... | collective-permute-start | bytes 442376 | tf_op jit(solution)/shard_map/ppermute | solution.py:28
  72.9 22.1 %copy-start = (f32[6,2560]{1,0:T(8,128)S(1)}, f32[6,2560]{1,0:T(8,128)}, u32[]{:S(2)}) copy-start(f32[6,2560]{1,0:T(8,128)} %param.19) | copy-start | bytes 184324
  73.0 22.1 %copy-start.1 = (f32[6,2560]{1,0:T(8,128)S(1)}, f32[6,2560]{1,0:T(8,128)}, u32[]{:S(2)}) copy-start(f32[6,2560]{1,0:T(8,128)} %param.21) | copy-start | bytes 184324
  73.0 22.1 %copy-start.2 = (f32[6,2560]{1,0:T(8,128)S(1)}, f32[6,2560]{1,0:T(8,128)}, u32[]{:S(2)}) copy-start(f32[6,2560]{1,0:T(8,128)} %param.20) | copy-start | bytes 184324
  73.1 22.7 %copy-start.3 = (f32[3,2560]{1,0:T(4,128)S(1)}, f32[3,2560]{1,0:T(4,128)}, u32[]{:S(2)}) copy-start(f32[3,2560]{1,0:T(4,128)} %param.22) | copy-start | bytes 92164
  73.1 22.7 %copy-start.4 = (f32[3,2560]{1,0:T(4,128)S(1)}, f32[3,2560]{1,0:T(4,128)}, u32[]{:S(2)}) copy-start(f32[3,2560]{1,0:T(4,128)} %param.24) | copy-start | bytes 92164
  73.1 22.7 %copy-start.5 = (f32[3,2560]{1,0:T(4,128)S(1)}, f32[3,2560]{1,0:T(4,128)}, u32[]{:S(2)}) copy-start(f32[3,2560]{1,0:T(4,128)} %param.23) | copy-start | bytes 92164
  74.3 20.5 %all-to-all-start = ((f16[8,180,128]{2,1,0:T(8,128)(2,1)}), f16[8,180,128]{2,1,0:T(8,128)(2,1)S(1)}, u32[]{:S(2)}, u32[]{:S(2)}) async-start(f16[8,180,128]{2,1,0:T(8,128)(2,1)} %reshape.386), calls=%async_computation | async-start | bytes 753664 | tf_op jit(solution)/shard_map/all_to_all | solution.py:216
  96.6 6.3 %collective-permute-start.16 = (bf16[180,128]{1,0:T(8,128)(2,1)S(1)}, bf16[180,128]{1,0:T(8,128)(2,1)S(1)}, u32[]{:S(2)}, u32[]{:S(2)}) collective-permute-start(bf16[180,128]{1,0:T(8,128)(2,1)S(1)} %reshape.387), channel_id=1, source_target_pairs={{0,8},{4,12},{8,16},{12,20},{16,24},{20,28},{24,0},{28,4},{1,9},{5... | collective-permute-start | bytes 138248 | tf_op jit(solution)/shard_map/ppermute | solution.py:36
  97.0 8.1 %collective-permute-start.17 = (bf16[180,128]{1,0:T(8,128)(2,1)S(1)}, bf16[180,128]{1,0:T(8,128)(2,1)S(1)}, u32[]{:S(2)}, u32[]{:S(2)}) collective-permute-start(bf16[180,128]{1,0:T(8,128)(2,1)S(1)} %reshape.387), channel_id=1, source_target_pairs={{0,16},{4,20},{8,24},{12,28},{16,0},{20,4},{24,8},{28,12},{1,17},{... | collective-permute-start | bytes 138248 | tf_op jit(solution)/shard_map/ppermute | solution.py:36
  98.8 7.2 %collective-permute-start.18 = (bf16[180,128]{1,0:T(8,128)(2,1)S(1)}, bf16[180,128]{1,0:T(8,128)(2,1)S(1)}, u32[]{:S(2)}, u32[]{:S(2)}) collective-permute-start(bf16[180,128]{1,0:T(8,128)(2,1)S(1)} %reshape.387), channel_id=1, source_target_pairs={{0,24},{4,28},{8,0},{12,4},{16,8},{20,12},{24,16},{28,20},{1,25},{... | collective-permute-start | bytes 138248 | tf_op jit(solution)/shard_map/ppermute | solution.py:36
  106.1 5.6 %collective-permute-start.19 = (bf16[720,128]{1,0:T(8,128)(2,1)S(1)}, bf16[720,128]{1,0:T(8,128)(2,1)S(1)}, u32[]{:S(2)}, u32[]{:S(2)}) collective-permute-start(bf16[720,128]{1,0:T(8,128)(2,1)S(1)} %pad_maximum_fusion.2), channel_id=1, source_target_pairs={{0,4},{4,0},{8,12},{12,8},{16,20},{20,16},{24,28},{28,24},{1,5},{5... | collective-permute-start | bytes 552968 | tf_op jit(solution)/shard_map/ppermute | solution.py:40
  112.8 12.7 %collective-permute-start.21 = (bf16[72,2560]{1,0:T(8,128)(2,1)S(1)}, bf16[72,2560]{1,0:T(8,128)(2,1)S(1)}, u32[]{:S(2)}, u32[]{:S(2)}) collective-permute-start(bf16[72,2560]{1,0:T(8,128)(2,1)S(1)} %reshape.388), channel_id=1, source_target_pairs={{0,3},{1,0},{2,1},{3,2},{4,7},{5,4},{6,5},{7,6},{8,11},{9,8},{10,9... | collective-permute-start | bytes 1105928 | tf_op jit(solution)/shard_map/ppermute | solution.py:28
  116.7 12.7 %collective-permute-start.20 = (bf16[72,2560]{1,0:T(8,128)(2,1)S(1)}, bf16[72,2560]{1,0:T(8,128)(2,1)S(1)}, u32[]{:S(2)}, u32[]{:S(2)}) collective-permute-start(bf16[72,2560]{1,0:T(8,128)(2,1)S(1)} %reshape.388), channel_id=1, source_target_pairs={{0,1},{1,2},{2,3},{3,0},{4,5},{5,6},{6,7},{7,4},{8,9},{9,10},{10,1... | collective-permute-start | bytes 1105928 | tf_op jit(solution)/shard_map/ppermute | solution.py:28
  116.7 12.8 %collective-permute-start.22 = (bf16[72,2560]{1,0:T(8,128)(2,1)S(1)}, bf16[72,2560]{1,0:T(8,128)(2,1)S(1)}, u32[]{:S(2)}, u32[]{:S(2)}) collective-permute-start(bf16[72,2560]{1,0:T(8,128)(2,1)S(1)} %reshape.388), channel_id=1, source_target_pairs={{0,32},{32,0},{1,33},{33,1},{2,34},{34,2},{3,35},{35,3},{4,36},{36... | collective-permute-start | bytes 1105928 | tf_op jit(solution)/shard_map/ppermute | solution.py:44
  125.6 10.4 %collective-permute-start.24 = (bf16[40,2560]{1,0:T(8,128)(2,1)S(1)}, bf16[40,2560]{1,0:T(8,128)(2,1)S(1)}, u32[]{:S(2)}, u32[]{:S(2)}) collective-permute-start(bf16[40,2560]{1,0:T(8,128)(2,1)S(1)} %slice.105), channel_id=1, source_target_pairs={{0,3},{1,0},{2,1},{3,2},{4,7},{5,4},{6,5},{7,6},{8,11},{9,8},{10,9... | collective-permute-start | bytes 614408 | tf_op jit(solution)/shard_map/ppermute | solution.py:28
  129.4 6.6 %collective-permute-start.23 = (bf16[32,2560]{1,0:T(8,128)(2,1)S(1)}, bf16[32,2560]{1,0:T(8,128)(2,1)S(1)}, u32[]{:S(2)}, u32[]{:S(2)}) collective-permute-start(bf16[32,2560]{1,0:T(8,128)(2,1)S(1)} %slice.104), channel_id=1, source_target_pairs={{0,1},{1,2},{2,3},{3,0},{4,5},{5,6},{6,7},{7,4},{8,9},{9,10},{10,1... | collective-permute-start | bytes 491528 | tf_op jit(solution)/shard_map/ppermute | solution.py:28
  129.5 12.0 %collective-permute-start.26 = (bf16[72,2560]{1,0:T(8,128)(2,1)S(1)}, bf16[72,2560]{1,0:T(8,128)(2,1)S(1)}, u32[]{:S(2)}, u32[]{:S(2)}) collective-permute-start(bf16[72,2560]{1,0:T(8,128)(2,1)S(1)} %collective-permute-done.22), channel_id=1, source_target_pairs={{0,3},{1,0},{2,1},{3,2},{4,7},{5,4},{6,5},{7,6},{8,11},{9,8},{10,9... | collective-permute-start | bytes 1105928 | tf_op jit(solution)/shard_map/ppermute | solution.py:28
  132.7 8.7 %collective-permute-start.25 = (bf16[72,2560]{1,0:T(8,128)(2,1)S(1)}, bf16[72,2560]{1,0:T(8,128)(2,1)S(1)}, u32[]{:S(2)}, u32[]{:S(2)}) collective-permute-start(bf16[72,2560]{1,0:T(8,128)(2,1)S(1)} %collective-permute-done.22), channel_id=1, source_target_pairs={{0,1},{1,2},{2,3},{3,0},{4,5},{5,6},{6,7},{7,4},{8,9},{9,10},{10,1... | collective-permute-start | bytes 1105928 | tf_op jit(solution)/shard_map/ppermute | solution.py:28
  136.0 7.6 %collective-permute-start.27 = (bf16[72,2560]{1,0:T(8,128)(2,1)S(1)}, bf16[72,2560]{1,0:T(8,128)(2,1)S(1)}, u32[]{:S(2)}, u32[]{:S(2)}) collective-permute-start(bf16[72,2560]{1,0:T(8,128)(2,1)S(1)} %pad_maximum_fusion.1), channel_id=1, source_target_pairs={{0,32},{32,0},{1,33},{33,1},{2,34},{34,2},{3,35},{35,3},{4,36},{36... | collective-permute-start | bytes 1105928 | tf_op jit(solution)/shard_map/ppermute | solution.py:44

commit v7 on v6

--- a/solution.py
+++ b/solution.py
@@ -30,14 +30,6 @@
 
 def y_ring(v, d):
     return lax.ppermute(v, ("yh", "yl"), [(i, (i + d) % NY) for i in range(NY)])
-
-
-def z_ring(v, d):
-    return lax.ppermute(v, "z", [(i, (i + d) % NZ) for i in range(NZ)])
-
-
-def z_swap(v):
-    return lax.ppermute(v, "z", [(i, i ^ 1) for i in range(NZ)])
 
 
 def y_swap(v):
@@ -146,12 +138,11 @@
     group = NZ * rows
     core = lax.axis_index("core")
     x = lax.axis_index("x")
-    z = lax.axis_index("z")
     yh, yl = lax.axis_index("yh"), lax.axis_index("yl")
     y = yh * 2 + yl
 
     shared_order, routed_order = (jnp.asarray(v) for v in row_order(sr, rr))
-    part_a = width * 3 // 5
+    part_a = width * 11 // 20
     out_far = core_swap(out_grad)
     far, near = ordered(core, slot_count, slot_token, hid_shared, hid_routed, shared_order, routed_order)
     far = core_swap(far).reshape(-1, tok)
@@ -188,7 +179,7 @@
     def relayed(total, dim, plus, minus):
         ahead = pick(total, dim, 1)[:2].astype(F32) + plus[:2].astype(F32)
         behind = pick(total, dim, 3)[2:].astype(F32) + minus[2:].astype(F32)
-        return both((ahead.astype(F16), behind.astype(F16)), dim)
+        return ahead.astype(F16), behind.astype(F16)
 
     def summed(total, dim, plus, minus, ahead, behind):
         got = jnp.where(front(plus), minus, plus).astype(F32)
@@ -201,8 +192,10 @@
     total_b = term(near, slice(part_a, width))
     first_a = both(first_a, 0)
     first_b = both(halves(total_b, 1), 1)
-    one_a = summed(total_a, 0, *first_a, *relayed(total_a, 0, *first_a))[None]
-    last_b = relayed(total_b, 1, *first_b)
+    last_a = relayed(total_a, 0, *first_a)
+    first_b = [after(last_a, v) for v in first_b]
+    one_a = summed(total_a, 0, *first_a, *both(last_a, 0))[None]
+    last_b = both(relayed(total_b, 1, *first_b), 1)
     chunks_a = cut(one_a, 1)
     last_b = [after(chunks_a, v) for v in last_b]
     two_a = send(chunks_a, 1)
@@ -219,9 +212,9 @@
     moment_s, second_s, weight_s = adamw(grad[:sr], master_shared, moment_shared, second_shared)
     moment_r, second_r, weight_r = adamw(grad[sr:], master_routed, moment_routed, second_routed)
 
-    weight = jnp.concatenate([weight_s, weight_r], axis=0).reshape(rows * width // 128, 128)
-    mine = jnp.concatenate([weight] + [z_ring(weight, d) for d in (2, 4, 6)], axis=0)
-    mine = jnp.concatenate([mine, z_swap(mine)], axis=0).reshape(group, width)
+    weight = jnp.concatenate([weight_s, weight_r], axis=0).reshape(1, rows * width // 128, 128)
+    weight = lax.all_to_all(jnp.broadcast_to(weight, (NZ,) + weight.shape[1:]), "z", 0, 0)
+    mine = weight.reshape(group, width)
     part = group // 32 * 16
     mine_plus, mine_minus = x_ring(mine, 1), x_ring(mine, 3)
     other = y_swap(mine)
@@ -239,10 +232,8 @@
         back = (x - (r // count) % NX) % NX
         zz = (r // (count * NX)) % NZ
         flip = (r // (count * NX * NZ)) ^ yl
-        odd = (zz ^ z) & 1
-        steps = ((z ^ odd) - zz) % NZ // 2
         block = slot[flip * NX + back]
-        want = (block * NZ + odd * (NZ // 2) + steps) * rows + low + r % count
+        want = (block * NZ + zz) * rows + low + r % count
         return lax.optimization_barrier(want)
 
     def take(want, start, full):

time: 148 us -> 147 us (level)
  waiting for transfers between devices: 59.6 us -> 53.4 us
  starting transfers between devices: 48.1 us -> 51.9 us
    all_to_all x0 -> x1, waiting for transfers between devices: none -> 11 us  [local(): lax.all_to_all(jnp.broadcast_to(weight, (NZ,) + weight.shape[1:]), 'z', 0...]
    ppermute x4 -> x0, waiting for transfers between devices: 10 us -> none  [the longest x3 5.01 us: z_ring(): return lax.ppermute(v, 'z', [(i, (i + d) % NZ) for i in range(NZ)])]
    ppermute x13, waiting for transfers between devices: 33.7 us -> 24.4 us  [x_ring(): return lax.ppermute(v, 'x', [(i, (i + d) % NX) for i in range(NX)])]
    ppermute x2, starting transfers between devices: 3.31 us -> 8.55 us  [y_swap(): return lax.ppermute(v, 'yl', [(0, 1), (1, 0)])]
    ppermute x4 -> x0, starting transfers between devices: 4.94 us -> none  [the longest x3 4.41 us: z_ring(): return lax.ppermute(v, 'z', [(i, (i + d) % NZ) for i in range(NZ)])]
    all_to_all x0 -> x1, starting transfers between devices: none -> 3.67 us  [local(): lax.all_to_all(jnp.broadcast_to(weight, (NZ,) + weight.shape[1:]), 'z', 0...]
  transfers between devices with their start and end apart: 29 -> 26, of which waited for: 14 -> 13; matrix products, arithmetic and copies ran while one was open for 12% -> 13% of each run, Pallas kernels for 5% -> 5%
where the time goes in v7:
time: 147 us; the launch traced here: 146 us
  waiting for transfers between devices  53.4 us (36%)
  starting transfers between devices  51.9 us (35%)
  matrix products  23.3 us (16%)
  Pallas kernels  6.8 us (5%)
  other arithmetic  5.38 us (4%)
  local copies, waits for them, and re-layouts  3.07 us (2%)
  between operations  1.72 us (1%)
    ppermute x13, waiting for transfers between devices, x_ring(): return lax.ppermute(v, 'x', [(i, (i + d) % NX) for i in range(NX)])  24.4 us
    ppermute x13, starting transfers between devices, x_ring(): return lax.ppermute(v, 'x', [(i, (i + d) % NX) for i in range(NX)])  23.4 us
    dot_general x8, matrix products, dot(): return jnp.dot(a, b, preferred_element_type=F32)  23.3 us
    all_to_all x1, waiting for transfers between devices, local(): last = lax.all_to_all(last, 'z', 0, 0)  11.6 us
    all_to_all x1, waiting for transfers between devices, local(): lax.all_to_all(jnp.broadcast_to(weight, (NZ,) + weight.shape[1:]), 'z', 0...  11 us
    ppermute x2, starting transfers between devices, y_swap(): return lax.ppermute(v, 'yl', [(0, 1), (1, 0)])  8.55 us
    all_to_all x1, starting transfers between devices, local(): last = lax.all_to_all(last, 'z', 0, 0)  8.47 us
    ppermute x7, starting transfers between devices, y_ring(): return lax.ppermute(v, ('yh', 'yl'), [(i, (i + d) % NY) for i in range(NY)])  7.3 us
  transfers between devices with their start and end apart: 26, of which 13 were waited for; matrix products, arithmetic and copies ran while one was open for 13% of the time, Pallas kernels for 5%

profile of v7, /device:TPU:16, one launch (start us, length us, event | category | flops | bytes accessed | tf_op | source)
XLA Modules:
  0.0 145.6 jit_solution(14156166059527831343)
XLA Ops:
  1.4 6.8 %shard_map.181 = (bf16[4,2,144,768]{3,2,1,0:T(8,128)(2,1)}, bf16[4,2,144,768]{3,2,1,0:T(8,128)(2,1)}) custom-call(s32[1]{0:T(128)} %bitcast.core_ref, s32[1]{0:T(128)S(6)} %copy.36.count_ref, s32[1,96]{1,0:T(1,128)} %bitcast.80, bf16[768,1536]{1,0:T(8,128)(2,1)} %shared_ref.1, bf16[96,768]{1,0:T(8,128)(2,1)} %routed_ref.1, ...), custom_call_target="tpu_custom_call" | custom-call | flops 2717908992 | bytes 8847360 | tf_op jit(solution)/shard_map/pallas_call | solution.py:101
  8.2 0.5 collective-permute-start
  8.8 5.1 %fusion.7 = f32[1152,1408]{1,0:T(8,128)S(1)} fusion(bf16[1152,768]{1,0:T(8,128)(2,1)} %bitcast.81, bf16[768,2560]{1,0:T(8,128)(2,1)} %param.16), kind=kOutput, calls=%fused_computation.11 | convolution fusion | flops 2491416576 | bytes 10420224 | tf_op jit(solution)/shard_map/dot_general | solution.py:67
  13.9 4.9 %fusion.3 = f16[1152,1408]{1,0:T(8,128)(2,1)S(1)} fusion(f32[1152,1408]{1,0:T(8,128)S(1)} %fusion.7, bf16[1152,768]{1,0:T(8,128)(2,1)S(1)} %bitcast.78, bf16[768,2560]{1,0:T(8,128)(2,1)} %collective-permute-done.1), kind=kOutput, calls=%fused_computation.5 | convolution fusion | flops 2496282624 | bytes 13664256 | tf_op jit(solution)/shard_map/dot_general | solution.py:67
  18.8 0.6 bitcast_select_fusion.1
  19.4 2.8 %collective-permute-start.2 = (f16[4,72,1408]{2,1,0:T(8,128)(2,1)S(1)}, f16[4,72,1408]{2,1,0:T(8,128)(2,1)S(1)}, u32[]{:S(2)}, u32[]{:S(2)}) collective-permute-start(f16[4,72,1408]{2,1,0:T(8,128)(2,1)S(1)} %get-tuple-element.38), channel_id=1, source_target_pairs={{0,3},{1,0},{2,1},{3,2},{4,7},{5,4},{6,5},{7,6},{8,11},{9,8},{10,9... | collective-permute-start | bytes 2433032 | tf_op jit(solution)/shard_map/ppermute | solution.py:28
  22.2 4.0 %fusion.10 = f32[1152,1152]{1,0:T(8,128)S(1)} fusion(bf16[1152,768]{1,0:T(8,128)(2,1)S(1)} %bitcast.82, bf16[768,2560]{1,0:T(8,128)(2,1)} %param.16), kind=kOutput, calls=%fused_computation.14 | convolution fusion | flops 2038431744 | bytes 8847360 | tf_op jit(solution)/shard_map/dot_general | solution.py:67
  26.2 4.1 %fusion.2 = f16[1152,1152]{1,0:T(8,128)(2,1)S(1)} fusion(f32[1152,1152]{1,0:T(8,128)S(1)} %fusion.10, bf16[1152,768]{1,0:T(8,128)(2,1)S(1)} %bitcast.79, bf16[768,2560]{1,0:T(8,128)(2,1)} %collective-permute-done.1), kind=kOutput, calls=%fused_computation.4 | convolution fusion | flops 2042413056 | bytes 11501568 | tf_op jit(solution)/shard_map/dot_general | solution.py:67
  30.3 0.5 bitcast_select_fusion.2
  30.9 1.5 %collective-permute-start.10 = (f16[4,72,1152]{2,1,0:T(8,128)(2,1)S(1)}, f16[4,72,1152]{2,1,0:T(8,128)(2,1)S(1)}, u32[]{:S(2)}, u32[]{:S(2)}) collective-permute-start(f16[4,72,1152]{2,1,0:T(8,128)(2,1)S(1)} %get-tuple-element.42), channel_id=1, source_target_pairs={{0,32},{32,128},{128,160},{160,0},{1,33},{33,129},{129,161},{161,1... | collective-permute-start | bytes 1990664 | tf_op jit(solution)/shard_map/ppermute | solution.py:32
  32.4 0.7 collective-permute-start.9
  33.4 6.3 %collective-permute-done.2 = f16[4,72,1408]{2,1,0:T(8,128)(2,1)S(1)} collective-permute-done((f16[4,72,1408]{2,1,0:T(8,128)(2,1)S(1)}, f16[4,72,1408]{2,1,0:T(8,128)(2,1)S(1)}, u32[]{:S(2)}, u32[]{:S(2)}) %collective-permute-start.2) | collective-permute-done | bytes 811040 | tf_op jit(solution)/shard_map/ppermute | solution.py:28
  39.7 3.4 %collective-permute-done.3 = f16[4,72,1408]{2,1,0:T(8,128)(2,1)S(1)} collective-permute-done((f16[4,72,1408]{2,1,0:T(8,128)(2,1)S(1)}, f16[4,72,1408]{2,1,0:T(8,128)(2,1)S(1)}, u32[]{:S(2)}, u32[]{:S(2)}) %collective-permute-start.3) | collective-permute-done | bytes 811040 | tf_op jit(solution)/shard_map/ppermute | solution.py:28
  43.5 3.2 %collective-permute-start.5 = (f16[2,72,1408]{2,1,0:T(8,128)(2,1)S(1)}, f16[2,72,1408]{2,1,0:T(8,128)(2,1)S(1)}, u32[]{:S(2)}, u32[]{:S(2)}) collective-permute-start(f16[2,72,1408]{2,1,0:T(8,128)(2,1)S(1)} %get-tuple-element.40), channel_id=1, source_target_pairs={{0,3},{1,0},{2,1},{3,2},{4,7},{5,4},{6,5},{7,6},{8,11},{9,8},{10,9... | collective-permute-start | bytes 1216520 | tf_op jit(solution)/shard_map/ppermute | solution.py:28
  46.7 1.0 collective-permute-done.10
  47.8 1.4 collective-permute-start.11
  49.3 0.8 collective-permute-start.12
  50.1 4.8 %collective-permute-done.4 = f16[2,72,1408]{2,1,0:T(8,128)(2,1)S(1)} collective-permute-done((f16[2,72,1408]{2,1,0:T(8,128)(2,1)S(1)}, f16[2,72,1408]{2,1,0:T(8,128)(2,1)S(1)}, u32[]{:S(2)}, u32[]{:S(2)}) %collective-permute-start.4) | collective-permute-done | bytes 405536 | tf_op jit(solution)/shard_map/ppermute | solution.py:28
  54.9 0.6 convert_add_fusion
  55.9 2.2 %collective-permute-start.7 = (f16[1,72,1408]{2,1,0:T(8,128)(2,1)S(1)}, f16[1,72,1408]{2,1,0:T(8,128)(2,1)S(1)}, u32[]{:S(2)}, u32[]{:S(2)}) collective-permute-start(f16[1,72,1408]{2,1,0:T(8,128)(2,1)S(1)} %get-tuple-element.47), channel_id=1, source_target_pairs={{0,32},{32,128},{128,160},{160,0},{1,33},{33,129},{129,161},{161,1... | collective-permute-start | bytes 608264 | tf_op jit(solution)/shard_map/ppermute | solution.py:32
  58.8 0.5 convert_add_fusion.1
  59.4 1.8 %collective-permute-start.13 = (f16[1,72,1152]{2,1,0:T(8,128)(2,1)S(1)}, f16[1,72,1152]{2,1,0:T(8,128)(2,1)S(1)}, u32[]{:S(2)}, u32[]{:S(2)}) collective-permute-start(f16[1,72,1152]{2,1,0:T(8,128)(2,1)S(1)} %get-tuple-element.49), channel_id=1, source_target_pairs={{0,2},{1,3},{2,0},{3,1},{4,6},{5,7},{6,4},{7,5},{8,10},{9,11},{10,... | collective-permute-start | bytes 497672 | tf_op jit(solution)/shard_map/ppermute | solution.py:28
  61.1 1.7 %collective-permute-start.14 = (f16[1,72,1152]{2,1,0:T(8,128)(2,1)S(1)}, f16[1,72,1152]{2,1,0:T(8,128)(2,1)S(1)}, u32[]{:S(2)}, u32[]{:S(2)}) collective-permute-start(f16[1,72,1152]{2,1,0:T(8,128)(2,1)S(1)} %get-tuple-element.51), channel_id=1, source_target_pairs={{0,1},{1,2},{2,3},{3,0},{4,5},{5,6},{6,7},{7,4},{8,9},{9,10},{10,1... | collective-permute-start | bytes 497672 | tf_op jit(solution)/shard_map/ppermute | solution.py:28
  62.8 1.5 %collective-permute-done.6 = f16[1,72,1408]{2,1,0:T(8,128)(2,1)S(1)} collective-permute-done((f16[1,72,1408]{2,1,0:T(8,128)(2,1)S(1)}, f16[1,72,1408]{2,1,0:T(8,128)(2,1)S(1)}, u32[]{:S(2)}, u32[]{:S(2)}) %collective-permute-start.6) | collective-permute-done | bytes 202784 | tf_op jit(solution)/shard_map/ppermute | solution.py:32
  64.3 2.6 %collective-permute-start.15 = (f16[1,72,1152]{2,1,0:T(8,128)(2,1)S(1)}, f16[1,72,1152]{2,1,0:T(8,128)(2,1)S(1)}, u32[]{:S(2)}, u32[]{:S(2)}) collective-permute-start(f16[1,72,1152]{2,1,0:T(8,128)(2,1)S(1)} %get-tuple-element.50), channel_id=1, source_target_pairs={{0,3},{1,0},{2,1},{3,2},{4,7},{5,4},{6,5},{7,6},{8,11},{9,8},{10,9... | collective-permute-start | bytes 497672 | tf_op jit(solution)/shard_map/ppermute | solution.py:28
  67.1 1.0 collective-permute-done.14
  68.1 1.7 %collective-permute-done.15 = f16[1,72,1152]{2,1,0:T(8,128)(2,1)S(1)} collective-permute-done((f16[1,72,1152]{2,1,0:T(8,128)(2,1)S(1)}, f16[1,72,1152]{2,1,0:T(8,128)(2,1)S(1)}, u32[]{:S(2)}, u32[]{:S(2)}) %collective-permute-start.15) | collective-permute-done | bytes 165920 | tf_op jit(solution)/shard_map/ppermute | solution.py:28
  70.1 1.2 reshape.385
  71.3 8.5 %all-to-all-start = ((f16[8,180,128]{2,1,0:T(8,128)(2,1)}), f16[8,180,128]{2,1,0:T(8,128)(2,1)S(1)}, u32[]{:S(2)}, u32[]{:S(2)}) async-start(f16[8,180,128]{2,1,0:T(8,128)(2,1)} %reshape.385), calls=%async_computation | async-start | bytes 753664 | tf_op jit(solution)/shard_map/all_to_all | solution.py:209
  79.9 11.6 %all-to-all-done = f16[8,180,128]{2,1,0:T(8,128)(2,1)S(1)} async-done(((f16[8,180,128]{2,1,0:T(8,128)(2,1)}), f16[8,180,128]{2,1,0:T(8,128)(2,1)S(1)}, u32[]{:S(2)}, u32[]{:S(2)}) %all-to-all-start) | async-done | bytes 368672 | tf_op jit(solution)/shard_map/all_to_all | solution.py:209
  91.6 0.7 subtract_convert_fusion
  92.4 0.7 subtract_convert_fusion.1
  93.2 0.8 broadcast_in_dim.5
  94.0 3.7 %all-to-all-start.1 = ((bf16[8,180,128]{2,1,0:T(8,128)(2,1)}), bf16[8,180,128]{2,1,0:T(8,128)(2,1)S(1)}, u32[]{:S(2)}, u32[]{:S(2)}) async-start(bf16[8,180,128]{2,1,0:T(8,128)(2,1)} %broadcast_in_dim.5), calls=%async_computation.1 | async-start | bytes 753664 | tf_op jit(solution)/shard_map/all_to_all | solution.py:216
  98.0 11.0 %all-to-all-done.1 = bf16[8,180,128]{2,1,0:T(8,128)(2,1)S(1)} async-done(((bf16[8,180,128]{2,1,0:T(8,128)(2,1)}), bf16[8,180,128]{2,1,0:T(8,128)(2,1)S(1)}, u32[]{:S(2)}, u32[]{:S(2)}) %all-to-all-start.1) | async-done | bytes 368672 | tf_op jit(solution)/shard_map/all_to_all | solution.py:216
  109.1 0.4 reshape.386
  109.5 3.8 %collective-permute-start.17 = (bf16[72,2560]{1,0:T(8,128)(2,1)S(1)}, bf16[72,2560]{1,0:T(8,128)(2,1)S(1)}, u32[]{:S(2)}, u32[]{:S(2)}) collective-permute-start(bf16[72,2560]{1,0:T(8,128)(2,1)S(1)} %reshape.386), channel_id=1, source_target_pairs={{0,3},{1,0},{2,1},{3,2},{4,7},{5,4},{6,5},{7,6},{8,11},{9,8},{10,9... | collective-permute-start | bytes 1105928 | tf_op jit(solution)/shard_map/ppermute | solution.py:28
  113.3 4.6 %collective-permute-start.18 = (bf16[72,2560]{1,0:T(8,128)(2,1)S(1)}, bf16[72,2560]{1,0:T(8,128)(2,1)S(1)}, u32[]{:S(2)}, u32[]{:S(2)}) collective-permute-start(bf16[72,2560]{1,0:T(8,128)(2,1)S(1)} %reshape.386), channel_id=1, source_target_pairs={{0,32},{32,0},{1,33},{33,1},{2,34},{34,2},{3,35},{35,3},{4,36},{36... | collective-permute-start | bytes 1105928 | tf_op jit(solution)/shard_map/ppermute | solution.py:36
  118.0 4.3 %collective-permute-done.17 = bf16[72,2560]{1,0:T(8,128)(2,1)S(1)} collective-permute-done((bf16[72,2560]{1,0:T(8,128)(2,1)S(1)}, bf16[72,2560]{1,0:T(8,128)(2,1)S(1)}, u32[]{:S(2)}, u32[]{:S(2)}) %collective-permute-start.17) | collective-permute-done | bytes 368672 | tf_op jit(solution)/shard_map/ppermute | solution.py:28
  122.3 3.8 %collective-permute-start.20 = (bf16[40,2560]{1,0:T(8,128)(2,1)S(1)}, bf16[40,2560]{1,0:T(8,128)(2,1)S(1)}, u32[]{:S(2)}, u32[]{:S(2)}) collective-permute-start(bf16[40,2560]{1,0:T(8,128)(2,1)S(1)} %slice.103), channel_id=1, source_target_pairs={{0,3},{1,0},{2,1},{3,2},{4,7},{5,4},{6,5},{7,6},{8,11},{9,8},{10,9... | collective-permute-start | bytes 614408 | tf_op jit(solution)/shard_map/ppermute | solution.py:28
  126.2 3.5 %collective-permute-start.22 = (bf16[72,2560]{1,0:T(8,128)(2,1)S(1)}, bf16[72,2560]{1,0:T(8,128)(2,1)S(1)}, u32[]{:S(2)}, u32[]{:S(2)}) collective-permute-start(bf16[72,2560]{1,0:T(8,128)(2,1)S(1)} %collective-permute-done.18), channel_id=1, source_target_pairs={{0,3},{1,0},{2,1},{3,2},{4,7},{5,4},{6,5},{7,6},{8,11},{9,8},{10,9... | collective-permute-start | bytes 1105928 | tf_op jit(solution)/shard_map/ppermute | solution.py:28
  129.8 2.9 %collective-permute-done.19 = bf16[32,2560]{1,0:T(8,128)(2,1)S(1)} collective-permute-done((bf16[32,2560]{1,0:T(8,128)(2,1)S(1)}, bf16[32,2560]{1,0:T(8,128)(2,1)S(1)}, u32[]{:S(2)}, u32[]{:S(2)}) %collective-permute-start.19) | collective-permute-done | bytes 163872 | tf_op jit(solution)/shard_map/ppermute | solution.py:28
  132.7 4.0 %collective-permute-start.23 = (bf16[72,2560]{1,0:T(8,128)(2,1)S(1)}, bf16[72,2560]{1,0:T(8,128)(2,1)S(1)}, u32[]{:S(2)}, u32[]{:S(2)}) collective-permute-start(bf16[72,2560]{1,0:T(8,128)(2,1)S(1)} %pad_maximum_fusion.1), channel_id=1, source_target_pairs={{0,32},{32,0},{1,33},{33,1},{2,34},{34,2},{3,35},{35,3},{4,36},{36... | collective-permute-start | bytes 1105928 | tf_op jit(solution)/shard_map/ppermute | solution.py:36
  136.7 1.2 fusion.52
  137.9 0.7 fusion.53
  138.7 3.5 %collective-permute-done.23 = bf16[72,2560]{1,0:T(8,128)(2,1)S(1)} collective-permute-done((bf16[72,2560]{1,0:T(8,128)(2,1)S(1)}, bf16[72,2560]{1,0:T(8,128)(2,1)S(1)}, u32[]{:S(2)}, u32[]{:S(2)}) %collective-permute-start.23) | collective-permute-done | bytes 368672 | tf_op jit(solution)/shard_map/ppermute | solution.py:36
  142.2 1.4 fusion.5
  143.6 2.0 %fusion.4 = bf16[384,2560]{1,0:T(8,128)(2,1)} fusion(f32[384,2560]{1,0:T(8,128)S(1)} %fusion.52, bf16[384,216]{1,0:T(8,128)(2,1)S(1)} %compare_convert_fusion, bf16[216,2560]{1,0:T(8,128)(2,1)S(1)} %constant_dynamic-update-slice_fusion.6), kind=kOutput, calls=%fused_computation.7 | convolution fusion | flops 426639360 | bytes 7170048 | tf_op jit(solution)/shard_map/dot_general | solution.py:67
  (77 shorter events, 3.8 us)
Async XLA Ops:
  0.6 13.2 %collective-permute-start.1 = (bf16[768,2560]{1,0:T(8,128)(2,1)}, bf16[768,2560]{1,0:T(8,128)(2,1)}, u32[]{:S(2)}, u32[]{:S(2)}) collective-permute-start(bf16[768,2560]{1,0:T(8,128)(2,1)} %param.16), channel_id=1, source_target_pairs={{0,64},{64,0},{1,65},{65,1},{2,66},{66,2},{3,67},{67,3},{4,68},{68... | collective-permute-start | bytes 11796488 | tf_op jit(solution)/shard_map/ppermute | solution.py:40
  8.2 5.7 %collective-permute-start = (bf16[4,2,144,768]{3,2,1,0:T(8,128)(2,1)}, bf16[4,2,144,768]{3,2,1,0:T(8,128)(2,1)S(1)}, u32[]{:S(2)}, u32[]{:S(2)}) collective-permute-start(bf16[4,2,144,768]{3,2,1,0:T(8,128)(2,1)} %get-tuple-element.20), channel_id=1, source_target_pairs={{0,64},{64,0},{1,65},{65,1},{2,66},{66,2},{3,67},{67,3},{4,68},{68... | collective-permute-start | bytes 5308424 | tf_op jit(solution)/shard_map/ppermute | solution.py:40
  18.7 3.5 %copy-start.6 = (bf16[4,2,144,768]{3,2,1,0:T(8,128)(2,1)S(1)}, bf16[4,2,144,768]{3,2,1,0:T(8,128)(2,1)}, u32[]{:S(2)}) copy-start(bf16[4,2,144,768]{3,2,1,0:T(8,128)(2,1)} %get-tuple-element.19) | copy-start | bytes 5308420
  19.4 20.4 %collective-permute-start.2 = (f16[4,72,1408]{2,1,0:T(8,128)(2,1)S(1)}, f16[4,72,1408]{2,1,0:T(8,128)(2,1)S(1)}, u32[]{:S(2)}, u32[]{:S(2)}) collective-permute-start(f16[4,72,1408]{2,1,0:T(8,128)(2,1)S(1)} %get-tuple-element.38), channel_id=1, source_target_pairs={{0,3},{1,0},{2,1},{3,2},{4,7},{5,4},{6,5},{7,6},{8,11},{9,8},{10,9... | collective-permute-start | bytes 2433032 | tf_op jit(solution)/shard_map/ppermute | solution.py:28
  22.2 20.9 %collective-permute-start.3 = (f16[4,72,1408]{2,1,0:T(8,128)(2,1)S(1)}, f16[4,72,1408]{2,1,0:T(8,128)(2,1)S(1)}, u32[]{:S(2)}, u32[]{:S(2)}) collective-permute-start(f16[4,72,1408]{2,1,0:T(8,128)(2,1)S(1)} %get-tuple-element.39), channel_id=1, source_target_pairs={{0,1},{1,2},{2,3},{3,0},{4,5},{5,6},{6,7},{7,4},{8,9},{9,10},{10,1... | collective-permute-start | bytes 2433032 | tf_op jit(solution)/shard_map/ppermute | solution.py:28
  30.9 16.8 %collective-permute-start.10 = (f16[4,72,1152]{2,1,0:T(8,128)(2,1)S(1)}, f16[4,72,1152]{2,1,0:T(8,128)(2,1)S(1)}, u32[]{:S(2)}, u32[]{:S(2)}) collective-permute-start(f16[4,72,1152]{2,1,0:T(8,128)(2,1)S(1)} %get-tuple-element.42), channel_id=1, source_target_pairs={{0,32},{32,128},{128,160},{160,0},{1,33},{33,129},{129,161},{161,1... | collective-permute-start | bytes 1990664 | tf_op jit(solution)/shard_map/ppermute | solution.py:32
  32.4 16.8 %collective-permute-start.9 = (f16[4,72,1152]{2,1,0:T(8,128)(2,1)S(1)}, f16[4,72,1152]{2,1,0:T(8,128)(2,1)S(1)}, u32[]{:S(2)}, u32[]{:S(2)}) collective-permute-start(f16[4,72,1152]{2,1,0:T(8,128)(2,1)S(1)} %get-tuple-element.43), channel_id=1, source_target_pairs={{0,160},{32,0},{128,32},{160,128},{1,161},{33,1},{129,33},{161,129... | collective-permute-start | bytes 1990664 | tf_op jit(solution)/shard_map/ppermute | solution.py:32
  43.4 11.4 %collective-permute-start.4 = (f16[2,72,1408]{2,1,0:T(8,128)(2,1)S(1)}, f16[2,72,1408]{2,1,0:T(8,128)(2,1)S(1)}, u32[]{:S(2)}, u32[]{:S(2)}) collective-permute-start(f16[2,72,1408]{2,1,0:T(8,128)(2,1)S(1)} %get-tuple-element.41), channel_id=1, source_target_pairs={{0,1},{1,2},{2,3},{3,0},{4,5},{5,6},{6,7},{7,4},{8,9},{9,10},{10,1... | collective-permute-start | bytes 1216520 | tf_op jit(solution)/shard_map/ppermute | solution.py:28
  43.5 11.3 %collective-permute-start.5 = (f16[2,72,1408]{2,1,0:T(8,128)(2,1)S(1)}, f16[2,72,1408]{2,1,0:T(8,128)(2,1)S(1)}, u32[]{:S(2)}, u32[]{:S(2)}) collective-permute-start(f16[2,72,1408]{2,1,0:T(8,128)(2,1)S(1)} %get-tuple-element.40), channel_id=1, source_target_pairs={{0,3},{1,0},{2,1},{3,2},{4,7},{5,4},{6,5},{7,6},{8,11},{9,8},{10,9... | collective-permute-start | bytes 1216520 | tf_op jit(solution)/shard_map/ppermute | solution.py:28
  47.8 10.6 %collective-permute-start.11 = (f16[2,72,1152]{2,1,0:T(8,128)(2,1)S(1)}, f16[2,72,1152]{2,1,0:T(8,128)(2,1)S(1)}, u32[]{:S(2)}, u32[]{:S(2)}) collective-permute-start(f16[2,72,1152]{2,1,0:T(8,128)(2,1)S(1)} %fusion.15), channel_id=1, source_target_pairs={{0,32},{32,128},{128,160},{160,0},{1,33},{33,129},{129,161},{161,1... | collective-permute-start | bytes 995336 | tf_op jit(solution)/shard_map/ppermute | solution.py:32
  49.3 9.5 %collective-permute-start.12 = (f16[2,72,1152]{2,1,0:T(8,128)(2,1)S(1)}, f16[2,72,1152]{2,1,0:T(8,128)(2,1)S(1)}, u32[]{:S(2)}, u32[]{:S(2)}) collective-permute-start(f16[2,72,1152]{2,1,0:T(8,128)(2,1)S(1)} %fusion.14), channel_id=1, source_target_pairs={{0,160},{32,0},{128,32},{160,128},{1,161},{33,1},{129,33},{161,129... | collective-permute-start | bytes 995336 | tf_op jit(solution)/shard_map/ppermute | solution.py:32
  55.5 8.8 %collective-permute-start.6 = (f16[1,72,1408]{2,1,0:T(8,128)(2,1)S(1)}, f16[1,72,1408]{2,1,0:T(8,128)(2,1)S(1)}, u32[]{:S(2)}, u32[]{:S(2)}) collective-permute-start(f16[1,72,1408]{2,1,0:T(8,128)(2,1)S(1)} %get-tuple-element.48), channel_id=1, source_target_pairs={{0,128},{32,160},{128,0},{160,32},{1,129},{33,161},{129,1},{161,33... | collective-permute-start | bytes 608264 | tf_op jit(solution)/shard_map/ppermute | solution.py:32
  55.9 11.0 %collective-permute-start.7 = (f16[1,72,1408]{2,1,0:T(8,128)(2,1)S(1)}, f16[1,72,1408]{2,1,0:T(8,128)(2,1)S(1)}, u32[]{:S(2)}, u32[]{:S(2)}) collective-permute-start(f16[1,72,1408]{2,1,0:T(8,128)(2,1)S(1)} %get-tuple-element.47), channel_id=1, source_target_pairs={{0,32},{32,128},{128,160},{160,0},{1,33},{33,129},{129,161},{161,1... | collective-permute-start | bytes 608264 | tf_op jit(solution)/shard_map/ppermute | solution.py:32
  58.1 8.8 %collective-permute-start.8 = (f16[1,72,1408]{2,1,0:T(8,128)(2,1)S(1)}, f16[1,72,1408]{2,1,0:T(8,128)(2,1)S(1)}, u32[]{:S(2)}, u32[]{:S(2)}) collective-permute-start(f16[1,72,1408]{2,1,0:T(8,128)(2,1)S(1)} %get-tuple-element.46), channel_id=1, source_target_pairs={{0,160},{32,0},{128,32},{160,128},{1,161},{33,1},{129,33},{161,129... | collective-permute-start | bytes 608264 | tf_op jit(solution)/shard_map/ppermute | solution.py:32
  59.4 7.7 %collective-permute-start.13 = (f16[1,72,1152]{2,1,0:T(8,128)(2,1)S(1)}, f16[1,72,1152]{2,1,0:T(8,128)(2,1)S(1)}, u32[]{:S(2)}, u32[]{:S(2)}) collective-permute-start(f16[1,72,1152]{2,1,0:T(8,128)(2,1)S(1)} %get-tuple-element.49), channel_id=1, source_target_pairs={{0,2},{1,3},{2,0},{3,1},{4,6},{5,7},{6,4},{7,5},{8,10},{9,11},{10,... | collective-permute-start | bytes 497672 | tf_op jit(solution)/shard_map/ppermute | solution.py:28
  61.1 6.9 %collective-permute-start.14 = (f16[1,72,1152]{2,1,0:T(8,128)(2,1)S(1)}, f16[1,72,1152]{2,1,0:T(8,128)(2,1)S(1)}, u32[]{:S(2)}, u32[]{:S(2)}) collective-permute-start(f16[1,72,1152]{2,1,0:T(8,128)(2,1)S(1)} %get-tuple-element.51), channel_id=1, source_target_pairs={{0,1},{1,2},{2,3},{3,0},{4,5},{5,6},{6,7},{7,4},{8,9},{9,10},{10,1... | collective-permute-start | bytes 497672 | tf_op jit(solution)/shard_map/ppermute | solution.py:28
  64.3 5.5 %collective-permute-start.15 = (f16[1,72,1152]{2,1,0:T(8,128)(2,1)S(1)}, f16[1,72,1152]{2,1,0:T(8,128)(2,1)S(1)}, u32[]{:S(2)}, u32[]{:S(2)}) collective-permute-start(f16[1,72,1152]{2,1,0:T(8,128)(2,1)S(1)} %get-tuple-element.50), channel_id=1, source_target_pairs={{0,3},{1,0},{2,1},{3,2},{4,7},{5,4},{6,5},{7,6},{8,11},{9,8},{10,9... | collective-permute-start | bytes 497672 | tf_op jit(solution)/shard_map/ppermute | solution.py:28
  69.9 21.7 %copy-start = (f32[6,2560]{1,0:T(8,128)S(1)}, f32[6,2560]{1,0:T(8,128)}, u32[]{:S(2)}) copy-start(f32[6,2560]{1,0:T(8,128)} %param.19) | copy-start | bytes 184324
  69.9 21.7 %copy-start.1 = (f32[6,2560]{1,0:T(8,128)S(1)}, f32[6,2560]{1,0:T(8,128)}, u32[]{:S(2)}) copy-start(f32[6,2560]{1,0:T(8,128)} %param.21) | copy-start | bytes 184324
  69.9 21.7 %copy-start.2 = (f32[6,2560]{1,0:T(8,128)S(1)}, f32[6,2560]{1,0:T(8,128)}, u32[]{:S(2)}) copy-start(f32[6,2560]{1,0:T(8,128)} %param.20) | copy-start | bytes 184324
  69.9 22.4 %copy-start.3 = (f32[3,2560]{1,0:T(4,128)S(1)}, f32[3,2560]{1,0:T(4,128)}, u32[]{:S(2)}) copy-start(f32[3,2560]{1,0:T(4,128)} %param.22) | copy-start | bytes 92164
  69.9 22.4 %copy-start.4 = (f32[3,2560]{1,0:T(4,128)S(1)}, f32[3,2560]{1,0:T(4,128)}, u32[]{:S(2)}) copy-start(f32[3,2560]{1,0:T(4,128)} %param.24) | copy-start | bytes 92164
  70.0 22.4 %copy-start.5 = (f32[3,2560]{1,0:T(4,128)S(1)}, f32[3,2560]{1,0:T(4,128)}, u32[]{:S(2)}) copy-start(f32[3,2560]{1,0:T(4,128)} %param.23) | copy-start | bytes 92164
  71.3 20.2 %all-to-all-start = ((f16[8,180,128]{2,1,0:T(8,128)(2,1)}), f16[8,180,128]{2,1,0:T(8,128)(2,1)S(1)}, u32[]{:S(2)}, u32[]{:S(2)}) async-start(f16[8,180,128]{2,1,0:T(8,128)(2,1)} %reshape.385), calls=%async_computation | async-start | bytes 753664 | tf_op jit(solution)/shard_map/all_to_all | solution.py:209
  94.0 15.1 %all-to-all-start.1 = ((bf16[8,180,128]{2,1,0:T(8,128)(2,1)}), bf16[8,180,128]{2,1,0:T(8,128)(2,1)S(1)}, u32[]{:S(2)}, u32[]{:S(2)}) async-start(bf16[8,180,128]{2,1,0:T(8,128)(2,1)} %broadcast_in_dim.5), calls=%async_computation.1 | async-start | bytes 753664 | tf_op jit(solution)/shard_map/all_to_all | solution.py:216
  109.5 12.8 %collective-permute-start.17 = (bf16[72,2560]{1,0:T(8,128)(2,1)S(1)}, bf16[72,2560]{1,0:T(8,128)(2,1)S(1)}, u32[]{:S(2)}, u32[]{:S(2)}) collective-permute-start(bf16[72,2560]{1,0:T(8,128)(2,1)S(1)} %reshape.386), channel_id=1, source_target_pairs={{0,3},{1,0},{2,1},{3,2},{4,7},{5,4},{6,5},{7,6},{8,11},{9,8},{10,9... | collective-permute-start | bytes 1105928 | tf_op jit(solution)/shard_map/ppermute | solution.py:28
  113.3 12.8 %collective-permute-start.16 = (bf16[72,2560]{1,0:T(8,128)(2,1)S(1)}, bf16[72,2560]{1,0:T(8,128)(2,1)S(1)}, u32[]{:S(2)}, u32[]{:S(2)}) collective-permute-start(bf16[72,2560]{1,0:T(8,128)(2,1)S(1)} %reshape.386), channel_id=1, source_target_pairs={{0,1},{1,2},{2,3},{3,0},{4,5},{5,6},{6,7},{7,4},{8,9},{9,10},{10,1... | collective-permute-start | bytes 1105928 | tf_op jit(solution)/shard_map/ppermute | solution.py:28
  113.3 12.9 %collective-permute-start.18 = (bf16[72,2560]{1,0:T(8,128)(2,1)S(1)}, bf16[72,2560]{1,0:T(8,128)(2,1)S(1)}, u32[]{:S(2)}, u32[]{:S(2)}) collective-permute-start(bf16[72,2560]{1,0:T(8,128)(2,1)S(1)} %reshape.386), channel_id=1, source_target_pairs={{0,32},{32,0},{1,33},{33,1},{2,34},{34,2},{3,35},{35,3},{4,36},{36... | collective-permute-start | bytes 1105928 | tf_op jit(solution)/shard_map/ppermute | solution.py:36
  122.3 10.4 %collective-permute-start.20 = (bf16[40,2560]{1,0:T(8,128)(2,1)S(1)}, bf16[40,2560]{1,0:T(8,128)(2,1)S(1)}, u32[]{:S(2)}, u32[]{:S(2)}) collective-permute-start(bf16[40,2560]{1,0:T(8,128)(2,1)S(1)} %slice.103), channel_id=1, source_target_pairs={{0,3},{1,0},{2,1},{3,2},{4,7},{5,4},{6,5},{7,6},{8,11},{9,8},{10,9... | collective-permute-start | bytes 614408 | tf_op jit(solution)/shard_map/ppermute | solution.py:28
  126.1 6.6 %collective-permute-start.19 = (bf16[32,2560]{1,0:T(8,128)(2,1)S(1)}, bf16[32,2560]{1,0:T(8,128)(2,1)S(1)}, u32[]{:S(2)}, u32[]{:S(2)}) collective-permute-start(bf16[32,2560]{1,0:T(8,128)(2,1)S(1)} %slice.102), channel_id=1, source_target_pairs={{0,1},{1,2},{2,3},{3,0},{4,5},{5,6},{6,7},{7,4},{8,9},{9,10},{10,1... | collective-permute-start | bytes 491528 | tf_op jit(solution)/shard_map/ppermute | solution.py:28
  126.2 12.5 %collective-permute-start.22 = (bf16[72,2560]{1,0:T(8,128)(2,1)S(1)}, bf16[72,2560]{1,0:T(8,128)(2,1)S(1)}, u32[]{:S(2)}, u32[]{:S(2)}) collective-permute-start(bf16[72,2560]{1,0:T(8,128)(2,1)S(1)} %collective-permute-done.18), channel_id=1, source_target_pairs={{0,3},{1,0},{2,1},{3,2},{4,7},{5,4},{6,5},{7,6},{8,11},{9,8},{10,9... | collective-permute-start | bytes 1105928 | tf_op jit(solution)/shard_map/ppermute | solution.py:28
  129.7 8.9 %collective-permute-start.21 = (bf16[72,2560]{1,0:T(8,128)(2,1)S(1)}, bf16[72,2560]{1,0:T(8,128)(2,1)S(1)}, u32[]{:S(2)}, u32[]{:S(2)}) collective-permute-start(bf16[72,2560]{1,0:T(8,128)(2,1)S(1)} %collective-permute-done.18), channel_id=1, source_target_pairs={{0,1},{1,2},{2,3},{3,0},{4,5},{5,6},{6,7},{7,4},{8,9},{9,10},{10,1... | collective-permute-start | bytes 1105928 | tf_op jit(solution)/shard_map/ppermute | solution.py:28
  132.7 9.5 %collective-permute-start.23 = (bf16[72,2560]{1,0:T(8,128)(2,1)S(1)}, bf16[72,2560]{1,0:T(8,128)(2,1)S(1)}, u32[]{:S(2)}, u32[]{:S(2)}) collective-permute-start(bf16[72,2560]{1,0:T(8,128)(2,1)S(1)} %pad_maximum_fusion.1), channel_id=1, source_target_pairs={{0,32},{32,0},{1,33},{33,1},{2,34},{34,2},{3,35},{35,3},{4,36},{36... | collective-permute-start | bytes 1105928 | tf_op jit(solution)/shard_map/ppermute | solution.py:36

commit v8 on v7

--- a/solution.py
+++ b/solution.py
@@ -228,7 +228,7 @@
 
     def wanted(count, low):
         n = 2 * NZ * NX * count
-        r = lax.iota(jnp.int32, n)
+        r = after([weight_s, weight_r], lax.iota(jnp.int32, n))
         back = (x - (r // count) % NX) % NX
         zz = (r // (count * NX)) % NZ
         flip = (r // (count * NX * NZ)) ^ yl
@@ -237,13 +237,14 @@
         return lax.optimization_barrier(want)
 
     def take(want, start, full):
-        q = lax.broadcasted_iota(jnp.int32, (want.shape[0], full.shape[0]), 1) + start
-        return dot(lax.optimization_barrier((want[:, None] == q).astype(BF)), full)
+        want = lax.optimization_barrier(want - start)
+        q = lax.broadcasted_iota(jnp.int32, (want.shape[0], full.shape[0]), 1)
+        return dot(lax.optimization_barrier((want[:, None] == q).astype(BF)), full).astype(BF)
 
     wants = [wanted(sr, 0), wanted(rr, sr)]
     firsts = [take(want, 0, early) for want in wants]
     late = jnp.concatenate([after(firsts, v) for v in late], axis=0)
-    shared, routed = ((f + take(want, early.shape[0], late)).astype(BF) for f, want in zip(firsts, wants))
+    shared, routed = (f + take(want, early.shape[0], late) for f, want in zip(firsts, wants))
     return (moment_s, second_s, moment_r, second_r, shared, routed)
 
 

time: 147 us -> 146 us (level)
  blocking collectives: 0 us -> 20 us
  waiting for transfers between devices: 53.4 us -> 42.1 us
  starting transfers between devices: 51.9 us -> 43.2 us
    all_to_all x0 -> x1, blocking collectives: none -> 20 us  [local(): last = lax.all_to_all(last, 'z', 0, 0)]
    all_to_all x1 -> x0, waiting for transfers between devices: 11.6 us -> none  [local(): last = lax.all_to_all(last, 'z', 0, 0)]
    all_to_all x1 -> x0, starting transfers between devices: 8.47 us -> none  [local(): last = lax.all_to_all(last, 'z', 0, 0)]
  transfers between devices with their start and end apart: 26 -> 25, of which waited for: 13 -> 12; matrix products, arithmetic and copies ran while one was open for 13% -> 13% of each run, Pallas kernels for 5% -> 5%
where the time goes in v8:
time: 146 us; the launch traced here: 145 us
  starting transfers between devices  43.2 us (30%)
  waiting for transfers between devices  42.1 us (29%)
  matrix products  23.1 us (16%)
  blocking collectives  20 us (14%)
  Pallas kernels  6.78 us (5%)
  other arithmetic  5.26 us (4%)
  local copies, waits for them, and re-layouts  2.34 us (2%)
  between operations  1.74 us (1%)
    ppermute x13, waiting for transfers between devices, x_ring(): return lax.ppermute(v, 'x', [(i, (i + d) % NX) for i in range(NX)])  25 us
    ppermute x13, starting transfers between devices, x_ring(): return lax.ppermute(v, 'x', [(i, (i + d) % NX) for i in range(NX)])  23.3 us
    dot_general x8, matrix products, dot(): return jnp.dot(a, b, preferred_element_type=F32)  23.1 us
    all_to_all x1, blocking collectives, local(): last = lax.all_to_all(last, 'z', 0, 0)  20 us
    all_to_all x1, waiting for transfers between devices, local(): lax.all_to_all(jnp.broadcast_to(weight, (NZ,) + weight.shape[1:]), 'z', 0...  11 us
    ppermute x2, starting transfers between devices, y_swap(): return lax.ppermute(v, 'yl', [(0, 1), (1, 0)])  8.43 us
    ppermute x7, starting transfers between devices, y_ring(): return lax.ppermute(v, ('yh', 'yl'), [(i, (i + d) % NY) for i in range(NY)])  7.3 us
    pallas_call x1, Pallas kernels, ordered(): pl.pallas_call(order_kernel, grid_spec=pltpu.PrefetchScalarGridSpec(num_s...  6.78 us
  transfers between devices with their start and end apart: 25, of which 12 were waited for; matrix products, arithmetic and copies ran while one was open for 13% of the time, Pallas kernels for 5%

profile of v8, /device:TPU:16, one launch (start us, length us, event | category | flops | bytes accessed | tf_op | source)
XLA Modules:
  0.0 144.6 jit_solution(6920763472113210003)
XLA Ops:
  1.4 6.8 %shard_map.181 = (bf16[4,2,144,768]{3,2,1,0:T(8,128)(2,1)}, bf16[4,2,144,768]{3,2,1,0:T(8,128)(2,1)}) custom-call(s32[1]{0:T(128)} %bitcast.core_ref, s32[1]{0:T(128)S(6)} %copy.36.count_ref, s32[1,96]{1,0:T(1,128)} %bitcast.78, bf16[768,1536]{1,0:T(8,128)(2,1)} %shared_ref.1, bf16[96,768]{1,0:T(8,128)(2,1)} %routed_ref.1, ...), custom_call_target="tpu_custom_call" | custom-call | flops 2717908992 | bytes 8847360 | tf_op jit(solution)/shard_map/pallas_call | solution.py:101
  8.2 0.5 collective-permute-start
  8.7 5.1 %fusion.7 = f32[1152,1408]{1,0:T(8,128)S(1)} fusion(bf16[1152,768]{1,0:T(8,128)(2,1)} %bitcast.79, bf16[768,2560]{1,0:T(8,128)(2,1)} %param.16), kind=kOutput, calls=%fused_computation.13 | convolution fusion | flops 2491416576 | bytes 10420224 | tf_op jit(solution)/shard_map/dot_general | solution.py:67
  13.8 4.8 %fusion.3 = f16[1152,1408]{1,0:T(8,128)(2,1)S(1)} fusion(f32[1152,1408]{1,0:T(8,128)S(1)} %fusion.7, bf16[1152,768]{1,0:T(8,128)(2,1)S(1)} %bitcast.76, bf16[768,2560]{1,0:T(8,128)(2,1)} %collective-permute-done.1), kind=kOutput, calls=%fused_computation.5 | convolution fusion | flops 2496282624 | bytes 13664256 | tf_op jit(solution)/shard_map/dot_general | solution.py:67
  18.6 0.6 bitcast_select_fusion.1
  19.2 2.8 %collective-permute-start.2 = (f16[4,72,1408]{2,1,0:T(8,128)(2,1)S(1)}, f16[4,72,1408]{2,1,0:T(8,128)(2,1)S(1)}, u32[]{:S(2)}, u32[]{:S(2)}) collective-permute-start(f16[4,72,1408]{2,1,0:T(8,128)(2,1)S(1)} %get-tuple-element.42), channel_id=1, source_target_pairs={{0,3},{1,0},{2,1},{3,2},{4,7},{5,4},{6,5},{7,6},{8,11},{9,8},{10,9... | collective-permute-start | bytes 2433032 | tf_op jit(solution)/shard_map/ppermute | solution.py:28
  22.0 4.0 %fusion.10 = f32[1152,1152]{1,0:T(8,128)S(1)} fusion(bf16[1152,768]{1,0:T(8,128)(2,1)S(1)} %bitcast.80, bf16[768,2560]{1,0:T(8,128)(2,1)} %param.16), kind=kOutput, calls=%fused_computation.16 | convolution fusion | flops 2038431744 | bytes 8847360 | tf_op jit(solution)/shard_map/dot_general | solution.py:67
  26.0 4.0 %fusion.2 = f16[1152,1152]{1,0:T(8,128)(2,1)S(1)} fusion(f32[1152,1152]{1,0:T(8,128)S(1)} %fusion.10, bf16[1152,768]{1,0:T(8,128)(2,1)S(1)} %bitcast.77, bf16[768,2560]{1,0:T(8,128)(2,1)} %collective-permute-done.1), kind=kOutput, calls=%fused_computation.4 | convolution fusion | flops 2042413056 | bytes 11501568 | tf_op jit(solution)/shard_map/dot_general | solution.py:67
  30.1 0.5 bitcast_select_fusion.2
  30.6 1.5 %collective-permute-start.10 = (f16[4,72,1152]{2,1,0:T(8,128)(2,1)S(1)}, f16[4,72,1152]{2,1,0:T(8,128)(2,1)S(1)}, u32[]{:S(2)}, u32[]{:S(2)}) collective-permute-start(f16[4,72,1152]{2,1,0:T(8,128)(2,1)S(1)} %get-tuple-element.46), channel_id=1, source_target_pairs={{0,32},{32,128},{128,160},{160,0},{1,33},{33,129},{129,161},{161,1... | collective-permute-start | bytes 1990664 | tf_op jit(solution)/shard_map/ppermute | solution.py:32
  32.1 0.7 collective-permute-start.9
  33.1 6.4 %collective-permute-done.2 = f16[4,72,1408]{2,1,0:T(8,128)(2,1)S(1)} collective-permute-done((f16[4,72,1408]{2,1,0:T(8,128)(2,1)S(1)}, f16[4,72,1408]{2,1,0:T(8,128)(2,1)S(1)}, u32[]{:S(2)}, u32[]{:S(2)}) %collective-permute-start.2) | collective-permute-done | bytes 811040 | tf_op jit(solution)/shard_map/ppermute | solution.py:28
  39.5 3.4 %collective-permute-done.3 = f16[4,72,1408]{2,1,0:T(8,128)(2,1)S(1)} collective-permute-done((f16[4,72,1408]{2,1,0:T(8,128)(2,1)S(1)}, f16[4,72,1408]{2,1,0:T(8,128)(2,1)S(1)}, u32[]{:S(2)}, u32[]{:S(2)}) %collective-permute-start.3) | collective-permute-done | bytes 811040 | tf_op jit(solution)/shard_map/ppermute | solution.py:28
  43.3 3.2 %collective-permute-start.5 = (f16[2,72,1408]{2,1,0:T(8,128)(2,1)S(1)}, f16[2,72,1408]{2,1,0:T(8,128)(2,1)S(1)}, u32[]{:S(2)}, u32[]{:S(2)}) collective-permute-start(f16[2,72,1408]{2,1,0:T(8,128)(2,1)S(1)} %get-tuple-element.44), channel_id=1, source_target_pairs={{0,3},{1,0},{2,1},{3,2},{4,7},{5,4},{6,5},{7,6},{8,11},{9,8},{10,9... | collective-permute-start | bytes 1216520 | tf_op jit(solution)/shard_map/ppermute | solution.py:28
  46.6 0.9 collective-permute-done.10
  47.5 1.4 collective-permute-start.11
  49.0 0.8 collective-permute-start.12
  49.8 4.9 %collective-permute-done.4 = f16[2,72,1408]{2,1,0:T(8,128)(2,1)S(1)} collective-permute-done((f16[2,72,1408]{2,1,0:T(8,128)(2,1)S(1)}, f16[2,72,1408]{2,1,0:T(8,128)(2,1)S(1)}, u32[]{:S(2)}, u32[]{:S(2)}) %collective-permute-start.4) | collective-permute-done | bytes 405536 | tf_op jit(solution)/shard_map/ppermute | solution.py:28
  54.7 0.6 convert_add_fusion
  55.3 0.4 collective-permute-start.6
  55.8 2.2 %collective-permute-start.7 = (f16[1,72,1408]{2,1,0:T(8,128)(2,1)S(1)}, f16[1,72,1408]{2,1,0:T(8,128)(2,1)S(1)}, u32[]{:S(2)}, u32[]{:S(2)}) collective-permute-start(f16[1,72,1408]{2,1,0:T(8,128)(2,1)S(1)} %get-tuple-element.51), channel_id=1, source_target_pairs={{0,32},{32,128},{128,160},{160,0},{1,33},{33,129},{129,161},{161,1... | collective-permute-start | bytes 608264 | tf_op jit(solution)/shard_map/ppermute | solution.py:32
  58.4 0.5 convert_add_fusion.1
  59.0 1.8 %collective-permute-start.13 = (f16[1,72,1152]{2,1,0:T(8,128)(2,1)S(1)}, f16[1,72,1152]{2,1,0:T(8,128)(2,1)S(1)}, u32[]{:S(2)}, u32[]{:S(2)}) collective-permute-start(f16[1,72,1152]{2,1,0:T(8,128)(2,1)S(1)} %get-tuple-element.53), channel_id=1, source_target_pairs={{0,2},{1,3},{2,0},{3,1},{4,6},{5,7},{6,4},{7,5},{8,10},{9,11},{10,... | collective-permute-start | bytes 497672 | tf_op jit(solution)/shard_map/ppermute | solution.py:28
  60.8 1.8 %collective-permute-start.14 = (f16[1,72,1152]{2,1,0:T(8,128)(2,1)S(1)}, f16[1,72,1152]{2,1,0:T(8,128)(2,1)S(1)}, u32[]{:S(2)}, u32[]{:S(2)}) collective-permute-start(f16[1,72,1152]{2,1,0:T(8,128)(2,1)S(1)} %get-tuple-element.55), channel_id=1, source_target_pairs={{0,1},{1,2},{2,3},{3,0},{4,5},{5,6},{6,7},{7,4},{8,9},{9,10},{10,1... | collective-permute-start | bytes 497672 | tf_op jit(solution)/shard_map/ppermute | solution.py:28
  62.6 1.5 %collective-permute-done.6 = f16[1,72,1408]{2,1,0:T(8,128)(2,1)S(1)} collective-permute-done((f16[1,72,1408]{2,1,0:T(8,128)(2,1)S(1)}, f16[1,72,1408]{2,1,0:T(8,128)(2,1)S(1)}, u32[]{:S(2)}, u32[]{:S(2)}) %collective-permute-start.6) | collective-permute-done | bytes 202784 | tf_op jit(solution)/shard_map/ppermute | solution.py:32
  64.1 2.6 %collective-permute-start.15 = (f16[1,72,1152]{2,1,0:T(8,128)(2,1)S(1)}, f16[1,72,1152]{2,1,0:T(8,128)(2,1)S(1)}, u32[]{:S(2)}, u32[]{:S(2)}) collective-permute-start(f16[1,72,1152]{2,1,0:T(8,128)(2,1)S(1)} %get-tuple-element.54), channel_id=1, source_target_pairs={{0,3},{1,0},{2,1},{3,2},{4,7},{5,4},{6,5},{7,6},{8,11},{9,8},{10,9... | collective-permute-start | bytes 497672 | tf_op jit(solution)/shard_map/ppermute | solution.py:28
  66.9 0.8 collective-permute-done.14
  67.7 1.9 %collective-permute-done.15 = f16[1,72,1152]{2,1,0:T(8,128)(2,1)S(1)} collective-permute-done((f16[1,72,1152]{2,1,0:T(8,128)(2,1)S(1)}, f16[1,72,1152]{2,1,0:T(8,128)(2,1)S(1)}, u32[]{:S(2)}, u32[]{:S(2)}) %collective-permute-start.15) | collective-permute-done | bytes 165920 | tf_op jit(solution)/shard_map/ppermute | solution.py:28
  69.9 0.5 reshape.97
  70.4 20.0 %all_to_all.10 = f16[8,180,128]{2,1,0:T(8,128)(2,1)S(1)} all-to-all(f16[8,180,128]{2,1,0:T(8,128)(2,1)S(1)} %reshape.97), channel_id=1, replica_groups=mesh['yh'=2,'core'=2,'yl'=2,'z'=8,'x'=4] {'z'}, dimensions={0} | all-to-all | bytes 737280 | tf_op jit(solution)/shard_map/all_to_all | solution.py:209
  90.5 0.7 subtract_convert_fusion
  91.3 0.7 subtract_convert_fusion.1
  92.2 0.8 broadcast_in_dim.10
  93.0 3.7 %all-to-all-start.1 = ((bf16[8,180,128]{2,1,0:T(8,128)(2,1)}), bf16[8,180,128]{2,1,0:T(8,128)(2,1)S(1)}, u32[]{:S(2)}, u32[]{:S(2)}) async-start(bf16[8,180,128]{2,1,0:T(8,128)(2,1)} %broadcast_in_dim.10), calls=%async_computation.1 | async-start | bytes 753664 | tf_op jit(solution)/shard_map/all_to_all | solution.py:216
  97.0 11.0 %all-to-all-done.1 = bf16[8,180,128]{2,1,0:T(8,128)(2,1)S(1)} async-done(((bf16[8,180,128]{2,1,0:T(8,128)(2,1)}), bf16[8,180,128]{2,1,0:T(8,128)(2,1)S(1)}, u32[]{:S(2)}, u32[]{:S(2)}) %all-to-all-start.1) | async-done | bytes 368672 | tf_op jit(solution)/shard_map/all_to_all | solution.py:216
  108.1 0.4 reshape.98
  108.5 3.8 %collective-permute-start.17 = (bf16[72,2560]{1,0:T(8,128)(2,1)S(1)}, bf16[72,2560]{1,0:T(8,128)(2,1)S(1)}, u32[]{:S(2)}, u32[]{:S(2)}) collective-permute-start(bf16[72,2560]{1,0:T(8,128)(2,1)S(1)} %reshape.98), channel_id=1, source_target_pairs={{0,3},{1,0},{2,1},{3,2},{4,7},{5,4},{6,5},{7,6},{8,11},{9,8},{10,9... | collective-permute-start | bytes 1105928 | tf_op jit(solution)/shard_map/ppermute | solution.py:28
  112.3 4.4 %collective-permute-start.18 = (bf16[72,2560]{1,0:T(8,128)(2,1)S(1)}, bf16[72,2560]{1,0:T(8,128)(2,1)S(1)}, u32[]{:S(2)}, u32[]{:S(2)}) collective-permute-start(bf16[72,2560]{1,0:T(8,128)(2,1)S(1)} %reshape.98), channel_id=1, source_target_pairs={{0,32},{32,0},{1,33},{33,1},{2,34},{34,2},{3,35},{35,3},{4,36},{36... | collective-permute-start | bytes 1105928 | tf_op jit(solution)/shard_map/ppermute | solution.py:36
  116.9 4.4 %collective-permute-done.17 = bf16[72,2560]{1,0:T(8,128)(2,1)S(1)} collective-permute-done((bf16[72,2560]{1,0:T(8,128)(2,1)S(1)}, bf16[72,2560]{1,0:T(8,128)(2,1)S(1)}, u32[]{:S(2)}, u32[]{:S(2)}) %collective-permute-start.17) | collective-permute-done | bytes 368672 | tf_op jit(solution)/shard_map/ppermute | solution.py:28
  121.3 3.8 %collective-permute-start.20 = (bf16[40,2560]{1,0:T(8,128)(2,1)S(1)}, bf16[40,2560]{1,0:T(8,128)(2,1)S(1)}, u32[]{:S(2)}, u32[]{:S(2)}) collective-permute-start(bf16[40,2560]{1,0:T(8,128)(2,1)S(1)} %slice.103), channel_id=1, source_target_pairs={{0,3},{1,0},{2,1},{3,2},{4,7},{5,4},{6,5},{7,6},{8,11},{9,8},{10,9... | collective-permute-start | bytes 614408 | tf_op jit(solution)/shard_map/ppermute | solution.py:28
  125.2 3.2 %collective-permute-start.22 = (bf16[72,2560]{1,0:T(8,128)(2,1)S(1)}, bf16[72,2560]{1,0:T(8,128)(2,1)S(1)}, u32[]{:S(2)}, u32[]{:S(2)}) collective-permute-start(bf16[72,2560]{1,0:T(8,128)(2,1)S(1)} %collective-permute-done.18), channel_id=1, source_target_pairs={{0,3},{1,0},{2,1},{3,2},{4,7},{5,4},{6,5},{7,6},{8,11},{9,8},{10,9... | collective-permute-start | bytes 1105928 | tf_op jit(solution)/shard_map/ppermute | solution.py:28
  128.5 3.2 %collective-permute-done.19 = bf16[32,2560]{1,0:T(8,128)(2,1)S(1)} collective-permute-done((bf16[32,2560]{1,0:T(8,128)(2,1)S(1)}, bf16[32,2560]{1,0:T(8,128)(2,1)S(1)}, u32[]{:S(2)}, u32[]{:S(2)}) %collective-permute-start.19) | collective-permute-done | bytes 163872 | tf_op jit(solution)/shard_map/ppermute | solution.py:28
  131.7 4.0 %collective-permute-start.23 = (bf16[72,2560]{1,0:T(8,128)(2,1)S(1)}, bf16[72,2560]{1,0:T(8,128)(2,1)S(1)}, u32[]{:S(2)}, u32[]{:S(2)}) collective-permute-start(bf16[72,2560]{1,0:T(8,128)(2,1)S(1)} %pad_maximum_fusion.1), channel_id=1, source_target_pairs={{0,32},{32,0},{1,33},{33,1},{2,34},{34,2},{3,35},{35,3},{4,36},{36... | collective-permute-start | bytes 1105928 | tf_op jit(solution)/shard_map/ppermute | solution.py:36
  135.7 1.2 convolution_convert_fusion.1
  137.0 0.7 convolution_convert_fusion.3
  137.8 3.5 %collective-permute-done.23 = bf16[72,2560]{1,0:T(8,128)(2,1)S(1)} collective-permute-done((bf16[72,2560]{1,0:T(8,128)(2,1)S(1)}, bf16[72,2560]{1,0:T(8,128)(2,1)S(1)}, u32[]{:S(2)}, u32[]{:S(2)}) %collective-permute-start.23) | collective-permute-done | bytes 368672 | tf_op jit(solution)/shard_map/ppermute | solution.py:36
  141.3 1.4 fusion.5
  142.6 2.0 %fusion.4 = bf16[384,2560]{1,0:T(8,128)(2,1)} fusion(bf16[384,2560]{1,0:T(8,128)(2,1)S(1)} %convolution_convert_fusion.1, bf16[384,216]{1,0:T(8,128)(2,1)S(1)} %fusion.17, bf16[216,2560]{1,0:T(8,128)(2,1)S(1)} %constant_dynamic-update-slice_fusion.6), kind=kOutput, calls=%fused_computation.8 | convolution fusion | flops 426639360 | bytes 5203968 | tf_op jit(solution)/shard_map/dot_general | solution.py:67
  (75 shorter events, 3.0 us)
Async XLA Ops:
  0.6 13.1 %collective-permute-start.1 = (bf16[768,2560]{1,0:T(8,128)(2,1)}, bf16[768,2560]{1,0:T(8,128)(2,1)}, u32[]{:S(2)}, u32[]{:S(2)}) collective-permute-start(bf16[768,2560]{1,0:T(8,128)(2,1)} %param.16), channel_id=1, source_target_pairs={{0,64},{64,0},{1,65},{65,1},{2,66},{66,2},{3,67},{67,3},{4,68},{68... | collective-permute-start | bytes 11796488 | tf_op jit(solution)/shard_map/ppermute | solution.py:40
  8.2 5.6 %collective-permute-start = (bf16[4,2,144,768]{3,2,1,0:T(8,128)(2,1)}, bf16[4,2,144,768]{3,2,1,0:T(8,128)(2,1)S(1)}, u32[]{:S(2)}, u32[]{:S(2)}) collective-permute-start(bf16[4,2,144,768]{3,2,1,0:T(8,128)(2,1)} %get-tuple-element.22), channel_id=1, source_target_pairs={{0,64},{64,0},{1,65},{65,1},{2,66},{66,2},{3,67},{67,3},{4,68},{68... | collective-permute-start | bytes 5308424 | tf_op jit(solution)/shard_map/ppermute | solution.py:40
  18.6 3.5 %copy-start.6 = (bf16[4,2,144,768]{3,2,1,0:T(8,128)(2,1)S(1)}, bf16[4,2,144,768]{3,2,1,0:T(8,128)(2,1)}, u32[]{:S(2)}) copy-start(bf16[4,2,144,768]{3,2,1,0:T(8,128)(2,1)} %get-tuple-element.21) | copy-start | bytes 5308420
  19.2 20.4 %collective-permute-start.2 = (f16[4,72,1408]{2,1,0:T(8,128)(2,1)S(1)}, f16[4,72,1408]{2,1,0:T(8,128)(2,1)S(1)}, u32[]{:S(2)}, u32[]{:S(2)}) collective-permute-start(f16[4,72,1408]{2,1,0:T(8,128)(2,1)S(1)} %get-tuple-element.42), channel_id=1, source_target_pairs={{0,3},{1,0},{2,1},{3,2},{4,7},{5,4},{6,5},{7,6},{8,11},{9,8},{10,9... | collective-permute-start | bytes 2433032 | tf_op jit(solution)/shard_map/ppermute | solution.py:28
  22.0 20.9 %collective-permute-start.3 = (f16[4,72,1408]{2,1,0:T(8,128)(2,1)S(1)}, f16[4,72,1408]{2,1,0:T(8,128)(2,1)S(1)}, u32[]{:S(2)}, u32[]{:S(2)}) collective-permute-start(f16[4,72,1408]{2,1,0:T(8,128)(2,1)S(1)} %get-tuple-element.43), channel_id=1, source_target_pairs={{0,1},{1,2},{2,3},{3,0},{4,5},{5,6},{6,7},{7,4},{8,9},{9,10},{10,1... | collective-permute-start | bytes 2433032 | tf_op jit(solution)/shard_map/ppermute | solution.py:28
  30.6 16.8 %collective-permute-start.10 = (f16[4,72,1152]{2,1,0:T(8,128)(2,1)S(1)}, f16[4,72,1152]{2,1,0:T(8,128)(2,1)S(1)}, u32[]{:S(2)}, u32[]{:S(2)}) collective-permute-start(f16[4,72,1152]{2,1,0:T(8,128)(2,1)S(1)} %get-tuple-element.46), channel_id=1, source_target_pairs={{0,32},{32,128},{128,160},{160,0},{1,33},{33,129},{129,161},{161,1... | collective-permute-start | bytes 1990664 | tf_op jit(solution)/shard_map/ppermute | solution.py:32
  32.1 16.7 %collective-permute-start.9 = (f16[4,72,1152]{2,1,0:T(8,128)(2,1)S(1)}, f16[4,72,1152]{2,1,0:T(8,128)(2,1)S(1)}, u32[]{:S(2)}, u32[]{:S(2)}) collective-permute-start(f16[4,72,1152]{2,1,0:T(8,128)(2,1)S(1)} %get-tuple-element.47), channel_id=1, source_target_pairs={{0,160},{32,0},{128,32},{160,128},{1,161},{33,1},{129,33},{161,129... | collective-permute-start | bytes 1990664 | tf_op jit(solution)/shard_map/ppermute | solution.py:32
  43.2 11.4 %collective-permute-start.4 = (f16[2,72,1408]{2,1,0:T(8,128)(2,1)S(1)}, f16[2,72,1408]{2,1,0:T(8,128)(2,1)S(1)}, u32[]{:S(2)}, u32[]{:S(2)}) collective-permute-start(f16[2,72,1408]{2,1,0:T(8,128)(2,1)S(1)} %get-tuple-element.45), channel_id=1, source_target_pairs={{0,1},{1,2},{2,3},{3,0},{4,5},{5,6},{6,7},{7,4},{8,9},{9,10},{10,1... | collective-permute-start | bytes 1216520 | tf_op jit(solution)/shard_map/ppermute | solution.py:28
  43.3 11.3 %collective-permute-start.5 = (f16[2,72,1408]{2,1,0:T(8,128)(2,1)S(1)}, f16[2,72,1408]{2,1,0:T(8,128)(2,1)S(1)}, u32[]{:S(2)}, u32[]{:S(2)}) collective-permute-start(f16[2,72,1408]{2,1,0:T(8,128)(2,1)S(1)} %get-tuple-element.44), channel_id=1, source_target_pairs={{0,3},{1,0},{2,1},{3,2},{4,7},{5,4},{6,5},{7,6},{8,11},{9,8},{10,9... | collective-permute-start | bytes 1216520 | tf_op jit(solution)/shard_map/ppermute | solution.py:28
  47.5 10.7 %collective-permute-start.11 = (f16[2,72,1152]{2,1,0:T(8,128)(2,1)S(1)}, f16[2,72,1152]{2,1,0:T(8,128)(2,1)S(1)}, u32[]{:S(2)}, u32[]{:S(2)}) collective-permute-start(f16[2,72,1152]{2,1,0:T(8,128)(2,1)S(1)} %fusion.15), channel_id=1, source_target_pairs={{0,32},{32,128},{128,160},{160,0},{1,33},{33,129},{129,161},{161,1... | collective-permute-start | bytes 995336 | tf_op jit(solution)/shard_map/ppermute | solution.py:32
  49.0 9.4 %collective-permute-start.12 = (f16[2,72,1152]{2,1,0:T(8,128)(2,1)S(1)}, f16[2,72,1152]{2,1,0:T(8,128)(2,1)S(1)}, u32[]{:S(2)}, u32[]{:S(2)}) collective-permute-start(f16[2,72,1152]{2,1,0:T(8,128)(2,1)S(1)} %fusion.14), channel_id=1, source_target_pairs={{0,160},{32,0},{128,32},{160,128},{1,161},{33,1},{129,33},{161,129... | collective-permute-start | bytes 995336 | tf_op jit(solution)/shard_map/ppermute | solution.py:32
  55.3 8.8 %collective-permute-start.6 = (f16[1,72,1408]{2,1,0:T(8,128)(2,1)S(1)}, f16[1,72,1408]{2,1,0:T(8,128)(2,1)S(1)}, u32[]{:S(2)}, u32[]{:S(2)}) collective-permute-start(f16[1,72,1408]{2,1,0:T(8,128)(2,1)S(1)} %get-tuple-element.52), channel_id=1, source_target_pairs={{0,128},{32,160},{128,0},{160,32},{1,129},{33,161},{129,1},{161,33... | collective-permute-start | bytes 608264 | tf_op jit(solution)/shard_map/ppermute | solution.py:32
  55.8 11.0 %collective-permute-start.7 = (f16[1,72,1408]{2,1,0:T(8,128)(2,1)S(1)}, f16[1,72,1408]{2,1,0:T(8,128)(2,1)S(1)}, u32[]{:S(2)}, u32[]{:S(2)}) collective-permute-start(f16[1,72,1408]{2,1,0:T(8,128)(2,1)S(1)} %get-tuple-element.51), channel_id=1, source_target_pairs={{0,32},{32,128},{128,160},{160,0},{1,33},{33,129},{129,161},{161,1... | collective-permute-start | bytes 608264 | tf_op jit(solution)/shard_map/ppermute | solution.py:32
  58.0 8.8 %collective-permute-start.8 = (f16[1,72,1408]{2,1,0:T(8,128)(2,1)S(1)}, f16[1,72,1408]{2,1,0:T(8,128)(2,1)S(1)}, u32[]{:S(2)}, u32[]{:S(2)}) collective-permute-start(f16[1,72,1408]{2,1,0:T(8,128)(2,1)S(1)} %get-tuple-element.50), channel_id=1, source_target_pairs={{0,160},{32,0},{128,32},{160,128},{1,161},{33,1},{129,33},{161,129... | collective-permute-start | bytes 608264 | tf_op jit(solution)/shard_map/ppermute | solution.py:32
  59.0 7.9 %collective-permute-start.13 = (f16[1,72,1152]{2,1,0:T(8,128)(2,1)S(1)}, f16[1,72,1152]{2,1,0:T(8,128)(2,1)S(1)}, u32[]{:S(2)}, u32[]{:S(2)}) collective-permute-start(f16[1,72,1152]{2,1,0:T(8,128)(2,1)S(1)} %get-tuple-element.53), channel_id=1, source_target_pairs={{0,2},{1,3},{2,0},{3,1},{4,6},{5,7},{6,4},{7,5},{8,10},{9,11},{10,... | collective-permute-start | bytes 497672 | tf_op jit(solution)/shard_map/ppermute | solution.py:28
  60.8 6.9 %collective-permute-start.14 = (f16[1,72,1152]{2,1,0:T(8,128)(2,1)S(1)}, f16[1,72,1152]{2,1,0:T(8,128)(2,1)S(1)}, u32[]{:S(2)}, u32[]{:S(2)}) collective-permute-start(f16[1,72,1152]{2,1,0:T(8,128)(2,1)S(1)} %get-tuple-element.55), channel_id=1, source_target_pairs={{0,1},{1,2},{2,3},{3,0},{4,5},{5,6},{6,7},{7,4},{8,9},{9,10},{10,1... | collective-permute-start | bytes 497672 | tf_op jit(solution)/shard_map/ppermute | solution.py:28
  64.1 5.5 %collective-permute-start.15 = (f16[1,72,1152]{2,1,0:T(8,128)(2,1)S(1)}, f16[1,72,1152]{2,1,0:T(8,128)(2,1)S(1)}, u32[]{:S(2)}, u32[]{:S(2)}) collective-permute-start(f16[1,72,1152]{2,1,0:T(8,128)(2,1)S(1)} %get-tuple-element.54), channel_id=1, source_target_pairs={{0,3},{1,0},{2,1},{3,2},{4,7},{5,4},{6,5},{7,6},{8,11},{9,8},{10,9... | collective-permute-start | bytes 497672 | tf_op jit(solution)/shard_map/ppermute | solution.py:28
  69.7 20.8 %copy-start = (f32[6,2560]{1,0:T(8,128)S(1)}, f32[6,2560]{1,0:T(8,128)}, u32[]{:S(2)}) copy-start(f32[6,2560]{1,0:T(8,128)} %param.19) | copy-start | bytes 184324
  69.7 20.8 %copy-start.1 = (f32[6,2560]{1,0:T(8,128)S(1)}, f32[6,2560]{1,0:T(8,128)}, u32[]{:S(2)}) copy-start(f32[6,2560]{1,0:T(8,128)} %param.21) | copy-start | bytes 184324
  69.8 20.8 %copy-start.2 = (f32[6,2560]{1,0:T(8,128)S(1)}, f32[6,2560]{1,0:T(8,128)}, u32[]{:S(2)}) copy-start(f32[6,2560]{1,0:T(8,128)} %param.20) | copy-start | bytes 184324
  69.8 21.5 %copy-start.3 = (f32[3,2560]{1,0:T(4,128)S(1)}, f32[3,2560]{1,0:T(4,128)}, u32[]{:S(2)}) copy-start(f32[3,2560]{1,0:T(4,128)} %param.22) | copy-start | bytes 92164
  69.8 21.5 %copy-start.4 = (f32[3,2560]{1,0:T(4,128)S(1)}, f32[3,2560]{1,0:T(4,128)}, u32[]{:S(2)}) copy-start(f32[3,2560]{1,0:T(4,128)} %param.24) | copy-start | bytes 92164
  69.8 21.5 %copy-start.5 = (f32[3,2560]{1,0:T(4,128)S(1)}, f32[3,2560]{1,0:T(4,128)}, u32[]{:S(2)}) copy-start(f32[3,2560]{1,0:T(4,128)} %param.23) | copy-start | bytes 92164
  93.0 15.1 %all-to-all-start.1 = ((bf16[8,180,128]{2,1,0:T(8,128)(2,1)}), bf16[8,180,128]{2,1,0:T(8,128)(2,1)S(1)}, u32[]{:S(2)}, u32[]{:S(2)}) async-start(bf16[8,180,128]{2,1,0:T(8,128)(2,1)} %broadcast_in_dim.10), calls=%async_computation.1 | async-start | bytes 753664 | tf_op jit(solution)/shard_map/all_to_all | solution.py:216
  108.5 12.8 %collective-permute-start.17 = (bf16[72,2560]{1,0:T(8,128)(2,1)S(1)}, bf16[72,2560]{1,0:T(8,128)(2,1)S(1)}, u32[]{:S(2)}, u32[]{:S(2)}) collective-permute-start(bf16[72,2560]{1,0:T(8,128)(2,1)S(1)} %reshape.98), channel_id=1, source_target_pairs={{0,3},{1,0},{2,1},{3,2},{4,7},{5,4},{6,5},{7,6},{8,11},{9,8},{10,9... | collective-permute-start | bytes 1105928 | tf_op jit(solution)/shard_map/ppermute | solution.py:28
  112.3 12.8 %collective-permute-start.16 = (bf16[72,2560]{1,0:T(8,128)(2,1)S(1)}, bf16[72,2560]{1,0:T(8,128)(2,1)S(1)}, u32[]{:S(2)}, u32[]{:S(2)}) collective-permute-start(bf16[72,2560]{1,0:T(8,128)(2,1)S(1)} %reshape.98), channel_id=1, source_target_pairs={{0,1},{1,2},{2,3},{3,0},{4,5},{5,6},{6,7},{7,4},{8,9},{9,10},{10,1... | collective-permute-start | bytes 1105928 | tf_op jit(solution)/shard_map/ppermute | solution.py:28
  112.3 12.9 %collective-permute-start.18 = (bf16[72,2560]{1,0:T(8,128)(2,1)S(1)}, bf16[72,2560]{1,0:T(8,128)(2,1)S(1)}, u32[]{:S(2)}, u32[]{:S(2)}) collective-permute-start(bf16[72,2560]{1,0:T(8,128)(2,1)S(1)} %reshape.98), channel_id=1, source_target_pairs={{0,32},{32,0},{1,33},{33,1},{2,34},{34,2},{3,35},{35,3},{4,36},{36... | collective-permute-start | bytes 1105928 | tf_op jit(solution)/shard_map/ppermute | solution.py:36
  121.3 10.4 %collective-permute-start.20 = (bf16[40,2560]{1,0:T(8,128)(2,1)S(1)}, bf16[40,2560]{1,0:T(8,128)(2,1)S(1)}, u32[]{:S(2)}, u32[]{:S(2)}) collective-permute-start(bf16[40,2560]{1,0:T(8,128)(2,1)S(1)} %slice.103), channel_id=1, source_target_pairs={{0,3},{1,0},{2,1},{3,2},{4,7},{5,4},{6,5},{7,6},{8,11},{9,8},{10,9... | collective-permute-start | bytes 614408 | tf_op jit(solution)/shard_map/ppermute | solution.py:28
  125.1 6.6 %collective-permute-start.19 = (bf16[32,2560]{1,0:T(8,128)(2,1)S(1)}, bf16[32,2560]{1,0:T(8,128)(2,1)S(1)}, u32[]{:S(2)}, u32[]{:S(2)}) collective-permute-start(bf16[32,2560]{1,0:T(8,128)(2,1)S(1)} %slice.102), channel_id=1, source_target_pairs={{0,1},{1,2},{2,3},{3,0},{4,5},{5,6},{6,7},{7,4},{8,9},{9,10},{10,1... | collective-permute-start | bytes 491528 | tf_op jit(solution)/shard_map/ppermute | solution.py:28
  125.2 12.5 %collective-permute-start.22 = (bf16[72,2560]{1,0:T(8,128)(2,1)S(1)}, bf16[72,2560]{1,0:T(8,128)(2,1)S(1)}, u32[]{:S(2)}, u32[]{:S(2)}) collective-permute-start(bf16[72,2560]{1,0:T(8,128)(2,1)S(1)} %collective-permute-done.18), channel_id=1, source_target_pairs={{0,3},{1,0},{2,1},{3,2},{4,7},{5,4},{6,5},{7,6},{8,11},{9,8},{10,9... | collective-permute-start | bytes 1105928 | tf_op jit(solution)/shard_map/ppermute | solution.py:28
  128.4 9.3 %collective-permute-start.21 = (bf16[72,2560]{1,0:T(8,128)(2,1)S(1)}, bf16[72,2560]{1,0:T(8,128)(2,1)S(1)}, u32[]{:S(2)}, u32[]{:S(2)}) collective-permute-start(bf16[72,2560]{1,0:T(8,128)(2,1)S(1)} %collective-permute-done.18), channel_id=1, source_target_pairs={{0,1},{1,2},{2,3},{3,0},{4,5},{5,6},{6,7},{7,4},{8,9},{9,10},{10,1... | collective-permute-start | bytes 1105928 | tf_op jit(solution)/shard_map/ppermute | solution.py:28
  131.7 9.5 %collective-permute-start.23 = (bf16[72,2560]{1,0:T(8,128)(2,1)S(1)}, bf16[72,2560]{1,0:T(8,128)(2,1)S(1)}, u32[]{:S(2)}, u32[]{:S(2)}) collective-permute-start(bf16[72,2560]{1,0:T(8,128)(2,1)S(1)} %pad_maximum_fusion.1), channel_id=1, source_target_pairs={{0,32},{32,0},{1,33},{33,1},{2,34},{34,2},{3,35},{35,3},{4,36},{36... | collective-permute-start | bytes 1105928 | tf_op jit(solution)/shard_map/ppermute | solution.py:36

commit v9 on v8

--- a/solution.py
+++ b/solution.py
@@ -215,12 +215,10 @@
     weight = jnp.concatenate([weight_s, weight_r], axis=0).reshape(1, rows * width // 128, 128)
     weight = lax.all_to_all(jnp.broadcast_to(weight, (NZ,) + weight.shape[1:]), "z", 0, 0)
     mine = weight.reshape(group, width)
-    part = group // 32 * 16
     mine_plus, mine_minus = x_ring(mine, 1), x_ring(mine, 3)
     other = y_swap(mine)
-    two = [x_ring(mine_plus[:part], 1), x_ring(mine_minus[part:], 3)]
+    mine_two = x_ring(mine, 2)
     other_plus, other_minus = x_ring(other, 1), x_ring(other, 3)
-    mine_two = jnp.concatenate(two, axis=0)
     other_two = y_swap(mine_two)
     early = jnp.concatenate([mine, mine_plus, mine_minus, other, mine_two], axis=0)
     late = [other_plus, other_minus, other_two]

time: 146 us -> 141 us (0.966)
  starting transfers between devices: 43.2 us -> 38.2 us
    ppermute x13 -> x12, waiting for transfers between devices: 25 us -> 20 us  [x_ring(): return lax.ppermute(v, 'x', [(i, (i + d) % NX) for i in range(NX)])]
    ppermute x13 -> x12, starting transfers between devices: 23.3 us -> 19.3 us  [x_ring(): return lax.ppermute(v, 'x', [(i, (i + d) % NX) for i in range(NX)])]
    ppermute x2, waiting for transfers between devices: 3.47 us -> 7.24 us  [y_swap(): return lax.ppermute(v, 'yl', [(0, 1), (1, 0)])]
  transfers between devices with their start and end apart: 25 -> 24, of which waited for: 12 -> 13; matrix products, arithmetic and copies ran while one was open for 13% -> 13% of each run, Pallas kernels for 5% -> 5%
where the time goes in v9:
time: 141 us; the launch traced here: 138 us
  waiting for transfers between devices  40.9 us (29%)
  starting transfers between devices  38.2 us (27%)
  matrix products  23.1 us (16%)
  blocking collectives  20 us (14%)
  Pallas kernels  6.79 us (5%)
  other arithmetic  5.23 us (4%)
  local copies, waits for them, and re-layouts  2.31 us (2%)
  between operations  1.68 us (1%)
    dot_general x8, matrix products, dot(): return jnp.dot(a, b, preferred_element_type=F32)  23.1 us
    ppermute x12, waiting for transfers between devices, x_ring(): return lax.ppermute(v, 'x', [(i, (i + d) % NX) for i in range(NX)])  20 us
    all_to_all x1, blocking collectives, local(): last = lax.all_to_all(last, 'z', 0, 0)  20 us
    ppermute x12, starting transfers between devices, x_ring(): return lax.ppermute(v, 'x', [(i, (i + d) % NX) for i in range(NX)])  19.3 us
    all_to_all x1, waiting for transfers between devices, local(): lax.all_to_all(jnp.broadcast_to(weight, (NZ,) + weight.shape[1:]), 'z', 0...  11 us
    ppermute x2, starting transfers between devices, y_swap(): return lax.ppermute(v, 'yl', [(0, 1), (1, 0)])  7.34 us
    ppermute x7, starting transfers between devices, y_ring(): return lax.ppermute(v, ('yh', 'yl'), [(i, (i + d) % NY) for i in range(NY)])  7.3 us
    ppermute x2, waiting for transfers between devices, y_swap(): return lax.ppermute(v, 'yl', [(0, 1), (1, 0)])  7.24 us
  transfers between devices with their start and end apart: 24, of which 13 were waited for; matrix products, arithmetic and copies ran while one was open for 13% of the time, Pallas kernels for 5%

profile of v9, /device:TPU:16, one launch (start us, length us, event | category | flops | bytes accessed | tf_op | source)
XLA Modules:
  0.0 138.2 jit_solution(5372316395953624324)
XLA Ops:
  1.4 6.8 %shard_map.181 = (bf16[4,2,144,768]{3,2,1,0:T(8,128)(2,1)}, bf16[4,2,144,768]{3,2,1,0:T(8,128)(2,1)}) custom-call(s32[1]{0:T(128)} %bitcast.core_ref, s32[1]{0:T(128)S(6)} %copy.35.count_ref, s32[1,96]{1,0:T(1,128)} %bitcast.78, bf16[768,1536]{1,0:T(8,128)(2,1)} %shared_ref.1, bf16[96,768]{1,0:T(8,128)(2,1)} %routed_ref.1, ...), custom_call_target="tpu_custom_call" | custom-call | flops 2717908992 | bytes 8847360 | tf_op jit(solution)/shard_map/pallas_call | solution.py:101
  8.2 0.5 collective-permute-start
  8.7 5.1 %fusion.7 = f32[1152,1408]{1,0:T(8,128)S(1)} fusion(bf16[1152,768]{1,0:T(8,128)(2,1)} %bitcast.79, bf16[768,2560]{1,0:T(8,128)(2,1)} %param.16), kind=kOutput, calls=%fused_computation.13 | convolution fusion | flops 2491416576 | bytes 10420224 | tf_op jit(solution)/shard_map/dot_general | solution.py:67
  13.8 4.8 %fusion.3 = f16[1152,1408]{1,0:T(8,128)(2,1)S(1)} fusion(f32[1152,1408]{1,0:T(8,128)S(1)} %fusion.7, bf16[1152,768]{1,0:T(8,128)(2,1)S(1)} %bitcast.76, bf16[768,2560]{1,0:T(8,128)(2,1)} %collective-permute-done.1), kind=kOutput, calls=%fused_computation.5 | convolution fusion | flops 2496282624 | bytes 13664256 | tf_op jit(solution)/shard_map/dot_general | solution.py:67
  18.6 0.6 bitcast_select_fusion.1
  19.2 2.8 %collective-permute-start.2 = (f16[4,72,1408]{2,1,0:T(8,128)(2,1)S(1)}, f16[4,72,1408]{2,1,0:T(8,128)(2,1)S(1)}, u32[]{:S(2)}, u32[]{:S(2)}) collective-permute-start(f16[4,72,1408]{2,1,0:T(8,128)(2,1)S(1)} %get-tuple-element.42), channel_id=1, source_target_pairs={{0,3},{1,0},{2,1},{3,2},{4,7},{5,4},{6,5},{7,6},{8,11},{9,8},{10,9... | collective-permute-start | bytes 2433032 | tf_op jit(solution)/shard_map/ppermute | solution.py:28
  22.0 4.0 %fusion.10 = f32[1152,1152]{1,0:T(8,128)S(1)} fusion(bf16[1152,768]{1,0:T(8,128)(2,1)S(1)} %bitcast.80, bf16[768,2560]{1,0:T(8,128)(2,1)} %param.16), kind=kOutput, calls=%fused_computation.16 | convolution fusion | flops 2038431744 | bytes 8847360 | tf_op jit(solution)/shard_map/dot_general | solution.py:67
  26.0 4.0 %fusion.2 = f16[1152,1152]{1,0:T(8,128)(2,1)S(1)} fusion(f32[1152,1152]{1,0:T(8,128)S(1)} %fusion.10, bf16[1152,768]{1,0:T(8,128)(2,1)S(1)} %bitcast.77, bf16[768,2560]{1,0:T(8,128)(2,1)} %collective-permute-done.1), kind=kOutput, calls=%fused_computation.4 | convolution fusion | flops 2042413056 | bytes 11501568 | tf_op jit(solution)/shard_map/dot_general | solution.py:67
  30.1 0.5 bitcast_select_fusion.2
  30.6 1.5 %collective-permute-start.10 = (f16[4,72,1152]{2,1,0:T(8,128)(2,1)S(1)}, f16[4,72,1152]{2,1,0:T(8,128)(2,1)S(1)}, u32[]{:S(2)}, u32[]{:S(2)}) collective-permute-start(f16[4,72,1152]{2,1,0:T(8,128)(2,1)S(1)} %get-tuple-element.46), channel_id=1, source_target_pairs={{0,32},{32,128},{128,160},{160,0},{1,33},{33,129},{129,161},{161,1... | collective-permute-start | bytes 1990664 | tf_op jit(solution)/shard_map/ppermute | solution.py:32
  32.1 0.7 collective-permute-start.9
  33.1 6.4 %collective-permute-done.2 = f16[4,72,1408]{2,1,0:T(8,128)(2,1)S(1)} collective-permute-done((f16[4,72,1408]{2,1,0:T(8,128)(2,1)S(1)}, f16[4,72,1408]{2,1,0:T(8,128)(2,1)S(1)}, u32[]{:S(2)}, u32[]{:S(2)}) %collective-permute-start.2) | collective-permute-done | bytes 811040 | tf_op jit(solution)/shard_map/ppermute | solution.py:28
  39.6 3.4 %collective-permute-done.3 = f16[4,72,1408]{2,1,0:T(8,128)(2,1)S(1)} collective-permute-done((f16[4,72,1408]{2,1,0:T(8,128)(2,1)S(1)}, f16[4,72,1408]{2,1,0:T(8,128)(2,1)S(1)}, u32[]{:S(2)}, u32[]{:S(2)}) %collective-permute-start.3) | collective-permute-done | bytes 811040 | tf_op jit(solution)/shard_map/ppermute | solution.py:28
  43.3 3.2 %collective-permute-start.5 = (f16[2,72,1408]{2,1,0:T(8,128)(2,1)S(1)}, f16[2,72,1408]{2,1,0:T(8,128)(2,1)S(1)}, u32[]{:S(2)}, u32[]{:S(2)}) collective-permute-start(f16[2,72,1408]{2,1,0:T(8,128)(2,1)S(1)} %get-tuple-element.44), channel_id=1, source_target_pairs={{0,3},{1,0},{2,1},{3,2},{4,7},{5,4},{6,5},{7,6},{8,11},{9,8},{10,9... | collective-permute-start | bytes 1216520 | tf_op jit(solution)/shard_map/ppermute | solution.py:28
  46.6 0.9 collective-permute-done.10
  47.5 1.4 collective-permute-start.11
  49.0 0.8 collective-permute-start.12
  49.8 4.9 %collective-permute-done.4 = f16[2,72,1408]{2,1,0:T(8,128)(2,1)S(1)} collective-permute-done((f16[2,72,1408]{2,1,0:T(8,128)(2,1)S(1)}, f16[2,72,1408]{2,1,0:T(8,128)(2,1)S(1)}, u32[]{:S(2)}, u32[]{:S(2)}) %collective-permute-start.4) | collective-permute-done | bytes 405536 | tf_op jit(solution)/shard_map/ppermute | solution.py:28
  54.7 0.6 convert_add_fusion
  55.4 0.4 collective-permute-start.6
  55.8 2.2 %collective-permute-start.7 = (f16[1,72,1408]{2,1,0:T(8,128)(2,1)S(1)}, f16[1,72,1408]{2,1,0:T(8,128)(2,1)S(1)}, u32[]{:S(2)}, u32[]{:S(2)}) collective-permute-start(f16[1,72,1408]{2,1,0:T(8,128)(2,1)S(1)} %get-tuple-element.51), channel_id=1, source_target_pairs={{0,32},{32,128},{128,160},{160,0},{1,33},{33,129},{129,161},{161,1... | collective-permute-start | bytes 608264 | tf_op jit(solution)/shard_map/ppermute | solution.py:32
  58.4 0.5 convert_add_fusion.1
  59.0 1.8 %collective-permute-start.13 = (f16[1,72,1152]{2,1,0:T(8,128)(2,1)S(1)}, f16[1,72,1152]{2,1,0:T(8,128)(2,1)S(1)}, u32[]{:S(2)}, u32[]{:S(2)}) collective-permute-start(f16[1,72,1152]{2,1,0:T(8,128)(2,1)S(1)} %get-tuple-element.53), channel_id=1, source_target_pairs={{0,2},{1,3},{2,0},{3,1},{4,6},{5,7},{6,4},{7,5},{8,10},{9,11},{10,... | collective-permute-start | bytes 497672 | tf_op jit(solution)/shard_map/ppermute | solution.py:28
  60.8 1.8 %collective-permute-start.14 = (f16[1,72,1152]{2,1,0:T(8,128)(2,1)S(1)}, f16[1,72,1152]{2,1,0:T(8,128)(2,1)S(1)}, u32[]{:S(2)}, u32[]{:S(2)}) collective-permute-start(f16[1,72,1152]{2,1,0:T(8,128)(2,1)S(1)} %get-tuple-element.55), channel_id=1, source_target_pairs={{0,1},{1,2},{2,3},{3,0},{4,5},{5,6},{6,7},{7,4},{8,9},{9,10},{10,1... | collective-permute-start | bytes 497672 | tf_op jit(solution)/shard_map/ppermute | solution.py:28
  62.6 1.5 %collective-permute-done.6 = f16[1,72,1408]{2,1,0:T(8,128)(2,1)S(1)} collective-permute-done((f16[1,72,1408]{2,1,0:T(8,128)(2,1)S(1)}, f16[1,72,1408]{2,1,0:T(8,128)(2,1)S(1)}, u32[]{:S(2)}, u32[]{:S(2)}) %collective-permute-start.6) | collective-permute-done | bytes 202784 | tf_op jit(solution)/shard_map/ppermute | solution.py:32
  64.1 2.6 %collective-permute-start.15 = (f16[1,72,1152]{2,1,0:T(8,128)(2,1)S(1)}, f16[1,72,1152]{2,1,0:T(8,128)(2,1)S(1)}, u32[]{:S(2)}, u32[]{:S(2)}) collective-permute-start(f16[1,72,1152]{2,1,0:T(8,128)(2,1)S(1)} %get-tuple-element.54), channel_id=1, source_target_pairs={{0,3},{1,0},{2,1},{3,2},{4,7},{5,4},{6,5},{7,6},{8,11},{9,8},{10,9... | collective-permute-start | bytes 497672 | tf_op jit(solution)/shard_map/ppermute | solution.py:28
  66.9 0.8 collective-permute-done.14
  67.7 1.9 %collective-permute-done.15 = f16[1,72,1152]{2,1,0:T(8,128)(2,1)S(1)} collective-permute-done((f16[1,72,1152]{2,1,0:T(8,128)(2,1)S(1)}, f16[1,72,1152]{2,1,0:T(8,128)(2,1)S(1)}, u32[]{:S(2)}, u32[]{:S(2)}) %collective-permute-start.15) | collective-permute-done | bytes 165920 | tf_op jit(solution)/shard_map/ppermute | solution.py:28
  69.9 0.5 reshape.97
  70.4 20.0 %all_to_all.10 = f16[8,180,128]{2,1,0:T(8,128)(2,1)S(1)} all-to-all(f16[8,180,128]{2,1,0:T(8,128)(2,1)S(1)} %reshape.97), channel_id=1, replica_groups=mesh['yh'=2,'core'=2,'yl'=2,'z'=8,'x'=4] {'z'}, dimensions={0} | all-to-all | bytes 737280 | tf_op jit(solution)/shard_map/all_to_all | solution.py:209
  90.5 0.7 subtract_convert_fusion
  91.3 0.7 subtract_convert_fusion.1
  92.2 0.8 broadcast_in_dim.10
  93.0 3.7 %all-to-all-start.1 = ((bf16[8,180,128]{2,1,0:T(8,128)(2,1)}), bf16[8,180,128]{2,1,0:T(8,128)(2,1)S(1)}, u32[]{:S(2)}, u32[]{:S(2)}) async-start(bf16[8,180,128]{2,1,0:T(8,128)(2,1)} %broadcast_in_dim.10), calls=%async_computation.1 | async-start | bytes 753664 | tf_op jit(solution)/shard_map/all_to_all | solution.py:216
  97.0 11.0 %all-to-all-done.1 = bf16[8,180,128]{2,1,0:T(8,128)(2,1)S(1)} async-done(((bf16[8,180,128]{2,1,0:T(8,128)(2,1)}), bf16[8,180,128]{2,1,0:T(8,128)(2,1)S(1)}, u32[]{:S(2)}, u32[]{:S(2)}) %all-to-all-start.1) | async-done | bytes 368672 | tf_op jit(solution)/shard_map/all_to_all | solution.py:216
  108.1 0.4 reshape.98
  108.6 5.6 %collective-permute-start.18 = (bf16[72,2560]{1,0:T(8,128)(2,1)S(1)}, bf16[72,2560]{1,0:T(8,128)(2,1)S(1)}, u32[]{:S(2)}, u32[]{:S(2)}) collective-permute-start(bf16[72,2560]{1,0:T(8,128)(2,1)S(1)} %reshape.98), channel_id=1, source_target_pairs={{0,32},{32,0},{1,33},{33,1},{2,34},{34,2},{3,35},{35,3},{4,36},{36... | collective-permute-start | bytes 1105928 | tf_op jit(solution)/shard_map/ppermute | solution.py:36
  114.3 2.8 %collective-permute-start.17 = (bf16[72,2560]{1,0:T(8,128)(2,1)S(1)}, bf16[72,2560]{1,0:T(8,128)(2,1)S(1)}, u32[]{:S(2)}, u32[]{:S(2)}) collective-permute-start(bf16[72,2560]{1,0:T(8,128)(2,1)S(1)} %reshape.98), channel_id=1, source_target_pairs={{0,3},{1,0},{2,1},{3,2},{4,7},{5,4},{6,5},{7,6},{8,11},{9,8},{10,9... | collective-permute-start | bytes 1105928 | tf_op jit(solution)/shard_map/ppermute | solution.py:28
  117.1 1.4 %collective-permute-start.19 = (bf16[72,2560]{1,0:T(8,128)(2,1)S(1)}, bf16[72,2560]{1,0:T(8,128)(2,1)S(1)}, u32[]{:S(2)}, u32[]{:S(2)}) collective-permute-start(bf16[72,2560]{1,0:T(8,128)(2,1)S(1)} %reshape.98), channel_id=1, source_target_pairs={{0,2},{1,3},{2,0},{3,1},{4,6},{5,7},{6,4},{7,5},{8,10},{9,11},{10,... | collective-permute-start | bytes 1105928 | tf_op jit(solution)/shard_map/ppermute | solution.py:28
  118.5 3.4 %collective-permute-done.18 = bf16[72,2560]{1,0:T(8,128)(2,1)S(1)} collective-permute-done((bf16[72,2560]{1,0:T(8,128)(2,1)S(1)}, bf16[72,2560]{1,0:T(8,128)(2,1)S(1)}, u32[]{:S(2)}, u32[]{:S(2)}) %collective-permute-start.18) | collective-permute-done | bytes 368672 | tf_op jit(solution)/shard_map/ppermute | solution.py:36
  121.9 2.6 %collective-permute-start.21 = (bf16[72,2560]{1,0:T(8,128)(2,1)S(1)}, bf16[72,2560]{1,0:T(8,128)(2,1)S(1)}, u32[]{:S(2)}, u32[]{:S(2)}) collective-permute-start(bf16[72,2560]{1,0:T(8,128)(2,1)S(1)} %collective-permute-done.18), channel_id=1, source_target_pairs={{0,3},{1,0},{2,1},{3,2},{4,7},{5,4},{6,5},{7,6},{8,11},{9,8},{10,9... | collective-permute-start | bytes 1105928 | tf_op jit(solution)/shard_map/ppermute | solution.py:28
  124.6 2.2 %collective-permute-done.17 = bf16[72,2560]{1,0:T(8,128)(2,1)S(1)} collective-permute-done((bf16[72,2560]{1,0:T(8,128)(2,1)S(1)}, bf16[72,2560]{1,0:T(8,128)(2,1)S(1)}, u32[]{:S(2)}, u32[]{:S(2)}) %collective-permute-start.17) | collective-permute-done | bytes 368672 | tf_op jit(solution)/shard_map/ppermute | solution.py:28
  127.2 1.7 %collective-permute-start.22 = (bf16[72,2560]{1,0:T(8,128)(2,1)S(1)}, bf16[72,2560]{1,0:T(8,128)(2,1)S(1)}, u32[]{:S(2)}, u32[]{:S(2)}) collective-permute-start(bf16[72,2560]{1,0:T(8,128)(2,1)S(1)} %collective-permute-done.19), channel_id=1, source_target_pairs={{0,32},{32,0},{1,33},{33,1},{2,34},{34,2},{3,35},{35,3},{4,36},{36... | collective-permute-start | bytes 1105928 | tf_op jit(solution)/shard_map/ppermute | solution.py:36
  129.0 0.7 convolution_convert_fusion.3
  129.7 1.2 convolution_convert_fusion.1
  130.9 3.8 %collective-permute-done.22 = bf16[72,2560]{1,0:T(8,128)(2,1)S(1)} collective-permute-done((bf16[72,2560]{1,0:T(8,128)(2,1)S(1)}, bf16[72,2560]{1,0:T(8,128)(2,1)S(1)}, u32[]{:S(2)}, u32[]{:S(2)}) %collective-permute-start.22) | collective-permute-done | bytes 368672 | tf_op jit(solution)/shard_map/ppermute | solution.py:36
  134.8 1.4 fusion.5
  136.2 2.0 %fusion.4 = bf16[384,2560]{1,0:T(8,128)(2,1)} fusion(bf16[384,2560]{1,0:T(8,128)(2,1)S(1)} %convolution_convert_fusion.1, bf16[384,216]{1,0:T(8,128)(2,1)S(1)} %fusion.17, bf16[216,2560]{1,0:T(8,128)(2,1)S(1)} %constant_dynamic-update-slice_fusion.5), kind=kOutput, calls=%fused_computation.8 | convolution fusion | flops 426639360 | bytes 5203968 | tf_op jit(solution)/shard_map/dot_general | solution.py:67
  (69 shorter events, 3.3 us)
Async XLA Ops:
  0.6 13.1 %collective-permute-start.1 = (bf16[768,2560]{1,0:T(8,128)(2,1)}, bf16[768,2560]{1,0:T(8,128)(2,1)}, u32[]{:S(2)}, u32[]{:S(2)}) collective-permute-start(bf16[768,2560]{1,0:T(8,128)(2,1)} %param.16), channel_id=1, source_target_pairs={{0,64},{64,0},{1,65},{65,1},{2,66},{66,2},{3,67},{67,3},{4,68},{68... | collective-permute-start | bytes 11796488 | tf_op jit(solution)/shard_map/ppermute | solution.py:40
  8.2 5.6 %collective-permute-start = (bf16[4,2,144,768]{3,2,1,0:T(8,128)(2,1)}, bf16[4,2,144,768]{3,2,1,0:T(8,128)(2,1)S(1)}, u32[]{:S(2)}, u32[]{:S(2)}) collective-permute-start(bf16[4,2,144,768]{3,2,1,0:T(8,128)(2,1)} %get-tuple-element.22), channel_id=1, source_target_pairs={{0,64},{64,0},{1,65},{65,1},{2,66},{66,2},{3,67},{67,3},{4,68},{68... | collective-permute-start | bytes 5308424 | tf_op jit(solution)/shard_map/ppermute | solution.py:40
  18.6 3.5 %copy-start.6 = (bf16[4,2,144,768]{3,2,1,0:T(8,128)(2,1)S(1)}, bf16[4,2,144,768]{3,2,1,0:T(8,128)(2,1)}, u32[]{:S(2)}) copy-start(bf16[4,2,144,768]{3,2,1,0:T(8,128)(2,1)} %get-tuple-element.21) | copy-start | bytes 5308420
  19.2 20.4 %collective-permute-start.2 = (f16[4,72,1408]{2,1,0:T(8,128)(2,1)S(1)}, f16[4,72,1408]{2,1,0:T(8,128)(2,1)S(1)}, u32[]{:S(2)}, u32[]{:S(2)}) collective-permute-start(f16[4,72,1408]{2,1,0:T(8,128)(2,1)S(1)} %get-tuple-element.42), channel_id=1, source_target_pairs={{0,3},{1,0},{2,1},{3,2},{4,7},{5,4},{6,5},{7,6},{8,11},{9,8},{10,9... | collective-permute-start | bytes 2433032 | tf_op jit(solution)/shard_map/ppermute | solution.py:28
  22.0 20.9 %collective-permute-start.3 = (f16[4,72,1408]{2,1,0:T(8,128)(2,1)S(1)}, f16[4,72,1408]{2,1,0:T(8,128)(2,1)S(1)}, u32[]{:S(2)}, u32[]{:S(2)}) collective-permute-start(f16[4,72,1408]{2,1,0:T(8,128)(2,1)S(1)} %get-tuple-element.43), channel_id=1, source_target_pairs={{0,1},{1,2},{2,3},{3,0},{4,5},{5,6},{6,7},{7,4},{8,9},{9,10},{10,1... | collective-permute-start | bytes 2433032 | tf_op jit(solution)/shard_map/ppermute | solution.py:28
  30.6 16.8 %collective-permute-start.10 = (f16[4,72,1152]{2,1,0:T(8,128)(2,1)S(1)}, f16[4,72,1152]{2,1,0:T(8,128)(2,1)S(1)}, u32[]{:S(2)}, u32[]{:S(2)}) collective-permute-start(f16[4,72,1152]{2,1,0:T(8,128)(2,1)S(1)} %get-tuple-element.46), channel_id=1, source_target_pairs={{0,32},{32,128},{128,160},{160,0},{1,33},{33,129},{129,161},{161,1... | collective-permute-start | bytes 1990664 | tf_op jit(solution)/shard_map/ppermute | solution.py:32
  32.1 16.8 %collective-permute-start.9 = (f16[4,72,1152]{2,1,0:T(8,128)(2,1)S(1)}, f16[4,72,1152]{2,1,0:T(8,128)(2,1)S(1)}, u32[]{:S(2)}, u32[]{:S(2)}) collective-permute-start(f16[4,72,1152]{2,1,0:T(8,128)(2,1)S(1)} %get-tuple-element.47), channel_id=1, source_target_pairs={{0,160},{32,0},{128,32},{160,128},{1,161},{33,1},{129,33},{161,129... | collective-permute-start | bytes 1990664 | tf_op jit(solution)/shard_map/ppermute | solution.py:32
  43.3 11.4 %collective-permute-start.4 = (f16[2,72,1408]{2,1,0:T(8,128)(2,1)S(1)}, f16[2,72,1408]{2,1,0:T(8,128)(2,1)S(1)}, u32[]{:S(2)}, u32[]{:S(2)}) collective-permute-start(f16[2,72,1408]{2,1,0:T(8,128)(2,1)S(1)} %get-tuple-element.45), channel_id=1, source_target_pairs={{0,1},{1,2},{2,3},{3,0},{4,5},{5,6},{6,7},{7,4},{8,9},{9,10},{10,1... | collective-permute-start | bytes 1216520 | tf_op jit(solution)/shard_map/ppermute | solution.py:28
  43.3 11.3 %collective-permute-start.5 = (f16[2,72,1408]{2,1,0:T(8,128)(2,1)S(1)}, f16[2,72,1408]{2,1,0:T(8,128)(2,1)S(1)}, u32[]{:S(2)}, u32[]{:S(2)}) collective-permute-start(f16[2,72,1408]{2,1,0:T(8,128)(2,1)S(1)} %get-tuple-element.44), channel_id=1, source_target_pairs={{0,3},{1,0},{2,1},{3,2},{4,7},{5,4},{6,5},{7,6},{8,11},{9,8},{10,9... | collective-permute-start | bytes 1216520 | tf_op jit(solution)/shard_map/ppermute | solution.py:28
  47.5 10.7 %collective-permute-start.11 = (f16[2,72,1152]{2,1,0:T(8,128)(2,1)S(1)}, f16[2,72,1152]{2,1,0:T(8,128)(2,1)S(1)}, u32[]{:S(2)}, u32[]{:S(2)}) collective-permute-start(f16[2,72,1152]{2,1,0:T(8,128)(2,1)S(1)} %fusion.15), channel_id=1, source_target_pairs={{0,32},{32,128},{128,160},{160,0},{1,33},{33,129},{129,161},{161,1... | collective-permute-start | bytes 995336 | tf_op jit(solution)/shard_map/ppermute | solution.py:32
  49.0 9.4 %collective-permute-start.12 = (f16[2,72,1152]{2,1,0:T(8,128)(2,1)S(1)}, f16[2,72,1152]{2,1,0:T(8,128)(2,1)S(1)}, u32[]{:S(2)}, u32[]{:S(2)}) collective-permute-start(f16[2,72,1152]{2,1,0:T(8,128)(2,1)S(1)} %fusion.14), channel_id=1, source_target_pairs={{0,160},{32,0},{128,32},{160,128},{1,161},{33,1},{129,33},{161,129... | collective-permute-start | bytes 995336 | tf_op jit(solution)/shard_map/ppermute | solution.py:32
  55.4 8.8 %collective-permute-start.6 = (f16[1,72,1408]{2,1,0:T(8,128)(2,1)S(1)}, f16[1,72,1408]{2,1,0:T(8,128)(2,1)S(1)}, u32[]{:S(2)}, u32[]{:S(2)}) collective-permute-start(f16[1,72,1408]{2,1,0:T(8,128)(2,1)S(1)} %get-tuple-element.52), channel_id=1, source_target_pairs={{0,128},{32,160},{128,0},{160,32},{1,129},{33,161},{129,1},{161,33... | collective-permute-start | bytes 608264 | tf_op jit(solution)/shard_map/ppermute | solution.py:32
  55.8 11.0 %collective-permute-start.7 = (f16[1,72,1408]{2,1,0:T(8,128)(2,1)S(1)}, f16[1,72,1408]{2,1,0:T(8,128)(2,1)S(1)}, u32[]{:S(2)}, u32[]{:S(2)}) collective-permute-start(f16[1,72,1408]{2,1,0:T(8,128)(2,1)S(1)} %get-tuple-element.51), channel_id=1, source_target_pairs={{0,32},{32,128},{128,160},{160,0},{1,33},{33,129},{129,161},{161,1... | collective-permute-start | bytes 608264 | tf_op jit(solution)/shard_map/ppermute | solution.py:32
  58.0 8.8 %collective-permute-start.8 = (f16[1,72,1408]{2,1,0:T(8,128)(2,1)S(1)}, f16[1,72,1408]{2,1,0:T(8,128)(2,1)S(1)}, u32[]{:S(2)}, u32[]{:S(2)}) collective-permute-start(f16[1,72,1408]{2,1,0:T(8,128)(2,1)S(1)} %get-tuple-element.50), channel_id=1, source_target_pairs={{0,160},{32,0},{128,32},{160,128},{1,161},{33,1},{129,33},{161,129... | collective-permute-start | bytes 608264 | tf_op jit(solution)/shard_map/ppermute | solution.py:32
  59.0 7.9 %collective-permute-start.13 = (f16[1,72,1152]{2,1,0:T(8,128)(2,1)S(1)}, f16[1,72,1152]{2,1,0:T(8,128)(2,1)S(1)}, u32[]{:S(2)}, u32[]{:S(2)}) collective-permute-start(f16[1,72,1152]{2,1,0:T(8,128)(2,1)S(1)} %get-tuple-element.53), channel_id=1, source_target_pairs={{0,2},{1,3},{2,0},{3,1},{4,6},{5,7},{6,4},{7,5},{8,10},{9,11},{10,... | collective-permute-start | bytes 497672 | tf_op jit(solution)/shard_map/ppermute | solution.py:28
  60.8 6.9 %collective-permute-start.14 = (f16[1,72,1152]{2,1,0:T(8,128)(2,1)S(1)}, f16[1,72,1152]{2,1,0:T(8,128)(2,1)S(1)}, u32[]{:S(2)}, u32[]{:S(2)}) collective-permute-start(f16[1,72,1152]{2,1,0:T(8,128)(2,1)S(1)} %get-tuple-element.55), channel_id=1, source_target_pairs={{0,1},{1,2},{2,3},{3,0},{4,5},{5,6},{6,7},{7,4},{8,9},{9,10},{10,1... | collective-permute-start | bytes 497672 | tf_op jit(solution)/shard_map/ppermute | solution.py:28
  64.1 5.5 %collective-permute-start.15 = (f16[1,72,1152]{2,1,0:T(8,128)(2,1)S(1)}, f16[1,72,1152]{2,1,0:T(8,128)(2,1)S(1)}, u32[]{:S(2)}, u32[]{:S(2)}) collective-permute-start(f16[1,72,1152]{2,1,0:T(8,128)(2,1)S(1)} %get-tuple-element.54), channel_id=1, source_target_pairs={{0,3},{1,0},{2,1},{3,2},{4,7},{5,4},{6,5},{7,6},{8,11},{9,8},{10,9... | collective-permute-start | bytes 497672 | tf_op jit(solution)/shard_map/ppermute | solution.py:28
  69.7 20.8 %copy-start = (f32[6,2560]{1,0:T(8,128)S(1)}, f32[6,2560]{1,0:T(8,128)}, u32[]{:S(2)}) copy-start(f32[6,2560]{1,0:T(8,128)} %param.19) | copy-start | bytes 184324
  69.8 20.8 %copy-start.1 = (f32[6,2560]{1,0:T(8,128)S(1)}, f32[6,2560]{1,0:T(8,128)}, u32[]{:S(2)}) copy-start(f32[6,2560]{1,0:T(8,128)} %param.21) | copy-start | bytes 184324
  69.8 20.8 %copy-start.2 = (f32[6,2560]{1,0:T(8,128)S(1)}, f32[6,2560]{1,0:T(8,128)}, u32[]{:S(2)}) copy-start(f32[6,2560]{1,0:T(8,128)} %param.20) | copy-start | bytes 184324
  69.8 21.5 %copy-start.3 = (f32[3,2560]{1,0:T(4,128)S(1)}, f32[3,2560]{1,0:T(4,128)}, u32[]{:S(2)}) copy-start(f32[3,2560]{1,0:T(4,128)} %param.22) | copy-start | bytes 92164
  69.8 21.5 %copy-start.4 = (f32[3,2560]{1,0:T(4,128)S(1)}, f32[3,2560]{1,0:T(4,128)}, u32[]{:S(2)}) copy-start(f32[3,2560]{1,0:T(4,128)} %param.24) | copy-start | bytes 92164
  69.8 21.5 %copy-start.5 = (f32[3,2560]{1,0:T(4,128)S(1)}, f32[3,2560]{1,0:T(4,128)}, u32[]{:S(2)}) copy-start(f32[3,2560]{1,0:T(4,128)} %param.23) | copy-start | bytes 92164
  93.0 15.1 %all-to-all-start.1 = ((bf16[8,180,128]{2,1,0:T(8,128)(2,1)}), bf16[8,180,128]{2,1,0:T(8,128)(2,1)S(1)}, u32[]{:S(2)}, u32[]{:S(2)}) async-start(bf16[8,180,128]{2,1,0:T(8,128)(2,1)} %broadcast_in_dim.10), calls=%async_computation.1 | async-start | bytes 753664 | tf_op jit(solution)/shard_map/all_to_all | solution.py:216
  108.5 16.0 %collective-permute-start.16 = (bf16[72,2560]{1,0:T(8,128)(2,1)S(1)}, bf16[72,2560]{1,0:T(8,128)(2,1)S(1)}, u32[]{:S(2)}, u32[]{:S(2)}) collective-permute-start(bf16[72,2560]{1,0:T(8,128)(2,1)S(1)} %reshape.98), channel_id=1, source_target_pairs={{0,1},{1,2},{2,3},{3,0},{4,5},{5,6},{6,7},{7,4},{8,9},{9,10},{10,1... | collective-permute-start | bytes 1105928 | tf_op jit(solution)/shard_map/ppermute | solution.py:28
  108.6 13.3 %collective-permute-start.18 = (bf16[72,2560]{1,0:T(8,128)(2,1)S(1)}, bf16[72,2560]{1,0:T(8,128)(2,1)S(1)}, u32[]{:S(2)}, u32[]{:S(2)}) collective-permute-start(bf16[72,2560]{1,0:T(8,128)(2,1)S(1)} %reshape.98), channel_id=1, source_target_pairs={{0,32},{32,0},{1,33},{33,1},{2,34},{34,2},{3,35},{35,3},{4,36},{36... | collective-permute-start | bytes 1105928 | tf_op jit(solution)/shard_map/ppermute | solution.py:36
  114.3 12.5 %collective-permute-start.17 = (bf16[72,2560]{1,0:T(8,128)(2,1)S(1)}, bf16[72,2560]{1,0:T(8,128)(2,1)S(1)}, u32[]{:S(2)}, u32[]{:S(2)}) collective-permute-start(bf16[72,2560]{1,0:T(8,128)(2,1)S(1)} %reshape.98), channel_id=1, source_target_pairs={{0,3},{1,0},{2,1},{3,2},{4,7},{5,4},{6,5},{7,6},{8,11},{9,8},{10,9... | collective-permute-start | bytes 1105928 | tf_op jit(solution)/shard_map/ppermute | solution.py:28
  117.1 10.1 %collective-permute-start.19 = (bf16[72,2560]{1,0:T(8,128)(2,1)S(1)}, bf16[72,2560]{1,0:T(8,128)(2,1)S(1)}, u32[]{:S(2)}, u32[]{:S(2)}) collective-permute-start(bf16[72,2560]{1,0:T(8,128)(2,1)S(1)} %reshape.98), channel_id=1, source_target_pairs={{0,2},{1,3},{2,0},{3,1},{4,6},{5,7},{6,4},{7,5},{8,10},{9,11},{10,... | collective-permute-start | bytes 1105928 | tf_op jit(solution)/shard_map/ppermute | solution.py:28
  121.9 12.8 %collective-permute-start.21 = (bf16[72,2560]{1,0:T(8,128)(2,1)S(1)}, bf16[72,2560]{1,0:T(8,128)(2,1)S(1)}, u32[]{:S(2)}, u32[]{:S(2)}) collective-permute-start(bf16[72,2560]{1,0:T(8,128)(2,1)S(1)} %collective-permute-done.18), channel_id=1, source_target_pairs={{0,3},{1,0},{2,1},{3,2},{4,7},{5,4},{6,5},{7,6},{8,11},{9,8},{10,9... | collective-permute-start | bytes 1105928 | tf_op jit(solution)/shard_map/ppermute | solution.py:28
  124.5 10.2 %collective-permute-start.20 = (bf16[72,2560]{1,0:T(8,128)(2,1)S(1)}, bf16[72,2560]{1,0:T(8,128)(2,1)S(1)}, u32[]{:S(2)}, u32[]{:S(2)}) collective-permute-start(bf16[72,2560]{1,0:T(8,128)(2,1)S(1)} %collective-permute-done.18), channel_id=1, source_target_pairs={{0,1},{1,2},{2,3},{3,0},{4,5},{5,6},{6,7},{7,4},{8,9},{9,10},{10,1... | collective-permute-start | bytes 1105928 | tf_op jit(solution)/shard_map/ppermute | solution.py:28
  127.2 7.5 %collective-permute-start.22 = (bf16[72,2560]{1,0:T(8,128)(2,1)S(1)}, bf16[72,2560]{1,0:T(8,128)(2,1)S(1)}, u32[]{:S(2)}, u32[]{:S(2)}) collective-permute-start(bf16[72,2560]{1,0:T(8,128)(2,1)S(1)} %collective-permute-done.19), channel_id=1, source_target_pairs={{0,32},{32,0},{1,33},{33,1},{2,34},{34,2},{3,35},{35,3},{4,36},{36... | collective-permute-start | bytes 1105928 | tf_op jit(solution)/shard_map/ppermute | solution.py:36

commit v10 on v9

--- a/solution.py
+++ b/solution.py
@@ -215,11 +215,11 @@
     weight = jnp.concatenate([weight_s, weight_r], axis=0).reshape(1, rows * width // 128, 128)
     weight = lax.all_to_all(jnp.broadcast_to(weight, (NZ,) + weight.shape[1:]), "z", 0, 0)
     mine = weight.reshape(group, width)
+    mine_two = x_ring(mine, 2)
     mine_plus, mine_minus = x_ring(mine, 1), x_ring(mine, 3)
-    other = y_swap(mine)
-    mine_two = x_ring(mine, 2)
-    other_plus, other_minus = x_ring(other, 1), x_ring(other, 3)
     other_two = y_swap(mine_two)
+    other = after([mine_two], y_swap(mine))
+    other_plus, other_minus = (after([other_two], x_ring(other, d)) for d in (1, 3))
     early = jnp.concatenate([mine, mine_plus, mine_minus, other, mine_two], axis=0)
     late = [other_plus, other_minus, other_two]
     slot = jnp.array([0, 1, 4, 2, 3, 5, 7, 6], jnp.int32)

time: 141 us -> 141 us (level); the launches traced: 138 us -> 141 us
  waiting for transfers between devices: 40.9 us -> 44.3 us
    ppermute x12, waiting for transfers between devices: 20 us -> 24.4 us  [x_ring(): return lax.ppermute(v, 'x', [(i, (i + d) % NX) for i in range(NX)])]
where the time goes in v10:
time: 141 us
  waiting for transfers between devices  44.3 us (31%)
  starting transfers between devices  37.5 us (27%)
  matrix products  23.1 us (16%)
  blocking collectives  20 us (14%)
  Pallas kernels  6.79 us (5%)
  other arithmetic  5.23 us (4%)
  local copies, waits for them, and re-layouts  2.31 us (2%)
  between operations  1.69 us (1%)
    ppermute x12, waiting for transfers between devices, x_ring(): return lax.ppermute(v, 'x', [(i, (i + d) % NX) for i in range(NX)])  24.4 us
    dot_general x8, matrix products, dot(): return jnp.dot(a, b, preferred_element_type=F32)  23.1 us
    all_to_all x1, blocking collectives, local(): last = lax.all_to_all(last, 'z', 0, 0)  20 us
    ppermute x12, starting transfers between devices, x_ring(): return lax.ppermute(v, 'x', [(i, (i + d) % NX) for i in range(NX)])  19.7 us
    all_to_all x1, waiting for transfers between devices, local(): lax.all_to_all(jnp.broadcast_to(weight, (NZ,) + weight.shape[1:]), 'z', 0...  11 us
    ppermute x7, starting transfers between devices, y_ring(): return lax.ppermute(v, ('yh', 'yl'), [(i, (i + d) % NY) for i in range(NY)])  7.3 us
    pallas_call x1, Pallas kernels, ordered(): pl.pallas_call(order_kernel, grid_spec=pltpu.PrefetchScalarGridSpec(num_s...  6.79 us
    ppermute x2, starting transfers between devices, y_swap(): return lax.ppermute(v, 'yl', [(0, 1), (1, 0)])  6.27 us
  transfers between devices with their start and end apart: 24, of which 13 were waited for; matrix products, arithmetic and copies ran while one was open for 13% of the time, Pallas kernels for 5%

profile of v10, /device:TPU:16, one launch (start us, length us, event | category | flops | bytes accessed | tf_op | source)
XLA Modules:
  0.0 140.9 jit_solution(2540465201667171405)
XLA Ops:
  1.4 6.8 %shard_map.181 = (bf16[4,2,144,768]{3,2,1,0:T(8,128)(2,1)}, bf16[4,2,144,768]{3,2,1,0:T(8,128)(2,1)}) custom-call(s32[1]{0:T(128)} %bitcast.core_ref, s32[1]{0:T(128)S(6)} %copy.35.count_ref, s32[1,96]{1,0:T(1,128)} %bitcast.78, bf16[768,1536]{1,0:T(8,128)(2,1)} %shared_ref.1, bf16[96,768]{1,0:T(8,128)(2,1)} %routed_ref.1, ...), custom_call_target="tpu_custom_call" | custom-call | flops 2717908992 | bytes 8847360 | tf_op jit(solution)/shard_map/pallas_call | solution.py:101
  8.2 0.5 collective-permute-start
  8.7 5.1 %fusion.7 = f32[1152,1408]{1,0:T(8,128)S(1)} fusion(bf16[1152,768]{1,0:T(8,128)(2,1)} %bitcast.79, bf16[768,2560]{1,0:T(8,128)(2,1)} %param.16), kind=kOutput, calls=%fused_computation.13 | convolution fusion | flops 2491416576 | bytes 10420224 | tf_op jit(solution)/shard_map/dot_general | solution.py:67
  13.8 4.8 %fusion.3 = f16[1152,1408]{1,0:T(8,128)(2,1)S(1)} fusion(f32[1152,1408]{1,0:T(8,128)S(1)} %fusion.7, bf16[1152,768]{1,0:T(8,128)(2,1)S(1)} %bitcast.76, bf16[768,2560]{1,0:T(8,128)(2,1)} %collective-permute-done.1), kind=kOutput, calls=%fused_computation.5 | convolution fusion | flops 2496282624 | bytes 13664256 | tf_op jit(solution)/shard_map/dot_general | solution.py:67
  18.6 0.6 bitcast_select_fusion.1
  19.2 2.8 %collective-permute-start.2 = (f16[4,72,1408]{2,1,0:T(8,128)(2,1)S(1)}, f16[4,72,1408]{2,1,0:T(8,128)(2,1)S(1)}, u32[]{:S(2)}, u32[]{:S(2)}) collective-permute-start(f16[4,72,1408]{2,1,0:T(8,128)(2,1)S(1)} %get-tuple-element.48), channel_id=1, source_target_pairs={{0,3},{1,0},{2,1},{3,2},{4,7},{5,4},{6,5},{7,6},{8,11},{9,8},{10,9... | collective-permute-start | bytes 2433032 | tf_op jit(solution)/shard_map/ppermute | solution.py:28
  22.0 4.0 %fusion.10 = f32[1152,1152]{1,0:T(8,128)S(1)} fusion(bf16[1152,768]{1,0:T(8,128)(2,1)S(1)} %bitcast.80, bf16[768,2560]{1,0:T(8,128)(2,1)} %param.16), kind=kOutput, calls=%fused_computation.16 | convolution fusion | flops 2038431744 | bytes 8847360 | tf_op jit(solution)/shard_map/dot_general | solution.py:67
  26.0 4.0 %fusion.2 = f16[1152,1152]{1,0:T(8,128)(2,1)S(1)} fusion(f32[1152,1152]{1,0:T(8,128)S(1)} %fusion.10, bf16[1152,768]{1,0:T(8,128)(2,1)S(1)} %bitcast.77, bf16[768,2560]{1,0:T(8,128)(2,1)} %collective-permute-done.1), kind=kOutput, calls=%fused_computation.4 | convolution fusion | flops 2042413056 | bytes 11501568 | tf_op jit(solution)/shard_map/dot_general | solution.py:67
  30.1 0.5 bitcast_select_fusion.2
  30.6 1.5 %collective-permute-start.10 = (f16[4,72,1152]{2,1,0:T(8,128)(2,1)S(1)}, f16[4,72,1152]{2,1,0:T(8,128)(2,1)S(1)}, u32[]{:S(2)}, u32[]{:S(2)}) collective-permute-start(f16[4,72,1152]{2,1,0:T(8,128)(2,1)S(1)} %get-tuple-element.52), channel_id=1, source_target_pairs={{0,32},{32,128},{128,160},{160,0},{1,33},{33,129},{129,161},{161,1... | collective-permute-start | bytes 1990664 | tf_op jit(solution)/shard_map/ppermute | solution.py:32
  32.1 0.7 collective-permute-start.9
  33.1 6.4 %collective-permute-done.2 = f16[4,72,1408]{2,1,0:T(8,128)(2,1)S(1)} collective-permute-done((f16[4,72,1408]{2,1,0:T(8,128)(2,1)S(1)}, f16[4,72,1408]{2,1,0:T(8,128)(2,1)S(1)}, u32[]{:S(2)}, u32[]{:S(2)}) %collective-permute-start.2) | collective-permute-done | bytes 811040 | tf_op jit(solution)/shard_map/ppermute | solution.py:28
  39.6 3.4 %collective-permute-done.3 = f16[4,72,1408]{2,1,0:T(8,128)(2,1)S(1)} collective-permute-done((f16[4,72,1408]{2,1,0:T(8,128)(2,1)S(1)}, f16[4,72,1408]{2,1,0:T(8,128)(2,1)S(1)}, u32[]{:S(2)}, u32[]{:S(2)}) %collective-permute-start.3) | collective-permute-done | bytes 811040 | tf_op jit(solution)/shard_map/ppermute | solution.py:28
  43.3 3.2 %collective-permute-start.5 = (f16[2,72,1408]{2,1,0:T(8,128)(2,1)S(1)}, f16[2,72,1408]{2,1,0:T(8,128)(2,1)S(1)}, u32[]{:S(2)}, u32[]{:S(2)}) collective-permute-start(f16[2,72,1408]{2,1,0:T(8,128)(2,1)S(1)} %get-tuple-element.50), channel_id=1, source_target_pairs={{0,3},{1,0},{2,1},{3,2},{4,7},{5,4},{6,5},{7,6},{8,11},{9,8},{10,9... | collective-permute-start | bytes 1216520 | tf_op jit(solution)/shard_map/ppermute | solution.py:28
  46.6 0.9 collective-permute-done.10
  47.5 1.4 collective-permute-start.11
  49.0 0.8 collective-permute-start.12
  49.8 4.9 %collective-permute-done.4 = f16[2,72,1408]{2,1,0:T(8,128)(2,1)S(1)} collective-permute-done((f16[2,72,1408]{2,1,0:T(8,128)(2,1)S(1)}, f16[2,72,1408]{2,1,0:T(8,128)(2,1)S(1)}, u32[]{:S(2)}, u32[]{:S(2)}) %collective-permute-start.4) | collective-permute-done | bytes 405536 | tf_op jit(solution)/shard_map/ppermute | solution.py:28
  54.7 0.6 convert_add_fusion
  55.8 2.2 %collective-permute-start.7 = (f16[1,72,1408]{2,1,0:T(8,128)(2,1)S(1)}, f16[1,72,1408]{2,1,0:T(8,128)(2,1)S(1)}, u32[]{:S(2)}, u32[]{:S(2)}) collective-permute-start(f16[1,72,1408]{2,1,0:T(8,128)(2,1)S(1)} %get-tuple-element.57), channel_id=1, source_target_pairs={{0,32},{32,128},{128,160},{160,0},{1,33},{33,129},{129,161},{161,1... | collective-permute-start | bytes 608264 | tf_op jit(solution)/shard_map/ppermute | solution.py:32
  58.4 0.5 convert_add_fusion.1
  59.0 1.8 %collective-permute-start.13 = (f16[1,72,1152]{2,1,0:T(8,128)(2,1)S(1)}, f16[1,72,1152]{2,1,0:T(8,128)(2,1)S(1)}, u32[]{:S(2)}, u32[]{:S(2)}) collective-permute-start(f16[1,72,1152]{2,1,0:T(8,128)(2,1)S(1)} %get-tuple-element.59), channel_id=1, source_target_pairs={{0,2},{1,3},{2,0},{3,1},{4,6},{5,7},{6,4},{7,5},{8,10},{9,11},{10,... | collective-permute-start | bytes 497672 | tf_op jit(solution)/shard_map/ppermute | solution.py:28
  60.8 1.8 %collective-permute-start.14 = (f16[1,72,1152]{2,1,0:T(8,128)(2,1)S(1)}, f16[1,72,1152]{2,1,0:T(8,128)(2,1)S(1)}, u32[]{:S(2)}, u32[]{:S(2)}) collective-permute-start(f16[1,72,1152]{2,1,0:T(8,128)(2,1)S(1)} %get-tuple-element.61), channel_id=1, source_target_pairs={{0,1},{1,2},{2,3},{3,0},{4,5},{5,6},{6,7},{7,4},{8,9},{9,10},{10,1... | collective-permute-start | bytes 497672 | tf_op jit(solution)/shard_map/ppermute | solution.py:28
  62.6 1.5 %collective-permute-done.6 = f16[1,72,1408]{2,1,0:T(8,128)(2,1)S(1)} collective-permute-done((f16[1,72,1408]{2,1,0:T(8,128)(2,1)S(1)}, f16[1,72,1408]{2,1,0:T(8,128)(2,1)S(1)}, u32[]{:S(2)}, u32[]{:S(2)}) %collective-permute-start.6) | collective-permute-done | bytes 202784 | tf_op jit(solution)/shard_map/ppermute | solution.py:32
  64.1 2.6 %collective-permute-start.15 = (f16[1,72,1152]{2,1,0:T(8,128)(2,1)S(1)}, f16[1,72,1152]{2,1,0:T(8,128)(2,1)S(1)}, u32[]{:S(2)}, u32[]{:S(2)}) collective-permute-start(f16[1,72,1152]{2,1,0:T(8,128)(2,1)S(1)} %get-tuple-element.60), channel_id=1, source_target_pairs={{0,3},{1,0},{2,1},{3,2},{4,7},{5,4},{6,5},{7,6},{8,11},{9,8},{10,9... | collective-permute-start | bytes 497672 | tf_op jit(solution)/shard_map/ppermute | solution.py:28
  66.9 0.8 collective-permute-done.14
  67.7 1.9 %collective-permute-done.15 = f16[1,72,1152]{2,1,0:T(8,128)(2,1)S(1)} collective-permute-done((f16[1,72,1152]{2,1,0:T(8,128)(2,1)S(1)}, f16[1,72,1152]{2,1,0:T(8,128)(2,1)S(1)}, u32[]{:S(2)}, u32[]{:S(2)}) %collective-permute-start.15) | collective-permute-done | bytes 165920 | tf_op jit(solution)/shard_map/ppermute | solution.py:28
  69.9 0.5 reshape.97
  70.4 20.0 %all_to_all.10 = f16[8,180,128]{2,1,0:T(8,128)(2,1)S(1)} all-to-all(f16[8,180,128]{2,1,0:T(8,128)(2,1)S(1)} %reshape.97), channel_id=1, replica_groups=mesh['yh'=2,'core'=2,'yl'=2,'z'=8,'x'=4] {'z'}, dimensions={0} | all-to-all | bytes 737280 | tf_op jit(solution)/shard_map/all_to_all | solution.py:209
  90.5 0.7 subtract_convert_fusion
  91.3 0.7 subtract_convert_fusion.1
  92.2 0.8 broadcast_in_dim.10
  93.0 3.7 %all-to-all-start.1 = ((bf16[8,180,128]{2,1,0:T(8,128)(2,1)}), bf16[8,180,128]{2,1,0:T(8,128)(2,1)S(1)}, u32[]{:S(2)}, u32[]{:S(2)}) async-start(bf16[8,180,128]{2,1,0:T(8,128)(2,1)} %broadcast_in_dim.10), calls=%async_computation.1 | async-start | bytes 753664 | tf_op jit(solution)/shard_map/all_to_all | solution.py:216
  97.0 11.0 %all-to-all-done.1 = bf16[8,180,128]{2,1,0:T(8,128)(2,1)S(1)} async-done(((bf16[8,180,128]{2,1,0:T(8,128)(2,1)}), bf16[8,180,128]{2,1,0:T(8,128)(2,1)S(1)}, u32[]{:S(2)}, u32[]{:S(2)}) %all-to-all-start.1) | async-done | bytes 368672 | tf_op jit(solution)/shard_map/all_to_all | solution.py:216
  108.5 5.1 %collective-permute-start.18 = (bf16[72,2560]{1,0:T(8,128)(2,1)S(1)}, bf16[72,2560]{1,0:T(8,128)(2,1)S(1)}, u32[]{:S(2)}, u32[]{:S(2)}) collective-permute-start(bf16[72,2560]{1,0:T(8,128)(2,1)S(1)} %reshape.98), channel_id=1, source_target_pairs={{0,32},{32,0},{1,33},{33,1},{2,34},{34,2},{3,35},{35,3},{4,36},{36... | collective-permute-start | bytes 1105928 | tf_op jit(solution)/shard_map/ppermute | solution.py:36
  113.7 1.9 %collective-permute-start.19 = (bf16[72,2560]{1,0:T(8,128)(2,1)S(1)}, bf16[72,2560]{1,0:T(8,128)(2,1)S(1)}, u32[]{:S(2)}, u32[]{:S(2)}) collective-permute-start(bf16[72,2560]{1,0:T(8,128)(2,1)S(1)} %reshape.98), channel_id=1, source_target_pairs={{0,2},{1,3},{2,0},{3,1},{4,6},{5,7},{6,4},{7,5},{8,10},{9,11},{10,... | collective-permute-start | bytes 1105928 | tf_op jit(solution)/shard_map/ppermute | solution.py:28
  115.6 2.0 %collective-permute-start.16 = (bf16[72,2560]{1,0:T(8,128)(2,1)S(1)}, bf16[72,2560]{1,0:T(8,128)(2,1)S(1)}, u32[]{:S(2)}, u32[]{:S(2)}) collective-permute-start(bf16[72,2560]{1,0:T(8,128)(2,1)S(1)} %reshape.98), channel_id=1, source_target_pairs={{0,1},{1,2},{2,3},{3,0},{4,5},{5,6},{6,7},{7,4},{8,9},{9,10},{10,1... | collective-permute-start | bytes 1105928 | tf_op jit(solution)/shard_map/ppermute | solution.py:28
  117.7 1.3 collective-permute-start.17
  119.0 1.7 %collective-permute-done.18 = bf16[72,2560]{1,0:T(8,128)(2,1)S(1)} collective-permute-done((bf16[72,2560]{1,0:T(8,128)(2,1)S(1)}, bf16[72,2560]{1,0:T(8,128)(2,1)S(1)}, u32[]{:S(2)}, u32[]{:S(2)}) %collective-permute-start.18) | collective-permute-done | bytes 368672 | tf_op jit(solution)/shard_map/ppermute | solution.py:36
  120.7 3.7 %collective-permute-done.19 = bf16[72,2560]{1,0:T(8,128)(2,1)S(1)} collective-permute-done((bf16[72,2560]{1,0:T(8,128)(2,1)S(1)}, bf16[72,2560]{1,0:T(8,128)(2,1)S(1)}, u32[]{:S(2)}, u32[]{:S(2)}) %collective-permute-start.19) | collective-permute-done | bytes 368672 | tf_op jit(solution)/shard_map/ppermute | solution.py:28
  124.4 2.0 %collective-permute-start.22 = (bf16[72,2560]{1,0:T(8,128)(2,1)S(1)}, bf16[72,2560]{1,0:T(8,128)(2,1)S(1)}, u32[]{:S(2)}, u32[]{:S(2)}) collective-permute-start(bf16[72,2560]{1,0:T(8,128)(2,1)S(1)} %collective-permute-done.18), channel_id=1, source_target_pairs={{0,3},{1,0},{2,1},{3,2},{4,7},{5,4},{6,5},{7,6},{8,11},{9,8},{10,9... | collective-permute-start | bytes 1105928 | tf_op jit(solution)/shard_map/ppermute | solution.py:28
  126.4 3.3 %collective-permute-done.16 = bf16[72,2560]{1,0:T(8,128)(2,1)S(1)} collective-permute-done((bf16[72,2560]{1,0:T(8,128)(2,1)S(1)}, bf16[72,2560]{1,0:T(8,128)(2,1)S(1)}, u32[]{:S(2)}, u32[]{:S(2)}) %collective-permute-start.16) | collective-permute-done | bytes 368672 | tf_op jit(solution)/shard_map/ppermute | solution.py:28
  129.8 1.1 collective-permute-start.21
  131.0 0.7 convolution_convert_fusion.3
  131.7 1.2 convolution_convert_fusion.1
  132.9 4.5 %collective-permute-done.21 = bf16[72,2560]{1,0:T(8,128)(2,1)S(1)} collective-permute-done((bf16[72,2560]{1,0:T(8,128)(2,1)S(1)}, bf16[72,2560]{1,0:T(8,128)(2,1)S(1)}, u32[]{:S(2)}, u32[]{:S(2)}) %collective-permute-start.21) | collective-permute-done | bytes 368672 | tf_op jit(solution)/shard_map/ppermute | solution.py:36
  137.5 1.4 fusion.5
  138.9 2.0 %fusion.4 = bf16[384,2560]{1,0:T(8,128)(2,1)} fusion(bf16[384,2560]{1,0:T(8,128)(2,1)S(1)} %convolution_convert_fusion.1, bf16[384,216]{1,0:T(8,128)(2,1)S(1)} %fusion.17, bf16[216,2560]{1,0:T(8,128)(2,1)S(1)} %constant_dynamic-update-slice_fusion.5), kind=kOutput, calls=%fused_computation.8 | convolution fusion | flops 426639360 | bytes 5203968 | tf_op jit(solution)/shard_map/dot_general | solution.py:67
  (69 shorter events, 3.7 us)
Async XLA Ops:
  0.6 13.1 %collective-permute-start.1 = (bf16[768,2560]{1,0:T(8,128)(2,1)}, bf16[768,2560]{1,0:T(8,128)(2,1)}, u32[]{:S(2)}, u32[]{:S(2)}) collective-permute-start(bf16[768,2560]{1,0:T(8,128)(2,1)} %param.16), channel_id=1, source_target_pairs={{0,64},{64,0},{1,65},{65,1},{2,66},{66,2},{3,67},{67,3},{4,68},{68... | collective-permute-start | bytes 11796488 | tf_op jit(solution)/shard_map/ppermute | solution.py:40
  8.2 5.6 %collective-permute-start = (bf16[4,2,144,768]{3,2,1,0:T(8,128)(2,1)}, bf16[4,2,144,768]{3,2,1,0:T(8,128)(2,1)S(1)}, u32[]{:S(2)}, u32[]{:S(2)}) collective-permute-start(bf16[4,2,144,768]{3,2,1,0:T(8,128)(2,1)} %get-tuple-element.25), channel_id=1, source_target_pairs={{0,64},{64,0},{1,65},{65,1},{2,66},{66,2},{3,67},{67,3},{4,68},{68... | collective-permute-start | bytes 5308424 | tf_op jit(solution)/shard_map/ppermute | solution.py:40
  18.6 3.5 %copy-start.6 = (bf16[4,2,144,768]{3,2,1,0:T(8,128)(2,1)S(1)}, bf16[4,2,144,768]{3,2,1,0:T(8,128)(2,1)}, u32[]{:S(2)}) copy-start(bf16[4,2,144,768]{3,2,1,0:T(8,128)(2,1)} %get-tuple-element.24) | copy-start | bytes 5308420
  19.2 20.4 %collective-permute-start.2 = (f16[4,72,1408]{2,1,0:T(8,128)(2,1)S(1)}, f16[4,72,1408]{2,1,0:T(8,128)(2,1)S(1)}, u32[]{:S(2)}, u32[]{:S(2)}) collective-permute-start(f16[4,72,1408]{2,1,0:T(8,128)(2,1)S(1)} %get-tuple-element.48), channel_id=1, source_target_pairs={{0,3},{1,0},{2,1},{3,2},{4,7},{5,4},{6,5},{7,6},{8,11},{9,8},{10,9... | collective-permute-start | bytes 2433032 | tf_op jit(solution)/shard_map/ppermute | solution.py:28
  22.0 20.9 %collective-permute-start.3 = (f16[4,72,1408]{2,1,0:T(8,128)(2,1)S(1)}, f16[4,72,1408]{2,1,0:T(8,128)(2,1)S(1)}, u32[]{:S(2)}, u32[]{:S(2)}) collective-permute-start(f16[4,72,1408]{2,1,0:T(8,128)(2,1)S(1)} %get-tuple-element.49), channel_id=1, source_target_pairs={{0,1},{1,2},{2,3},{3,0},{4,5},{5,6},{6,7},{7,4},{8,9},{9,10},{10,1... | collective-permute-start | bytes 2433032 | tf_op jit(solution)/shard_map/ppermute | solution.py:28
  30.6 16.8 %collective-permute-start.10 = (f16[4,72,1152]{2,1,0:T(8,128)(2,1)S(1)}, f16[4,72,1152]{2,1,0:T(8,128)(2,1)S(1)}, u32[]{:S(2)}, u32[]{:S(2)}) collective-permute-start(f16[4,72,1152]{2,1,0:T(8,128)(2,1)S(1)} %get-tuple-element.52), channel_id=1, source_target_pairs={{0,32},{32,128},{128,160},{160,0},{1,33},{33,129},{129,161},{161,1... | collective-permute-start | bytes 1990664 | tf_op jit(solution)/shard_map/ppermute | solution.py:32
  32.1 16.8 %collective-permute-start.9 = (f16[4,72,1152]{2,1,0:T(8,128)(2,1)S(1)}, f16[4,72,1152]{2,1,0:T(8,128)(2,1)S(1)}, u32[]{:S(2)}, u32[]{:S(2)}) collective-permute-start(f16[4,72,1152]{2,1,0:T(8,128)(2,1)S(1)} %get-tuple-element.53), channel_id=1, source_target_pairs={{0,160},{32,0},{128,32},{160,128},{1,161},{33,1},{129,33},{161,129... | collective-permute-start | bytes 1990664 | tf_op jit(solution)/shard_map/ppermute | solution.py:32
  43.3 11.4 %collective-permute-start.4 = (f16[2,72,1408]{2,1,0:T(8,128)(2,1)S(1)}, f16[2,72,1408]{2,1,0:T(8,128)(2,1)S(1)}, u32[]{:S(2)}, u32[]{:S(2)}) collective-permute-start(f16[2,72,1408]{2,1,0:T(8,128)(2,1)S(1)} %get-tuple-element.51), channel_id=1, source_target_pairs={{0,1},{1,2},{2,3},{3,0},{4,5},{5,6},{6,7},{7,4},{8,9},{9,10},{10,1... | collective-permute-start | bytes 1216520 | tf_op jit(solution)/shard_map/ppermute | solution.py:28
  43.3 11.3 %collective-permute-start.5 = (f16[2,72,1408]{2,1,0:T(8,128)(2,1)S(1)}, f16[2,72,1408]{2,1,0:T(8,128)(2,1)S(1)}, u32[]{:S(2)}, u32[]{:S(2)}) collective-permute-start(f16[2,72,1408]{2,1,0:T(8,128)(2,1)S(1)} %get-tuple-element.50), channel_id=1, source_target_pairs={{0,3},{1,0},{2,1},{3,2},{4,7},{5,4},{6,5},{7,6},{8,11},{9,8},{10,9... | collective-permute-start | bytes 1216520 | tf_op jit(solution)/shard_map/ppermute | solution.py:28
  47.5 10.7 %collective-permute-start.11 = (f16[2,72,1152]{2,1,0:T(8,128)(2,1)S(1)}, f16[2,72,1152]{2,1,0:T(8,128)(2,1)S(1)}, u32[]{:S(2)}, u32[]{:S(2)}) collective-permute-start(f16[2,72,1152]{2,1,0:T(8,128)(2,1)S(1)} %fusion.15), channel_id=1, source_target_pairs={{0,32},{32,128},{128,160},{160,0},{1,33},{33,129},{129,161},{161,1... | collective-permute-start | bytes 995336 | tf_op jit(solution)/shard_map/ppermute | solution.py:32
  49.0 9.4 %collective-permute-start.12 = (f16[2,72,1152]{2,1,0:T(8,128)(2,1)S(1)}, f16[2,72,1152]{2,1,0:T(8,128)(2,1)S(1)}, u32[]{:S(2)}, u32[]{:S(2)}) collective-permute-start(f16[2,72,1152]{2,1,0:T(8,128)(2,1)S(1)} %fusion.14), channel_id=1, source_target_pairs={{0,160},{32,0},{128,32},{160,128},{1,161},{33,1},{129,33},{161,129... | collective-permute-start | bytes 995336 | tf_op jit(solution)/shard_map/ppermute | solution.py:32
  55.4 8.8 %collective-permute-start.6 = (f16[1,72,1408]{2,1,0:T(8,128)(2,1)S(1)}, f16[1,72,1408]{2,1,0:T(8,128)(2,1)S(1)}, u32[]{:S(2)}, u32[]{:S(2)}) collective-permute-start(f16[1,72,1408]{2,1,0:T(8,128)(2,1)S(1)} %get-tuple-element.58), channel_id=1, source_target_pairs={{0,128},{32,160},{128,0},{160,32},{1,129},{33,161},{129,1},{161,33... | collective-permute-start | bytes 608264 | tf_op jit(solution)/shard_map/ppermute | solution.py:32
  55.8 11.0 %collective-permute-start.7 = (f16[1,72,1408]{2,1,0:T(8,128)(2,1)S(1)}, f16[1,72,1408]{2,1,0:T(8,128)(2,1)S(1)}, u32[]{:S(2)}, u32[]{:S(2)}) collective-permute-start(f16[1,72,1408]{2,1,0:T(8,128)(2,1)S(1)} %get-tuple-element.57), channel_id=1, source_target_pairs={{0,32},{32,128},{128,160},{160,0},{1,33},{33,129},{129,161},{161,1... | collective-permute-start | bytes 608264 | tf_op jit(solution)/shard_map/ppermute | solution.py:32
  58.0 8.8 %collective-permute-start.8 = (f16[1,72,1408]{2,1,0:T(8,128)(2,1)S(1)}, f16[1,72,1408]{2,1,0:T(8,128)(2,1)S(1)}, u32[]{:S(2)}, u32[]{:S(2)}) collective-permute-start(f16[1,72,1408]{2,1,0:T(8,128)(2,1)S(1)} %get-tuple-element.56), channel_id=1, source_target_pairs={{0,160},{32,0},{128,32},{160,128},{1,161},{33,1},{129,33},{161,129... | collective-permute-start | bytes 608264 | tf_op jit(solution)/shard_map/ppermute | solution.py:32
  59.0 7.9 %collective-permute-start.13 = (f16[1,72,1152]{2,1,0:T(8,128)(2,1)S(1)}, f16[1,72,1152]{2,1,0:T(8,128)(2,1)S(1)}, u32[]{:S(2)}, u32[]{:S(2)}) collective-permute-start(f16[1,72,1152]{2,1,0:T(8,128)(2,1)S(1)} %get-tuple-element.59), channel_id=1, source_target_pairs={{0,2},{1,3},{2,0},{3,1},{4,6},{5,7},{6,4},{7,5},{8,10},{9,11},{10,... | collective-permute-start | bytes 497672 | tf_op jit(solution)/shard_map/ppermute | solution.py:28
  60.8 6.9 %collective-permute-start.14 = (f16[1,72,1152]{2,1,0:T(8,128)(2,1)S(1)}, f16[1,72,1152]{2,1,0:T(8,128)(2,1)S(1)}, u32[]{:S(2)}, u32[]{:S(2)}) collective-permute-start(f16[1,72,1152]{2,1,0:T(8,128)(2,1)S(1)} %get-tuple-element.61), channel_id=1, source_target_pairs={{0,1},{1,2},{2,3},{3,0},{4,5},{5,6},{6,7},{7,4},{8,9},{9,10},{10,1... | collective-permute-start | bytes 497672 | tf_op jit(solution)/shard_map/ppermute | solution.py:28
  64.1 5.5 %collective-permute-start.15 = (f16[1,72,1152]{2,1,0:T(8,128)(2,1)S(1)}, f16[1,72,1152]{2,1,0:T(8,128)(2,1)S(1)}, u32[]{:S(2)}, u32[]{:S(2)}) collective-permute-start(f16[1,72,1152]{2,1,0:T(8,128)(2,1)S(1)} %get-tuple-element.60), channel_id=1, source_target_pairs={{0,3},{1,0},{2,1},{3,2},{4,7},{5,4},{6,5},{7,6},{8,11},{9,8},{10,9... | collective-permute-start | bytes 497672 | tf_op jit(solution)/shard_map/ppermute | solution.py:28
  69.7 20.8 %copy-start = (f32[6,2560]{1,0:T(8,128)S(1)}, f32[6,2560]{1,0:T(8,128)}, u32[]{:S(2)}) copy-start(f32[6,2560]{1,0:T(8,128)} %param.19) | copy-start | bytes 184324
  69.8 20.8 %copy-start.1 = (f32[6,2560]{1,0:T(8,128)S(1)}, f32[6,2560]{1,0:T(8,128)}, u32[]{:S(2)}) copy-start(f32[6,2560]{1,0:T(8,128)} %param.21) | copy-start | bytes 184324
  69.8 20.8 %copy-start.2 = (f32[6,2560]{1,0:T(8,128)S(1)}, f32[6,2560]{1,0:T(8,128)}, u32[]{:S(2)}) copy-start(f32[6,2560]{1,0:T(8,128)} %param.20) | copy-start | bytes 184324
  69.8 21.5 %copy-start.3 = (f32[3,2560]{1,0:T(4,128)S(1)}, f32[3,2560]{1,0:T(4,128)}, u32[]{:S(2)}) copy-start(f32[3,2560]{1,0:T(4,128)} %param.22) | copy-start | bytes 92164
  69.8 21.5 %copy-start.4 = (f32[3,2560]{1,0:T(4,128)S(1)}, f32[3,2560]{1,0:T(4,128)}, u32[]{:S(2)}) copy-start(f32[3,2560]{1,0:T(4,128)} %param.24) | copy-start | bytes 92164
  69.8 21.5 %copy-start.5 = (f32[3,2560]{1,0:T(4,128)S(1)}, f32[3,2560]{1,0:T(4,128)}, u32[]{:S(2)}) copy-start(f32[3,2560]{1,0:T(4,128)} %param.23) | copy-start | bytes 92164
  93.0 15.1 %all-to-all-start.1 = ((bf16[8,180,128]{2,1,0:T(8,128)(2,1)}), bf16[8,180,128]{2,1,0:T(8,128)(2,1)S(1)}, u32[]{:S(2)}, u32[]{:S(2)}) async-start(bf16[8,180,128]{2,1,0:T(8,128)(2,1)} %broadcast_in_dim.10), calls=%async_computation.1 | async-start | bytes 753664 | tf_op jit(solution)/shard_map/all_to_all | solution.py:216
  108.5 12.2 %collective-permute-start.18 = (bf16[72,2560]{1,0:T(8,128)(2,1)S(1)}, bf16[72,2560]{1,0:T(8,128)(2,1)S(1)}, u32[]{:S(2)}, u32[]{:S(2)}) collective-permute-start(bf16[72,2560]{1,0:T(8,128)(2,1)S(1)} %reshape.98), channel_id=1, source_target_pairs={{0,32},{32,0},{1,33},{33,1},{2,34},{34,2},{3,35},{35,3},{4,36},{36... | collective-permute-start | bytes 1105928 | tf_op jit(solution)/shard_map/ppermute | solution.py:36
  113.7 10.7 %collective-permute-start.19 = (bf16[72,2560]{1,0:T(8,128)(2,1)S(1)}, bf16[72,2560]{1,0:T(8,128)(2,1)S(1)}, u32[]{:S(2)}, u32[]{:S(2)}) collective-permute-start(bf16[72,2560]{1,0:T(8,128)(2,1)S(1)} %reshape.98), channel_id=1, source_target_pairs={{0,2},{1,3},{2,0},{3,1},{4,6},{5,7},{6,4},{7,5},{8,10},{9,11},{10,... | collective-permute-start | bytes 1105928 | tf_op jit(solution)/shard_map/ppermute | solution.py:28
  115.6 14.2 %collective-permute-start.16 = (bf16[72,2560]{1,0:T(8,128)(2,1)S(1)}, bf16[72,2560]{1,0:T(8,128)(2,1)S(1)}, u32[]{:S(2)}, u32[]{:S(2)}) collective-permute-start(bf16[72,2560]{1,0:T(8,128)(2,1)S(1)} %reshape.98), channel_id=1, source_target_pairs={{0,1},{1,2},{2,3},{3,0},{4,5},{5,6},{6,7},{7,4},{8,9},{9,10},{10,1... | collective-permute-start | bytes 1105928 | tf_op jit(solution)/shard_map/ppermute | solution.py:28
  117.7 12.1 %collective-permute-start.17 = (bf16[72,2560]{1,0:T(8,128)(2,1)S(1)}, bf16[72,2560]{1,0:T(8,128)(2,1)S(1)}, u32[]{:S(2)}, u32[]{:S(2)}) collective-permute-start(bf16[72,2560]{1,0:T(8,128)(2,1)S(1)} %reshape.98), channel_id=1, source_target_pairs={{0,3},{1,0},{2,1},{3,2},{4,7},{5,4},{6,5},{7,6},{8,11},{9,8},{10,9... | collective-permute-start | bytes 1105928 | tf_op jit(solution)/shard_map/ppermute | solution.py:28
  124.4 13.0 %collective-permute-start.22 = (bf16[72,2560]{1,0:T(8,128)(2,1)S(1)}, bf16[72,2560]{1,0:T(8,128)(2,1)S(1)}, u32[]{:S(2)}, u32[]{:S(2)}) collective-permute-start(bf16[72,2560]{1,0:T(8,128)(2,1)S(1)} %collective-permute-done.18), channel_id=1, source_target_pairs={{0,3},{1,0},{2,1},{3,2},{4,7},{5,4},{6,5},{7,6},{8,11},{9,8},{10,9... | collective-permute-start | bytes 1105928 | tf_op jit(solution)/shard_map/ppermute | solution.py:28
  126.4 11.0 %collective-permute-start.20 = (bf16[72,2560]{1,0:T(8,128)(2,1)S(1)}, bf16[72,2560]{1,0:T(8,128)(2,1)S(1)}, u32[]{:S(2)}, u32[]{:S(2)}) collective-permute-start(bf16[72,2560]{1,0:T(8,128)(2,1)S(1)} %collective-permute-done.18), channel_id=1, source_target_pairs={{0,1},{1,2},{2,3},{3,0},{4,5},{5,6},{6,7},{7,4},{8,9},{9,10},{10,1... | collective-permute-start | bytes 1105928 | tf_op jit(solution)/shard_map/ppermute | solution.py:28
  129.8 7.6 %collective-permute-start.21 = (bf16[72,2560]{1,0:T(8,128)(2,1)S(1)}, bf16[72,2560]{1,0:T(8,128)(2,1)S(1)}, u32[]{:S(2)}, u32[]{:S(2)}) collective-permute-start(bf16[72,2560]{1,0:T(8,128)(2,1)S(1)} %collective-permute-done.19), channel_id=1, source_target_pairs={{0,32},{32,0},{1,33},{33,1},{2,34},{34,2},{3,35},{35,3},{4,36},{36... | collective-permute-start | bytes 1105928 | tf_op jit(solution)/shard_map/ppermute | solution.py:36
